TPU v7x, 32 devices: a whole 2x2x4 slice. The times are simulated.
32 devices in a mesh: dp: 16 (over z, y, x), mod: 2 (over core).
Axes of the slice: x: 2, y: 2, z: 4, core: 2. Of those that a mesh axis runs over, the one named last changes fastest.
Arguments:
- latents: float32 [128, 256, 16], P(('dp', 'mod')), may hold values from -6 to 6
- noise: float32 [128, 256, 16], P(('dp', 'mod')), may hold values from -6 to 6
- timesteps: int32 [128], P(('dp', 'mod')), may hold values from 0 to 999
- labels: int32 [128], P(('dp', 'mod')), may hold values from 0 to 999
- drops: int32 [128], P(('dp', 'mod')), may hold values 0 or 1
- block_weights: float32 [1152, 13824], P('dp'), may hold values from -0.1875 to 0.1875
- block_first: float32 [1152, 13824], P('dp'), may hold values from -5.722046e-06 to 5.722046e-06
- block_second: float32 [1152, 13824], P('dp'), may hold values from 8.512235e-14 to 3.404894e-13
- mod_weights: float32 [1152, 9216], P('dp', 'mod'), may hold values from -0.1875 to 0.1875
- mod_first: float32 [1152, 9216], P('dp', 'mod'), may hold values from -5.722046e-06 to 5.722046e-06
- mod_second: float32 [1152, 9216], P('dp', 'mod'), may hold values from 8.512235e-14 to 3.404894e-13
- embed_weights: float32 [2441, 1152], P(None, 'dp'), may hold values from -0.375 to 0.375
- embed_first: float32 [2441, 1152], P(None, 'dp'), may hold values from -5.722046e-06 to 5.722046e-06
- embed_second: float32 [2441, 1152], P(None, 'dp'), may hold values from 8.512235e-14 to 3.404894e-13
- rel_bias: float32 [16, 961], replicated, may hold values from -3 to 3
- rel_first: float32 [16, 961], replicated, may hold values from -3.545532e-08 to 3.545532e-08
- rel_second: float32 [16, 961], replicated, may hold values from 1.2681992e-20 to 1.298636e-17
Outputs:
- loss_sum: float32 [], replicated
- grad_norm: float32 [], replicated
- matrix_norms: float32 [2, 12], replicated
- block_new: float32 [1152, 13824], P('dp')
- block_first_new: float32 [1152, 13824], P('dp')
- block_second_new: float32 [1152, 13824], P('dp')
- block_copy: bfloat16 [1152, 13824], P('dp')
- mod_new: float32 [1152, 9216], P('dp', 'mod')
- mod_first_new: float32 [1152, 9216], P('dp', 'mod')
- mod_second_new: float32 [1152, 9216], P('dp', 'mod')
- mod_copy: bfloat16 [1152, 9216], P('dp', 'mod')
- embed_new: float32 [2441, 1152], P(None, 'dp')
- embed_first_new: float32 [2441, 1152], P(None, 'dp')
- embed_second_new: float32 [2441, 1152], P(None, 'dp')
- embed_copy: bfloat16 [2441, 1152], P(None, 'dp')
- rel_new: float32 [16, 961], replicated
- rel_first_new: float32 [16, 961], replicated
- rel_second_new: float32 [16, 961], replicated
- rel_copy: bfloat16 [16, 961], replicated
- rel_clipped: float32 [16, 961], replicated
All inputs are finite; a program needn't handle non-finite values. No bound on the sum of `drops` on one device may be relied on, other than what follows from the above.
Results may differ from a plain program's by a relative error of at most 0.023.
Values may be sent and summed in bfloat16 or wider, within the bound.
No kernel may reach another device: no remote copies, remote signals or barrier semaphores. Data moves between devices by JAX's collectives and lax.ppermute only.
A program may use at most 280 MiB of HBM per device.

v0:
```python
import math

import jax
import jax.numpy as jnp
from jax import lax
from jax.sharding import PartitionSpec as P

D = 1152
HEADS = 16
HD = 72
MLPW = 4608
NCLASS = 1000
FREQ = 256
GRID = 16
PDIM = 16
NSTEPS = 1000
STEP = 10
MB = 2


FIRST_DECAY = 0.9
SECOND_DECAY = 0.999
ADAM_EPSILON = 1e-08
WEIGHT_DECAY = 0.01
LEARN_RATE = 0.25
CLIP_NORM = 0.05
HIGH = lax.Precision.HIGHEST


def dense(left, right):
    return jnp.dot(left, right, preferred_element_type=jnp.float32)


def dense_trans(left, right):
    return lax.dot_general(
        left, right, (((left.ndim - 1,), (1,)), ((), ())), preferred_element_type=jnp.float32
    )


def outer_sum(left, right):
    flat_left = left.reshape(-1, left.shape[-1])
    flat_right = right.reshape(-1, right.shape[-1])
    return lax.dot_general(
        flat_left, flat_right, (((0,), (0,)), ((), ())), preferred_element_type=jnp.float32
    )


def first_contract(left, right):
    return lax.dot_general(
        left, right, (((0,), (0,)), ((), ())), precision=HIGH, preferred_element_type=jnp.float32
    )


def layer_norm(values):
    center = values - jnp.mean(values, -1, keepdims=True)
    inverse = lax.rsqrt(jnp.mean(center * center, -1, keepdims=True) + 1e-06)
    return (center * inverse, inverse)


def norm_back(upstream, normed, inverse):
    return inverse * (
        upstream
        - jnp.mean(upstream, -1, keepdims=True)
        - normed * jnp.mean(upstream * normed, -1, keepdims=True)
    )


def silu_slope(values):
    sigma = jax.nn.sigmoid(values)
    return sigma * (1.0 + values * (1.0 - sigma))


def plan_table():
    betas = jnp.linspace(0.0001, 0.02, NSTEPS, dtype=jnp.float32)
    return jnp.exp(jnp.cumsum(jnp.log(1.0 - betas)))


def sinusoid(steps):
    half_width = FREQ // 2
    freqs = jnp.exp(-math.log(10000.0) * jnp.arange(half_width, dtype=jnp.float32) / half_width)
    angles = steps.astype(jnp.float32)[:, None] * freqs[None, :]
    return jnp.concatenate([jnp.cos(angles), jnp.sin(angles)], 1)


def relative_index():
    places = jnp.arange(GRID * GRID, dtype=jnp.int32)
    rows_of = places // GRID
    cols_of = places % GRID
    offset = (rows_of[:, None] - rows_of[None, :] + GRID - 1) * (2 * GRID - 1)
    return offset + cols_of[:, None] - cols_of[None, :] + GRID - 1


def fetch_weights(block_weights, mod_weights, embed_weights):
    return (
        lax.all_gather(block_weights.astype(jnp.bfloat16), "dp", axis=0, tiled=True),
        lax.all_gather(mod_weights.astype(jnp.bfloat16), "dp", axis=0, tiled=True),
        lax.all_gather(embed_weights.astype(jnp.bfloat16), "dp", axis=1, tiled=True),
    )


def reduce_grads(grads):
    return (
        lax.psum_scatter(grads[0], "dp", scatter_dimension=0, tiled=True),
        lax.psum_scatter(grads[1], "dp", scatter_dimension=0, tiled=True),
        lax.psum_scatter(grads[2], "dp", scatter_dimension=1, tiled=True),
    )


def split_block(block_low):
    return (
        block_low[:, : 3 * D],
        block_low[:, 3 * D : 4 * D],
        block_low[:, 4 * D : 4 * D + MLPW],
        block_low[:, 4 * D + MLPW :],
    )


def attention_scores(query, keys, position_bias):
    scores = jnp.einsum("bqhd,bkhd->bhqk", query, keys, preferred_element_type=jnp.float32)
    return scores * HD ** (-0.5) + position_bias[None]


def block_forward(hidden0, modulation, block_low, position_bias):
    w_qkv, w_proj, w_in, w_out = split_block(block_low)
    batch, length = (hidden0.shape[0], hidden0.shape[1])
    normed1, inverse1 = layer_norm(hidden0)
    attn_in = (normed1 * (1.0 + modulation[:, 1:2]) + modulation[:, 0:1]).astype(jnp.bfloat16)
    qkv = dense(attn_in, w_qkv).astype(jnp.bfloat16).reshape(batch, length, 3, HEADS, HD)
    query, keys, values = (qkv[:, :, 0], qkv[:, :, 1], qkv[:, :, 2])
    scores = attention_scores(query, keys, position_bias)
    log_total = jax.nn.logsumexp(scores, -1, keepdims=True)
    probs = jnp.exp(scores - log_total).astype(jnp.bfloat16)
    attn_out = jnp.einsum("bhqk,bkhd->bqhd", probs, values, preferred_element_type=jnp.float32)
    attn_out = attn_out.astype(jnp.bfloat16).reshape(batch, length, D)
    branch_one = dense(attn_out, w_proj)
    hidden1 = hidden0 + modulation[:, 2:3] * branch_one
    normed2, inverse2 = layer_norm(hidden1)
    mlp_in = (normed2 * (1.0 + modulation[:, 4:5]) + modulation[:, 3:4]).astype(jnp.bfloat16)
    pre_act = dense(mlp_in, w_in)
    act = jax.nn.gelu(pre_act, approximate=True).astype(jnp.bfloat16)
    branch_two = dense_trans(act, w_out)
    hidden2 = hidden1 + modulation[:, 5:6] * branch_two
    kept = (
        normed1,
        inverse1,
        attn_in,
        query,
        keys,
        values,
        log_total,
        attn_out,
        branch_one,
        normed2,
        inverse2,
        mlp_in,
        pre_act,
        act,
        branch_two,
    )
    return (hidden2, kept)


def block_backward(d_hidden2, kept, modulation, block_low, position_bias):
    (
        normed1,
        inverse1,
        attn_in,
        query,
        keys,
        values,
        log_total,
        attn_out,
        branch_one,
        normed2,
        inverse2,
        mlp_in,
        pre_act,
        act,
        branch_two,
    ) = kept
    w_qkv, w_proj, w_in, w_out = split_block(block_low)
    batch, length = (attn_in.shape[0], attn_in.shape[1])
    d_branch_two = (modulation[:, 5:6] * d_hidden2).astype(jnp.bfloat16)
    d_gate2 = jnp.sum(d_hidden2 * branch_two, 1)
    d_act = dense(d_branch_two, w_out)
    g_out = outer_sum(d_branch_two, act)
    gelu_pull = jax.vjp(lambda entries: jax.nn.gelu(entries, approximate=True), pre_act)[1]
    d_pre = gelu_pull(d_act)[0].astype(jnp.bfloat16)
    d_mlp_in = dense_trans(d_pre, w_in)
    g_in = outer_sum(mlp_in, d_pre)
    d_scale2 = jnp.sum(d_mlp_in * normed2, 1)
    d_shift2 = jnp.sum(d_mlp_in, 1)
    d_hidden1 = d_hidden2 + norm_back(d_mlp_in * (1.0 + modulation[:, 4:5]), normed2, inverse2)
    d_branch_one = (modulation[:, 2:3] * d_hidden1).astype(jnp.bfloat16)
    d_gate1 = jnp.sum(d_hidden1 * branch_one, 1)
    d_attn_out = dense_trans(d_branch_one, w_proj).astype(jnp.bfloat16)
    g_proj = outer_sum(attn_out, d_branch_one)
    scores = attention_scores(query, keys, position_bias)
    probs = jnp.exp(scores - log_total)
    d_heads = d_attn_out.reshape(batch, length, HEADS, HD)
    d_probs = jnp.einsum("bqhd,bkhd->bhqk", d_heads, values, preferred_element_type=jnp.float32)
    d_scores = (probs * (d_probs - jnp.sum(probs * d_probs, -1, keepdims=True))).astype(
        jnp.bfloat16
    )
    d_bias = jnp.sum(d_scores.astype(jnp.float32), 0)
    d_query = jnp.einsum(
        "bhqk,bkhd->bqhd", d_scores, keys, preferred_element_type=jnp.float32
    ) * HD ** (-0.5)
    d_keys = jnp.einsum(
        "bhqk,bqhd->bkhd", d_scores, query, preferred_element_type=jnp.float32
    ) * HD ** (-0.5)
    d_values = jnp.einsum(
        "bhqk,bqhd->bkhd", probs.astype(jnp.bfloat16), d_heads, preferred_element_type=jnp.float32
    )
    d_qkv = (
        jnp.stack([d_query, d_keys, d_values], 2).astype(jnp.bfloat16).reshape(batch, length, 3 * D)
    )
    d_attn_in = dense_trans(d_qkv, w_qkv)
    g_qkv = outer_sum(attn_in, d_qkv)
    d_scale1 = jnp.sum(d_attn_in * normed1, 1)
    d_shift1 = jnp.sum(d_attn_in, 1)
    d_hidden0 = d_hidden1 + norm_back(d_attn_in * (1.0 + modulation[:, 1:2]), normed1, inverse1)
    d_modulation = jnp.stack([d_shift1, d_scale1, d_gate1, d_shift2, d_scale2, d_gate2], 1)
    g_block = jnp.concatenate([g_qkv, g_proj, g_in, g_out], 1)
    return (d_hidden0, d_modulation, g_block, d_bias)


def part_squares(block_part, mod_part, embed_part, first_core, core_index):
    column_sq = jnp.sum(block_part * block_part, 0)
    block_terms = [
        jnp.sum(column_sq[: 3 * D]),
        jnp.sum(column_sq[3 * D : 4 * D]),
        jnp.sum(column_sq[4 * D : 4 * D + MLPW]),
        jnp.sum(column_sq[4 * D + MLPW :]),
    ]
    mod_sq = jnp.sum(mod_part * mod_part, 0)
    global_cols = core_index * mod_part.shape[1] + jnp.arange(mod_part.shape[1], dtype=jnp.int32)
    first_mod = jnp.sum(jnp.where(global_cols < 6 * D, mod_sq, 0.0))
    second_mod = jnp.sum(jnp.where(global_cols < 6 * D, 0.0, mod_sq))
    row_sq = jnp.sum(embed_part * embed_part, 1)
    bounds = [
        0,
        NCLASS + 1,
        NCLASS + 1 + FREQ,
        NCLASS + 1 + FREQ + D,
        NCLASS + 1 + FREQ + D + PDIM,
        NCLASS + 1 + FREQ + D + 2 * PDIM,
    ]
    embed_terms = [jnp.sum(row_sq[bounds[pos] : bounds[pos + 1]]) for pos in range(5)]
    replicated = jnp.stack(block_terms + embed_terms) * first_core
    return jnp.concatenate([replicated[:4], jnp.stack([first_mod, second_mod]), replicated[4:]])


def adam_update(grad, first, second, weight, clip):
    first_new = FIRST_DECAY * first + (1.0 - FIRST_DECAY) * (grad * clip)
    second_new = SECOND_DECAY * second + (1.0 - SECOND_DECAY) * (grad * clip) ** 2
    update = (
        first_new
        / (1.0 - FIRST_DECAY**STEP)
        / (jnp.sqrt(second_new / (1.0 - SECOND_DECAY**STEP)) + ADAM_EPSILON)
        + WEIGHT_DECAY * weight
    )
    return (first_new, second_new, update)


def on_device(
    latents,
    noise,
    timesteps,
    labels,
    drops,
    block_weights,
    block_first,
    block_second,
    mod_weights,
    mod_first,
    mod_second,
    embed_weights,
    embed_first,
    embed_second,
    rel_bias,
    rel_first,
    rel_second,
):
    core_index = lax.axis_index("mod")
    images_here = latents.shape[0]
    per_micro = images_here // MB
    count = float(
        images_here
        * lax.axis_size("dp")
        * lax.axis_size("mod")
        * latents.shape[1]
        * latents.shape[2]
    )
    rel_ids = relative_index()
    position_bias = rel_bias[:, rel_ids]
    alpha_table = plan_table()
    start = NCLASS + 1
    grad_total = None
    loss_total = jnp.zeros((), jnp.float32)
    bias_grad = jnp.zeros(position_bias.shape, jnp.float32)
    for micro_step in range(MB):
        first_row = micro_step * per_micro
        latent = latents[first_row : first_row + per_micro]
        noisy = noise[first_row : first_row + per_micro]
        steps_here = timesteps[first_row : first_row + per_micro]
        chosen = jnp.where(
            drops[first_row : first_row + per_micro] == 1,
            NCLASS,
            labels[first_row : first_row + per_micro],
        )
        weights = fetch_weights(block_weights, mod_weights, embed_weights)
        block_low, mod_low, embed_low = weights
        table = embed_low[:start]
        time_in = embed_low[start : start + FREQ].astype(jnp.float32)
        time_out = embed_low[start + FREQ : start + FREQ + D].astype(jnp.float32)
        patch = embed_low[start + FREQ + D : start + FREQ + D + PDIM]
        head = embed_low[start + FREQ + D + PDIM :]
        sinus = sinusoid(steps_here)
        pre_time = jnp.dot(sinus, time_in, precision=HIGH, preferred_element_type=jnp.float32)
        time_act = jax.nn.silu(pre_time)
        onehot = chosen[:, None] == jnp.arange(NCLASS + 1, dtype=jnp.int32)[None, :]
        class_embed = dense(onehot.astype(jnp.bfloat16), table)
        cond = (
            jnp.dot(time_act, time_out, precision=HIGH, preferred_element_type=jnp.float32)
            + class_embed
        )
        scaled = jax.nn.silu(cond).astype(jnp.bfloat16)
        paired = lax.all_gather(scaled, "mod", axis=0, tiled=True)
        half_mod = dense(paired, mod_low)
        modulation = lax.all_to_all(
            half_mod, "mod", split_axis=0, concat_axis=1, tiled=True
        ).reshape(per_micro, 8, D)
        alpha_bar = jnp.sum(
            jnp.where(
                steps_here[:, None] == jnp.arange(NSTEPS, dtype=jnp.int32)[None, :],
                alpha_table[None, :],
                0.0,
            ),
            1,
        )
        mixed = (
            jnp.sqrt(alpha_bar)[:, None, None] * latent
            + jnp.sqrt(1.0 - alpha_bar)[:, None, None] * noisy
        )
        mixed = mixed.astype(jnp.bfloat16)
        hidden0 = dense(mixed, patch)
        hidden2, kept = block_forward(hidden0, modulation, block_low, position_bias)
        normed3, inverse3 = layer_norm(hidden2)
        final_in = (normed3 * (1.0 + modulation[:, 7:8]) + modulation[:, 6:7]).astype(jnp.bfloat16)
        predicted = dense_trans(final_in, head)
        error = predicted - noisy
        loss_total = loss_total + jnp.sum(error * error)
        d_predicted = (error * (2.0 / count)).astype(jnp.bfloat16)
        d_final = dense(d_predicted, head)
        g_head = outer_sum(d_predicted, final_in)
        d_scale3 = jnp.sum(d_final * normed3, 1)
        d_shift3 = jnp.sum(d_final, 1)
        d_hidden2 = norm_back(d_final * (1.0 + modulation[:, 7:8]), normed3, inverse3)
        weights = fetch_weights(block_weights, mod_weights, embed_weights)
        block_low, mod_low, embed_low = weights
        d_hidden0, d_mod_block, g_block, d_bias = block_backward(
            d_hidden2, kept, modulation, block_low, position_bias
        )
        bias_grad = bias_grad + d_bias
        g_patch = outer_sum(mixed, d_hidden0.astype(jnp.bfloat16))
        d_modulation = jnp.concatenate([d_mod_block, jnp.stack([d_shift3, d_scale3], 1)], 1)
        d_modulation = d_modulation.reshape(per_micro, 8 * D).astype(jnp.bfloat16)
        back_mod = lax.all_to_all(d_modulation, "mod", split_axis=1, concat_axis=0, tiled=True)
        g_mod = outer_sum(paired, back_mod)
        d_paired = dense_trans(back_mod, mod_low)
        d_scaled = lax.psum_scatter(d_paired, "mod", scatter_dimension=0, tiled=True)
        d_cond = d_scaled * silu_slope(cond)
        g_table = first_contract(onehot.astype(jnp.float32), d_cond)
        g_time_out = first_contract(time_act, d_cond)
        d_time = lax.dot_general(
            d_cond,
            time_out,
            (((1,), (1,)), ((), ())),
            precision=HIGH,
            preferred_element_type=jnp.float32,
        )
        g_time_in = first_contract(sinus, d_time * silu_slope(pre_time))
        g_embed = jnp.concatenate([g_table, g_time_in, g_time_out, g_patch, g_head], 0)
        grads = (g_block, g_mod, g_embed)
        grads = reduce_grads(grads)
        if grad_total is None:
            grad_total = grads
        else:
            grad_total = jax.tree.map(jnp.add, grad_total, grads)
    block_grad, mod_grad, embed_grad = grad_total
    block_grad, embed_grad = (
        lax.psum(block_grad.astype(jnp.bfloat16), "mod").astype(jnp.float32),
        lax.psum(embed_grad.astype(jnp.bfloat16), "mod").astype(jnp.float32),
    )
    rel_pull = jax.vjp(lambda entries: entries[:, rel_ids], rel_bias)[1]
    rel_local = rel_pull(bias_grad)[0]
    rel_grad, loss_sum = lax.psum((rel_local, loss_total), ("dp", "mod"))
    first_core = (core_index == 0).astype(jnp.float32)
    grad_parts, weight_parts = lax.psum(
        (
            part_squares(block_grad, mod_grad, embed_grad, first_core, core_index),
            part_squares(block_weights, mod_weights, embed_weights, first_core, core_index),
        ),
        ("dp", "mod"),
    )
    grad_sq = jnp.concatenate([grad_parts, jnp.sum(rel_grad * rel_grad)[None]])
    weight_sq = jnp.concatenate([weight_parts, jnp.sum(rel_bias * rel_bias)[None]])
    grad_norm = jnp.sqrt(jnp.sum(grad_sq))
    clip = jnp.minimum(1.0, CLIP_NORM / grad_norm)
    block_m, block_s, block_step = adam_update(
        block_grad, block_first, block_second, block_weights, clip
    )
    mod_m, mod_s, mod_step = adam_update(mod_grad, mod_first, mod_second, mod_weights, clip)
    embed_m, embed_s, embed_step = adam_update(
        embed_grad, embed_first, embed_second, embed_weights, clip
    )
    rel_m, rel_s, rel_step = adam_update(rel_grad, rel_first, rel_second, rel_bias, clip)
    update_parts = lax.psum(
        part_squares(block_step, mod_step, embed_step, first_core, core_index), ("dp", "mod")
    )
    update_sq = jnp.concatenate([update_parts, jnp.sum(rel_step * rel_step)[None]])
    weight_norm = jnp.sqrt(weight_sq)
    update_norm = jnp.sqrt(update_sq)
    ratio = weight_norm / update_norm
    block_ratio = jnp.concatenate(
        [
            jnp.broadcast_to(ratio[0], (3 * D,)),
            jnp.broadcast_to(ratio[1], (D,)),
            jnp.broadcast_to(ratio[2], (MLPW,)),
            jnp.broadcast_to(ratio[3], (MLPW,)),
        ]
    )
    global_cols = core_index * mod_weights.shape[1] + jnp.arange(
        mod_weights.shape[1], dtype=jnp.int32
    )
    mod_ratio = jnp.where(global_cols < 6 * D, ratio[4], ratio[5])
    embed_ratio = jnp.concatenate(
        [
            jnp.broadcast_to(ratio[6], (NCLASS + 1,)),
            jnp.broadcast_to(ratio[7], (FREQ,)),
            jnp.broadcast_to(ratio[8], (D,)),
            jnp.broadcast_to(ratio[9], (PDIM,)),
            jnp.broadcast_to(ratio[10], (PDIM,)),
        ]
    )
    block_new = block_weights - LEARN_RATE * block_ratio[None, :] * block_step
    mod_new = mod_weights - LEARN_RATE * mod_ratio[None, :] * mod_step
    embed_new = embed_weights - LEARN_RATE * embed_ratio[:, None] * embed_step
    rel_new = rel_bias - LEARN_RATE * ratio[11] * rel_step
    matrix_norms = jnp.stack([weight_norm, update_norm])
    return (
        loss_sum,
        grad_norm,
        matrix_norms,
        block_new,
        block_m,
        block_s,
        block_new.astype(jnp.bfloat16),
        mod_new,
        mod_m,
        mod_s,
        mod_new.astype(jnp.bfloat16),
        embed_new,
        embed_m,
        embed_s,
        embed_new.astype(jnp.bfloat16),
        rel_new,
        rel_m,
        rel_s,
        rel_new.astype(jnp.bfloat16),
        rel_grad * clip,
    )


def solution(mesh):
    placed = (
        P(("dp", "mod"), None, None),
        P(("dp", "mod"), None, None),
        P(("dp", "mod")),
        P(("dp", "mod")),
        P(("dp", "mod")),
        P("dp", None),
        P("dp", None),
        P("dp", None),
        P("dp", "mod"),
        P("dp", "mod"),
        P("dp", "mod"),
        P(None, "dp"),
        P(None, "dp"),
        P(None, "dp"),
        P(),
        P(),
        P(),
    )
    return jax.shard_map(
        on_device,
        mesh=mesh,
        in_specs=placed,
        out_specs=(
            P(),
            P(),
            P(),
            P("dp", None),
            P("dp", None),
            P("dp", None),
            P("dp", None),
            P("dp", "mod"),
            P("dp", "mod"),
            P("dp", "mod"),
            P("dp", "mod"),
            P(None, "dp"),
            P(None, "dp"),
            P(None, "dp"),
            P(None, "dp"),
            P(),
            P(),
            P(),
            P(),
            P(),
        ),
        check_vma=False,
    )
```

profile of v0, /device:TPU:0, one launch (start us, length us, event | category | flops | bytes accessed | tf_op | source)
XLA Modules:
  0.0 2713.7 jit_solution(5024839799057778659)
XLA Ops:
  15.0 215.5 %gather_fusion = f32[65536,16]{1,0:T(8,128)} fusion(f32[16,961]{0,1:T(8,128)S(1)} %copy.401, s32[65536]{0:T(1024)S(1)} %broadcast_clamp_fusion), kind=kCustom, calls=%fused_computation | custom fusion | bytes 8650752 | tf_op jit(solution)/shard_map/gather | solution.py:296
  230.6 20.1 copy.402
  304.8 271.6 %all-gather.10.cloned.1.call-done = bf16[1152,13824]{1,0:T(8,128)(2,1)} async-done(((bf16[72,13824]{1,0:T(8,128)(2,1)}), bf16[1152,13824]{1,0:T(8,128)(2,1)}) %all-gather.10.cloned.1.call-update) | async-done | bytes 31850512 | tf_op jit(solution)/shard_map/all_gather | solution.py:95
  640.2 12.8 fusion.26
  652.9 16.8 fusion.114
  678.6 17.1 fusion.13
  695.8 12.8 multiply_reduce_fusion.7
  745.6 13.0 fusion.27
  758.7 17.5 fusion.112
  786.2 17.2 fusion.6
  803.4 13.3 multiply_reduce_fusion.13
  840.0 18.1 convert_reduce_fusion
  958.2 33.4 %concatenate.94 = f32[2441,1152]{1,0:T(8,128)} concatenate(f32[1001,1152]{1,0:T(8,128)} %fusion.71, f32[256,1152]{1,0:T(8,128)S(1)} %fusion.85, f32[1152,1152]{1,0:T(8,128)} %fusion.98, f32[16,1152]{1,0:T(8,128)} %convolution_bitcast_fusion.5, f32[16,1152]{1,0:T(8,128)} %convolution_bitcast_fusion.4), dimensions={0} | concatenate | bytes 22496256 | tf_op jit(solution)/shard_map/concatenate | solution.py:384
  991.6 33.0 %concatenate.92 = f32[2441,1152]{1,0:T(8,128)} concatenate(f32[1001,1152]{1,0:T(8,128)} %fusion.72, f32[256,1152]{1,0:T(8,128)S(1)} %copy-done.52, f32[1152,1152]{1,0:T(8,128)} %fusion.101, f32[16,1152]{1,0:T(8,128)S(1)} %copy-done.80, f32[16,1152]{1,0:T(8,128)S(1)} %copy-done.81), dimensions={0} | concatenate | bytes 22496256 | tf_op jit(solution)/shard_map/concatenate | solution.py:384
  1037.2 13.4 copy.461
  1085.8 13.4 convolution_bitcast_fusion.2
  1138.3 60.0 %maximum_add_fusion = f32[1152,13824]{1,0:T(8,128)} fusion(f32[1152,4608]{1,0:T(8,128)} %convolution_bitcast_fusion.2, f32[1152,4608]{1,0:T(8,128)} %convolution_bitcast_fusion.3, f32[1152,1152]{1,0:T(8,128)S(1)} %bitcast.433, f32[1152,3456]{1,0:T(8,128)} %fusion.123, f32[1152,4608]{1,0:T(8,128)} %convolution_bitcast_fusion, ...), kind=kLoop, calls=%fused_computation.2 | loop fusion | flops 111476736 | bytes 191102976 | tf_op jit(solution)/shard_map/add | solution.py:390
  1208.1 13.9 convolution_add_fusion
  1222.1 21.4 reduce-scatter.10.cloned.1.call-done
  1245.3 917.3 %reduce-scatter.12.cloned.1.call-done = f32[72,13824]{1,0:T(8,128)} async-done(((f32[1152,13824]{1,0:T(8,128)}), f32[72,13824]{1,0:T(8,128)}) %reduce-scatter.12.cloned.1.call-update) | async-done | bytes 3981328
  2172.4 17.7 copy.460
  2190.1 347.5 %scatter_custom_fusion = f32[16,961]{0,1:T(8,128)S(1)} fusion(s32[65536]{0:T(1024)} %bitcast.447, f32[65536,16]{1,0:T(8,128)} %bitcast.405, f32[]{:T(128)} %constant.166.clone.1), kind=kCustom, calls=%fused_computation.195 | custom fusion | flops 1048576 | bytes 62016 | tf_op jit(solution)/shard_map/transpose(jvp())/scatter-add | solution.py:396
  2556.3 40.9 %all-reduce.5 = (f32[11]{0:T(128)S(1)}, f32[16,961]{1,0:T(8,128)S(1)}) all-reduce(f32[11]{0:T(128)S(1)} %pad_maximum_fusion.7, f32[16,961]{1,0:T(8,128)S(1)} %copy.441), channel_id=1, replica_groups=mesh['dp'=16,'mod'=2] {'dp','mod'}, use_global_device_ids=true, to_apply=%region_77.78 | all-reduce | flops 15387 | bytes 123096 | tf_op jit(solution)/shard_map/psum | solution.py:400
  2640.6 39.3 %all-reduce.4 = (f32[]{:T(128)}, f32[11]{0:T(128)S(1)}, f32[11]{0:T(128)S(1)}) all-reduce(f32[]{:T(128)S(6)} %add.524, f32[11]{0:T(128)S(1)} %pad_maximum_fusion.9, f32[11]{0:T(128)S(1)} %pad_maximum_fusion.8), channel_id=1, replica_groups=mesh['dp'=16,'mod'=2] {'dp','mod'}, use_global_device_ids=true, to_apply=%region_22.23 | all-reduce | flops 23 | bytes 184 | tf_op jit(solution)/shard_map/psum | solution.py:398
  (652 shorter events, 494.8 us)
Async XLA Ops:
  7.2 245.7 %all-gather.6.cloned.1.call-start = ((), (), s32[]{:S(2)}) async-start(), calls=%async_computation.7 | async-start | bytes 6266880 | tf_op jit(solution)/shard_map/all_gather | solution.py:97
  9.3 271.7 %all-gather.8.cloned.1.call-start = ((), (), s32[]{:S(2)}) async-start(), calls=%async_computation.8 | async-start | bytes 11280384 | tf_op jit(solution)/shard_map/all_gather | solution.py:96
  10.3 566.2 %all-gather.10.cloned.1.call-start = ((), (), s32[]{:S(2)}) async-start(), calls=%async_computation.9 | async-start | bytes 33841152 | tf_op jit(solution)/shard_map/all_gather | solution.py:95
  14.7 215.8 %copy-start.69 = (s32[32,2,8,128]{3,1,2,0:T(2,128)}, s32[32,2,8,128]{3,1,2,0:T(2,128)S(1)}, u32[]{:S(2)}) copy-start(s32[32,2,8,128]{3,1,2,0:T(2,128)S(1)} %copy.472) | copy-start | bytes 786436
  276.3 357.6 %copy-start.4 = (f32[2,256,1152]{2,1,0:T(8,128)}, f32[2,256,1152]{2,1,0:T(8,128)S(1)}, u32[]{:S(2)}) copy-start(f32[2,256,1152]{2,1,0:T(8,128)S(1)} %get-tuple-element.293) | copy-start | bytes 7077892
  287.2 9.5 all-to-all-start.1
  296.8 4.7 all-to-all-start
  300.1 943.3 %reduce-scatter.10.cloned.1.call-start = ((), (), s32[]{:S(2)}) async-start(), calls=%async_computation.11 | async-start | bytes 12533760
  304.8 281.2 %copy-start.62 = (bf16[2,256,1152]{2,1,0:T(8,128)(2,1)}, bf16[2,256,1152]{2,1,0:T(8,128)(2,1)S(1)}, u32[]{:S(2)}) copy-start(bf16[2,256,1152]{2,1,0:T(8,128)(2,1)S(1)} %add_convert_fusion.7) | copy-start | bytes 3538948
  618.3 104.1 %copy-start.74 = (f32[2,16,256]{2,1,0:T(8,128)}, f32[2,16,256]{2,1,0:T(8,128)S(1)}, u32[]{:S(2)}) copy-start(f32[2,16,256]{2,1,0:T(8,128)S(1)} %log_add_fusion) | copy-start | bytes 98308
  639.4 69.2 %copy-start.130 = (f32[2,256]{1,0:T(2,128)}, f32[2,256]{1,0:T(2,128)S(1)}, u32[]{:S(2)}) copy-start(f32[2,256]{1,0:T(2,128)S(1)} %broadcast_multiply_fusion.15) | copy-start | bytes 6148
  639.8 68.8 %copy-start.150 = (f32[2,256]{1,0:T(2,128)}, f32[2,256]{1,0:T(2,128)S(1)}, u32[]{:S(2)}) copy-start(f32[2,256]{1,0:T(2,128)S(1)} %add_rsqrt_fusion.1) | copy-start | bytes 6148
  744.9 71.8 %copy-start.132 = (f32[2,256]{1,0:T(2,128)}, f32[2,256]{1,0:T(2,128)S(1)}, u32[]{:S(2)}) copy-start(f32[2,256]{1,0:T(2,128)S(1)} %broadcast_multiply_fusion.18) | copy-start | bytes 6148
  745.3 71.4 %copy-start.152 = (f32[2,256]{1,0:T(2,128)}, f32[2,256]{1,0:T(2,128)S(1)}, u32[]{:S(2)}) copy-start(f32[2,256]{1,0:T(2,128)S(1)} %add_rsqrt_fusion.4) | copy-start | bytes 6148
  958.2 33.4 %copy-start.80 = (f32[16,1152]{1,0:T(8,128)S(1)}, f32[16,1152]{1,0:T(8,128)}, u32[]{:S(2)}) copy-start(f32[16,1152]{1,0:T(8,128)} %convolution_bitcast_fusion.7) | copy-start | bytes 221188
  958.2 33.4 %copy-start.81 = (f32[16,1152]{1,0:T(8,128)S(1)}, f32[16,1152]{1,0:T(8,128)}, u32[]{:S(2)}) copy-start(f32[16,1152]{1,0:T(8,128)} %convolution_bitcast_fusion.6) | copy-start | bytes 221188
  1050.6 1112.0 %reduce-scatter.12.cloned.1.call-start = ((), (), s32[]{:S(2)}) async-start(), calls=%async_computation.12 | async-start | bytes 67682304
  1198.3 1339.5 %reduce-scatter.8.cloned.1.call-start = ((), (), s32[]{:S(2)}) async-start(), calls=%async_computation.10 | async-start | bytes 22560768 | tf_op jit(solution)/shard_map/reduce_scatter | solution.py:104
  1222.0 1317.9 %all-reduce.10.cloned.1.call-start = ((), (), s32[]{:S(2)}) async-start(), calls=%async_computation.13 | async-start | bytes 4718592 | tf_op jit(solution)/shard_map/psum | solution.py:393
  2537.6 62.2 %copy-start.47 = (f32[2441,72]{0,1:T(8,128)S(1)}, f32[2441,72]{0,1:T(8,128)}, u32[]{:S(2)}) copy-start(f32[2441,72]{0,1:T(8,128)} %param.28) | copy-start | bytes 2109028
  2539.9 59.9 %copy-start.59 = (bf16[2441,72]{0,1:T(8,128)(2,1)S(1)}, bf16[2441,72]{0,1:T(8,128)(2,1)}, u32[]{:S(2)}) copy-start(bf16[2441,72]{0,1:T(8,128)(2,1)} %get-tuple-element.204) | copy-start | bytes 1054516
  2543.6 64.8 %copy-start.46 = (bf16[72,13824]{1,0:T(8,128)(2,1)S(1)}, bf16[72,13824]{1,0:T(8,128)(2,1)}, u32[]{:S(2)}) copy-start(bf16[72,13824]{1,0:T(8,128)(2,1)} %get-tuple-element.203) | copy-start | bytes 5971972
  2620.4 70.6 %copy-start.48 = (f32[2441,72]{0,1:T(8,128)S(1)}, f32[2441,72]{0,1:T(8,128)}, u32[]{:S(2)}) copy-start(f32[2441,72]{0,1:T(8,128)} %param.28) | copy-start | bytes 2109028
  2622.6 73.3 %copy-start.49 = (f32[72,4608]{1,0:T(8,128)}, f32[72,4608]{1,0:T(8,128)S(1)}, u32[]{:S(2)}) copy-start(f32[72,4608]{1,0:T(8,128)S(1)} %get-tuple-element.216) | copy-start | bytes 3981316
  (174 other events, 1525.6 us)
Sparse Core Ops, SparseCore 0:
  11.4 93.3 all-gather.5
  108.2 131.8 all-gather.7
  243.4 332.9 all-gather.9
  1050.8 192.6 reduce-scatter.9
  1249.3 913.2 reduce-scatter.11
  2169.5 312.8 reduce-scatter.7
  2486.0 20.7 all-reduce.9
where the time goes:
time: 2730 us; the launch traced here: 2710 us
  waiting for transfers between devices  1210 us (44%)
  other arithmetic  549 us (20%)
  matrix products  421 us (15%)
  local copies, waits for them, and re-layouts  407 us (15%)
  blocking collectives  95.3 us (3%)
    unnamed x9, waiting for transfers between devices  939 us
    scatter-add x1, other arithmetic, on_device(): rel_pull = jax.vjp(lambda entries: entries[:, rel_ids], rel_bias)[1]  347 us
    all_gather x1, waiting for transfers between devices, fetch_weights(): lax.all_gather(block_weights.astype(jnp.bfloat16), 'dp', axis=0, tiled=True)  272 us
    gather x2, local copies, waits for them, and re-layouts, on_device(): position_bias = rel_bias[:, rel_ids]  236 us
    dot_general x16, matrix products, dense(): return jnp.dot(left, right, preferred_element_type=jnp.float32)  116 us
    dot_general x12, matrix products, dense_trans(): lax.dot_general(left, right, (((left.ndim - 1,), (1,)), ((), ())), prefer...  108 us
    dot_general x14, matrix products, outer_sum(): lax.dot_general(flat_left, flat_right, (((0,), (0,)), ((), ())), preferre...  99.8 us
    add x2, other arithmetic, on_device(): grad_total = jax.tree.map(jnp.add, grad_total, grads)  72.6 us
  transfers between devices with their start and end apart: 9, of which 4 were waited for; matrix products, arithmetic and copies ran while one was open for 30% of the time, Pallas kernels for 0%

commit v1 on v0

v1 whole, which is shorter than its diff:
```python
import functools
import math

import jax
import jax.numpy as jnp
from jax import lax
from jax.experimental import pallas as pl
from jax.experimental.pallas import tpu as pltpu
from jax.sharding import PartitionSpec as P

D = 1152
HEADS = 16
HD = 72
MLPW = 4608
NCLASS = 1000
FREQ = 256
GRID = 16
PDIM = 16
NSTEPS = 1000
STEP = 10
SIDE = 2 * GRID - 1
QKV_HALF = 3 * D // 2
QKV_PAD = -(-QKV_HALF // 128) * 128
SPREAD = 2 * GRID * GRID


FIRST_DECAY = 0.9
SECOND_DECAY = 0.999
ADAM_EPSILON = 1e-08
WEIGHT_DECAY = 0.01
LEARN_RATE = 0.25
CLIP_NORM = 0.05
HIGH = lax.Precision.HIGHEST


def dense(left, right):
    return jnp.dot(left, right, preferred_element_type=jnp.float32)


def dense_trans(left, right):
    return lax.dot_general(
        left, right, (((left.ndim - 1,), (1,)), ((), ())), preferred_element_type=jnp.float32
    )


def outer_sum(left, right):
    flat_left = left.reshape(-1, left.shape[-1])
    flat_right = right.reshape(-1, right.shape[-1])
    return lax.dot_general(
        flat_left, flat_right, (((0,), (0,)), ((), ())), preferred_element_type=jnp.float32
    )


def first_contract(left, right):
    return lax.dot_general(
        left, right, (((0,), (0,)), ((), ())), precision=HIGH, preferred_element_type=jnp.float32
    )


def layer_norm(values):
    center = values - jnp.mean(values, -1, keepdims=True)
    inverse = lax.rsqrt(jnp.mean(center * center, -1, keepdims=True) + 1e-06)
    return (center * inverse, inverse)


def norm_back(upstream, normed, inverse):
    return inverse * (
        upstream
        - jnp.mean(upstream, -1, keepdims=True)
        - normed * jnp.mean(upstream * normed, -1, keepdims=True)
    )


def silu_slope(values):
    sigma = jax.nn.sigmoid(values)
    return sigma * (1.0 + values * (1.0 - sigma))


def plan_table():
    betas = jnp.linspace(0.0001, 0.02, NSTEPS, dtype=jnp.float32)
    return jnp.exp(jnp.cumsum(jnp.log(1.0 - betas)))


def sinusoid(steps):
    half_width = FREQ // 2
    freqs = jnp.exp(-math.log(10000.0) * jnp.arange(half_width, dtype=jnp.float32) / half_width)
    angles = steps.astype(jnp.float32)[:, None] * freqs[None, :]
    return jnp.concatenate([jnp.cos(angles), jnp.sin(angles)], 1)


def dp_peers(mask):
    spread, pair = lax.axis_size("dp"), lax.axis_size("mod")
    return [(i * pair + c, (i ^ mask) * pair + c) for i in range(spread) for c in range(pair)]


def plane_peers(masks):
    spread, pair = lax.axis_size("dp"), lax.axis_size("mod")
    return [(i * pair + c, (i ^ masks[c]) * pair + c) for i in range(spread) for c in range(pair)]


def send(values, peers):
    return lax.ppermute(values, ("dp", "mod"), peers)


def swap_cores(values):
    return lax.ppermute(values, "mod", [(0, 1), (1, 0)])


def far_groups():
    spread = lax.axis_size("dp")
    bits = [1 << k for k in range(2, spread.bit_length() - 1)]
    if len(bits) == 2:
        return [[bits[0], bits[1], bits[0] | bits[1]]]
    return [[bit] for bit in bits]


def far_masks():
    masks = [0]
    for group in far_groups():
        masks = masks + [mask | have for mask in group for have in masks]
    return masks


def block_places():
    me, core = lax.axis_index("dp"), lax.axis_index("mod")
    second = jnp.where(core == 0, 1, 2)
    third = jnp.where(core == 0, 2, 1)
    far = jnp.array(far_masks(), jnp.int32)
    near = jnp.stack([jnp.zeros_like(second), second, third, second | third])
    return (me ^ (near[:, None] | far[None, :])).reshape(-1).astype(jnp.int32)


def place_kernel(counts, places, *refs):
    ins, out, sems = (refs[: len(counts)], refs[len(counts)], refs[len(counts) + 1])
    copies = []
    for part, count in enumerate(counts):
        for row in range(count):
            at = len(copies)
            copies.append(
                pltpu.make_async_copy(ins[part].at[row], out.at[places[at]], sems.at[at])
            )
            copies[-1].start()
    for copy in copies:
        copy.wait()


def pick_kernel(counts, places, source, *refs):
    outs, sems = (refs[: len(counts)], refs[len(counts)])
    copies = []
    for part, count in enumerate(counts):
        for row in range(count):
            at = len(copies)
            copies.append(
                pltpu.make_async_copy(source.at[places[at]], outs[part].at[row], sems.at[at])
            )
            copies[-1].start()
    for copy in copies:
        copy.wait()


def place_blocks(parts, places):
    counts = [part.shape[0] for part in parts]
    total = sum(counts)
    return pl.pallas_call(
        functools.partial(place_kernel, counts),
        grid_spec=pltpu.PrefetchScalarGridSpec(
            num_scalar_prefetch=1,
            grid=(1,),
            in_specs=[pl.BlockSpec(memory_space=pl.ANY)] * len(parts),
            out_specs=pl.BlockSpec(memory_space=pl.ANY),
            scratch_shapes=[pltpu.SemaphoreType.DMA((total,))],
        ),
        out_shape=jax.ShapeDtypeStruct((total,) + parts[0].shape[1:], parts[0].dtype),
        name="place_blocks",
    )(places, *parts)


def pick_blocks(values, places):
    total = values.shape[0]
    counts = [total // 4] * 4
    return pl.pallas_call(
        functools.partial(pick_kernel, counts),
        grid_spec=pltpu.PrefetchScalarGridSpec(
            num_scalar_prefetch=1,
            grid=(1,),
            in_specs=[pl.BlockSpec(memory_space=pl.ANY)],
            out_specs=[pl.BlockSpec(memory_space=pl.ANY)] * 4,
            scratch_shapes=[pltpu.SemaphoreType.DMA((total,))],
        ),
        out_shape=[
            jax.ShapeDtypeStruct((count,) + values.shape[1:], values.dtype) for count in counts
        ],
        name="pick_blocks",
    )(places, values)


def gather_blocks(block, places):
    stack = block[None]
    for group in far_groups():
        stack = jnp.concatenate([stack] + [send(stack, dp_peers(mask)) for mask in group], 0)
    second = send(stack, plane_peers((1, 2)))
    third = send(stack, plane_peers((2, 1)))
    both = send(second, plane_peers((2, 1)))
    return place_blocks([stack, second, third, both], places)


def scatter_blocks(values, places):
    kind = values.dtype
    wide = jnp.float32
    own, second, third, both = pick_blocks(values, places)
    from_both = send(both, plane_peers((2, 1)))
    from_third = send(third, plane_peers((2, 1)))
    second = (second.astype(wide) + from_both.astype(wide)).astype(kind)
    from_second = send(second, plane_peers((1, 2)))
    own = (own.astype(wide) + from_third.astype(wide) + from_second.astype(wide)).astype(kind)
    for group in reversed(far_groups()):
        count = own.shape[0] // (len(group) + 1)
        total = own[:count].astype(wide)
        for pos, mask in enumerate(group):
            total = total + send(
                own[(pos + 1) * count : (pos + 2) * count], dp_peers(mask)
            ).astype(wide)
        own = total if count == 1 else total.astype(kind)
    return own[0].astype(wide)


def all_sum(values):
    values = values + swap_cores(values)
    return dp_sum(values)


def dp_sum(values):
    for bit in range(lax.axis_size("dp").bit_length() - 1):
        values = values + send(values, dp_peers(1 << bit))
    return values


def product(left, right, dims):
    return lax.dot_general(left, right, (dims, ((), ())), preferred_element_type=jnp.float32)


def fill_bias(spread_ref, bias):
    tokens = GRID * GRID
    for head in range(bias.shape[0]):
        spread = spread_ref[head]
        for row in range(GRID):
            off = (GRID - 1 - row) * GRID
            moved = spread if off == 0 else pltpu.roll(spread, SPREAD - off, 1)
            bias[head, row * GRID : (row + 1) * GRID, :] = moved[:, :tokens]


def head_slices(values, head, heads):
    width = heads * HD
    return [
        values[:, part * width + head * HD : part * width + (head + 1) * HD] for part in range(3)
    ]


def attention_kernel(heads, qkv_ref, spread_ref, out_ref, log_ref, bias):
    @pl.when(pl.program_id(0) == 0)
    def _():
        fill_bias(spread_ref, bias)

    values = qkv_ref[...]
    outs, logs = ([], [])
    for head in range(heads):
        query, key, value = head_slices(values, head, heads)
        scores = product(query, key, ((1,), (1,))) * HD ** (-0.5) + bias[head]
        top = jnp.max(scores, -1, keepdims=True)
        powers = jnp.exp(scores - top)
        total = jnp.sum(powers, -1, keepdims=True)
        probs = (powers * (1.0 / total)).astype(jnp.bfloat16)
        outs.append(product(probs, value, ((1,), (0,))).astype(jnp.bfloat16))
        logs.append(top + jnp.log(total))
    out_ref[...] = jnp.concatenate(outs, 1)
    log_ref[...] = jnp.concatenate(logs, 1)


def attention(qkv, spread):
    rows, columns = qkv.shape
    heads = spread.shape[0]
    tokens = GRID * GRID
    return pl.pallas_call(
        functools.partial(attention_kernel, heads),
        grid=(rows // tokens,),
        in_specs=[
            pl.BlockSpec((tokens, columns), lambda step: (step, 0)),
            pl.BlockSpec(spread.shape, lambda step: (0, 0, 0)),
        ],
        out_specs=[
            pl.BlockSpec((tokens, heads * HD), lambda step: (step, 0)),
            pl.BlockSpec((tokens, heads), lambda step: (step, 0)),
        ],
        out_shape=[
            jax.ShapeDtypeStruct((rows, heads * HD), jnp.bfloat16),
            jax.ShapeDtypeStruct((rows, heads), jnp.float32),
        ],
        scratch_shapes=[pltpu.VMEM((heads, tokens, tokens), jnp.float32)],
        compiler_params=pltpu.CompilerParams(vmem_limit_bytes=48 << 20),
        cost_estimate=pl.CostEstimate(
            flops=4 * rows * tokens * heads * 256,
            bytes_accessed=rows * columns * 4,
            transcendentals=rows * tokens * heads,
        ),
        name="attention",
    )(qkv, spread)


def attention_back_kernel(
    heads, qkv_ref, upstream_ref, log_ref, spread_ref, d_qkv_ref, d_spread_ref, bias, d_bias
):
    tokens = GRID * GRID

    @pl.when(pl.program_id(0) == 0)
    def _():
        fill_bias(spread_ref, bias)
        d_bias[...] = jnp.zeros_like(d_bias)

    values, upstream, logs = (qkv_ref[...], upstream_ref[...], log_ref[...])
    d_query, d_key, d_value = ([], [], [])
    for head in range(heads):
        query, key, value = head_slices(values, head, heads)
        d_out = upstream[:, head * HD : (head + 1) * HD]
        scores = product(query, key, ((1,), (1,))) * HD ** (-0.5) + bias[head]
        probs = jnp.exp(scores - logs[:, head : head + 1])
        d_probs = product(d_out, value, ((1,), (1,)))
        d_scores = probs * (d_probs - jnp.sum(probs * d_probs, -1, keepdims=True))
        d_scores = d_scores.astype(jnp.bfloat16)
        d_bias[head] += d_scores.astype(jnp.float32)
        d_query.append((product(d_scores, key, ((1,), (0,))) * HD ** (-0.5)).astype(jnp.bfloat16))
        d_key.append((product(d_scores, query, ((0,), (0,))) * HD ** (-0.5)).astype(jnp.bfloat16))
        d_value.append(
            product(probs.astype(jnp.bfloat16), d_out, ((0,), (0,))).astype(jnp.bfloat16)
        )
    pieces = d_query + d_key + d_value
    spare = d_qkv_ref.shape[1] - 3 * heads * HD
    if spare:
        pieces = pieces + [jnp.zeros((tokens, spare), jnp.bfloat16)]
    d_qkv_ref[...] = jnp.concatenate(pieces, 1)

    @pl.when(pl.program_id(0) == pl.num_programs(0) - 1)
    def _():
        for head in range(heads):
            total = jnp.zeros((GRID, SPREAD), jnp.float32)
            for row in range(GRID):
                off = (GRID - 1 - row) * GRID
                rows = d_bias[head, row * GRID : (row + 1) * GRID, :]
                wide = jnp.concatenate([rows, jnp.zeros((GRID, SPREAD - tokens), jnp.float32)], 1)
                total += wide if off == 0 else pltpu.roll(wide, off, 1)
            d_spread_ref[head] = total


def attention_back(qkv, upstream, logs, spread):
    rows, columns = qkv.shape
    heads = spread.shape[0]
    tokens = GRID * GRID
    return pl.pallas_call(
        functools.partial(attention_back_kernel, heads),
        grid=(rows // tokens,),
        in_specs=[
            pl.BlockSpec((tokens, columns), lambda step: (step, 0)),
            pl.BlockSpec((tokens, heads * HD), lambda step: (step, 0)),
            pl.BlockSpec((tokens, heads), lambda step: (step, 0)),
            pl.BlockSpec(spread.shape, lambda step: (0, 0, 0)),
        ],
        out_specs=[
            pl.BlockSpec((tokens, columns), lambda step: (step, 0)),
            pl.BlockSpec(spread.shape, lambda step: (0, 0, 0)),
        ],
        out_shape=[
            jax.ShapeDtypeStruct((rows, columns), jnp.bfloat16),
            jax.ShapeDtypeStruct(spread.shape, jnp.float32),
        ],
        scratch_shapes=[pltpu.VMEM((heads, tokens, tokens), jnp.float32)] * 2,
        compiler_params=pltpu.CompilerParams(vmem_limit_bytes=48 << 20),
        cost_estimate=pl.CostEstimate(
            flops=10 * rows * tokens * heads * 256,
            bytes_accessed=rows * columns * 6,
            transcendentals=rows * tokens * heads,
        ),
        name="attention_back",
    )(qkv, upstream, logs, spread)


def spread_bias(relative):
    turned = relative.reshape(-1, SIDE, SIDE)[:, ::-1, ::-1]
    rows = [turned[:, :, GRID - 1 - row : SIDE - row] for row in range(GRID)]
    spread = jnp.stack(rows, 1).reshape(-1, GRID, SIDE * GRID)
    return jnp.pad(spread, ((0, 0), (0, 0), (0, SPREAD - SIDE * GRID)))


def gather_bias(d_spread):
    parts = d_spread[:, :, : SIDE * GRID].reshape(-1, GRID, SIDE, GRID)
    total = sum(
        jnp.pad(parts[:, row], ((0, 0), (0, 0), (GRID - 1 - row, row))) for row in range(GRID)
    )
    return total[:, ::-1, ::-1].reshape(-1, SIDE * SIDE)


def core_half(values, core, starts, width):
    return [
        jnp.where(
            core == 0,
            values[:, start : start + width],
            values[:, start + width : start + 2 * width],
        )
        for start in starts
    ]


def both_cores(mine, other, core, axis):
    return jnp.where(
        core == 0,
        jnp.concatenate([mine, other], axis),
        jnp.concatenate([other, mine], axis),
    )


def part_squares(block_part, mod_part, embed_part, first_core, core_index):
    column_sq = jnp.sum(block_part * block_part, 0)
    block_terms = [
        jnp.sum(column_sq[: 3 * D]),
        jnp.sum(column_sq[3 * D : 4 * D]),
        jnp.sum(column_sq[4 * D : 4 * D + MLPW]),
        jnp.sum(column_sq[4 * D + MLPW :]),
    ]
    mod_sq = jnp.sum(mod_part * mod_part, 0)
    global_cols = core_index * mod_part.shape[1] + jnp.arange(mod_part.shape[1], dtype=jnp.int32)
    first_mod = jnp.sum(jnp.where(global_cols < 6 * D, mod_sq, 0.0))
    second_mod = jnp.sum(jnp.where(global_cols < 6 * D, 0.0, mod_sq))
    row_sq = jnp.sum(embed_part * embed_part, 1)
    bounds = [
        0,
        NCLASS + 1,
        NCLASS + 1 + FREQ,
        NCLASS + 1 + FREQ + D,
        NCLASS + 1 + FREQ + D + PDIM,
        NCLASS + 1 + FREQ + D + 2 * PDIM,
    ]
    embed_terms = [jnp.sum(row_sq[bounds[pos] : bounds[pos + 1]]) for pos in range(5)]
    replicated = jnp.stack(block_terms + embed_terms) * first_core
    return jnp.concatenate([replicated[:4], jnp.stack([first_mod, second_mod]), replicated[4:]])


def adam_update(grad, first, second, weight, clip):
    first_new = FIRST_DECAY * first + (1.0 - FIRST_DECAY) * (grad * clip)
    second_new = SECOND_DECAY * second + (1.0 - SECOND_DECAY) * (grad * clip) ** 2
    update = (
        first_new
        / (1.0 - FIRST_DECAY**STEP)
        / (jnp.sqrt(second_new / (1.0 - SECOND_DECAY**STEP)) + ADAM_EPSILON)
        + WEIGHT_DECAY * weight
    )
    return (first_new, second_new, update)


def on_device(
    latents,
    noise,
    timesteps,
    labels,
    drops,
    block_weights,
    block_first,
    block_second,
    mod_weights,
    mod_first,
    mod_second,
    embed_weights,
    embed_first,
    embed_second,
    rel_bias,
    rel_first,
    rel_second,
):
    low = jnp.bfloat16
    wide = jnp.float32
    core = lax.axis_index("mod")
    spread = lax.axis_size("dp")
    images = latents.shape[0]
    length = latents.shape[1]
    rows = images * length
    share = embed_weights.shape[1]
    count = float(images * spread * lax.axis_size("mod") * length * latents.shape[2])
    places = block_places()

    half = D // 2
    wide_half = MLPW // 2
    block_low = block_weights.astype(low)
    q_part, k_part, v_part, p_part = core_half(
        block_low, core, [0, D, 2 * D, 3 * D], half
    )
    in_part, out_part = core_half(block_low, core, [4 * D, 4 * D + MLPW], wide_half)
    pad_part = jnp.zeros((block_low.shape[0], QKV_PAD - QKV_HALF), low)
    attn_part = jnp.concatenate([q_part, k_part, v_part, pad_part, p_part], 1)

    start = NCLASS + 1
    chosen = jnp.where(drops == 1, NCLASS, labels)
    codes = jnp.stack([timesteps // 32, timesteps % 32, chosen // 32, chosen % 32], 1)
    codes = codes.astype(low)
    codes = both_cores(codes, swap_cores(codes), core, 0)
    code_rows = -(-codes.size // share)
    codes = jnp.pad(codes.reshape(-1), (0, code_rows * share - codes.size))
    embed_low = embed_weights.astype(low)
    table = embed_low[:start]
    time_out = embed_low[start + FREQ : start + FREQ + D].astype(wide)
    small = jnp.concatenate(
        [
            embed_low[start : start + FREQ],
            embed_low[start + FREQ + D :],
            codes.reshape(code_rows, share),
        ],
        0,
    )
    small = gather_blocks(small, places)
    everyone = small[:, FREQ + 2 * PDIM :].reshape(spread, -1)[:, : 2 * images * 4]
    everyone = everyone.reshape(spread * 2 * images, 4).astype(wide)
    all_steps = 32.0 * everyone[:, 0] + everyone[:, 1]
    all_chosen = (32.0 * everyone[:, 2] + everyone[:, 3]).astype(jnp.int32)
    small = small[:, : FREQ + 2 * PDIM].transpose(1, 0, 2).reshape(FREQ + 2 * PDIM, D)
    time_in = small[:FREQ].astype(wide)
    patch = small[FREQ : FREQ + PDIM]
    head = small[FREQ + PDIM :]

    attn_low = gather_blocks(attn_part, places).reshape(D, -1)
    in_low = gather_blocks(in_part, places).reshape(D, -1)
    out_low = gather_blocks(out_part, places).reshape(D, -1)
    qkv_low = attn_low[:, :QKV_PAD]
    proj_half = attn_low[:, QKV_PAD:]
    proj_low = both_cores(proj_half, swap_cores(proj_half), core, 1)

    sinus = sinusoid(all_steps)
    pre_time = jnp.dot(sinus, time_in, precision=HIGH, preferred_element_type=wide)
    time_act = jax.nn.silu(pre_time)
    onehot = all_chosen[:, None] == jnp.arange(start, dtype=jnp.int32)[None, :]
    cond = jnp.dot(time_act, time_out, precision=HIGH, preferred_element_type=wide) + dense(
        onehot.astype(low), table
    )
    scaled = jax.nn.silu(cond).astype(low)
    mod_low = mod_weights.astype(low)
    mod_partial = dense(scaled, mod_low).astype(low)
    half_mod = scatter_blocks(mod_partial.reshape(spread, 2 * images, -1), places)
    mine = jnp.where(core == 0, half_mod[:images], half_mod[images:])
    theirs = jnp.where(core == 0, half_mod[images:], half_mod[:images])
    modulation = both_cores(mine, swap_cores(theirs), core, 1).reshape(images, 8, D)

    def moved(normed, shift):
        return (
            normed * (1.0 + modulation[:, shift + 1 : shift + 2]) + modulation[:, shift : shift + 1]
        ).astype(low)

    def with_sibling(values):
        flat = values.reshape(rows, -1)
        return jnp.concatenate([flat, swap_cores(flat)], 0)

    def sum_cores(partial):
        return (partial[:rows] + swap_cores(partial[rows:].astype(low)).astype(wide)).reshape(
            images, length, -1
        )

    alpha_bar = jnp.sum(
        jnp.where(
            timesteps[:, None] == jnp.arange(NSTEPS, dtype=jnp.int32)[None, :],
            plan_table()[None, :],
            0.0,
        ),
        1,
    )
    mixed = (
        jnp.sqrt(alpha_bar)[:, None, None] * latents
        + jnp.sqrt(1.0 - alpha_bar)[:, None, None] * noise
    ).astype(low)
    hidden0 = dense(mixed, patch)
    normed1, inverse1 = layer_norm(hidden0)
    attn_in = with_sibling(moved(normed1, 0))
    qkv = dense(attn_in, qkv_low).astype(low)
    heads = HEADS // 2
    bias_rows = spread_bias(jnp.where(core == 0, rel_bias[:heads], rel_bias[heads:]))
    heads_out, logs = attention(qkv, bias_rows)
    attn_out = both_cores(heads_out[:rows], swap_cores(heads_out[rows:]), core, 1)
    branch_one = dense(attn_out, proj_low).reshape(images, length, D)
    hidden1 = hidden0 + modulation[:, 2:3] * branch_one
    normed2, inverse2 = layer_norm(hidden1)
    mlp_in = with_sibling(moved(normed2, 3))
    pre_act = dense(mlp_in, in_low)
    act = jax.nn.gelu(pre_act, approximate=True).astype(low)
    branch_two = sum_cores(dense_trans(act, out_low))
    hidden2 = hidden1 + modulation[:, 5:6] * branch_two

    normed3, inverse3 = layer_norm(hidden2)
    final_in = moved(normed3, 6)
    predicted = dense_trans(final_in, head)
    error = predicted - noise
    loss_here = jnp.sum(error * error)
    d_predicted = (error * (2.0 / count)).astype(low)
    d_final = dense(d_predicted, head)
    g_head = outer_sum(d_predicted, final_in)
    d_scale3 = jnp.sum(d_final * normed3, 1)
    d_shift3 = jnp.sum(d_final, 1)
    d_hidden2 = norm_back(d_final * (1.0 + modulation[:, 7:8]), normed3, inverse3)

    d_branch_two = with_sibling((modulation[:, 5:6] * d_hidden2).astype(low))
    d_gate2 = jnp.sum(d_hidden2 * branch_two, 1)
    d_act = dense(d_branch_two, out_low)
    gelu_pull = jax.vjp(lambda entries: jax.nn.gelu(entries, approximate=True), pre_act)[1]
    d_pre = gelu_pull(d_act)[0].astype(low)
    g_out = scatter_blocks(
        outer_sum(d_branch_two, act).astype(low).reshape(spread, -1, wide_half), places
    )
    d_mlp_in = sum_cores(dense_trans(d_pre, in_low))
    g_in = scatter_blocks(
        outer_sum(mlp_in, d_pre).astype(low).reshape(spread, -1, wide_half), places
    )
    d_scale2 = jnp.sum(d_mlp_in * normed2, 1)
    d_shift2 = jnp.sum(d_mlp_in, 1)
    d_hidden1 = d_hidden2 + norm_back(d_mlp_in * (1.0 + modulation[:, 4:5]), normed2, inverse2)
    d_branch_one = (modulation[:, 2:3] * d_hidden1).astype(low).reshape(rows, D)
    d_gate1 = jnp.sum(d_hidden1 * branch_one, 1)
    d_attn_out = dense_trans(d_branch_one, proj_low).astype(low)
    d_mine = jnp.where(core == 0, d_attn_out[:, :half], d_attn_out[:, half:])
    d_theirs = jnp.where(core == 0, d_attn_out[:, half:], d_attn_out[:, :half])
    d_heads = jnp.concatenate([d_mine, swap_cores(d_theirs)], 0)
    g_proj = outer_sum(attn_out, d_branch_one)
    g_proj_mine = jnp.where(core == 0, g_proj[:, :half], g_proj[:, half:])
    g_proj_theirs = jnp.where(core == 0, g_proj[:, half:], g_proj[:, :half]).astype(low)
    g_proj = (g_proj_mine + swap_cores(g_proj_theirs).astype(wide)).astype(low)
    d_qkv, d_spread = attention_back(qkv, d_heads, logs, bias_rows)
    d_attn_in = sum_cores(dense_trans(d_qkv, qkv_low))
    g_qkv = outer_sum(attn_in, d_qkv).astype(low)
    g_attn = scatter_blocks(
        jnp.concatenate([g_qkv, g_proj], 1).reshape(spread, -1, QKV_PAD + half), places
    )
    d_scale1 = jnp.sum(d_attn_in * normed1, 1)
    d_shift1 = jnp.sum(d_attn_in, 1)
    d_hidden0 = d_hidden1 + norm_back(d_attn_in * (1.0 + modulation[:, 1:2]), normed1, inverse1)
    g_patch = outer_sum(mixed, d_hidden0.astype(low))

    d_modulation = jnp.stack(
        [d_shift1, d_scale1, d_gate1, d_shift2, d_scale2, d_gate2, d_shift3, d_scale3], 1
    )
    d_modulation = d_modulation.reshape(images, 8 * D).astype(low)
    mod_half = 4 * D
    d_keep = jnp.where(core == 0, d_modulation[:, :mod_half], d_modulation[:, mod_half:])
    d_give = jnp.where(core == 0, d_modulation[:, mod_half:], d_modulation[:, :mod_half])
    d_pair = both_cores(d_keep, swap_cores(d_give), core, 0)
    d_all = gather_blocks(d_pair, places).reshape(spread * 2 * images, mod_half)
    mod_grad = outer_sum(scaled, d_all)
    d_scaled = dense_trans(d_all, mod_low)
    d_scaled = d_scaled + swap_cores(d_scaled)
    d_cond = d_scaled * silu_slope(cond)
    g_table = first_contract(onehot.astype(wide), d_cond)
    g_time_out = first_contract(time_act, d_cond)
    d_time = lax.dot_general(
        d_cond, time_out, (((1,), (1,)), ((), ())), precision=HIGH, preferred_element_type=wide
    )
    g_ends = jnp.concatenate([g_patch, g_head], 0)
    g_ends = g_ends + swap_cores(g_ends)
    tail = jnp.concatenate([d_time, g_ends], 0)
    tail = scatter_blocks(tail.reshape(-1, spread, share).transpose(1, 0, 2), places)
    d_time_here, g_ends = (tail[: -2 * PDIM], tail[-2 * PDIM :])
    first_column = lax.axis_index("dp") * share
    pre_time_here = lax.dynamic_slice_in_dim(pre_time, first_column, share, 1)
    g_time_in = first_contract(sinus, d_time_here * silu_slope(pre_time_here))
    embed_grad = jnp.concatenate([g_table, g_time_in, g_time_out, g_ends], 0)

    g_here = jnp.concatenate([g_attn, g_in, g_out], 1).astype(low)
    g_there = swap_cores(g_here)
    zero_part = jnp.where(core == 0, g_here, g_there).astype(wide)
    one_part = jnp.where(core == 0, g_there, g_here).astype(wide)
    bounds = [0, half, 2 * half, 3 * half, QKV_PAD, QKV_PAD + half]
    bounds = bounds + [bounds[-1] + wide_half, bounds[-1] + 2 * wide_half]
    pieces = []
    for low_end, high_end in zip(bounds[:-1], bounds[1:]):
        if (low_end, high_end) != (3 * half, QKV_PAD):
            pieces = pieces + [zero_part[:, low_end:high_end], one_part[:, low_end:high_end]]
    block_grad = jnp.concatenate(pieces, 1)

    rel_half = gather_bias(d_spread)
    packed = jnp.concatenate([rel_half.reshape(-1), (loss_here * jnp.ones(1, wide))])
    packed = dp_sum(packed)
    packed_other = swap_cores(packed)
    rel_grad = both_cores(
        packed[:-1].reshape(heads, -1), packed_other[:-1].reshape(heads, -1), core, 0
    )
    loss_sum = packed[-1] + packed_other[-1]

    first_core = (core == 0).astype(wide)
    grad_parts, weight_parts = jnp.split(
        all_sum(
            jnp.concatenate(
                [
                    part_squares(block_grad, mod_grad, embed_grad, first_core, core),
                    part_squares(block_weights, mod_weights, embed_weights, first_core, core),
                ]
            )
        ),
        2,
    )
    grad_sq = jnp.concatenate([grad_parts, jnp.sum(rel_grad * rel_grad)[None]])
    weight_sq = jnp.concatenate([weight_parts, jnp.sum(rel_bias * rel_bias)[None]])
    grad_norm = jnp.sqrt(jnp.sum(grad_sq))
    clip = jnp.minimum(1.0, CLIP_NORM / grad_norm)
    block_m, block_s, block_step = adam_update(
        block_grad, block_first, block_second, block_weights, clip
    )
    mod_m, mod_s, mod_step = adam_update(mod_grad, mod_first, mod_second, mod_weights, clip)
    embed_m, embed_s, embed_step = adam_update(
        embed_grad, embed_first, embed_second, embed_weights, clip
    )
    rel_m, rel_s, rel_step = adam_update(rel_grad, rel_first, rel_second, rel_bias, clip)
    update_parts = all_sum(part_squares(block_step, mod_step, embed_step, first_core, core))
    update_sq = jnp.concatenate([update_parts, jnp.sum(rel_step * rel_step)[None]])
    weight_norm = jnp.sqrt(weight_sq)
    update_norm = jnp.sqrt(update_sq)
    ratio = weight_norm / update_norm
    block_ratio = jnp.concatenate(
        [
            jnp.broadcast_to(ratio[0], (3 * D,)),
            jnp.broadcast_to(ratio[1], (D,)),
            jnp.broadcast_to(ratio[2], (MLPW,)),
            jnp.broadcast_to(ratio[3], (MLPW,)),
        ]
    )
    global_cols = core * mod_weights.shape[1] + jnp.arange(
        mod_weights.shape[1], dtype=jnp.int32
    )
    mod_ratio = jnp.where(global_cols < 6 * D, ratio[4], ratio[5])
    embed_ratio = jnp.concatenate(
        [
            jnp.broadcast_to(ratio[6], (NCLASS + 1,)),
            jnp.broadcast_to(ratio[7], (FREQ,)),
            jnp.broadcast_to(ratio[8], (D,)),
            jnp.broadcast_to(ratio[9], (PDIM,)),
            jnp.broadcast_to(ratio[10], (PDIM,)),
        ]
    )
    block_new = block_weights - LEARN_RATE * block_ratio[None, :] * block_step
    mod_new = mod_weights - LEARN_RATE * mod_ratio[None, :] * mod_step
    embed_new = embed_weights - LEARN_RATE * embed_ratio[:, None] * embed_step
    rel_new = rel_bias - LEARN_RATE * ratio[11] * rel_step
    matrix_norms = jnp.stack([weight_norm, update_norm])
    return (
        loss_sum,
        grad_norm,
        matrix_norms,
        block_new,
        block_m,
        block_s,
        block_new.astype(jnp.bfloat16),
        mod_new,
        mod_m,
        mod_s,
        mod_new.astype(jnp.bfloat16),
        embed_new,
        embed_m,
        embed_s,
        embed_new.astype(jnp.bfloat16),
        rel_new,
        rel_m,
        rel_s,
        rel_new.astype(jnp.bfloat16),
        rel_grad * clip,
    )


def solution(mesh):
    placed = (
        P(("dp", "mod"), None, None),
        P(("dp", "mod"), None, None),
        P(("dp", "mod")),
        P(("dp", "mod")),
        P(("dp", "mod")),
        P("dp", None),
        P("dp", None),
        P("dp", None),
        P("dp", "mod"),
        P("dp", "mod"),
        P("dp", "mod"),
        P(None, "dp"),
        P(None, "dp"),
        P(None, "dp"),
        P(),
        P(),
        P(),
    )
    return jax.shard_map(
        on_device,
        mesh=mesh,
        in_specs=placed,
        out_specs=(
            P(),
            P(),
            P(),
            P("dp", None),
            P("dp", None),
            P("dp", None),
            P("dp", None),
            P("dp", "mod"),
            P("dp", "mod"),
            P("dp", "mod"),
            P("dp", "mod"),
            P(None, "dp"),
            P(None, "dp"),
            P(None, "dp"),
            P(None, "dp"),
            P(),
            P(),
            P(),
            P(),
            P(),
        ),
        check_vma=False,
    )
```

time: 2730 us -> 2080 us (0.76)
  Pallas kernels: 0 us -> 1220 us
  waiting for transfers between devices: 1210 us -> 240 us
  other arithmetic: 549 us -> 168 us
  local copies, waits for them, and re-layouts: 407 us -> 120 us
  matrix products: 421 us -> 216 us
  starting transfers between devices: 7.34 us -> 104 us
  blocking collectives: 95.3 us -> 0 us
    pallas_call x0 -> x12, Pallas kernels: none -> 1220 us  [the longest x5 577 us: pick_blocks(): pl.pallas_call(functools.partial(pick_kernel, counts), grid_spec=pltpu.Pr...]
    unnamed x9 -> x0, waiting for transfers between devices: 939 us -> none
    scatter-add x1 -> x0, other arithmetic: 347 us -> none  [on_device(): rel_pull = jax.vjp(lambda entries: entries[:, rel_ids], rel_bias)[1]]
    all_gather x3 -> x0, waiting for transfers between devices: 272 us -> none  [the longest x1 272 us: fetch_weights(): lax.all_gather(block_weights.astype(jnp.bfloat16), 'dp', axis=0, tiled=True)]
    ppermute x0 -> x91, waiting for transfers between devices: none -> 240 us  [the longest x72 234 us: send(): return lax.ppermute(values, ('dp', 'mod'), peers)]
    gather x2 -> x0, local copies, waits for them, and re-layouts: 236 us -> none  [on_device(): position_bias = rel_bias[:, rel_ids]]
    ppermute x0 -> x91, starting transfers between devices: none -> 104 us  [the longest x72 99.8 us: send(): return lax.ppermute(values, ('dp', 'mod'), peers)]
    psum x2 -> x0, blocking collectives: 80.2 us -> none  [the longest x1 40.9 us: on_device(): lax.psum((part_squares(block_grad, mod_grad, embed_grad, first_core, core...]
  transfers between devices with their start and end apart: 9 -> 91, of which waited for: 4 -> 41; matrix products, arithmetic and copies ran while one was open for 30% -> 15% of each run, Pallas kernels for 0% -> 51%
where the time goes in v1:
time: 2080 us; the launch traced here: 2070 us
  Pallas kernels  1220 us (59%)
  waiting for transfers between devices  240 us (12%)
  matrix products  216 us (10%)
  other arithmetic  168 us (8%)
  local copies, waits for them, and re-layouts  120 us (6%)
  starting transfers between devices  104 us (5%)
    pallas_call x5, Pallas kernels, pick_blocks(): pl.pallas_call(functools.partial(pick_kernel, counts), grid_spec=pltpu.Pr...  577 us
    pallas_call x5, Pallas kernels, place_blocks(): pl.pallas_call(functools.partial(place_kernel, counts), grid_spec=pltpu.P...  573 us
    ppermute x72, waiting for transfers between devices, send(): return lax.ppermute(values, ('dp', 'mod'), peers)  234 us
    ppermute x72, starting transfers between devices, send(): return lax.ppermute(values, ('dp', 'mod'), peers)  99.8 us
    dot_general x8, matrix products, dense(): return jnp.dot(left, right, preferred_element_type=jnp.float32)  76.8 us
    dot_general x7, matrix products, outer_sum(): lax.dot_general(flat_left, flat_right, (((0,), (0,)), ((), ())), preferre...  66.7 us
    dot_general x6, matrix products, dense_trans(): lax.dot_general(left, right, (((left.ndim - 1,), (1,)), ((), ())), prefer...  63 us
  transfers between devices with their start and end apart: 91, of which 41 were waited for; matrix products, arithmetic and copies ran while one was open for 15% of the time, Pallas kernels for 51%

profile of v1, /device:TPU:0, one launch (start us, length us, event | category | flops | bytes accessed | tf_op | source)
XLA Modules:
  0.0 2074.4 jit_solution(334835796893552545)
XLA Ops:
  32.2 17.9 collective-permute-start.15
  68.1 38.6 %place_blocks.5 = bf16[16,289,72]{2,1,0:T(8,128)(2,1)} custom-call(s32[16]{0:T(128)} %xor.12.places, bf16[4,289,72]{2,1,0:T(8,128)(2,1)} %copy-done.41, bf16[4,289,72]{2,1,0:T(8,128)(2,1)} %copy-done.57, bf16[4,289,72]{2,1,0:T(8,128)(2,1)} %copy-done.58, bf16[4,289,72]{2,1,0:T(8,128)(2,1)} %copy-done.59), custom_call_target="tpu_custom_call" | custom-call | tf_op jit(solution)/shard_map/place_blocks/pallas_call | solution.py:164
  119.7 37.6 %pick_blocks.5 = (bf16[4,8,4608]{2,1,0:T(8,128)(2,1)}, bf16[4,8,4608]{2,1,0:T(8,128)(2,1)}, bf16[4,8,4608]{2,1,0:T(8,128)(2,1)}, bf16[4,8,4608]{2,1,0:T(8,128)(2,1)}) custom-call(s32[16]{0:T(128)} %xor.12.places, bf16[16,8,4608]{2,1,0:T(8,128)(2,1)} %fusion.7.source), custom_call_target="tpu_custom_call" | custom-call | tf_op jit(solution)/shard_map/pick_blocks/pallas_call | solution.py:181
  219.9 15.0 collective-permute-done.20.refs_3_
  234.9 171.7 %place_blocks.6 = bf16[16,72,2368]{2,1,0:T(8,128)(2,1)} custom-call(s32[16]{0:T(128)} %xor.12.places, bf16[4,72,2368]{2,1,0:T(8,128)(2,1)} %copy-done.19, bf16[4,72,2368]{2,1,0:T(8,128)(2,1)} %collective-permute-done.18.refs_1_, bf16[4,72,2368]{2,1,0:T(8,128)(2,1)} %collective-permute-done.19.refs_2_, bf16[4,72,2368]{2,1,0:T(8,128)(2,1)} %collective-permute-done.20.refs_3_), custom_call_target="tpu_custom_call" | custom-call | tf_op jit(solution)/shard_map/place_blocks/pallas_call | solution.py:164
  409.8 15.5 convolution_convert_fusion.2.qkv_ref
  425.3 28.6 %attention.1 = (bf16[2048,576]{1,0:T(8,128)(2,1)S(1)}, f32[2048,8]{1,0:T(8,128)S(1)}) custom-call(bf16[2048,1792]{1,0:T(8,128)(2,1)} %convolution_convert_fusion.2.qkv_ref, f32[8,16,512]{2,1,0:T(8,128)S(1)} %pad.77.spread_ref), custom_call_target="tpu_custom_call" | custom-call | flops 4294967296 | bytes 14680064 | tf_op jit(solution)/shard_map/attention/pallas_call | solution.py:283
  473.5 23.2 %collective-permute-done.31 = bf16[1,72,2304]{2,1,0:T(8,128)(2,1)S(1)} collective-permute-done((bf16[1,72,2304]{2,1,0:T(8,128)(2,1)S(1)}, bf16[1,72,2304]{2,1,0:T(8,128)(2,1)S(1)}, u32[]{:S(2)}, u32[]{:S(2)}) %collective-permute-start.31) | collective-permute-done | bytes 331808 | tf_op jit(solution)/shard_map/ppermute | solution.py:102
  500.6 16.5 collective-permute-done.25
  571.1 162.7 %place_blocks.8 = bf16[16,72,2304]{2,1,0:T(8,128)(2,1)} custom-call(s32[16]{0:T(128)} %xor.12.places, bf16[4,72,2304]{2,1,0:T(8,128)(2,1)} %copy-done.25, bf16[4,72,2304]{2,1,0:T(8,128)(2,1)} %collective-permute-done.33.refs_1_, bf16[4,72,2304]{2,1,0:T(8,128)(2,1)} %copy-done.39, bf16[4,72,2304]{2,1,0:T(8,128)(2,1)} %collective-permute-done.35.refs_3_), custom_call_target="tpu_custom_call" | custom-call | tf_op jit(solution)/shard_map/place_blocks/pallas_call | solution.py:164
  733.9 162.7 %place_blocks.7 = bf16[16,72,2304]{2,1,0:T(8,128)(2,1)} custom-call(s32[16]{0:T(128)} %xor.12.places, bf16[4,72,2304]{2,1,0:T(8,128)(2,1)} %pad_maximum_fusion.14.refs_0_, bf16[4,72,2304]{2,1,0:T(8,128)(2,1)} %collective-permute-done.27.refs_1_, bf16[4,72,2304]{2,1,0:T(8,128)(2,1)} %collective-permute-done.28.refs_2_, ...), custom_call_target="tpu_custom_call" | custom-call | tf_op jit(solution)/shard_map/place_blocks/pallas_call | solution.py:164
  896.6 18.5 fusion.16
  915.1 23.5 %fusion.89 = f32[2048,1152]{1,0:T(8,128)} fusion(bf16[1152,2304]{1,0:T(8,128)(2,1)} %bitcast.302, f32[2048,2304]{1,0:T(8,128)} %fusion.16), kind=kOutput, calls=%fused_computation.361 | convolution fusion | flops 10914103296 | bytes 33619968 | tf_op jit(solution)/shard_map/dot_general | solution.py:41
  973.8 29.2 %fusion.6 = bf16[2048,2304]{1,0:T(8,128)(2,1)} fusion(f32[2048,2304]{1,0:T(8,128)} %fusion.16, bf16[1152,2304]{1,0:T(8,128)(2,1)} %bitcast.303, bf16[1024,1152]{1,0:T(8,128)(2,1)} %collective-permute-done.37, bf16[1024,1152]{1,0:T(8,128)(2,1)} %bitcast.25), kind=kOutput, calls=%fused_computation.8 | convolution fusion | flops 10975444992 | bytes 38338560 | tf_op jit(solution)/shard_map/dot_general | solution.py:37
  1003.0 17.2 fusion.113
  1034.9 162.7 %pick_blocks.7 = (bf16[4,72,2304]{2,1,0:T(8,128)(2,1)}, bf16[4,72,2304]{2,1,0:T(8,128)(2,1)}, bf16[4,72,2304]{2,1,0:T(8,128)(2,1)}, bf16[4,72,2304]{2,1,0:T(8,128)(2,1)}) custom-call(s32[16]{0:T(128)} %xor.12.places, bf16[16,72,2304]{2,1,0:T(8,128)(2,1)} %bitcast.308), custom_call_target="tpu_custom_call" | custom-call | tf_op jit(solution)/shard_map/pick_blocks/pallas_call | solution.py:181
  1203.3 19.7 convolution_convert_fusion
  1223.0 162.9 %pick_blocks.8 = (bf16[4,72,2304]{2,1,0:T(8,128)(2,1)}, bf16[4,72,2304]{2,1,0:T(8,128)(2,1)}, bf16[4,72,2304]{2,1,0:T(8,128)(2,1)}, bf16[4,72,2304]{2,1,0:T(8,128)(2,1)}) custom-call(s32[16]{0:T(128)} %xor.12.places, bf16[16,72,2304]{2,1,0:T(8,128)(2,1)} %bitcast.309), custom_call_target="tpu_custom_call" | custom-call | tf_op jit(solution)/shard_map/pick_blocks/pallas_call | solution.py:181
  1470.8 38.5 %attention_back.1 = (bf16[2048,1792]{1,0:T(8,128)(2,1)}, f32[8,16,512]{2,1,0:T(8,128)S(1)}) custom-call(bf16[2048,1792]{1,0:T(8,128)(2,1)} %convolution_convert_fusion.2.qkv_ref, bf16[2048,576]{1,0:T(8,128)(2,1)S(1)} %pad_maximum_fusion.12.upstream_ref, f32[2048,8]{1,0:T(8,128)S(1)} %get-tuple-element.49.log_ref, f32[8,16,512]{2,1,0:T(8,128)S(1)} %copy-done.1), custom_call_target="tpu_custom_call" | custom-call | flops 10737418240 | bytes 22020096 | tf_op jit(solution)/shard_map/attention_back/pallas_call | solution.py:357
  1530.9 16.5 convolution_convert_fusion.3
  1563.8 171.8 %pick_blocks.6 = (bf16[4,72,2368]{2,1,0:T(8,128)(2,1)}, bf16[4,72,2368]{2,1,0:T(8,128)(2,1)}, bf16[4,72,2368]{2,1,0:T(8,128)(2,1)}, bf16[4,72,2368]{2,1,0:T(8,128)(2,1)}) custom-call(s32[16]{0:T(128)} %xor.12.places, bf16[16,72,2368]{2,1,0:T(8,128)(2,1)} %bitcast.297), custom_call_target="tpu_custom_call" | custom-call | tf_op jit(solution)/shard_map/pick_blocks/pallas_call | solution.py:181
  1753.9 15.2 collective-permute-done.62
  1818.2 37.6 %place_blocks.9 = bf16[16,8,4608]{2,1,0:T(8,128)(2,1)} custom-call(s32[16]{0:T(128)} %xor.12.places, bf16[4,8,4608]{2,1,0:T(8,128)(2,1)} %copy-done.42, bf16[4,8,4608]{2,1,0:T(8,128)(2,1)} %copy-done.63, bf16[4,8,4608]{2,1,0:T(8,128)(2,1)} %copy-done.62, bf16[4,8,4608]{2,1,0:T(8,128)(2,1)} %collective-permute-done.72.refs_3_), custom_call_target="tpu_custom_call" | custom-call | tf_op jit(solution)/shard_map/place_blocks/pallas_call | solution.py:164
  1870.2 41.6 %pick_blocks.9 = (f32[4,160,72]{2,1,0:T(8,128)}, f32[4,160,72]{2,1,0:T(8,128)}, f32[4,160,72]{2,1,0:T(8,128)}, f32[4,160,72]{2,1,0:T(8,128)}) custom-call(s32[16]{0:T(128)} %xor.12.places, f32[16,160,72]{2,1,0:T(8,128)} %bitcast.310), custom_call_target="tpu_custom_call" | custom-call | tf_op jit(solution)/shard_map/pick_blocks/pallas_call | solution.py:181
  (714 shorter events, 620.7 us)
Async XLA Ops:
  8.7 149.3 %collective-permute-start.17 = (bf16[1,72,2368]{2,1,0:T(8,128)(2,1)}, bf16[1,72,2368]{2,1,0:T(8,128)(2,1)}, u32[]{:S(2)}, u32[]{:S(2)}) collective-permute-start(bf16[1,72,2368]{2,1,0:T(8,128)(2,1)} %bitcast.16), channel_id=1, source_target_pairs={{0,24},{1,25},{2,26},{3,27},{4,28},{5,29},{6,30},{7,31},{8,16},{9,... | collective-permute-start | bytes 1022984 | tf_op jit(solution)/shard_map/ppermute | solution.py:102
  13.7 144.3 %collective-permute-start.16 = (bf16[1,72,2368]{2,1,0:T(8,128)(2,1)}, bf16[1,72,2368]{2,1,0:T(8,128)(2,1)}, u32[]{:S(2)}, u32[]{:S(2)}) collective-permute-start(bf16[1,72,2368]{2,1,0:T(8,128)(2,1)} %bitcast.16), channel_id=1, source_target_pairs={{0,16},{1,17},{2,18},{3,19},{4,20},{5,21},{6,22},{7,23},{8,24},{9,... | collective-permute-start | bytes 1022984 | tf_op jit(solution)/shard_map/ppermute | solution.py:102
  32.2 125.8 %collective-permute-start.15 = (bf16[1,72,2368]{2,1,0:T(8,128)(2,1)}, bf16[1,72,2368]{2,1,0:T(8,128)(2,1)}, u32[]{:S(2)}, u32[]{:S(2)}) collective-permute-start(bf16[1,72,2368]{2,1,0:T(8,128)(2,1)} %bitcast.16), channel_id=1, source_target_pairs={{0,8},{1,9},{2,10},{3,11},{4,12},{5,13},{6,14},{7,15},{8,0},{9,1},... | collective-permute-start | bytes 1022984 | tf_op jit(solution)/shard_map/ppermute | solution.py:102
  201.0 208.8 %collective-permute-start.14 = (bf16[1024,1152]{1,0:T(8,128)(2,1)}, bf16[1024,1152]{1,0:T(8,128)(2,1)}, u32[]{:S(2)}, u32[]{:S(2)}) collective-permute-start(bf16[1024,1152]{1,0:T(8,128)(2,1)} %bitcast.15), channel_id=1, source_target_pairs={{0,1},{1,0},{2,3},{3,2},{4,5},{5,4},{6,7},{7,6},{8,9},{9,8},{10,11... | collective-permute-start | bytes 7077896 | tf_op jit(solution)/shard_map/ppermute | solution.py:106
  409.8 111.9 %collective-permute-start.22 = (bf16[1152,576]{0,1:T(8,128)(2,1)}, bf16[1152,576]{0,1:T(8,128)(2,1)}, u32[]{:S(2)}, u32[]{:S(2)}) collective-permute-start(bf16[1152,576]{0,1:T(8,128)(2,1)} %copy.319), channel_id=1, source_target_pairs={{0,1},{1,0},{2,3},{3,2},{4,5},{5,4},{6,7},{7,6},{8,9},{9,8},{10,11... | collective-permute-start | bytes 3981320 | tf_op jit(solution)/shard_map/ppermute | solution.py:106
  456.7 62.2 %collective-permute-start.21 = (bf16[1024,576]{0,1:T(8,128)(2,1)}, bf16[1024,576]{0,1:T(8,128)(2,1)}, u32[]{:S(2)}, u32[]{:S(2)}) collective-permute-start(bf16[1024,576]{0,1:T(8,128)(2,1)} %copy.280), channel_id=1, source_target_pairs={{0,1},{1,0},{2,3},{3,2},{4,5},{5,4},{6,7},{7,6},{8,9},{9,8},{10,11... | collective-permute-start | bytes 3538952 | tf_op jit(solution)/shard_map/ppermute | solution.py:106
  538.9 357.7 %collective-permute-start.23 = (bf16[1024,1152]{1,0:T(8,128)(2,1)}, bf16[1024,1152]{1,0:T(8,128)(2,1)}, u32[]{:S(2)}, u32[]{:S(2)}) collective-permute-start(bf16[1024,1152]{1,0:T(8,128)(2,1)} %bitcast.19), channel_id=1, source_target_pairs={{0,1},{1,0},{2,3},{3,2},{4,5},{5,4},{6,7},{7,6},{8,9},{9,8},{10,11... | collective-permute-start | bytes 7077896 | tf_op jit(solution)/shard_map/ppermute | solution.py:106
  541.0 192.8 %collective-permute-start.28 = (bf16[4,72,2304]{2,1,0:T(8,128)(2,1)}, bf16[4,72,2304]{2,1,0:T(8,128)(2,1)}, u32[]{:S(2)}, u32[]{:S(2)}) collective-permute-start(bf16[4,72,2304]{2,1,0:T(8,128)(2,1)} %pad_maximum_fusion.14.refs_0_), channel_id=1, source_target_pairs={{0,4},{1,3},{2,6},{3,1},{4,0},{5,7},{6,2},{7,5},{8,12},{9,11},{10,... | collective-permute-start | bytes 3981320 | tf_op jit(solution)/shard_map/ppermute | solution.py:102
  542.3 191.6 %collective-permute-start.29 = (bf16[4,72,2304]{2,1,0:T(8,128)(2,1)}, bf16[4,72,2304]{2,1,0:T(8,128)(2,1)}, u32[]{:S(2)}, u32[]{:S(2)}) collective-permute-start(bf16[4,72,2304]{2,1,0:T(8,128)(2,1)} %collective-permute-done.27.refs_1_), channel_id=1, source_target_pairs={{0,4},{1,3},{2,6},{3,1},{4,0},{5,7},{6,2},{7,5},{8,12},{9,11},{10,... | collective-permute-start | bytes 3981320 | tf_op jit(solution)/shard_map/ppermute | solution.py:102
  1197.6 196.8 %collective-permute-start.53 = (bf16[4,72,2304]{2,1,0:T(8,128)(2,1)}, bf16[4,72,2304]{2,1,0:T(8,128)(2,1)}, u32[]{:S(2)}, u32[]{:S(2)}) collective-permute-start(bf16[4,72,2304]{2,1,0:T(8,128)(2,1)} %get-tuple-element.59), channel_id=1, source_target_pairs={{0,4},{1,3},{2,6},{3,1},{4,0},{5,7},{6,2},{7,5},{8,12},{9,11},{10,... | collective-permute-start | bytes 3981320 | tf_op jit(solution)/shard_map/ppermute | solution.py:102
  1202.9 209.5 %collective-permute-start.38 = (bf16[1024,1152]{1,0:T(8,128)(2,1)}, bf16[1024,1152]{1,0:T(8,128)(2,1)}, u32[]{:S(2)}, u32[]{:S(2)}) collective-permute-start(bf16[1024,1152]{1,0:T(8,128)(2,1)} %slice.1083), channel_id=1, source_target_pairs={{0,1},{1,0},{2,3},{3,2},{4,5},{5,4},{6,7},{7,6},{8,9},{9,8},{10,11... | collective-permute-start | bytes 7077896 | tf_op jit(solution)/shard_map/ppermute | solution.py:106
  1392.4 58.6 %collective-permute-start.52 = (bf16[4,72,2304]{2,1,0:T(8,128)(2,1)}, bf16[4,72,2304]{2,1,0:T(8,128)(2,1)}, u32[]{:S(2)}, u32[]{:S(2)}) collective-permute-start(bf16[4,72,2304]{2,1,0:T(8,128)(2,1)} %get-tuple-element.57), channel_id=1, source_target_pairs={{0,4},{1,3},{2,6},{3,1},{4,0},{5,7},{6,2},{7,5},{8,12},{9,11},{10,... | collective-permute-start | bytes 3981320 | tf_op jit(solution)/shard_map/ppermute | solution.py:102
  1393.3 67.6 %collective-permute-start.58 = (bf16[4,72,2304]{2,1,0:T(8,128)(2,1)}, bf16[4,72,2304]{2,1,0:T(8,128)(2,1)}, u32[]{:S(2)}, u32[]{:S(2)}) collective-permute-start(bf16[4,72,2304]{2,1,0:T(8,128)(2,1)} %get-tuple-element.61), channel_id=1, source_target_pairs={{0,4},{1,3},{2,6},{3,1},{4,0},{5,7},{6,2},{7,5},{8,12},{9,11},{10,... | collective-permute-start | bytes 3981320 | tf_op jit(solution)/shard_map/ppermute | solution.py:102
  1397.1 54.4 %collective-permute-start.54 = (bf16[4,72,2304]{2,1,0:T(8,128)(2,1)}, bf16[4,72,2304]{2,1,0:T(8,128)(2,1)}, u32[]{:S(2)}, u32[]{:S(2)}) collective-permute-start(bf16[4,72,2304]{2,1,0:T(8,128)(2,1)} %add_convert_fusion.9), channel_id=1, source_target_pairs={{0,2},{1,5},{2,0},{3,7},{4,6},{5,1},{6,4},{7,3},{8,10},{9,13},{10,... | collective-permute-start | bytes 3981320 | tf_op jit(solution)/shard_map/ppermute | solution.py:102
  1411.2 52.0 %collective-permute-start.60 = (bf16[4,72,2304]{2,1,0:T(8,128)(2,1)}, bf16[4,72,2304]{2,1,0:T(8,128)(2,1)}, u32[]{:S(2)}, u32[]{:S(2)}) collective-permute-start(bf16[4,72,2304]{2,1,0:T(8,128)(2,1)} %add_convert_fusion.7), channel_id=1, source_target_pairs={{0,2},{1,5},{2,0},{3,7},{4,6},{5,1},{6,4},{7,3},{8,10},{9,13},{10,... | collective-permute-start | bytes 3981320 | tf_op jit(solution)/shard_map/ppermute | solution.py:102
  1451.0 98.1 %collective-permute-start.45 = (bf16[1152,576]{0,1:T(8,128)(2,1)}, bf16[1152,576]{0,1:T(8,128)(2,1)}, u32[]{:S(2)}, u32[]{:S(2)}) collective-permute-start(bf16[1152,576]{0,1:T(8,128)(2,1)} %select_convert_fusion), channel_id=1, source_target_pairs={{0,1},{1,0},{2,3},{3,2},{4,5},{5,4},{6,7},{7,6},{8,9},{9,8},{10,11... | collective-permute-start | bytes 3981320 | tf_op jit(solution)/shard_map/ppermute | solution.py:106
  1456.1 279.5 %collective-permute-start.55 = (bf16[1,72,2304]{2,1,0:T(8,128)(2,1)}, bf16[1,72,2304]{2,1,0:T(8,128)(2,1)}, u32[]{:S(2)}, u32[]{:S(2)}) collective-permute-start(bf16[1,72,2304]{2,1,0:T(8,128)(2,1)} %get-tuple-element.178), channel_id=1, source_target_pairs={{0,8},{1,9},{2,10},{3,11},{4,12},{5,13},{6,14},{7,15},{8,0},{9,1},... | collective-permute-start | bytes 995336 | tf_op jit(solution)/shard_map/ppermute | solution.py:102
  1460.9 274.8 %collective-permute-start.57 = (bf16[1,72,2304]{2,1,0:T(8,128)(2,1)}, bf16[1,72,2304]{2,1,0:T(8,128)(2,1)}, u32[]{:S(2)}, u32[]{:S(2)}) collective-permute-start(bf16[1,72,2304]{2,1,0:T(8,128)(2,1)} %get-tuple-element.179), channel_id=1, source_target_pairs={{0,24},{1,25},{2,26},{3,27},{4,28},{5,29},{6,30},{7,31},{8,16},{9,... | collective-permute-start | bytes 995336 | tf_op jit(solution)/shard_map/ppermute | solution.py:102
  1463.2 274.8 %collective-permute-start.56 = (bf16[1,72,2304]{2,1,0:T(8,128)(2,1)}, bf16[1,72,2304]{2,1,0:T(8,128)(2,1)}, u32[]{:S(2)}, u32[]{:S(2)}) collective-permute-start(bf16[1,72,2304]{2,1,0:T(8,128)(2,1)} %get-tuple-element.180), channel_id=1, source_target_pairs={{0,16},{1,17},{2,18},{3,19},{4,20},{5,21},{6,22},{7,23},{8,24},{9,... | collective-permute-start | bytes 995336 | tf_op jit(solution)/shard_map/ppermute | solution.py:102
  1549.1 227.5 %collective-permute-start.65 = (bf16[1024,1152]{1,0:T(8,128)(2,1)}, bf16[1024,1152]{1,0:T(8,128)(2,1)S(1)}, u32[]{:S(2)}, u32[]{:S(2)}) collective-permute-start(bf16[1024,1152]{1,0:T(8,128)(2,1)} %slice.1082), channel_id=1, source_target_pairs={{0,1},{1,0},{2,3},{3,2},{4,5},{5,4},{6,7},{7,6},{8,9},{9,8},{10,11... | collective-permute-start | bytes 7077896 | tf_op jit(solution)/shard_map/ppermute | solution.py:106
  1549.1 190.1 %collective-permute-start.42 = (f32[7689]{0:T(1024)S(1)}, f32[7689]{0:T(1024)S(1)}, u32[]{:S(2)}, u32[]{:S(2)}) collective-permute-start(f32[7689]{0:T(1024)S(1)} %add.506), channel_id=1, source_target_pairs={{0,8},{1,9},{2,10},{3,11},{4,12},{5,13},{6,14},{7,15},{8,0},{9,1},... | collective-permute-start | bytes 92276 | tf_op jit(solution)/shard_map/ppermute | solution.py:102
  1797.6 189.5 %collective-permute-start.44 = (f32[7689]{0:T(1024)}, f32[7689]{0:T(1024)}, u32[]{:S(2)}, u32[]{:S(2)}) collective-permute-start(f32[7689]{0:T(1024)} %add.508), channel_id=1, source_target_pairs={{0,1},{1,0},{2,3},{3,2},{4,5},{5,4},{6,7},{7,6},{8,9},{9,8},{10,11... | collective-permute-start | bytes 92276 | tf_op jit(solution)/shard_map/ppermute | solution.py:106
  1815.2 117.4 %collective-permute-start.49 = (bf16[1,72,2368]{2,1,0:T(8,128)(2,1)}, bf16[1,72,2368]{2,1,0:T(8,128)(2,1)}, u32[]{:S(2)}, u32[]{:S(2)}) collective-permute-start(bf16[1,72,2368]{2,1,0:T(8,128)(2,1)} %get-tuple-element.172), channel_id=1, source_target_pairs={{0,8},{1,9},{2,10},{3,11},{4,12},{5,13},{6,14},{7,15},{8,0},{9,1},... | collective-permute-start | bytes 1022984 | tf_op jit(solution)/shard_map/ppermute | solution.py:102
  1815.2 119.0 %collective-permute-start.51 = (bf16[1,72,2368]{2,1,0:T(8,128)(2,1)}, bf16[1,72,2368]{2,1,0:T(8,128)(2,1)}, u32[]{:S(2)}, u32[]{:S(2)}) collective-permute-start(bf16[1,72,2368]{2,1,0:T(8,128)(2,1)} %get-tuple-element.173), channel_id=1, source_target_pairs={{0,24},{1,25},{2,26},{3,27},{4,28},{5,29},{6,30},{7,31},{8,16},{9,... | collective-permute-start | bytes 1022984 | tf_op jit(solution)/shard_map/ppermute | solution.py:102
  (180 other events, 3756.8 us)

commit v2 on v1

--- a/solution.py
+++ b/solution.py
@@ -130,68 +130,86 @@
     return (me ^ (near[:, None] | far[None, :])).reshape(-1).astype(jnp.int32)
 
 
-def place_kernel(counts, places, *refs):
-    ins, out, sems = (refs[: len(counts)], refs[len(counts)], refs[len(counts) + 1])
-    copies = []
-    for part, count in enumerate(counts):
-        for row in range(count):
-            at = len(copies)
-            copies.append(
-                pltpu.make_async_copy(ins[part].at[row], out.at[places[at]], sems.at[at])
+def move_kernel(slots, sources, targets, hold, in_sems, out_sems):
+    total = len(sources)
+    for first in range(0, total, slots):
+        wave = range(first, min(first + slots, total))
+        arriving = [
+            pltpu.make_async_copy(sources[at], hold.at[at - first], in_sems.at[at]) for at in wave
+        ]
+        for copy in arriving:
+            copy.start()
+        leaving = []
+        for at, copy in zip(wave, arriving):
+            copy.wait()
+            leaving.append(
+                pltpu.make_async_copy(hold.at[at - first], targets[at], out_sems.at[at])
             )
-            copies[-1].start()
-    for copy in copies:
-        copy.wait()
-
-
-def pick_kernel(counts, places, source, *refs):
-    outs, sems = (refs[: len(counts)], refs[len(counts)])
-    copies = []
-    for part, count in enumerate(counts):
-        for row in range(count):
-            at = len(copies)
-            copies.append(
-                pltpu.make_async_copy(source.at[places[at]], outs[part].at[row], sems.at[at])
-            )
-            copies[-1].start()
-    for copy in copies:
-        copy.wait()
-
-
-def place_blocks(parts, places):
-    counts = [part.shape[0] for part in parts]
+            leaving[-1].start()
+        for copy in leaving:
+            copy.wait()
+
+
+def place_kernel(counts, slots, places, *refs):
+    ins, out = (refs[: len(counts)], refs[len(counts)])
+    sources = [ins[part].at[row] for part, count in enumerate(counts) for row in range(count)]
+    targets = [out.at[places[at]] for at in range(len(sources))]
+    move_kernel(slots, sources, targets, *refs[len(counts) + 1 :])
+
+
+def pick_kernel(counts, slots, places, source, *refs):
+    outs = refs[: len(counts)]
+    targets = [outs[part].at[row] for part, count in enumerate(counts) for row in range(count)]
+    sources = [source.at[places[at]] for at in range(len(targets))]
+    move_kernel(slots, sources, targets, *refs[len(counts) :])
+
+
+def plane_slots(total, plane, kind):
+    rows, columns = plane
+    padded = -(-rows // 16) * 16 * -(-columns // 128) * 128 * jnp.dtype(kind).itemsize
+    return max(1, min(total, (24 << 20) // padded))
+
+
+def move_call(kernel, counts, places, operands, out_shape, out_count, plane, kind):
     total = sum(counts)
+    slots = plane_slots(total, plane, kind)
+    any_space = pl.BlockSpec(memory_space=pl.ANY)
     return pl.pallas_call(
-        functools.partial(place_kernel, counts),
+        functools.partial(kernel, counts, slots),
         grid_spec=pltpu.PrefetchScalarGridSpec(
             num_scalar_prefetch=1,
             grid=(1,),
-            in_specs=[pl.BlockSpec(memory_space=pl.ANY)] * len(parts),
-            out_specs=pl.BlockSpec(memory_space=pl.ANY),
-            scratch_shapes=[pltpu.SemaphoreType.DMA((total,))],
+            in_specs=[any_space] * len(operands),
+            out_specs=any_space if out_count is None else [any_space] * out_count,
+            scratch_shapes=[
+                pltpu.VMEM((slots,) + plane, kind),
+                pltpu.SemaphoreType.DMA((total,)),
+                pltpu.SemaphoreType.DMA((total,)),
+            ],
         ),
-        out_shape=jax.ShapeDtypeStruct((total,) + parts[0].shape[1:], parts[0].dtype),
-        name="place_blocks",
-    )(places, *parts)
+        out_shape=out_shape,
+        compiler_params=pltpu.CompilerParams(vmem_limit_bytes=40 << 20),
+        cost_estimate=pl.CostEstimate(
+            flops=0,
+            bytes_accessed=2 * total * plane[0] * plane[1] * jnp.dtype(kind).itemsize,
+            transcendentals=0,
+        ),
+        name="move_blocks",
+    )(places, *operands)
+
+
+def place_blocks(parts, places):
+    counts = [part.shape[0] for part in parts]
+    plane, kind = (parts[0].shape[1:], parts[0].dtype)
+    shape = jax.ShapeDtypeStruct((sum(counts),) + plane, kind)
+    return move_call(place_kernel, counts, places, parts, shape, None, plane, kind)
 
 
 def pick_blocks(values, places):
-    total = values.shape[0]
-    counts = [total // 4] * 4
-    return pl.pallas_call(
-        functools.partial(pick_kernel, counts),
-        grid_spec=pltpu.PrefetchScalarGridSpec(
-            num_scalar_prefetch=1,
-            grid=(1,),
-            in_specs=[pl.BlockSpec(memory_space=pl.ANY)],
-            out_specs=[pl.BlockSpec(memory_space=pl.ANY)] * 4,
-            scratch_shapes=[pltpu.SemaphoreType.DMA((total,))],
-        ),
-        out_shape=[
-            jax.ShapeDtypeStruct((count,) + values.shape[1:], values.dtype) for count in counts
-        ],
-        name="pick_blocks",
-    )(places, values)
+    counts = [values.shape[0] // 4] * 4
+    plane, kind = (values.shape[1:], values.dtype)
+    shape = [jax.ShapeDtypeStruct((count,) + plane, kind) for count in counts]
+    return move_call(pick_kernel, counts, places, [values], shape, 4, plane, kind)
 
 
 def gather_blocks(block, places):

time: 2080 us -> 972 us (0.47)
  Pallas kernels: 1220 us -> 112 us
    pallas_call x10, Pallas kernels: 1150 us -> 44.8 us  [move_call(): pl.pallas_call(functools.partial(kernel, counts, slots), grid_spec=pltpu....]
  transfers between devices with their start and end apart: 91 -> 91, of which waited for: 41 -> 42; matrix products, arithmetic and copies ran while one was open for 15% -> 32% of each run, Pallas kernels for 51% -> 11%
where the time goes in v2:
time: 972 us; the launch traced here: 967 us
  waiting for transfers between devices  241 us (25%)
  matrix products  208 us (21%)
  other arithmetic  151 us (16%)
  local copies, waits for them, and re-layouts  133 us (14%)
  starting transfers between devices  113 us (12%)
  Pallas kernels  112 us (12%)
    ppermute x72, waiting for transfers between devices, send(): return lax.ppermute(values, ('dp', 'mod'), peers)  234 us
    ppermute x72, starting transfers between devices, send(): return lax.ppermute(values, ('dp', 'mod'), peers)  111 us
    dot_general x8, matrix products, dense(): return jnp.dot(left, right, preferred_element_type=jnp.float32)  73.4 us
    dot_general x7, matrix products, outer_sum(): lax.dot_general(flat_left, flat_right, (((0,), (0,)), ((), ())), preferre...  63.8 us
    dot_general x6, matrix products, dense_trans(): lax.dot_general(left, right, (((left.ndim - 1,), (1,)), ((), ())), prefer...  62.2 us
    pallas_call x10, Pallas kernels, move_call(): pl.pallas_call(functools.partial(kernel, counts, slots), grid_spec=pltpu....  44.8 us
    pallas_call x1, Pallas kernels, attention_back(): pl.pallas_call(functools.partial(attention_back_kernel, heads), grid=(row...  38.4 us
    pallas_call x1, Pallas kernels, attention(): pl.pallas_call(functools.partial(attention_kernel, heads), grid=(rows //...  28.6 us
  transfers between devices with their start and end apart: 91, of which 42 were waited for; matrix products, arithmetic and copies ran while one was open for 32% of the time, Pallas kernels for 11%

profile of v2, /device:TPU:0, one launch (start us, length us, event | category | flops | bytes accessed | tf_op | source)
XLA Modules:
  0.0 966.9 jit_solution(2385039374246882386)
XLA Ops:
  17.8 12.2 %collective-permute-done.3 = bf16[1,289,72]{2,1,0:T(8,128)(2,1)S(1)} collective-permute-done((bf16[1,289,72]{2,1,0:T(8,128)(2,1)S(1)}, bf16[1,289,72]{2,1,0:T(8,128)(2,1)S(1)}, u32[]{:S(2)}, u32[]{:S(2)}) %collective-permute-start.3) | collective-permute-done | bytes 41648 | tf_op jit(solution)/shard_map/ppermute | solution.py:102
  30.0 17.9 %collective-permute-start.15 = (bf16[1,72,2368]{2,1,0:T(8,128)(2,1)}, bf16[1,72,2368]{2,1,0:T(8,128)(2,1)}, u32[]{:S(2)}, u32[]{:S(2)}) collective-permute-start(bf16[1,72,2368]{2,1,0:T(8,128)(2,1)} %bitcast.16), channel_id=1, source_target_pairs={{0,8},{1,9},{2,10},{3,11},{4,12},{5,13},{6,14},{7,15},{8,0},{9,1},... | collective-permute-start | bytes 1022984 | tf_op jit(solution)/shard_map/ppermute | solution.py:102
  97.7 8.7 collective-permute-done.9
  180.6 15.3 %convolution_convert_fusion.2.qkv_ref = bf16[2048,1792]{1,0:T(8,128)(2,1)} fusion(bf16[1152,2368]{1,0:T(8,128)(2,1)} %bitcast.288, bf16[1024,1152]{1,0:T(8,128)(2,1)} %collective-permute-done.14, bf16[1024,1152]{1,0:T(8,128)(2,1)} %bitcast.15), kind=kOutput, calls=%fused_computation.12 | convolution fusion | flops 8468824064 | bytes 16187392 | tf_op jit(solution)/shard_map/dot_general | solution.py:37
  195.9 28.6 %attention.1 = (bf16[2048,576]{1,0:T(8,128)(2,1)S(1)}, f32[2048,8]{1,0:T(8,128)S(1)}) custom-call(bf16[2048,1792]{1,0:T(8,128)(2,1)} %convolution_convert_fusion.2.qkv_ref, f32[8,16,512]{2,1,0:T(8,128)S(1)} %pad.77.spread_ref), custom_call_target="tpu_custom_call" | custom-call | flops 4294967296 | bytes 14680064 | tf_op jit(solution)/shard_map/attention/pallas_call | solution.py:301
  242.9 23.1 %collective-permute-done.31 = bf16[1,72,2304]{2,1,0:T(8,128)(2,1)S(1)} collective-permute-done((bf16[1,72,2304]{2,1,0:T(8,128)(2,1)S(1)}, bf16[1,72,2304]{2,1,0:T(8,128)(2,1)S(1)}, u32[]{:S(2)}, u32[]{:S(2)}) %collective-permute-start.31) | collective-permute-done | bytes 331808 | tf_op jit(solution)/shard_map/ppermute | solution.py:102
  270.4 16.1 %collective-permute-done.25 = bf16[1,72,2304]{2,1,0:T(8,128)(2,1)S(1)} collective-permute-done((bf16[1,72,2304]{2,1,0:T(8,128)(2,1)S(1)}, bf16[1,72,2304]{2,1,0:T(8,128)(2,1)S(1)}, u32[]{:S(2)}, u32[]{:S(2)}) %collective-permute-start.25) | collective-permute-done | bytes 331808 | tf_op jit(solution)/shard_map/ppermute | solution.py:102
  290.4 8.5 fusion.25
  307.8 13.7 %collective-permute-done.34.refs_2_ = bf16[4,72,2304]{2,1,0:T(8,128)(2,1)S(1)} collective-permute-done((bf16[4,72,2304]{2,1,0:T(8,128)(2,1)S(1)}, bf16[4,72,2304]{2,1,0:T(8,128)(2,1)S(1)}, u32[]{:S(2)}, u32[]{:S(2)}) %collective-permute-start.34) | collective-permute-done | bytes 1327136 | tf_op jit(solution)/shard_map/ppermute | solution.py:102
  321.5 14.2 %collective-permute-done.35.refs_3_ = bf16[4,72,2304]{2,1,0:T(8,128)(2,1)S(1)} collective-permute-done((bf16[4,72,2304]{2,1,0:T(8,128)(2,1)}, bf16[4,72,2304]{2,1,0:T(8,128)(2,1)S(1)}, u32[]{:S(2)}, u32[]{:S(2)}) %collective-permute-start.35) | collective-permute-done | bytes 1327136 | tf_op jit(solution)/shard_map/ppermute | solution.py:102
  339.7 10.3 %collective-permute-done.28.refs_2_ = bf16[4,72,2304]{2,1,0:T(8,128)(2,1)S(1)} collective-permute-done((bf16[4,72,2304]{2,1,0:T(8,128)(2,1)S(1)}, bf16[4,72,2304]{2,1,0:T(8,128)(2,1)S(1)}, u32[]{:S(2)}, u32[]{:S(2)}) %collective-permute-start.28) | collective-permute-done | bytes 1327136 | tf_op jit(solution)/shard_map/ppermute | solution.py:102
  350.0 14.2 %collective-permute-done.29.refs_3_ = bf16[4,72,2304]{2,1,0:T(8,128)(2,1)S(1)} collective-permute-done((bf16[4,72,2304]{2,1,0:T(8,128)(2,1)}, bf16[4,72,2304]{2,1,0:T(8,128)(2,1)S(1)}, u32[]{:S(2)}, u32[]{:S(2)}) %collective-permute-start.29) | collective-permute-done | bytes 1327136 | tf_op jit(solution)/shard_map/ppermute | solution.py:102
  368.2 16.4 %fusion.16 = f32[2048,2304]{1,0:T(8,128)} fusion(bf16[1152,2304]{1,0:T(8,128)(2,1)S(1)} %bitcast.292, bf16[1024,1152]{1,0:T(8,128)(2,1)} %collective-permute-done.23, bf16[1024,1152]{1,0:T(8,128)(2,1)S(1)} %bitcast.317), kind=kOutput, calls=%fused_computation.72 | convolution fusion | flops 10881073152 | bytes 28901376 | tf_op jit(solution)/shard_map/dot_general | solution.py:37
  384.6 22.0 %fusion.89 = f32[2048,1152]{1,0:T(8,128)} fusion(bf16[1152,2304]{1,0:T(8,128)(2,1)S(1)} %bitcast.290, f32[2048,2304]{1,0:T(8,128)} %fusion.16), kind=kOutput, calls=%fused_computation.361 | convolution fusion | flops 10914103296 | bytes 33619968 | tf_op jit(solution)/shard_map/dot_general | solution.py:41
  439.3 29.2 %fusion.6 = bf16[2048,2304]{1,0:T(8,128)(2,1)} fusion(f32[2048,2304]{1,0:T(8,128)} %fusion.16, bf16[1152,2304]{1,0:T(8,128)(2,1)} %bitcast.291, bf16[1024,1152]{1,0:T(8,128)(2,1)} %collective-permute-done.37, bf16[1024,1152]{1,0:T(8,128)(2,1)S(1)} %bitcast.320), kind=kOutput, calls=%fused_computation.8 | convolution fusion | flops 10975444992 | bytes 38338560 | tf_op jit(solution)/shard_map/dot_general | solution.py:37
  468.5 16.6 %fusion.113 = f32[2048,1152]{1,0:T(8,128)} fusion(bf16[2048,2304]{1,0:T(8,128)(2,1)} %fusion.6, bf16[1152,2304]{1,0:T(8,128)(2,1)S(1)} %bitcast.295), kind=kOutput, calls=%fused_computation.384 | convolution fusion | flops 10871635968 | bytes 24182784 | tf_op jit(solution)/shard_map/dot_general | solution.py:41
  485.1 14.6 %convolution_convert_fusion.1 = bf16[1152,2304]{1,0:T(8,128)(2,1)S(1)} fusion(bf16[2048,2304]{1,0:T(8,128)(2,1)} %fusion.6, bf16[1024,1152]{1,0:T(8,128)(2,1)} %collective-permute-done.23, bf16[1024,1152]{1,0:T(8,128)(2,1)S(1)} %bitcast.318), kind=kOutput, calls=%fused_computation.11 | convolution fusion | flops 10883727360 | bytes 19464192 | tf_op jit(solution)/shard_map/dot_general | solution.py:49
  509.7 17.4 %convolution_convert_fusion = bf16[1152,2304]{1,0:T(8,128)(2,1)S(1)} fusion(bf16[1024,1152]{1,0:T(8,128)(2,1)} %collective-permute-done.37, bf16[1024,1152]{1,0:T(8,128)(2,1)S(1)} %bitcast.321, f32[2048,2304]{1,0:T(8,128)} %fusion.16), kind=kOutput, calls=%fused_computation.10 | convolution fusion | flops 10926194688 | bytes 28901376 | tf_op jit(solution)/shard_map/dot_general | solution.py:49
  545.1 11.1 %collective-permute-done.59 = bf16[4,72,2304]{2,1,0:T(8,128)(2,1)} collective-permute-done((bf16[4,72,2304]{2,1,0:T(8,128)(2,1)}, bf16[4,72,2304]{2,1,0:T(8,128)(2,1)}, u32[]{:S(2)}, u32[]{:S(2)}) %collective-permute-start.59) | collective-permute-done | bytes 1327136 | tf_op jit(solution)/shard_map/ppermute | solution.py:102
  622.4 38.4 %attention_back.1 = (bf16[2048,1792]{1,0:T(8,128)(2,1)}, f32[8,16,512]{2,1,0:T(8,128)S(1)}) custom-call(bf16[2048,1792]{1,0:T(8,128)(2,1)} %convolution_convert_fusion.2.qkv_ref, bf16[2048,576]{1,0:T(8,128)(2,1)S(1)} %pad_maximum_fusion.12.upstream_ref, f32[2048,8]{1,0:T(8,128)S(1)} %copy-done.11, f32[8,16,512]{2,1,0:T(8,128)S(1)} %copy-done.8), custom_call_target="tpu_custom_call" | custom-call | flops 10737418240 | bytes 22020096 | tf_op jit(solution)/shard_map/attention_back/pallas_call | solution.py:375
  664.5 13.3 %fusion.12 = f32[2048,1152]{1,0:T(8,128)S(1)} fusion(bf16[2048,1792]{1,0:T(8,128)(2,1)} %get-tuple-element.51, bf16[1152,2368]{1,0:T(8,128)(2,1)} %bitcast.289), kind=kOutput, calls=%fused_computation.68 | convolution fusion | flops 8455716864 | bytes 20905984 | tf_op jit(solution)/shard_map/dot_general | solution.py:41
  679.6 16.5 %convolution_convert_fusion.3 = bf16[1152,1792]{1,0:T(8,128)(2,1)} fusion(bf16[2048,1792]{1,0:T(8,128)(2,1)} %get-tuple-element.51, bf16[1024,1152]{1,0:T(8,128)(2,1)} %collective-permute-done.14, bf16[1024,1152]{1,0:T(8,128)(2,1)} %bitcast.15), kind=kOutput, calls=%fused_computation.13 | convolution fusion | flops 8467218432 | bytes 16187392 | tf_op jit(solution)/shard_map/dot_general | solution.py:49
  728.9 13.8 %collective-permute-done.62 = bf16[1,72,2304]{2,1,0:T(8,128)(2,1)S(1)} collective-permute-done((bf16[1,72,2304]{2,1,0:T(8,128)(2,1)S(1)}, bf16[1,72,2304]{2,1,0:T(8,128)(2,1)S(1)}, u32[]{:S(2)}, u32[]{:S(2)}) %collective-permute-start.62) | collective-permute-done | bytes 331808 | tf_op jit(solution)/shard_map/ppermute | solution.py:102
  831.6 12.0 %collective-permute-done.50 = bf16[1,72,2368]{2,1,0:T(8,128)(2,1)S(1)} collective-permute-done((bf16[1,72,2368]{2,1,0:T(8,128)(2,1)S(1)}, bf16[1,72,2368]{2,1,0:T(8,128)(2,1)S(1)}, u32[]{:S(2)}, u32[]{:S(2)}) %collective-permute-start.50) | collective-permute-done | bytes 341024 | tf_op jit(solution)/shard_map/ppermute | solution.py:102
  (722 shorter events, 553.5 us)
Async XLA Ops:
  6.5 76.2 %collective-permute-start.17 = (bf16[1,72,2368]{2,1,0:T(8,128)(2,1)}, bf16[1,72,2368]{2,1,0:T(8,128)(2,1)}, u32[]{:S(2)}, u32[]{:S(2)}) collective-permute-start(bf16[1,72,2368]{2,1,0:T(8,128)(2,1)} %bitcast.16), channel_id=1, source_target_pairs={{0,24},{1,25},{2,26},{3,27},{4,28},{5,29},{6,30},{7,31},{8,16},{9,... | collective-permute-start | bytes 1022984 | tf_op jit(solution)/shard_map/ppermute | solution.py:102
  11.6 71.2 %collective-permute-start.16 = (bf16[1,72,2368]{2,1,0:T(8,128)(2,1)}, bf16[1,72,2368]{2,1,0:T(8,128)(2,1)}, u32[]{:S(2)}, u32[]{:S(2)}) collective-permute-start(bf16[1,72,2368]{2,1,0:T(8,128)(2,1)} %bitcast.16), channel_id=1, source_target_pairs={{0,16},{1,17},{2,18},{3,19},{4,20},{5,21},{6,22},{7,23},{8,24},{9,... | collective-permute-start | bytes 1022984 | tf_op jit(solution)/shard_map/ppermute | solution.py:102
  30.0 52.7 %collective-permute-start.15 = (bf16[1,72,2368]{2,1,0:T(8,128)(2,1)}, bf16[1,72,2368]{2,1,0:T(8,128)(2,1)}, u32[]{:S(2)}, u32[]{:S(2)}) collective-permute-start(bf16[1,72,2368]{2,1,0:T(8,128)(2,1)} %bitcast.16), channel_id=1, source_target_pairs={{0,8},{1,9},{2,10},{3,11},{4,12},{5,13},{6,14},{7,15},{8,0},{9,1},... | collective-permute-start | bytes 1022984 | tf_op jit(solution)/shard_map/ppermute | solution.py:102
  84.3 42.3 %collective-permute-start.18 = (bf16[4,72,2368]{2,1,0:T(8,128)(2,1)S(1)}, bf16[4,72,2368]{2,1,0:T(8,128)(2,1)S(1)}, u32[]{:S(2)}, u32[]{:S(2)}) collective-permute-start(bf16[4,72,2368]{2,1,0:T(8,128)(2,1)S(1)} %pad_maximum_fusion.13.refs_0_), channel_id=1, source_target_pairs={{0,2},{1,5},{2,0},{3,7},{4,6},{5,1},{6,4},{7,3},{8,10},{9,13},{10,... | collective-permute-start | bytes 4091912 | tf_op jit(solution)/shard_map/ppermute | solution.py:102
  125.5 55.0 %collective-permute-start.14 = (bf16[1024,1152]{1,0:T(8,128)(2,1)}, bf16[1024,1152]{1,0:T(8,128)(2,1)}, u32[]{:S(2)}, u32[]{:S(2)}) collective-permute-start(bf16[1024,1152]{1,0:T(8,128)(2,1)} %bitcast.15), channel_id=1, source_target_pairs={{0,1},{1,0},{2,3},{3,2},{4,5},{5,4},{6,7},{7,6},{8,9},{9,8},{10,11... | collective-permute-start | bytes 7077896 | tf_op jit(solution)/shard_map/ppermute | solution.py:106
  125.7 46.0 %collective-permute-start.19 = (bf16[4,72,2368]{2,1,0:T(8,128)(2,1)S(1)}, bf16[4,72,2368]{2,1,0:T(8,128)(2,1)}, u32[]{:S(2)}, u32[]{:S(2)}) collective-permute-start(bf16[4,72,2368]{2,1,0:T(8,128)(2,1)S(1)} %pad_maximum_fusion.13.refs_0_), channel_id=1, source_target_pairs={{0,4},{1,3},{2,6},{3,1},{4,0},{5,7},{6,2},{7,5},{8,12},{9,11},{10,... | collective-permute-start | bytes 4091912 | tf_op jit(solution)/shard_map/ppermute | solution.py:102
  126.6 45.1 %collective-permute-start.20 = (bf16[4,72,2368]{2,1,0:T(8,128)(2,1)S(1)}, bf16[4,72,2368]{2,1,0:T(8,128)(2,1)}, u32[]{:S(2)}, u32[]{:S(2)}) collective-permute-start(bf16[4,72,2368]{2,1,0:T(8,128)(2,1)S(1)} %collective-permute-done.18.refs_1_), channel_id=1, source_target_pairs={{0,4},{1,3},{2,6},{3,1},{4,0},{5,7},{6,2},{7,5},{8,12},{9,11},{10,... | collective-permute-start | bytes 4091912 | tf_op jit(solution)/shard_map/ppermute | solution.py:102
  180.6 109.8 %collective-permute-start.22 = (bf16[1152,576]{0,1:T(8,128)(2,1)}, bf16[1152,576]{0,1:T(8,128)(2,1)}, u32[]{:S(2)}, u32[]{:S(2)}) collective-permute-start(bf16[1152,576]{0,1:T(8,128)(2,1)} %copy.319), channel_id=1, source_target_pairs={{0,1},{1,0},{2,3},{3,2},{4,5},{5,4},{6,7},{7,6},{8,9},{9,8},{10,11... | collective-permute-start | bytes 3981320 | tf_op jit(solution)/shard_map/ppermute | solution.py:106
  227.4 60.3 %collective-permute-start.21 = (bf16[1024,576]{0,1:T(8,128)(2,1)}, bf16[1024,576]{0,1:T(8,128)(2,1)}, u32[]{:S(2)}, u32[]{:S(2)}) collective-permute-start(bf16[1024,576]{0,1:T(8,128)(2,1)} %copy.280), channel_id=1, source_target_pairs={{0,1},{1,0},{2,3},{3,2},{4,5},{5,4},{6,7},{7,6},{8,9},{9,8},{10,11... | collective-permute-start | bytes 3538952 | tf_op jit(solution)/shard_map/ppermute | solution.py:106
  303.6 64.5 %collective-permute-start.23 = (bf16[1024,1152]{1,0:T(8,128)(2,1)S(1)}, bf16[1024,1152]{1,0:T(8,128)(2,1)}, u32[]{:S(2)}, u32[]{:S(2)}) collective-permute-start(bf16[1024,1152]{1,0:T(8,128)(2,1)S(1)} %bitcast.316), channel_id=1, source_target_pairs={{0,1},{1,0},{2,3},{3,2},{4,5},{5,4},{6,7},{7,6},{8,9},{9,8},{10,11... | collective-permute-start | bytes 7077896 | tf_op jit(solution)/shard_map/ppermute | solution.py:106
  305.8 44.2 %collective-permute-start.28 = (bf16[4,72,2304]{2,1,0:T(8,128)(2,1)S(1)}, bf16[4,72,2304]{2,1,0:T(8,128)(2,1)S(1)}, u32[]{:S(2)}, u32[]{:S(2)}) collective-permute-start(bf16[4,72,2304]{2,1,0:T(8,128)(2,1)S(1)} %pad_maximum_fusion.14.refs_0_), channel_id=1, source_target_pairs={{0,4},{1,3},{2,6},{3,1},{4,0},{5,7},{6,2},{7,5},{8,12},{9,11},{10,... | collective-permute-start | bytes 3981320 | tf_op jit(solution)/shard_map/ppermute | solution.py:102
  306.8 57.4 %collective-permute-start.29 = (bf16[4,72,2304]{2,1,0:T(8,128)(2,1)}, bf16[4,72,2304]{2,1,0:T(8,128)(2,1)S(1)}, u32[]{:S(2)}, u32[]{:S(2)}) collective-permute-start(bf16[4,72,2304]{2,1,0:T(8,128)(2,1)} %collective-permute-done.27.refs_1_), channel_id=1, source_target_pairs={{0,4},{1,3},{2,6},{3,1},{4,0},{5,7},{6,2},{7,5},{8,12},{9,11},{10,... | collective-permute-start | bytes 3981320 | tf_op jit(solution)/shard_map/ppermute | solution.py:102
  509.7 50.6 %collective-permute-start.38 = (bf16[1024,1152]{1,0:T(8,128)(2,1)}, bf16[1024,1152]{1,0:T(8,128)(2,1)}, u32[]{:S(2)}, u32[]{:S(2)}) collective-permute-start(bf16[1024,1152]{1,0:T(8,128)(2,1)} %slice.1083), channel_id=1, source_target_pairs={{0,1},{1,0},{2,3},{3,2},{4,5},{5,4},{6,7},{7,6},{8,9},{9,8},{10,11... | collective-permute-start | bytes 7077896 | tf_op jit(solution)/shard_map/ppermute | solution.py:106
  539.1 61.9 %collective-permute-start.52 = (bf16[4,72,2304]{2,1,0:T(8,128)(2,1)}, bf16[4,72,2304]{2,1,0:T(8,128)(2,1)}, u32[]{:S(2)}, u32[]{:S(2)}) collective-permute-start(bf16[4,72,2304]{2,1,0:T(8,128)(2,1)} %get-tuple-element.57), channel_id=1, source_target_pairs={{0,4},{1,3},{2,6},{3,1},{4,0},{5,7},{6,2},{7,5},{8,12},{9,11},{10,... | collective-permute-start | bytes 3981320 | tf_op jit(solution)/shard_map/ppermute | solution.py:102
  540.2 69.7 %collective-permute-start.58 = (bf16[4,72,2304]{2,1,0:T(8,128)(2,1)}, bf16[4,72,2304]{2,1,0:T(8,128)(2,1)}, u32[]{:S(2)}, u32[]{:S(2)}) collective-permute-start(bf16[4,72,2304]{2,1,0:T(8,128)(2,1)} %get-tuple-element.61), channel_id=1, source_target_pairs={{0,4},{1,3},{2,6},{3,1},{4,0},{5,7},{6,2},{7,5},{8,12},{9,11},{10,... | collective-permute-start | bytes 3981320 | tf_op jit(solution)/shard_map/ppermute | solution.py:102
  543.9 57.6 %collective-permute-start.54 = (bf16[4,72,2304]{2,1,0:T(8,128)(2,1)}, bf16[4,72,2304]{2,1,0:T(8,128)(2,1)}, u32[]{:S(2)}, u32[]{:S(2)}) collective-permute-start(bf16[4,72,2304]{2,1,0:T(8,128)(2,1)} %add_convert_fusion.9), channel_id=1, source_target_pairs={{0,2},{1,5},{2,0},{3,7},{4,6},{5,1},{6,4},{7,3},{8,10},{9,13},{10,... | collective-permute-start | bytes 3981320 | tf_op jit(solution)/shard_map/ppermute | solution.py:102
  559.0 52.9 %collective-permute-start.60 = (bf16[4,72,2304]{2,1,0:T(8,128)(2,1)}, bf16[4,72,2304]{2,1,0:T(8,128)(2,1)}, u32[]{:S(2)}, u32[]{:S(2)}) collective-permute-start(bf16[4,72,2304]{2,1,0:T(8,128)(2,1)} %add_convert_fusion.7), channel_id=1, source_target_pairs={{0,2},{1,5},{2,0},{3,7},{4,6},{5,1},{6,4},{7,3},{8,10},{9,13},{10,... | collective-permute-start | bytes 3981320 | tf_op jit(solution)/shard_map/ppermute | solution.py:102
  601.1 96.7 %collective-permute-start.45 = (bf16[1152,576]{0,1:T(8,128)(2,1)}, bf16[1152,576]{0,1:T(8,128)(2,1)}, u32[]{:S(2)}, u32[]{:S(2)}) collective-permute-start(bf16[1152,576]{0,1:T(8,128)(2,1)} %select_convert_fusion), channel_id=1, source_target_pairs={{0,1},{1,0},{2,3},{3,2},{4,5},{5,4},{6,7},{7,6},{8,9},{9,8},{10,11... | collective-permute-start | bytes 3981320 | tf_op jit(solution)/shard_map/ppermute | solution.py:106
  605.0 103.8 %collective-permute-start.55 = (bf16[1,72,2304]{2,1,0:T(8,128)(2,1)}, bf16[1,72,2304]{2,1,0:T(8,128)(2,1)}, u32[]{:S(2)}, u32[]{:S(2)}) collective-permute-start(bf16[1,72,2304]{2,1,0:T(8,128)(2,1)} %get-tuple-element.178), channel_id=1, source_target_pairs={{0,8},{1,9},{2,10},{3,11},{4,12},{5,13},{6,14},{7,15},{8,0},{9,1},... | collective-permute-start | bytes 995336 | tf_op jit(solution)/shard_map/ppermute | solution.py:102
  609.8 101.0 %collective-permute-start.57 = (bf16[1,72,2304]{2,1,0:T(8,128)(2,1)}, bf16[1,72,2304]{2,1,0:T(8,128)(2,1)}, u32[]{:S(2)}, u32[]{:S(2)}) collective-permute-start(bf16[1,72,2304]{2,1,0:T(8,128)(2,1)} %get-tuple-element.179), channel_id=1, source_target_pairs={{0,24},{1,25},{2,26},{3,27},{4,28},{5,29},{6,30},{7,31},{8,16},{9,... | collective-permute-start | bytes 995336 | tf_op jit(solution)/shard_map/ppermute | solution.py:102
  611.9 101.2 %collective-permute-start.56 = (bf16[1,72,2304]{2,1,0:T(8,128)(2,1)}, bf16[1,72,2304]{2,1,0:T(8,128)(2,1)}, u32[]{:S(2)}, u32[]{:S(2)}) collective-permute-start(bf16[1,72,2304]{2,1,0:T(8,128)(2,1)} %get-tuple-element.180), channel_id=1, source_target_pairs={{0,16},{1,17},{2,18},{3,19},{4,20},{5,21},{6,22},{7,23},{8,24},{9,... | collective-permute-start | bytes 995336 | tf_op jit(solution)/shard_map/ppermute | solution.py:102
  697.7 50.9 %collective-permute-start.65 = (bf16[1024,1152]{1,0:T(8,128)(2,1)}, bf16[1024,1152]{1,0:T(8,128)(2,1)}, u32[]{:S(2)}, u32[]{:S(2)}) collective-permute-start(bf16[1024,1152]{1,0:T(8,128)(2,1)} %slice.1082), channel_id=1, source_target_pairs={{0,1},{1,0},{2,3},{3,2},{4,5},{5,4},{6,7},{7,6},{8,9},{9,8},{10,11... | collective-permute-start | bytes 7077896 | tf_op jit(solution)/shard_map/ppermute | solution.py:106
  745.2 41.9 %collective-permute-start.46 = (bf16[4,72,2368]{2,1,0:T(8,128)(2,1)S(1)}, bf16[4,72,2368]{2,1,0:T(8,128)(2,1)}, u32[]{:S(2)}, u32[]{:S(2)}) collective-permute-start(bf16[4,72,2368]{2,1,0:T(8,128)(2,1)S(1)} %get-tuple-element.53), channel_id=1, source_target_pairs={{0,4},{1,3},{2,6},{3,1},{4,0},{5,7},{6,2},{7,5},{8,12},{9,11},{10,... | collective-permute-start | bytes 4091912 | tf_op jit(solution)/shard_map/ppermute | solution.py:102
  774.9 104.2 %collective-permute-start.44 = (f32[7689]{0:T(1024)S(1)}, f32[7689]{0:T(1024)}, u32[]{:S(2)}, u32[]{:S(2)}) collective-permute-start(f32[7689]{0:T(1024)S(1)} %add.508), channel_id=1, source_target_pairs={{0,1},{1,0},{2,3},{3,2},{4,5},{5,4},{6,7},{7,6},{8,9},{9,8},{10,11... | collective-permute-start | bytes 92276 | tf_op jit(solution)/shard_map/ppermute | solution.py:106
  (183 other events, 2878.4 us)

commit v3 on v2

--- a/solution.py
+++ b/solution.py
@@ -22,6 +22,8 @@
 QKV_HALF = 3 * D // 2
 QKV_PAD = -(-QKV_HALF // 128) * 128
 SPREAD = 2 * GRID * GRID
+DP = ("far", "near")
+VMEM = 60 << 20
 
 
 FIRST_DECAY = 0.9
@@ -89,17 +91,17 @@
 
 
 def dp_peers(mask):
-    spread, pair = lax.axis_size("dp"), lax.axis_size("mod")
+    spread, pair = lax.axis_size(DP), lax.axis_size("mod")
     return [(i * pair + c, (i ^ mask) * pair + c) for i in range(spread) for c in range(pair)]
 
 
 def plane_peers(masks):
-    spread, pair = lax.axis_size("dp"), lax.axis_size("mod")
+    spread, pair = lax.axis_size(DP), lax.axis_size("mod")
     return [(i * pair + c, (i ^ masks[c]) * pair + c) for i in range(spread) for c in range(pair)]
 
 
 def send(values, peers):
-    return lax.ppermute(values, ("dp", "mod"), peers)
+    return lax.ppermute(values, DP + ("mod",), peers)
 
 
 def swap_cores(values):
@@ -107,7 +109,7 @@
 
 
 def far_groups():
-    spread = lax.axis_size("dp")
+    spread = lax.axis_size(DP)
     bits = [1 << k for k in range(2, spread.bit_length() - 1)]
     if len(bits) == 2:
         return [[bits[0], bits[1], bits[0] | bits[1]]]
@@ -121,13 +123,21 @@
     return masks
 
 
-def block_places():
-    me, core = lax.axis_index("dp"), lax.axis_index("mod")
+def block_places(far):
+    me, core = lax.axis_index(DP), lax.axis_index("mod")
     second = jnp.where(core == 0, 1, 2)
     third = jnp.where(core == 0, 2, 1)
-    far = jnp.array(far_masks(), jnp.int32)
     near = jnp.stack([jnp.zeros_like(second), second, third, second | third])
-    return (me ^ (near[:, None] | far[None, :])).reshape(-1).astype(jnp.int32)
+    return ((me ^ near)[:, None] ^ far[None, :]).reshape(-1).astype(jnp.int32)
+
+
+def relative_places():
+    return block_places(jnp.array(far_masks(), jnp.int32))
+
+
+def stacked_places():
+    far = jnp.arange(lax.axis_size("far"), dtype=jnp.int32)
+    return block_places(4 * (far ^ lax.axis_index("far")))
 
 
 def move_kernel(slots, sources, targets, hold, in_sems, out_sems):
@@ -188,7 +198,7 @@
             ],
         ),
         out_shape=out_shape,
-        compiler_params=pltpu.CompilerParams(vmem_limit_bytes=40 << 20),
+        compiler_params=pltpu.CompilerParams(vmem_limit_bytes=VMEM),
         cost_estimate=pl.CostEstimate(
             flops=0,
             bytes_accessed=2 * total * plane[0] * plane[1] * jnp.dtype(kind).itemsize,
@@ -212,25 +222,45 @@
     return move_call(pick_kernel, counts, places, [values], shape, 4, plane, kind)
 
 
-def gather_blocks(block, places):
+def tie(*values):
+    return lax.optimization_barrier(values)
+
+
+def gather_far(block):
     stack = block[None]
     for group in far_groups():
         stack = jnp.concatenate([stack] + [send(stack, dp_peers(mask)) for mask in group], 0)
-    second = send(stack, plane_peers((1, 2)))
-    third = send(stack, plane_peers((2, 1)))
-    both = send(second, plane_peers((2, 1)))
-    return place_blocks([stack, second, third, both], places)
-
-
-def scatter_blocks(values, places):
-    kind = values.dtype
+    return stack
+
+
+def gather_near(stack):
+    return send(stack, plane_peers((1, 2))), send(stack, plane_peers((2, 1)))
+
+
+def gather_last(second):
+    return send(second, plane_peers((2, 1)))
+
+
+def gather_parts(block):
+    stack = gather_far(block)
+    second, third = gather_near(stack)
+    return [stack, second, third, gather_last(second)]
+
+
+def far_stack(block):
+    return lax.all_gather(block, "far", axis=0)
+
+
+def far_share(stack):
+    return lax.psum_scatter(stack, "far", scatter_dimension=0)
+
+
+def add_low(left, right):
+    return (left.astype(jnp.float32) + right.astype(jnp.float32)).astype(left.dtype)
+
+
+def scatter_far(own):
     wide = jnp.float32
-    own, second, third, both = pick_blocks(values, places)
-    from_both = send(both, plane_peers((2, 1)))
-    from_third = send(third, plane_peers((2, 1)))
-    second = (second.astype(wide) + from_both.astype(wide)).astype(kind)
-    from_second = send(second, plane_peers((1, 2)))
-    own = (own.astype(wide) + from_third.astype(wide) + from_second.astype(wide)).astype(kind)
     for group in reversed(far_groups()):
         count = own.shape[0] // (len(group) + 1)
         total = own[:count].astype(wide)
@@ -238,8 +268,15 @@
             total = total + send(
                 own[(pos + 1) * count : (pos + 2) * count], dp_peers(mask)
             ).astype(wide)
-        own = total if count == 1 else total.astype(kind)
+        own = total if count == 1 else total.astype(own.dtype)
     return own[0].astype(wide)
+
+
+def scatter_parts(own, second, third, both):
+    second = add_low(second, send(both, plane_peers((2, 1))))
+    from_third = send(third, plane_peers((2, 1)))
+    from_second = send(second, plane_peers((1, 2)))
+    return scatter_far(add_low(add_low(own, from_third), from_second))
 
 
 def all_sum(values):
@@ -248,7 +285,7 @@
 
 
 def dp_sum(values):
-    for bit in range(lax.axis_size("dp").bit_length() - 1):
+    for bit in range(lax.axis_size(DP).bit_length() - 1):
         values = values + send(values, dp_peers(1 << bit))
     return values
 
@@ -314,7 +351,7 @@
             jax.ShapeDtypeStruct((rows, heads), jnp.float32),
         ],
         scratch_shapes=[pltpu.VMEM((heads, tokens, tokens), jnp.float32)],
-        compiler_params=pltpu.CompilerParams(vmem_limit_bytes=48 << 20),
+        compiler_params=pltpu.CompilerParams(vmem_limit_bytes=VMEM),
         cost_estimate=pl.CostEstimate(
             flops=4 * rows * tokens * heads * 256,
             bytes_accessed=rows * columns * 4,
@@ -390,7 +427,7 @@
             jax.ShapeDtypeStruct(spread.shape, jnp.float32),
         ],
         scratch_shapes=[pltpu.VMEM((heads, tokens, tokens), jnp.float32)] * 2,
-        compiler_params=pltpu.CompilerParams(vmem_limit_bytes=48 << 20),
+        compiler_params=pltpu.CompilerParams(vmem_limit_bytes=VMEM),
         cost_estimate=pl.CostEstimate(
             flops=10 * rows * tokens * heads * 256,
             bytes_accessed=rows * columns * 6,
@@ -400,18 +437,188 @@
     )(qkv, upstream, logs, spread)
 
 
+def whole_block(shape):
+    return pl.BlockSpec(shape, lambda step: (0,) * len(shape), pipeline_mode=pl.Buffered(1))
+
+
+def column_tile(columns):
+    return 256 if columns % 256 == 0 else 128
+
+
+def feed_in_kernel(values_ref, weights_ref, act_ref, slope_ref):
+    weights = weights_ref[...]
+    rate = math.sqrt(2.0 / math.pi)
+    cubic = 0.044715 * rate
+    for row in range(0, values_ref.shape[0], 256):
+        pre = product(values_ref[row : row + 256, :], weights, ((1,), (0,)))
+        square = pre * pre
+        gate = 0.5 + 0.5 * jnp.tanh(pre * (rate + cubic * square))
+        act = pre * gate
+        slope = gate + (act - act * gate) * (2.0 * rate + 6.0 * cubic * square)
+        act_ref[row : row + 256, :] = act.astype(jnp.bfloat16)
+        slope_ref[row : row + 256, :] = slope.astype(jnp.bfloat16)
+
+
+def feed_in(values, weights):
+    rows, depth = values.shape
+    columns = weights.shape[1]
+    tile = column_tile(columns)
+    return pl.pallas_call(
+        feed_in_kernel,
+        grid=(columns // tile,),
+        in_specs=[whole_block((rows, depth)), pl.BlockSpec((depth, tile), lambda step: (0, step))],
+        out_specs=[pl.BlockSpec((rows, tile), lambda step: (0, step))] * 2,
+        out_shape=[jax.ShapeDtypeStruct((rows, columns), jnp.bfloat16)] * 2,
+        compiler_params=pltpu.CompilerParams(vmem_limit_bytes=VMEM),
+        cost_estimate=pl.CostEstimate(
+            flops=2 * rows * depth * columns,
+            bytes_accessed=4 * rows * columns,
+            transcendentals=rows * columns,
+        ),
+        name="feed_in",
+    )(values, weights)
+
+
+def feed_back_kernel(values_ref, weights_ref, slope_ref, out_ref):
+    weights = weights_ref[...]
+    for row in range(0, values_ref.shape[0], 256):
+        d_act = product(values_ref[row : row + 256, :], weights, ((1,), (0,)))
+        d_pre = d_act * slope_ref[row : row + 256, :].astype(jnp.float32)
+        out_ref[row : row + 256, :] = d_pre.astype(jnp.bfloat16)
+
+
+def feed_back(values, weights, slope):
+    rows, depth = values.shape
+    columns = weights.shape[1]
+    tile = column_tile(columns)
+    return pl.pallas_call(
+        feed_back_kernel,
+        grid=(columns // tile,),
+        in_specs=[
+            whole_block((rows, depth)),
+            pl.BlockSpec((depth, tile), lambda step: (0, step)),
+            pl.BlockSpec((rows, tile), lambda step: (0, step)),
+        ],
+        out_specs=pl.BlockSpec((rows, tile), lambda step: (0, step)),
+        out_shape=jax.ShapeDtypeStruct((rows, columns), jnp.bfloat16),
+        compiler_params=pltpu.CompilerParams(vmem_limit_bytes=VMEM),
+        cost_estimate=pl.CostEstimate(
+            flops=2 * rows * depth * columns,
+            bytes_accessed=4 * rows * columns,
+            transcendentals=0,
+        ),
+        name="feed_back",
+    )(values, weights, slope)
+
+
+def into_heads_kernel(values_ref, weights_ref, out_ref):
+    weights = weights_ref[...]
+    for row in range(0, values_ref.shape[0], 256):
+        out_ref[row : row + 256, :] = product(
+            values_ref[row : row + 256, :], weights, ((1,), (0,))
+        ).astype(jnp.bfloat16)
+
+
+def into_heads(values, weights):
+    rows, depth = values.shape
+    columns = weights.shape[1]
+    tile = column_tile(columns)
+    return pl.pallas_call(
+        into_heads_kernel,
+        grid=(columns // tile,),
+        in_specs=[whole_block((rows, depth)), pl.BlockSpec((depth, tile), lambda step: (0, step))],
+        out_specs=pl.BlockSpec((rows, tile), lambda step: (0, step)),
+        out_shape=jax.ShapeDtypeStruct((rows, columns), jnp.bfloat16),
+        compiler_params=pltpu.CompilerParams(vmem_limit_bytes=VMEM),
+        cost_estimate=pl.CostEstimate(
+            flops=2 * rows * depth * columns, bytes_accessed=2 * rows * columns, transcendentals=0
+        ),
+        name="into_heads",
+    )(values, weights)
+
+
+def out_of_kernel(values_ref, weights_ref, out_ref):
+    out_ref[...] = product(values_ref[...], weights_ref[...], ((1,), (1,))).astype(out_ref.dtype)
+
+
+def out_of(values, weights, kind):
+    rows, depth = values.shape
+    columns = weights.shape[0]
+    tile = min(rows, 256)
+    return pl.pallas_call(
+        out_of_kernel,
+        grid=(rows // tile,),
+        in_specs=[pl.BlockSpec((tile, depth), lambda step: (step, 0)), whole_block(weights.shape)],
+        out_specs=pl.BlockSpec((tile, columns), lambda step: (step, 0)),
+        out_shape=jax.ShapeDtypeStruct((rows, columns), kind),
+        compiler_params=pltpu.CompilerParams(vmem_limit_bytes=VMEM),
+        cost_estimate=pl.CostEstimate(
+            flops=2 * rows * depth * columns, bytes_accessed=4 * rows * columns, transcendentals=0
+        ),
+        name="out_of",
+    )(values, weights)
+
+
+def weight_grad_kernel(places, left_one, left_two, right_one, right_two, *refs):
+    outs, total = (refs[:4], refs[4])
+    total[...] = product(left_one[...], right_one[...], ((0,), (0,))) + product(
+        left_two[...], right_two[...], ((0,), (0,))
+    )
+    count, rows = outs[0].shape[:2]
+    for part in range(4):
+        for row in range(count):
+            first = pl.multiple_of(places[part * count + row] * rows, 8)
+            outs[part][row] = total[pl.ds(first, rows), :].astype(jnp.bfloat16)
+
+
+def weight_grad(left, right, places):
+    rows, depth = left[0].shape
+    columns = right[0].shape[1]
+    total = places.shape[0]
+    block = depth // total
+    if block % 8:
+        whole = outer_sum(left[0], right[0]) + outer_sum(left[1], right[1])
+        return pick_blocks(whole.astype(jnp.bfloat16).reshape(total, block, columns), places)
+    tile = column_tile(columns)
+
+    def whole_left(shape):
+        return pl.BlockSpec(shape, lambda step, _: (0, 0), pipeline_mode=pl.Buffered(1))
+
+    return pl.pallas_call(
+        weight_grad_kernel,
+        grid_spec=pltpu.PrefetchScalarGridSpec(
+            num_scalar_prefetch=1,
+            grid=(columns // tile,),
+            in_specs=[whole_left((rows, depth))] * 2
+            + [pl.BlockSpec((rows, tile), lambda step, _: (0, step))] * 2,
+            out_specs=[pl.BlockSpec((total // 4, block, tile), lambda step, _: (0, 0, step))] * 4,
+            scratch_shapes=[pltpu.VMEM((depth, tile), jnp.float32)],
+        ),
+        out_shape=[jax.ShapeDtypeStruct((total // 4, block, columns), jnp.bfloat16)] * 4,
+        compiler_params=pltpu.CompilerParams(vmem_limit_bytes=VMEM),
+        cost_estimate=pl.CostEstimate(
+            flops=4 * rows * depth * columns, bytes_accessed=4 * depth * columns, transcendentals=0
+        ),
+        name="weight_grad",
+    )(places, *left, *right)
+
+
+def shifts():
+    offset = jnp.arange(SIDE, dtype=jnp.int32)[:, None, None]
+    column = jnp.arange(GRID, dtype=jnp.int32)
+    return (offset == GRID - 1 - column[:, None] + column[None, :]).astype(jnp.float32)
+
+
 def spread_bias(relative):
     turned = relative.reshape(-1, SIDE, SIDE)[:, ::-1, ::-1]
-    rows = [turned[:, :, GRID - 1 - row : SIDE - row] for row in range(GRID)]
-    spread = jnp.stack(rows, 1).reshape(-1, GRID, SIDE * GRID)
+    spread = jnp.einsum("hed,dxy->hxey", turned, shifts(), precision=HIGH)
+    spread = spread.reshape(-1, GRID, SIDE * GRID)
     return jnp.pad(spread, ((0, 0), (0, 0), (0, SPREAD - SIDE * GRID)))
 
 
 def gather_bias(d_spread):
     parts = d_spread[:, :, : SIDE * GRID].reshape(-1, GRID, SIDE, GRID)
-    total = sum(
-        jnp.pad(parts[:, row], ((0, 0), (0, 0), (GRID - 1 - row, row))) for row in range(GRID)
-    )
+    total = jnp.einsum("hxey,dxy->hed", parts, shifts(), precision=HIGH)
     return total[:, ::-1, ::-1].reshape(-1, SIDE * SIDE)
 
 
@@ -434,30 +641,26 @@
     )
 
 
-def part_squares(block_part, mod_part, embed_part, first_core, core_index):
-    column_sq = jnp.sum(block_part * block_part, 0)
-    block_terms = [
-        jnp.sum(column_sq[: 3 * D]),
-        jnp.sum(column_sq[3 * D : 4 * D]),
-        jnp.sum(column_sq[4 * D : 4 * D + MLPW]),
-        jnp.sum(column_sq[4 * D + MLPW :]),
-    ]
-    mod_sq = jnp.sum(mod_part * mod_part, 0)
-    global_cols = core_index * mod_part.shape[1] + jnp.arange(mod_part.shape[1], dtype=jnp.int32)
-    first_mod = jnp.sum(jnp.where(global_cols < 6 * D, mod_sq, 0.0))
-    second_mod = jnp.sum(jnp.where(global_cols < 6 * D, 0.0, mod_sq))
-    row_sq = jnp.sum(embed_part * embed_part, 1)
-    bounds = [
-        0,
-        NCLASS + 1,
-        NCLASS + 1 + FREQ,
-        NCLASS + 1 + FREQ + D,
-        NCLASS + 1 + FREQ + D + PDIM,
-        NCLASS + 1 + FREQ + D + 2 * PDIM,
-    ]
-    embed_terms = [jnp.sum(row_sq[bounds[pos] : bounds[pos + 1]]) for pos in range(5)]
-    replicated = jnp.stack(block_terms + embed_terms) * first_core
-    return jnp.concatenate([replicated[:4], jnp.stack([first_mod, second_mod]), replicated[4:]])
+def segment_sums(values, bounds, first):
+    place = jnp.arange(values.shape[0], dtype=jnp.int32)
+    segment = first + sum((place >= bound).astype(jnp.int32) for bound in bounds)
+    wanted = segment[None, :] == jnp.arange(11, dtype=jnp.int32)[:, None]
+    return jnp.sum(jnp.where(wanted, values[None, :], 0.0), 1)
+
+
+def mod_squares(values, core):
+    columns = jnp.sum(values * values, 0)
+    bound = 6 * D - core * values.shape[1]
+    return segment_sums(columns, [bound], 4)
+
+
+def embed_squares(values):
+    bounds = [NCLASS + 1, NCLASS + 1 + FREQ, NCLASS + 1 + FREQ + D, NCLASS + 1 + FREQ + D + PDIM]
+    return segment_sums(jnp.sum(values * values, 1), bounds, 6)
+
+
+def block_squares(values):
+    return segment_sums(jnp.sum(values * values, 0), [3 * D, 4 * D, 4 * D + MLPW], 0)
 
 
 def adam_update(grad, first, second, weight, clip):
@@ -494,13 +697,13 @@
     low = jnp.bfloat16
     wide = jnp.float32
     core = lax.axis_index("mod")
-    spread = lax.axis_size("dp")
+    spread = lax.axis_size(DP)
     images = latents.shape[0]
     length = latents.shape[1]
     rows = images * length
     share = embed_weights.shape[1]
     count = float(images * spread * lax.axis_size("mod") * length * latents.shape[2])
-    places = block_places()
+    relative, stacked = (relative_places(), stacked_places())
 
     half = D // 2
     wide_half = MLPW // 2
@@ -510,7 +713,8 @@
     )
     in_part, out_part = core_half(block_low, core, [4 * D, 4 * D + MLPW], wide_half)
     pad_part = jnp.zeros((block_low.shape[0], QKV_PAD - QKV_HALF), low)
-    attn_part = jnp.concatenate([q_part, k_part, v_part, pad_part, p_part], 1)
+    attn_part = jnp.concatenate([q_part, k_part, v_part, pad_part], 1)
+    in_part = jnp.concatenate([in_part, p_part], 1)
 
     start = NCLASS + 1
     chosen = jnp.where(drops == 1, NCLASS, labels)
@@ -530,34 +734,61 @@
         ],
         0,
     )
-    small = gather_blocks(small, places)
-    everyone = small[:, FREQ + 2 * PDIM :].reshape(spread, -1)[:, : 2 * images * 4]
+    small_far = gather_far(small)
+    attn_part, small_far = tie(attn_part, small_far)
+    attn_far = far_stack(attn_part)
+    small_second, small_third = gather_near(small_far)
+    small_second, attn_far = tie(small_second, attn_far)
+    small = [small_far, small_second, small_third, gather_last(small_second)]
+    everyone = jnp.concatenate([part[:, FREQ + 2 * PDIM :] for part in small], 0)
+    everyone = everyone.reshape(spread, -1)[:, : 2 * images * 4]
     everyone = everyone.reshape(spread * 2 * images, 4).astype(wide)
     all_steps = 32.0 * everyone[:, 0] + everyone[:, 1]
     all_chosen = (32.0 * everyone[:, 2] + everyone[:, 3]).astype(jnp.int32)
-    small = small[:, : FREQ + 2 * PDIM].transpose(1, 0, 2).reshape(FREQ + 2 * PDIM, D)
+    small = place_blocks(small, relative)[:, : FREQ + 2 * PDIM]
+    small = small.transpose(1, 0, 2).reshape(FREQ + 2 * PDIM, D)
     time_in = small[:FREQ].astype(wide)
     patch = small[FREQ : FREQ + PDIM]
     head = small[FREQ + PDIM :]
 
-    attn_low = gather_blocks(attn_part, places).reshape(D, -1)
-    in_low = gather_blocks(in_part, places).reshape(D, -1)
-    out_low = gather_blocks(out_part, places).reshape(D, -1)
-    qkv_low = attn_low[:, :QKV_PAD]
-    proj_half = attn_low[:, QKV_PAD:]
-    proj_low = both_cores(proj_half, swap_cores(proj_half), core, 1)
+    attn_second, attn_third = gather_near(attn_far)
+    in_part, attn_far = tie(in_part, attn_far)
+    in_far = far_stack(in_part)
 
     sinus = sinusoid(all_steps)
     pre_time = jnp.dot(sinus, time_in, precision=HIGH, preferred_element_type=wide)
     time_act = jax.nn.silu(pre_time)
-    onehot = all_chosen[:, None] == jnp.arange(start, dtype=jnp.int32)[None, :]
+    image_of = relative[:, None] * 2 * images + jnp.arange(2 * images, dtype=jnp.int32)[None, :]
+    sorting = image_of.reshape(1, -1) == jnp.arange(image_of.size, dtype=jnp.int32)[:, None]
+
+    def sort_images(values):
+        return jnp.dot(sorting.astype(wide), values, precision=HIGH, preferred_element_type=wide)
+
+    sorted_sinus = sort_images(sinus)
+    sorted_act = sort_images(time_act)
+    classes = jnp.arange(start, dtype=jnp.int32)[None, :]
+    sorted_onehot = sort_images(all_chosen[:, None].astype(wide)).astype(jnp.int32) == classes
+    first_column = lax.axis_index(DP) * share
+    sorted_slope = sort_images(
+        silu_slope(lax.dynamic_slice_in_dim(pre_time, first_column, share, 1))
+    )
+    onehot = all_chosen[:, None] == classes
     cond = jnp.dot(time_act, time_out, precision=HIGH, preferred_element_type=wide) + dense(
         onehot.astype(low), table
     )
     scaled = jax.nn.silu(cond).astype(low)
+    scaled, attn_second, attn_third = tie(scaled, attn_second, attn_third)
+    attn_both = gather_last(attn_second)
     mod_low = mod_weights.astype(low)
     mod_partial = dense(scaled, mod_low).astype(low)
-    half_mod = scatter_blocks(mod_partial.reshape(spread, 2 * images, -1), places)
+    half_mod = scatter_parts(*jnp.split(mod_partial.reshape(spread, 2 * images, -1), 4))
+    heads = HEADS // 2
+    bias_rows = spread_bias(jnp.where(core == 0, rel_bias[:heads], rel_bias[heads:]))
+    half_mod, attn_both, in_far, bias_rows = tie(half_mod, attn_both, in_far, bias_rows)
+    qkv_low = place_blocks([attn_far, attn_second, attn_third, attn_both], stacked).reshape(D, -1)
+    in_second, in_third = gather_near(in_far)
+    out_part, in_far = tie(out_part, in_far)
+    out_far = far_stack(out_part)
     mine = jnp.where(core == 0, half_mod[:images], half_mod[images:])
     theirs = jnp.where(core == 0, half_mod[images:], half_mod[:images])
     modulation = both_cores(mine, swap_cores(theirs), core, 1).reshape(images, 8, D)
@@ -567,14 +798,11 @@
             normed * (1.0 + modulation[:, shift + 1 : shift + 2]) + modulation[:, shift : shift + 1]
         ).astype(low)
 
-    def with_sibling(values):
-        flat = values.reshape(rows, -1)
-        return jnp.concatenate([flat, swap_cores(flat)], 0)
-
-    def sum_cores(partial):
-        return (partial[:rows] + swap_cores(partial[rows:].astype(low)).astype(wide)).reshape(
-            images, length, -1
-        )
+    def flat(values):
+        return values.reshape(rows, -1)
+
+    def sum_cores(mine, theirs):
+        return (mine + swap_cores(theirs).astype(wide)).reshape(images, length, -1)
 
     alpha_bar = jnp.sum(
         jnp.where(
@@ -590,19 +818,35 @@
     ).astype(low)
     hidden0 = dense(mixed, patch)
     normed1, inverse1 = layer_norm(hidden0)
-    attn_in = with_sibling(moved(normed1, 0))
-    qkv = dense(attn_in, qkv_low).astype(low)
-    heads = HEADS // 2
-    bias_rows = spread_bias(jnp.where(core == 0, rel_bias[:heads], rel_bias[heads:]))
-    heads_out, logs = attention(qkv, bias_rows)
-    attn_out = both_cores(heads_out[:rows], swap_cores(heads_out[rows:]), core, 1)
+    attn_in = flat(moved(normed1, 0))
+    attn_in_two = swap_cores(attn_in)
+    qkv = into_heads(attn_in, qkv_low)
+    qkv_two = into_heads(attn_in_two, qkv_low)
+    heads_two, logs_two = attention(qkv_two, bias_rows)
+    qkv, logs_two, in_second, in_third, out_far = tie(qkv, logs_two, in_second, in_third, out_far)
+    heads_two = swap_cores(heads_two)
+    in_both = gather_last(in_second)
+    out_second, out_third = gather_near(out_far)
+    heads_one, logs = attention(qkv, bias_rows)
+    heads_one, in_both = tie(heads_one, in_both)
+    in_low = place_blocks([in_far, in_second, in_third, in_both], stacked).reshape(D, -1)
+    proj_half = in_low[:, wide_half:]
+    in_low = in_low[:, :wide_half]
+    proj_low = both_cores(proj_half, swap_cores(proj_half), core, 1)
+    attn_out = both_cores(heads_one, heads_two, core, 1)
     branch_one = dense(attn_out, proj_low).reshape(images, length, D)
     hidden1 = hidden0 + modulation[:, 2:3] * branch_one
     normed2, inverse2 = layer_norm(hidden1)
-    mlp_in = with_sibling(moved(normed2, 3))
-    pre_act = dense(mlp_in, in_low)
-    act = jax.nn.gelu(pre_act, approximate=True).astype(low)
-    branch_two = sum_cores(dense_trans(act, out_low))
+    mlp_in = flat(moved(normed2, 3))
+    mlp_in_two = swap_cores(mlp_in)
+    act, slope = feed_in(mlp_in, in_low)
+    act, out_second, out_third, mlp_in_two = tie(act, out_second, out_third, mlp_in_two)
+    out_both = gather_last(out_second)
+    act_two, slope_two = feed_in(mlp_in_two, in_low)
+    act_two, out_both = tie(act_two, out_both)
+    out_low = place_blocks([out_far, out_second, out_third, out_both], stacked).reshape(D, -1)
+    branch_theirs = out_of(act_two, out_low, low)
+    branch_two = sum_cores(out_of(act, out_low, wide), branch_theirs)
     hidden2 = hidden1 + modulation[:, 5:6] * branch_two
 
     normed3, inverse3 = layer_norm(hidden2)
@@ -617,37 +861,79 @@
     d_shift3 = jnp.sum(d_final, 1)
     d_hidden2 = norm_back(d_final * (1.0 + modulation[:, 7:8]), normed3, inverse3)
 
-    d_branch_two = with_sibling((modulation[:, 5:6] * d_hidden2).astype(low))
+    d_branch_two = flat((modulation[:, 5:6] * d_hidden2).astype(low))
+    d_branch_two_two = swap_cores(d_branch_two)
     d_gate2 = jnp.sum(d_hidden2 * branch_two, 1)
-    d_act = dense(d_branch_two, out_low)
-    gelu_pull = jax.vjp(lambda entries: jax.nn.gelu(entries, approximate=True), pre_act)[1]
-    d_pre = gelu_pull(d_act)[0].astype(low)
-    g_out = scatter_blocks(
-        outer_sum(d_branch_two, act).astype(low).reshape(spread, -1, wide_half), places
-    )
-    d_mlp_in = sum_cores(dense_trans(d_pre, in_low))
-    g_in = scatter_blocks(
-        outer_sum(mlp_in, d_pre).astype(low).reshape(spread, -1, wide_half), places
-    )
+    d_pre = feed_back(d_branch_two, out_low, slope)
+    d_pre, d_branch_two_two = tie(d_pre, d_branch_two_two)
+    d_pre_two = feed_back(d_branch_two_two, out_low, slope_two)
+    out_own, out_second, out_third, out_both = weight_grad(
+        (d_branch_two, d_branch_two_two), (act, act_two), stacked
+    )
+    out_back = send(out_both, plane_peers((2, 1)))
+    d_pre, out_third = tie(d_pre, out_third)
+    d_mlp_theirs = swap_cores(out_of(d_pre_two, in_low, low))
+    d_mlp_mine = out_of(d_pre, in_low, wide)
+    d_pre, d_mlp_mine, out_back = tie(d_pre, d_mlp_mine, out_back)
+    out_second = send(add_low(out_second, out_back), plane_peers((1, 2)))
+    out_third = send(out_third, plane_peers((2, 1)))
+    in_own, in_second, in_third, in_both = weight_grad(
+        (mlp_in, mlp_in_two), (d_pre, d_pre_two), stacked
+    )
+    in_both, d_mlp_theirs, d_mlp_mine = tie(in_both, d_mlp_theirs, d_mlp_mine)
+    d_mlp_in = (d_mlp_mine + d_mlp_theirs.astype(wide)).reshape(images, length, D)
     d_scale2 = jnp.sum(d_mlp_in * normed2, 1)
     d_shift2 = jnp.sum(d_mlp_in, 1)
     d_hidden1 = d_hidden2 + norm_back(d_mlp_in * (1.0 + modulation[:, 4:5]), normed2, inverse2)
     d_branch_one = (modulation[:, 2:3] * d_hidden1).astype(low).reshape(rows, D)
+    d_branch_one, out_second, out_third, in_both = tie(
+        d_branch_one, out_second, out_third, in_both
+    )
+    in_back = send(in_both, plane_peers((2, 1)))
+    g_out = far_share(add_low(add_low(out_own, out_third), out_second))
     d_gate1 = jnp.sum(d_hidden1 * branch_one, 1)
     d_attn_out = dense_trans(d_branch_one, proj_low).astype(low)
     d_mine = jnp.where(core == 0, d_attn_out[:, :half], d_attn_out[:, half:])
     d_theirs = jnp.where(core == 0, d_attn_out[:, half:], d_attn_out[:, :half])
-    d_heads = jnp.concatenate([d_mine, swap_cores(d_theirs)], 0)
+    d_theirs = swap_cores(d_theirs)
     g_proj = outer_sum(attn_out, d_branch_one)
     g_proj_mine = jnp.where(core == 0, g_proj[:, :half], g_proj[:, half:])
     g_proj_theirs = jnp.where(core == 0, g_proj[:, half:], g_proj[:, :half]).astype(low)
     g_proj = (g_proj_mine + swap_cores(g_proj_theirs).astype(wide)).astype(low)
-    d_qkv, d_spread = attention_back(qkv, d_heads, logs, bias_rows)
-    d_attn_in = sum_cores(dense_trans(d_qkv, qkv_low))
-    g_qkv = outer_sum(attn_in, d_qkv).astype(low)
-    g_attn = scatter_blocks(
-        jnp.concatenate([g_qkv, g_proj], 1).reshape(spread, -1, QKV_PAD + half), places
-    )
+    d_mine, in_back, in_third, g_proj = tie(d_mine, in_back, in_third, g_proj)
+    in_second = send(add_low(in_second, in_back), plane_peers((1, 2)))
+    in_third = send(in_third, plane_peers((2, 1)))
+    d_qkv, d_spread = attention_back(qkv, d_mine, logs, bias_rows)
+    proj_own, proj_second, proj_third, proj_both = pick_blocks(
+        g_proj.reshape(spread, -1, half), stacked
+    )
+    d_qkv, proj_both, d_theirs, g_out, in_second, in_third = tie(
+        d_qkv, proj_both, d_theirs, g_out, in_second, in_third
+    )
+    g_in = far_share(add_low(add_low(in_own, in_third), in_second))
+    proj_back = send(proj_both, plane_peers((2, 1)))
+    d_qkv_two, d_spread_two = attention_back(qkv_two, d_theirs, logs_two, bias_rows)
+    d_spread = d_spread + d_spread_two
+    d_qkv_two, proj_back, proj_third = tie(d_qkv_two, proj_back, proj_third)
+    proj_second = send(add_low(proj_second, proj_back), plane_peers((1, 2)))
+    proj_third = send(proj_third, plane_peers((2, 1)))
+    rel_half = gather_bias(d_spread)
+    packed = jnp.concatenate([rel_half.reshape(-1), (loss_here * jnp.ones(1, wide))])
+    packed = dp_sum(packed)
+    d_attn_theirs = swap_cores(out_of(d_qkv_two, qkv_low, low))
+    d_attn_mine = out_of(d_qkv, qkv_low, wide)
+    d_qkv_two, d_attn_mine, proj_second, proj_third = tie(
+        d_qkv_two, d_attn_mine, proj_second, proj_third
+    )
+    g_proj = far_share(add_low(add_low(proj_own, proj_third), proj_second))
+    attn_own, attn_second, attn_third, attn_both = weight_grad(
+        (attn_in, attn_in_two), (d_qkv, d_qkv_two), stacked
+    )
+    attn_both, attn_third, packed, d_attn_mine, d_attn_theirs, g_in = tie(
+        attn_both, attn_third, packed, d_attn_mine, d_attn_theirs, g_in
+    )
+    attn_back = send(attn_both, plane_peers((2, 1)))
+    d_attn_in = (d_attn_mine + d_attn_theirs.astype(wide)).reshape(images, length, D)
     d_scale1 = jnp.sum(d_attn_in * normed1, 1)
     d_shift1 = jnp.sum(d_attn_in, 1)
     d_hidden0 = d_hidden1 + norm_back(d_attn_in * (1.0 + modulation[:, 1:2]), normed1, inverse1)
@@ -661,41 +947,51 @@
     d_keep = jnp.where(core == 0, d_modulation[:, :mod_half], d_modulation[:, mod_half:])
     d_give = jnp.where(core == 0, d_modulation[:, mod_half:], d_modulation[:, :mod_half])
     d_pair = both_cores(d_keep, swap_cores(d_give), core, 0)
-    d_all = gather_blocks(d_pair, places).reshape(spread * 2 * images, mod_half)
+    d_pair, attn_back = tie(d_pair, attn_back)
+    attn_second = send(add_low(attn_second, attn_back), plane_peers((1, 2)))
+    attn_third = send(attn_third, plane_peers((2, 1)))
+    d_parts = gather_parts(d_pair)
+    d_parts[0], attn_second, attn_third = tie(d_parts[0], attn_second, attn_third)
+    g_qkv = far_share(add_low(add_low(attn_own, attn_third), attn_second))
+    d_all = jnp.concatenate(d_parts, 0).reshape(spread * 2 * images, mod_half)
     mod_grad = outer_sum(scaled, d_all)
     d_scaled = dense_trans(d_all, mod_low)
-    d_scaled = d_scaled + swap_cores(d_scaled)
-    d_cond = d_scaled * silu_slope(cond)
-    g_table = first_contract(onehot.astype(wide), d_cond)
-    g_time_out = first_contract(time_act, d_cond)
+    theirs = jnp.split(swap_cores(d_scaled), 4)
+    d_scaled = d_scaled + jnp.concatenate([theirs[0], theirs[2], theirs[1], theirs[3]], 0)
+    d_cond = sort_images(d_scaled * silu_slope(cond))
+    g_table = first_contract(sorted_onehot.astype(wide), d_cond)
+    g_time_out = first_contract(sorted_act, d_cond)
     d_time = lax.dot_general(
         d_cond, time_out, (((1,), (1,)), ((), ())), precision=HIGH, preferred_element_type=wide
     )
     g_ends = jnp.concatenate([g_patch, g_head], 0)
     g_ends = g_ends + swap_cores(g_ends)
     tail = jnp.concatenate([d_time, g_ends], 0)
-    tail = scatter_blocks(tail.reshape(-1, spread, share).transpose(1, 0, 2), places)
+    tail = tail.reshape(-1, spread, share).transpose(1, 0, 2)
+    tail = scatter_parts(*pick_blocks(tail, relative))
+    tail, g_qkv, g_proj = tie(tail, g_qkv, g_proj)
     d_time_here, g_ends = (tail[: -2 * PDIM], tail[-2 * PDIM :])
-    first_column = lax.axis_index("dp") * share
-    pre_time_here = lax.dynamic_slice_in_dim(pre_time, first_column, share, 1)
-    g_time_in = first_contract(sinus, d_time_here * silu_slope(pre_time_here))
+    g_time_in = first_contract(sorted_sinus, d_time_here * sorted_slope)
     embed_grad = jnp.concatenate([g_table, g_time_in, g_time_out, g_ends], 0)
 
-    g_here = jnp.concatenate([g_attn, g_in, g_out], 1).astype(low)
+    g_here = jnp.concatenate([g_qkv, g_in, g_proj, g_out], 1)
     g_there = swap_cores(g_here)
-    zero_part = jnp.where(core == 0, g_here, g_there).astype(wide)
-    one_part = jnp.where(core == 0, g_there, g_here).astype(wide)
-    bounds = [0, half, 2 * half, 3 * half, QKV_PAD, QKV_PAD + half]
-    bounds = bounds + [bounds[-1] + wide_half, bounds[-1] + 2 * wide_half]
+    g_mine = g_here.astype(wide)
+    g_squares = segment_sums(
+        jnp.sum(g_mine * g_mine, 0), [QKV_PAD, QKV_PAD + wide_half, QKV_PAD + wide_half + half], 0
+    )
+    g_squares = g_squares[jnp.array([0, 2, 1, 3] + list(range(4, 11)))]
+    zero_part = jnp.where(core == 0, g_here, g_there)
+    one_part = jnp.where(core == 0, g_there, g_here)
+    after = QKV_PAD + wide_half
+    spans = [(part * half, half) for part in range(3)] + [(after, half)]
+    spans = spans + [(QKV_PAD, wide_half), (after + half, wide_half)]
     pieces = []
-    for low_end, high_end in zip(bounds[:-1], bounds[1:]):
-        if (low_end, high_end) != (3 * half, QKV_PAD):
-            pieces = pieces + [zero_part[:, low_end:high_end], one_part[:, low_end:high_end]]
-    block_grad = jnp.concatenate(pieces, 1)
-
-    rel_half = gather_bias(d_spread)
-    packed = jnp.concatenate([rel_half.reshape(-1), (loss_here * jnp.ones(1, wide))])
-    packed = dp_sum(packed)
+    for low_end, width in spans:
+        pieces.append(zero_part[:, low_end : low_end + width])
+        pieces.append(one_part[:, low_end : low_end + width])
+    block_grad = jnp.concatenate(pieces, 1).astype(wide)
+
     packed_other = swap_cores(packed)
     rel_grad = both_cores(
         packed[:-1].reshape(heads, -1), packed_other[:-1].reshape(heads, -1), core, 0
@@ -703,12 +999,17 @@
     loss_sum = packed[-1] + packed_other[-1]
 
     first_core = (core == 0).astype(wide)
+
+    def replica_squares(block, mod, embed):
+        copied = block_squares(block) + embed_squares(embed)
+        return first_core * copied + mod_squares(mod, core)
+
     grad_parts, weight_parts = jnp.split(
         all_sum(
             jnp.concatenate(
                 [
-                    part_squares(block_grad, mod_grad, embed_grad, first_core, core),
-                    part_squares(block_weights, mod_weights, embed_weights, first_core, core),
+                    g_squares + mod_squares(mod_grad, core) + first_core * embed_squares(embed_grad),
+                    replica_squares(block_weights, mod_weights, embed_weights),
                 ]
             )
         ),
@@ -726,7 +1027,7 @@
         embed_grad, embed_first, embed_second, embed_weights, clip
     )
     rel_m, rel_s, rel_step = adam_update(rel_grad, rel_first, rel_second, rel_bias, clip)
-    update_parts = all_sum(part_squares(block_step, mod_step, embed_step, first_core, core))
+    update_parts = all_sum(replica_squares(block_step, mod_step, embed_step))
     update_sq = jnp.concatenate([update_parts, jnp.sum(rel_step * rel_step)[None]])
     weight_norm = jnp.sqrt(weight_sq)
     update_norm = jnp.sqrt(update_sq)
@@ -782,45 +1083,47 @@
 
 
 def solution(mesh):
+    spread, pair = mesh.devices.shape
+    grid = jax.sharding.Mesh(mesh.devices.reshape(spread // 4, 4, pair), DP + ("mod",))
     placed = (
-        P(("dp", "mod"), None, None),
-        P(("dp", "mod"), None, None),
-        P(("dp", "mod")),
-        P(("dp", "mod")),
-        P(("dp", "mod")),
-        P("dp", None),
-        P("dp", None),
-        P("dp", None),
-        P("dp", "mod"),
-        P("dp", "mod"),
-        P("dp", "mod"),
-        P(None, "dp"),
-        P(None, "dp"),
-        P(None, "dp"),
+        P(DP + ("mod",), None, None),
+        P(DP + ("mod",), None, None),
+        P(DP + ("mod",)),
+        P(DP + ("mod",)),
+        P(DP + ("mod",)),
+        P(DP, None),
+        P(DP, None),
+        P(DP, None),
+        P(DP, "mod"),
+        P(DP, "mod"),
+        P(DP, "mod"),
+        P(None, DP),
+        P(None, DP),
+        P(None, DP),
         P(),
         P(),
         P(),
     )
     return jax.shard_map(
         on_device,
-        mesh=mesh,
+        mesh=grid,
         in_specs=placed,
         out_specs=(
             P(),
             P(),
             P(),
-            P("dp", None),
-            P("dp", None),
-            P("dp", None),
-            P("dp", None),
-            P("dp", "mod"),
-            P("dp", "mod"),
-            P("dp", "mod"),
-            P("dp", "mod"),
-            P(None, "dp"),
-            P(None, "dp"),
-            P(None, "dp"),
-            P(None, "dp"),
+            P(DP, None),
+            P(DP, None),
+            P(DP, None),
+            P(DP, None),
+            P(DP, "mod"),
+            P(DP, "mod"),
+            P(DP, "mod"),
+            P(DP, "mod"),
+            P(None, DP),
+            P(None, DP),
+            P(None, DP),
+            P(None, DP),
             P(),
             P(),
             P(),

time: 972 us -> 806 us (0.83)
  Pallas kernels: 112 us -> 289 us
  matrix products: 208 us -> 52.3 us
  waiting for transfers between devices: 241 us -> 131 us
  local copies, waits for them, and re-layouts: 133 us -> 76.8 us
  starting transfers between devices: 113 us -> 69 us
  blocking collectives: 0 us -> 21.5 us
  other arithmetic: 151 us -> 134 us
  between operations: 9.2 us -> 21.9 us
    pallas_call x0 -> x15, Pallas kernels: none -> 188 us  [the longest x6 62.1 us: out_of(): pl.pallas_call(out_of_kernel, grid=(rows // tile,), in_specs=[pl.BlockSpe...]
    ppermute x72 -> x57, waiting for transfers between devices: 234 us -> 110 us  [send(): return lax.ppermute(values, DP + ('mod',), peers)]
    dot_general x8 -> x5, matrix products: 73.4 us -> 12.8 us  [dense(): return jnp.dot(left, right, preferred_element_type=jnp.float32)]
    dot_general x6 -> x3, matrix products: 62.2 us -> 10 us  [dense_trans(): lax.dot_general(left, right, (((left.ndim - 1,), (1,)), ((), ())), prefer...]
    dot_general x7 -> x4, matrix products: 63.8 us -> 15.6 us  [outer_sum(): lax.dot_general(flat_left, flat_right, (((0,), (0,)), ((), ())), preferre...]
    ppermute x72 -> x57, starting transfers between devices: 111 us -> 64.9 us  [send(): return lax.ppermute(values, DP + ('mod',), peers)]
    another operation x22 -> x2, local copies, waits for them, and re-layouts: 39.5 us -> 0.12 us  [the longest x17 21.9 us: spread_bias(): spread = jnp.stack(rows, 1).reshape(-1, GRID, SIDE * GRID)]
    slice x37 -> x14, local copies, waits for them, and re-layouts: 41.2 us -> 10.6 us  [the longest x1 5.28 us: on_device(): in_low = in_low[:, :wide_half]]
  transfers between devices with their start and end apart: 91 -> 82, of which waited for: 42 -> 37; matrix products, arithmetic and copies ran while one was open for 32% -> 20% of each run, Pallas kernels for 11% -> 31%
where the time goes in v3:
time: 806 us; the launch traced here: 795 us
  Pallas kernels  289 us (36%)
  other arithmetic  134 us (17%)
  waiting for transfers between devices  131 us (16%)
  local copies, waits for them, and re-layouts  76.8 us (10%)
  starting transfers between devices  69 us (9%)
  matrix products  52.3 us (6%)
  between operations  21.9 us (3%)
  blocking collectives  21.5 us (3%)
    ppermute x57, waiting for transfers between devices, send(): return lax.ppermute(values, DP + ('mod',), peers)  110 us
    ppermute x57, starting transfers between devices, send(): return lax.ppermute(values, DP + ('mod',), peers)  64.9 us
    pallas_call x6, Pallas kernels, out_of(): pl.pallas_call(out_of_kernel, grid=(rows // tile,), in_specs=[pl.BlockSpe...  62.1 us
    pallas_call x3, Pallas kernels, weight_grad(): pl.pallas_call(weight_grad_kernel, grid_spec=pltpu.PrefetchScalarGridSpec...  50.8 us
    pallas_call x2, Pallas kernels, attention_back(): pl.pallas_call(functools.partial(attention_back_kernel, heads), grid=(row...  42.7 us
    pallas_call x2, Pallas kernels, attention(): pl.pallas_call(functools.partial(attention_kernel, heads), grid=(rows //...  32.1 us
    pallas_call x2, Pallas kernels, feed_in(): pl.pallas_call(feed_in_kernel, grid=(columns // tile,), in_specs=[whole_b...  29.2 us
    pallas_call x6, Pallas kernels, move_call(): pl.pallas_call(functools.partial(kernel, counts, slots), grid_spec=pltpu....  26.2 us
  transfers between devices with their start and end apart: 82, of which 37 were waited for; matrix products, arithmetic and copies ran while one was open for 20% of the time, Pallas kernels for 31%

profile of v3, /device:TPU:0, one launch (start us, length us, event | category | flops | bytes accessed | tf_op | source)
XLA Modules:
  0.0 795.1 jit_solution(9479212518322038671)
XLA Ops:
  35.6 21.5 %all-gather = bf16[288,1792]{1,0:T(8,128)(2,1)S(1)} all-gather(bf16[72,1792]{1,0:T(8,128)(2,1)S(1)} %concatenate.146), channel_id=2, replica_groups=mesh['far'=4,'near'=4,'mod'=2] {'far'}, dimensions={0}, use_global_device_ids=true | all-gather | bytes 1290240 | tf_op jit(solution)/shard_map/all_gather | solution.py:251
  121.1 14.9 %all-gather.6.cloned.1.call-done = bf16[288,2880]{1,0:T(8,128)(2,1)} async-done(((bf16[72,2880]{1,0:T(8,128)(2,1)}), bf16[288,2880]{1,0:T(8,128)(2,1)}) %all-gather.6.cloned.1.call-update) | async-done | bytes 1658896 | tf_op jit(solution)/shard_map/all_gather | solution.py:251
  149.6 9.9 %into_heads.2.qkv_ref = bf16[1024,1792]{1,0:T(8,128)(2,1)} custom-call(bf16[1024,1152]{1,0:T(8,128)(2,1)} %bitcast.224, bf16[1152,1792]{1,0:T(8,128)(2,1)} %bitcast.215), custom_call_target="tpu_custom_call" | custom-call | flops 4227858432 | bytes 3670016 | tf_op jit(solution)/shard_map/into_heads/pallas_call | solution.py:526
  159.5 9.9 %into_heads.3.qkv_ref = bf16[1024,1792]{1,0:T(8,128)(2,1)} custom-call(bf16[1024,1152]{1,0:T(8,128)(2,1)} %collective-permute-done.17.values_ref.left_two, bf16[1152,1792]{1,0:T(8,128)(2,1)} %bitcast.216), custom_call_target="tpu_custom_call" | custom-call | flops 4227858432 | bytes 3670016 | tf_op jit(solution)/shard_map/into_heads/pallas_call | solution.py:526
  169.4 16.0 %attention.2 = (bf16[1024,576]{1,0:T(8,128)(2,1)}, f32[1024,8]{1,0:T(8,128)}) custom-call(bf16[1024,1792]{1,0:T(8,128)(2,1)} %into_heads.3.qkv_ref, f32[8,16,512]{2,1,0:T(8,128)} %pad.13.spread_ref), custom_call_target="tpu_custom_call" | custom-call | flops 2147483648 | bytes 7340032 | tf_op jit(solution)/shard_map/attention/pallas_call | solution.py:338
  187.4 16.0 %attention.3 = (bf16[1024,576]{1,0:T(8,128)(2,1)}, f32[1024,8]{1,0:T(8,128)}) custom-call(bf16[1024,1792]{1,0:T(8,128)(2,1)} %into_heads.2.qkv_ref, f32[8,16,512]{2,1,0:T(8,128)} %pad.13.spread_ref), custom_call_target="tpu_custom_call" | custom-call | flops 2147483648 | bytes 7340032 | tf_op jit(solution)/shard_map/attention/pallas_call | solution.py:338
  250.1 14.6 %feed_in.2 = (bf16[1024,2304]{1,0:T(8,128)(2,1)}, bf16[1024,2304]{1,0:T(8,128)(2,1)}) custom-call(bf16[1024,1152]{1,0:T(8,128)(2,1)} %bitcast.37.values_ref.left_one, bf16[1152,2304]{1,0:T(8,128)(2,1)} %slice.434.weights_ref), custom_call_target="tpu_custom_call" | custom-call | flops 5435817984 | bytes 9437184 | tf_op jit(solution)/shard_map/feed_in/pallas_call | solution.py:466
  275.3 14.6 %feed_in.3 = (bf16[1024,2304]{1,0:T(8,128)(2,1)}, bf16[1024,2304]{1,0:T(8,128)(2,1)}) custom-call(bf16[1024,1152]{1,0:T(8,128)(2,1)} %collective-permute-done.25.values_ref.left_two, bf16[1152,2304]{1,0:T(8,128)(2,1)} %slice.434.weights_ref), custom_call_target="tpu_custom_call" | custom-call | flops 5435817984 | bytes 9437184 | tf_op jit(solution)/shard_map/feed_in/pallas_call | solution.py:466
  297.3 10.7 %out_of.7 = bf16[1024,1152]{1,0:T(8,128)(2,1)} custom-call(bf16[1024,2304]{1,0:T(8,128)(2,1)} %get-tuple-element.156.values_ref.right_two, bf16[1152,2304]{1,0:T(8,128)(2,1)} %bitcast.210), custom_call_target="tpu_custom_call" | custom-call | flops 5435817984 | bytes 4718592 | tf_op jit(solution)/shard_map/out_of/pallas_call | solution.py:548
  308.2 11.1 %out_of.6 = f32[1024,1152]{1,0:T(8,128)} custom-call(bf16[1024,2304]{1,0:T(8,128)(2,1)} %get-tuple-element.150.values_ref.right_one, bf16[1152,2304]{1,0:T(8,128)(2,1)} %bitcast.211), custom_call_target="tpu_custom_call" | custom-call | flops 5435817984 | bytes 4718592 | tf_op jit(solution)/shard_map/out_of/pallas_call | solution.py:548
  338.2 13.0 %feed_back.2.values_ref.right_one = bf16[1024,2304]{1,0:T(8,128)(2,1)} custom-call(bf16[1024,1152]{1,0:T(8,128)(2,1)} %bitcast.42.values_ref.left_one, bf16[1152,2304]{1,0:T(8,128)(2,1)} %bitcast.212, bf16[1024,2304]{1,0:T(8,128)(2,1)} %get-tuple-element.157.slope_ref), custom_call_target="tpu_custom_call" | custom-call | flops 5435817984 | bytes 9437184 | tf_op jit(solution)/shard_map/feed_back/pallas_call | solution.py:494
  351.2 18.0 %weight_grad.3 = (bf16[4,72,2304]{2,1,0:T(8,128)(2,1)}, bf16[4,72,2304]{2,1,0:T(8,128)(2,1)}, bf16[4,72,2304]{2,1,0:T(8,128)(2,1)}, bf16[4,72,2304]{2,1,0:T(8,128)(2,1)}) custom-call(s32[16]{0:T(128)} %xor.66.places, bf16[1024,1152]{1,0:T(8,128)(2,1)} %bitcast.42.values_ref.left_one, bf16[1024,1152]{1,0:T(8,128)(2,1)} %collective-permute-done.28.left_two.values_ref, ...), custom_call_target="tpu_custom_call" | custom-call | flops 10871635968 | bytes 10616832 | tf_op jit(solution)/shard_map/weight_grad/pallas_call | solution.py:587
  370.9 12.9 %feed_back.3.right_two.values_ref = bf16[1024,2304]{1,0:T(8,128)(2,1)} custom-call(bf16[1024,1152]{1,0:T(8,128)(2,1)} %collective-permute-done.28.left_two.values_ref, bf16[1152,2304]{1,0:T(8,128)(2,1)} %bitcast.213, bf16[1024,2304]{1,0:T(8,128)(2,1)} %get-tuple-element.164.slope_ref), custom_call_target="tpu_custom_call" | custom-call | flops 5435817984 | bytes 9437184 | tf_op jit(solution)/shard_map/feed_back/pallas_call | solution.py:494
  383.8 10.6 %out_of.9 = bf16[1024,1152]{1,0:T(8,128)(2,1)} custom-call(bf16[1024,2304]{1,0:T(8,128)(2,1)} %feed_back.3.right_two.values_ref, bf16[1152,2304]{1,0:T(8,128)(2,1)} %slice.434.weights_ref), custom_call_target="tpu_custom_call" | custom-call | flops 5435817984 | bytes 4718592 | tf_op jit(solution)/shard_map/out_of/pallas_call | solution.py:548
  395.9 11.3 %out_of.8 = f32[1024,1152]{1,0:T(8,128)} custom-call(bf16[1024,2304]{1,0:T(8,128)(2,1)} %feed_back.2.values_ref.right_one, bf16[1152,2304]{1,0:T(8,128)(2,1)} %slice.434.weights_ref), custom_call_target="tpu_custom_call" | custom-call | flops 5435817984 | bytes 4718592 | tf_op jit(solution)/shard_map/out_of/pallas_call | solution.py:548
  411.7 17.9 %weight_grad.4 = (bf16[4,72,2304]{2,1,0:T(8,128)(2,1)}, bf16[4,72,2304]{2,1,0:T(8,128)(2,1)}, bf16[4,72,2304]{2,1,0:T(8,128)(2,1)}, bf16[4,72,2304]{2,1,0:T(8,128)(2,1)}) custom-call(s32[16]{0:T(128)} %xor.66.places, bf16[1024,1152]{1,0:T(8,128)(2,1)} %bitcast.37.values_ref.left_one, bf16[1024,1152]{1,0:T(8,128)(2,1)} %collective-permute-done.25.values_ref.left_two, ...), custom_call_target="tpu_custom_call" | custom-call | flops 10871635968 | bytes 10616832 | tf_op jit(solution)/shard_map/weight_grad/pallas_call | solution.py:587
  491.2 21.2 %attention_back.2 = (bf16[1024,1792]{1,0:T(8,128)(2,1)}, f32[8,16,512]{2,1,0:T(8,128)}) custom-call(bf16[1024,1792]{1,0:T(8,128)(2,1)} %into_heads.2.qkv_ref, bf16[1024,576]{1,0:T(8,128)(2,1)} %get-tuple-element.176.upstream_ref, f32[1024,8]{1,0:T(8,128)} %get-tuple-element.177.log_ref, f32[8,16,512]{2,1,0:T(8,128)} %pad.13.spread_ref), custom_call_target="tpu_custom_call" | custom-call | flops 5368709120 | bytes 11010048 | tf_op jit(solution)/shard_map/attention_back/pallas_call | solution.py:412
  515.8 21.5 %attention_back.3 = (bf16[1024,1792]{1,0:T(8,128)(2,1)}, f32[8,16,512]{2,1,0:T(8,128)}) custom-call(bf16[1024,1792]{1,0:T(8,128)(2,1)} %into_heads.3.qkv_ref, bf16[1024,576]{1,0:T(8,128)(2,1)} %copy.121.upstream_ref, f32[1024,8]{1,0:T(8,128)} %get-tuple-element.189.log_ref, f32[8,16,512]{2,1,0:T(8,128)} %pad.13.spread_ref), custom_call_target="tpu_custom_call" | custom-call | flops 5368709120 | bytes 11010048 | tf_op jit(solution)/shard_map/attention_back/pallas_call | solution.py:412
  546.8 9.0 %out_of.11 = bf16[1024,1152]{1,0:T(8,128)(2,1)} custom-call(bf16[1024,1792]{1,0:T(8,128)(2,1)} %get-tuple-element.197.right_two.values_ref, bf16[1152,1792]{1,0:T(8,128)(2,1)} %bitcast.217), custom_call_target="tpu_custom_call" | custom-call | flops 4227858432 | bytes 4718592 | tf_op jit(solution)/shard_map/out_of/pallas_call | solution.py:548
  570.1 9.4 %out_of.10 = f32[1024,1152]{1,0:T(8,128)} custom-call(bf16[1024,1792]{1,0:T(8,128)(2,1)} %get-tuple-element.187.values_ref.right_one, bf16[1152,1792]{1,0:T(8,128)(2,1)} %bitcast.218), custom_call_target="tpu_custom_call" | custom-call | flops 4227858432 | bytes 4718592 | tf_op jit(solution)/shard_map/out_of/pallas_call | solution.py:548
  580.1 14.9 %weight_grad.5 = (bf16[4,72,1792]{2,1,0:T(8,128)(2,1)}, bf16[4,72,1792]{2,1,0:T(8,128)(2,1)}, bf16[4,72,1792]{2,1,0:T(8,128)(2,1)}, bf16[4,72,1792]{2,1,0:T(8,128)(2,1)}) custom-call(s32[16]{0:T(128)} %xor.66.places, bf16[1024,1152]{1,0:T(8,128)(2,1)} %bitcast.225, bf16[1024,1152]{1,0:T(8,128)(2,1)} %collective-permute-done.17.values_ref.left_two, ...), custom_call_target="tpu_custom_call" | custom-call | flops 8455716864 | bytes 8257536 | tf_op jit(solution)/shard_map/weight_grad/pallas_call | solution.py:587
  635.2 11.6 %collective-permute-done.54 = bf16[4,8,4608]{2,1,0:T(8,128)(2,1)} collective-permute-done((bf16[4,8,4608]{2,1,0:T(8,128)(2,1)S(1)}, bf16[4,8,4608]{2,1,0:T(8,128)(2,1)}, u32[]{:S(2)}, u32[]{:S(2)}) %collective-permute-start.54) | collective-permute-done | bytes 294944 | tf_op jit(solution)/shard_map/ppermute | solution.py:104
  735.5 8.9 %multiply_reduce_fusion.10 = (f32[13824]{0:T(1024)S(1)}, f32[72,13824]{1,0:T(8,128)}, f32[72,13824]{1,0:T(8,128)}) fusion(f32[72,13824]{1,0:T(8,128)} %param.24, f32[]{:T(128)S(6)} %min.3, bf16[72,13824]{1,0:T(8,128)(2,1)} %concatenate.178, f32[72,13824]{1,0:T(8,128)} %param.25, f32[72,13824]{1,0:T(8,128)} %param.26), kind=kLoop, calls=%fused_computation.40 | loop fusion | flops 16906752 | bytes 21952516 | tf_op jit(solution)/shard_map/reduce_sum | solution.py:663
  772.4 9.3 %fusion.102 = (bf16[72,13824]{1,0:T(8,128)(2,1)}, f32[72,13824]{1,0:T(8,128)}) fusion(f32[72,13824]{1,0:T(8,128)} %param.24, f32[72,13824]{1,0:T(8,128)} %get-tuple-element.261, f32[72,13824]{1,0:T(8,128)} %get-tuple-element.260, f32[13824]{0:T(1024)S(1)} %maximum_multiply_fusion), kind=kLoop, calls=%fused_computation.356 | loop fusion | flops 8957952 | bytes 17971200 | tf_op jit(solution)/shard_map/convert_element_type | solution.py:1068
  (661 shorter events, 444.5 us)
Async XLA Ops:
  7.2 128.8 %all-gather.6.cloned.1.call-start = ((), (), s32[]{:S(2)}) async-start(), calls=%async_computation.7 | async-start | bytes 2119680 | tf_op jit(solution)/shard_map/all_gather | solution.py:251
  34.1 26.4 %collective-permute-start.5 = (bf16[4,289,72]{2,1,0:T(8,128)(2,1)S(1)}, bf16[4,289,72]{2,1,0:T(8,128)(2,1)S(1)}, u32[]{:S(2)}, u32[]{:S(2)}) collective-permute-start(bf16[4,289,72]{2,1,0:T(8,128)(2,1)S(1)} %pad_maximum_fusion.2.refs_0_), channel_id=1, source_target_pairs={{0,4},{1,3},{2,6},{3,1},{4,0},{5,7},{6,2},{7,5},{8,12},{9,11},{10,... | collective-permute-start | bytes 499400 | tf_op jit(solution)/shard_map/ppermute | solution.py:104
  89.7 95.8 %all-gather.8.cloned.1.call-start = ((), (), s32[]{:S(2)}) async-start(), calls=%async_computation.8 | async-start | bytes 1658880 | tf_op jit(solution)/shard_map/all_gather | solution.py:251
  142.7 369.7 %reduce-scatter.7.cloned.1.call-start = ((), (), s32[]{:S(2)}) async-start(), calls=%async_computation.4 | async-start | bytes 1658880 | tf_op jit(solution)/shard_map/reduce_scatter | solution.py:255
  142.8 42.6 %collective-permute-start.18 = (bf16[4,72,2880]{2,1,0:T(8,128)(2,1)}, bf16[4,72,2880]{2,1,0:T(8,128)(2,1)}, u32[]{:S(2)}, u32[]{:S(2)}) collective-permute-start(bf16[4,72,2880]{2,1,0:T(8,128)(2,1)} %bitcast.228), channel_id=1, source_target_pairs={{0,2},{1,5},{2,0},{3,7},{4,6},{5,1},{6,4},{7,3},{8,10},{9,13},{10,... | collective-permute-start | bytes 4976648 | tf_op jit(solution)/shard_map/ppermute | solution.py:104
  143.8 41.6 %collective-permute-start.19 = (bf16[4,72,2880]{2,1,0:T(8,128)(2,1)}, bf16[4,72,2880]{2,1,0:T(8,128)(2,1)}, u32[]{:S(2)}, u32[]{:S(2)}) collective-permute-start(bf16[4,72,2880]{2,1,0:T(8,128)(2,1)} %bitcast.229), channel_id=1, source_target_pairs={{0,4},{1,3},{2,6},{3,1},{4,0},{5,7},{6,2},{7,5},{8,12},{9,11},{10,... | collective-permute-start | bytes 4976648 | tf_op jit(solution)/shard_map/ppermute | solution.py:104
  241.5 32.0 %collective-permute-start.25 = (bf16[1024,1152]{1,0:T(8,128)(2,1)}, bf16[1024,1152]{1,0:T(8,128)(2,1)}, u32[]{:S(2)}, u32[]{:S(2)}) collective-permute-start(bf16[1024,1152]{1,0:T(8,128)(2,1)} %bitcast.37.values_ref.left_one), channel_id=1, source_target_pairs={{0,1},{1,0},{2,3},{3,2},{4,5},{5,4},{6,7},{7,6},{8,9},{9,8},{10,11... | collective-permute-start | bytes 7077896 | tf_op jit(solution)/shard_map/ppermute | solution.py:108
  241.9 31.6 %collective-permute-start.23 = (bf16[4,72,2304]{2,1,0:T(8,128)(2,1)}, bf16[4,72,2304]{2,1,0:T(8,128)(2,1)}, u32[]{:S(2)}, u32[]{:S(2)}) collective-permute-start(bf16[4,72,2304]{2,1,0:T(8,128)(2,1)} %bitcast.30.refs_0_), channel_id=1, source_target_pairs={{0,2},{1,5},{2,0},{3,7},{4,6},{5,1},{6,4},{7,3},{8,10},{9,13},{10,... | collective-permute-start | bytes 3981320 | tf_op jit(solution)/shard_map/ppermute | solution.py:104
  243.8 29.8 %collective-permute-start.24 = (bf16[4,72,2304]{2,1,0:T(8,128)(2,1)}, bf16[4,72,2304]{2,1,0:T(8,128)(2,1)}, u32[]{:S(2)}, u32[]{:S(2)}) collective-permute-start(bf16[4,72,2304]{2,1,0:T(8,128)(2,1)} %bitcast.30.refs_0_), channel_id=1, source_target_pairs={{0,4},{1,3},{2,6},{3,1},{4,0},{5,7},{6,2},{7,5},{8,12},{9,11},{10,... | collective-permute-start | bytes 3981320 | tf_op jit(solution)/shard_map/ppermute | solution.py:104
  369.2 38.0 %collective-permute-start.29 = (bf16[4,72,2304]{2,1,0:T(8,128)(2,1)}, bf16[4,72,2304]{2,1,0:T(8,128)(2,1)}, u32[]{:S(2)}, u32[]{:S(2)}) collective-permute-start(bf16[4,72,2304]{2,1,0:T(8,128)(2,1)} %get-tuple-element.162), channel_id=1, source_target_pairs={{0,4},{1,3},{2,6},{3,1},{4,0},{5,7},{6,2},{7,5},{8,12},{9,11},{10,... | collective-permute-start | bytes 3981320 | tf_op jit(solution)/shard_map/ppermute | solution.py:104
  394.5 35.1 %collective-permute-start.30 = (bf16[1024,1152]{1,0:T(8,128)(2,1)}, bf16[1024,1152]{1,0:T(8,128)(2,1)}, u32[]{:S(2)}, u32[]{:S(2)}) collective-permute-start(bf16[1024,1152]{1,0:T(8,128)(2,1)} %out_of.9), channel_id=1, source_target_pairs={{0,1},{1,0},{2,3},{3,2},{4,5},{5,4},{6,7},{7,6},{8,9},{9,8},{10,11... | collective-permute-start | bytes 7077896 | tf_op jit(solution)/shard_map/ppermute | solution.py:108
  394.9 51.9 %collective-permute-start.32 = (bf16[4,72,2304]{2,1,0:T(8,128)(2,1)}, bf16[4,72,2304]{2,1,0:T(8,128)(2,1)}, u32[]{:S(2)}, u32[]{:S(2)}) collective-permute-start(bf16[4,72,2304]{2,1,0:T(8,128)(2,1)} %get-tuple-element.171), channel_id=1, source_target_pairs={{0,4},{1,3},{2,6},{3,1},{4,0},{5,7},{6,2},{7,5},{8,12},{9,11},{10,... | collective-permute-start | bytes 3981320 | tf_op jit(solution)/shard_map/ppermute | solution.py:104
  410.3 36.5 %collective-permute-start.31 = (bf16[4,72,2304]{2,1,0:T(8,128)(2,1)}, bf16[4,72,2304]{2,1,0:T(8,128)(2,1)}, u32[]{:S(2)}, u32[]{:S(2)}) collective-permute-start(bf16[4,72,2304]{2,1,0:T(8,128)(2,1)} %add_convert_fusion.10), channel_id=1, source_target_pairs={{0,2},{1,5},{2,0},{3,7},{4,6},{5,1},{6,4},{7,3},{8,10},{9,13},{10,... | collective-permute-start | bytes 3981320 | tf_op jit(solution)/shard_map/ppermute | solution.py:104
  446.8 27.3 %collective-permute-start.33 = (bf16[4,72,2304]{2,1,0:T(8,128)(2,1)}, bf16[4,72,2304]{2,1,0:T(8,128)(2,1)}, u32[]{:S(2)}, u32[]{:S(2)}) collective-permute-start(bf16[4,72,2304]{2,1,0:T(8,128)(2,1)} %get-tuple-element.174), channel_id=1, source_target_pairs={{0,4},{1,3},{2,6},{3,1},{4,0},{5,7},{6,2},{7,5},{8,12},{9,11},{10,... | collective-permute-start | bytes 3981320 | tf_op jit(solution)/shard_map/ppermute | solution.py:104
  465.8 129.3 %reduce-scatter.9.cloned.1.call-start = ((), (), s32[]{:S(2)}) async-start(), calls=%async_computation.5 | async-start | bytes 1658880 | tf_op jit(solution)/shard_map/reduce_scatter | solution.py:255
  476.9 35.4 %collective-permute-start.36 = (bf16[4,72,2304]{2,1,0:T(8,128)(2,1)}, bf16[4,72,2304]{2,1,0:T(8,128)(2,1)}, u32[]{:S(2)}, u32[]{:S(2)}) collective-permute-start(bf16[4,72,2304]{2,1,0:T(8,128)(2,1)} %add_convert_fusion.6), channel_id=1, source_target_pairs={{0,2},{1,5},{2,0},{3,7},{4,6},{5,1},{6,4},{7,3},{8,10},{9,13},{10,... | collective-permute-start | bytes 3981320 | tf_op jit(solution)/shard_map/ppermute | solution.py:104
  477.8 34.6 %collective-permute-start.37 = (bf16[4,72,2304]{2,1,0:T(8,128)(2,1)}, bf16[4,72,2304]{2,1,0:T(8,128)(2,1)}, u32[]{:S(2)}, u32[]{:S(2)}) collective-permute-start(bf16[4,72,2304]{2,1,0:T(8,128)(2,1)} %get-tuple-element.186), channel_id=1, source_target_pairs={{0,4},{1,3},{2,6},{3,1},{4,0},{5,7},{6,2},{7,5},{8,12},{9,11},{10,... | collective-permute-start | bytes 3981320 | tf_op jit(solution)/shard_map/ppermute | solution.py:104
  482.0 30.3 %collective-permute-start.35 = (bf16[1024,576]{0,1:T(8,128)(2,1)}, bf16[1024,576]{0,1:T(8,128)(2,1)}, u32[]{:S(2)}, u32[]{:S(2)}) collective-permute-start(bf16[1024,576]{0,1:T(8,128)(2,1)} %copy.120), channel_id=1, source_target_pairs={{0,1},{1,0},{2,3},{3,2},{4,5},{5,4},{6,7},{7,6},{8,9},{9,8},{10,11... | collective-permute-start | bytes 3538952 | tf_op jit(solution)/shard_map/ppermute | solution.py:108
  514.8 31.8 %collective-permute-start.38 = (bf16[4,72,576]{2,1,0:T(8,128)(2,1)}, bf16[4,72,576]{2,1,0:T(8,128)(2,1)S(1)}, u32[]{:S(2)}, u32[]{:S(2)}) collective-permute-start(bf16[4,72,576]{2,1,0:T(8,128)(2,1)} %get-tuple-element.191), channel_id=1, source_target_pairs={{0,4},{1,3},{2,6},{3,1},{4,0},{5,7},{6,2},{7,5},{8,12},{9,11},{10,... | collective-permute-start | bytes 995336 | tf_op jit(solution)/shard_map/ppermute | solution.py:104
  546.6 147.3 %reduce-scatter.13.cloned.1.call-start = ((), (), s32[]{:S(2)}) async-start(), calls=%async_computation.9 | async-start | bytes 460800
  555.8 39.3 %collective-permute-start.45 = (bf16[1024,1152]{1,0:T(8,128)(2,1)}, bf16[1024,1152]{1,0:T(8,128)(2,1)S(1)}, u32[]{:S(2)}, u32[]{:S(2)}) collective-permute-start(bf16[1024,1152]{1,0:T(8,128)(2,1)} %out_of.11), channel_id=1, source_target_pairs={{0,1},{1,0},{2,3},{3,2},{4,5},{5,4},{6,7},{7,6},{8,9},{9,8},{10,11... | collective-permute-start | bytes 7077896 | tf_op jit(solution)/shard_map/ppermute | solution.py:108
  604.6 43.2 %collective-permute-start.53 = (bf16[4,72,1792]{2,1,0:T(8,128)(2,1)}, bf16[4,72,1792]{2,1,0:T(8,128)(2,1)}, u32[]{:S(2)}, u32[]{:S(2)}) collective-permute-start(bf16[4,72,1792]{2,1,0:T(8,128)(2,1)} %get-tuple-element.213), channel_id=1, source_target_pairs={{0,4},{1,3},{2,6},{3,1},{4,0},{5,7},{6,2},{7,5},{8,12},{9,11},{10,... | collective-permute-start | bytes 3096584 | tf_op jit(solution)/shard_map/ppermute | solution.py:104
  631.5 62.4 %reduce-scatter.11.cloned.1.call-start = ((), (), s32[]{:S(2)}) async-start(), calls=%async_computation.6 | async-start | bytes 1290240 | tf_op jit(solution)/shard_map/reduce_scatter | solution.py:255
  633.0 68.7 %collective-permute-start.46 = (f32[7689]{0:T(1024)}, f32[7689]{0:T(1024)}, u32[]{:S(2)}, u32[]{:S(2)}) collective-permute-start(f32[7689]{0:T(1024)} %add.575), channel_id=1, source_target_pairs={{0,1},{1,0},{2,3},{3,2},{4,5},{5,4},{6,7},{7,6},{8,9},{9,8},{10,11... | collective-permute-start | bytes 92276 | tf_op jit(solution)/shard_map/ppermute | solution.py:108
  (175 other events, 1689.2 us)
Sparse Core Ops, SparseCore 0:
  89.8 46.1 all-gather.5
  142.8 30.5 all-gather.7
  465.9 29.2 reduce-scatter.6
  546.7 30.6 reduce-scatter.8
  631.6 19.6 reduce-scatter.12
  658.7 26.2 reduce-scatter.10

commit v4 on v3

--- a/solution.py
+++ b/solution.py
@@ -24,6 +24,8 @@
 SPREAD = 2 * GRID * GRID
 DP = ("far", "near")
 VMEM = 60 << 20
+PACE = 1
+LOG2E = math.log2(math.e)
 
 
 FIRST_DECAY = 0.9
@@ -272,22 +274,25 @@
     return own[0].astype(wide)
 
 
-def scatter_parts(own, second, third, both):
+def scatter_parts(own, second, third, both, meanwhile=()):
     second = add_low(second, send(both, plane_peers((2, 1))))
+    second, *meanwhile = tie(second, *meanwhile)
     from_third = send(third, plane_peers((2, 1)))
     from_second = send(second, plane_peers((1, 2)))
-    return scatter_far(add_low(add_low(own, from_third), from_second))
-
-
-def all_sum(values):
-    values = values + swap_cores(values)
-    return dp_sum(values)
-
-
-def dp_sum(values):
-    for bit in range(lax.axis_size(DP).bit_length() - 1):
-        values = values + send(values, dp_peers(1 << bit))
-    return values
+    share = scatter_far(add_low(add_low(own, from_third), from_second))
+    return (share, *meanwhile) if meanwhile else share
+
+
+def all_sum(values, meanwhile=()):
+    return dp_sum(values + swap_cores(values), meanwhile)
+
+
+def dp_sum(values, meanwhile=()):
+    for pos in range(lax.axis_size(DP).bit_length() - 1):
+        values = values + send(values, dp_peers(1 << pos))
+        if pos == 1:
+            values, *meanwhile = tie(values, *meanwhile)
+    return (values, *meanwhile) if meanwhile else values
 
 
 def product(left, right, dims):
@@ -297,7 +302,7 @@
 def fill_bias(spread_ref, bias):
     tokens = GRID * GRID
     for head in range(bias.shape[0]):
-        spread = spread_ref[head]
+        spread = spread_ref[head] * LOG2E
         for row in range(GRID):
             off = (GRID - 1 - row) * GRID
             moved = spread if off == 0 else pltpu.roll(spread, SPREAD - off, 1)
@@ -320,13 +325,13 @@
     outs, logs = ([], [])
     for head in range(heads):
         query, key, value = head_slices(values, head, heads)
-        scores = product(query, key, ((1,), (1,))) * HD ** (-0.5) + bias[head]
+        scores = product(query, key, ((1,), (1,))) * (HD ** (-0.5) * LOG2E) + bias[head]
         top = jnp.max(scores, -1, keepdims=True)
-        powers = jnp.exp(scores - top)
+        powers = jnp.exp2(scores - top)
         total = jnp.sum(powers, -1, keepdims=True)
-        probs = (powers * (1.0 / total)).astype(jnp.bfloat16)
-        outs.append(product(probs, value, ((1,), (0,))).astype(jnp.bfloat16))
-        logs.append(top + jnp.log(total))
+        summed = product(powers.astype(jnp.bfloat16), value, ((1,), (0,)))
+        outs.append((summed * (1.0 / total)).astype(jnp.bfloat16))
+        logs.append(top + jnp.log2(total))
     out_ref[...] = jnp.concatenate(outs, 1)
     log_ref[...] = jnp.concatenate(logs, 1)
 
@@ -376,12 +381,12 @@
     for head in range(heads):
         query, key, value = head_slices(values, head, heads)
         d_out = upstream[:, head * HD : (head + 1) * HD]
-        scores = product(query, key, ((1,), (1,))) * HD ** (-0.5) + bias[head]
-        probs = jnp.exp(scores - logs[:, head : head + 1])
+        scores = product(query, key, ((1,), (1,))) * (HD ** (-0.5) * LOG2E) + bias[head]
+        probs = jnp.exp2(scores - logs[:, head : head + 1])
         d_probs = product(d_out, value, ((1,), (1,)))
         d_scores = probs * (d_probs - jnp.sum(probs * d_probs, -1, keepdims=True))
+        d_bias[head] += d_scores
         d_scores = d_scores.astype(jnp.bfloat16)
-        d_bias[head] += d_scores.astype(jnp.float32)
         d_query.append((product(d_scores, key, ((1,), (0,))) * HD ** (-0.5)).astype(jnp.bfloat16))
         d_key.append((product(d_scores, query, ((0,), (0,))) * HD ** (-0.5)).astype(jnp.bfloat16))
         d_value.append(
@@ -441,8 +446,8 @@
     return pl.BlockSpec(shape, lambda step: (0,) * len(shape), pipeline_mode=pl.Buffered(1))
 
 
-def column_tile(columns):
-    return 256 if columns % 256 == 0 else 128
+def column_tile(columns, choices=(768, 896, 256)):
+    return next((tile for tile in choices if columns % tile == 0), 128)
 
 
 def feed_in_kernel(values_ref, weights_ref, act_ref, slope_ref):
@@ -459,9 +464,8 @@
         slope_ref[row : row + 256, :] = slope.astype(jnp.bfloat16)
 
 
-def feed_in(values, weights):
+def feed_in(values, weights, columns):
     rows, depth = values.shape
-    columns = weights.shape[1]
     tile = column_tile(columns)
     return pl.pallas_call(
         feed_in_kernel,
@@ -548,7 +552,7 @@
     return pl.pallas_call(
         out_of_kernel,
         grid=(rows // tile,),
-        in_specs=[pl.BlockSpec((tile, depth), lambda step: (step, 0)), whole_block(weights.shape)],
+        in_specs=[pl.BlockSpec((tile, depth), lambda step: (step, 0)), whole_block((columns, depth))],
         out_specs=pl.BlockSpec((tile, columns), lambda step: (step, 0)),
         out_shape=jax.ShapeDtypeStruct((rows, columns), kind),
         compiler_params=pltpu.CompilerParams(vmem_limit_bytes=VMEM),
@@ -579,7 +583,7 @@
     if block % 8:
         whole = outer_sum(left[0], right[0]) + outer_sum(left[1], right[1])
         return pick_blocks(whole.astype(jnp.bfloat16).reshape(total, block, columns), places)
-    tile = column_tile(columns)
+    tile = column_tile(columns, (256,))
 
     def whole_left(shape):
         return pl.BlockSpec(shape, lambda step, _: (0, 0), pipeline_mode=pl.Buffered(1))
@@ -705,17 +709,6 @@
     count = float(images * spread * lax.axis_size("mod") * length * latents.shape[2])
     relative, stacked = (relative_places(), stacked_places())
 
-    half = D // 2
-    wide_half = MLPW // 2
-    block_low = block_weights.astype(low)
-    q_part, k_part, v_part, p_part = core_half(
-        block_low, core, [0, D, 2 * D, 3 * D], half
-    )
-    in_part, out_part = core_half(block_low, core, [4 * D, 4 * D + MLPW], wide_half)
-    pad_part = jnp.zeros((block_low.shape[0], QKV_PAD - QKV_HALF), low)
-    attn_part = jnp.concatenate([q_part, k_part, v_part, pad_part], 1)
-    in_part = jnp.concatenate([in_part, p_part], 1)
-
     start = NCLASS + 1
     chosen = jnp.where(drops == 1, NCLASS, labels)
     codes = jnp.stack([timesteps // 32, timesteps % 32, chosen // 32, chosen % 32], 1)
@@ -723,23 +716,34 @@
     codes = both_cores(codes, swap_cores(codes), core, 0)
     code_rows = -(-codes.size // share)
     codes = jnp.pad(codes.reshape(-1), (0, code_rows * share - codes.size))
-    embed_low = embed_weights.astype(low)
-    table = embed_low[:start]
-    time_out = embed_low[start + FREQ : start + FREQ + D].astype(wide)
     small = jnp.concatenate(
         [
-            embed_low[start : start + FREQ],
-            embed_low[start + FREQ + D :],
+            embed_weights[start : start + FREQ].astype(low),
+            embed_weights[start + FREQ + D :].astype(low),
             codes.reshape(code_rows, share),
         ],
         0,
     )
+    half = D // 2
+    wide_half = MLPW // 2
     small_far = gather_far(small)
-    attn_part, small_far = tie(attn_part, small_far)
-    attn_far = far_stack(attn_part)
+    now_weights, small_far = tie(block_weights, small_far)
+    block_low = now_weights.astype(low)
+    q_part, k_part, v_part, p_part = core_half(
+        block_low, core, [0, D, 2 * D, 3 * D], half
+    )
+    in_part, out_part = core_half(block_low, core, [4 * D, 4 * D + MLPW], wide_half)
+    pad_part = jnp.zeros((block_low.shape[0], QKV_PAD - QKV_HALF), low)
+    attn_part = jnp.concatenate([q_part, k_part, v_part, pad_part], 1)
+    in_part = jnp.concatenate([in_part, p_part], 1)
+    attn_far = gather_far(attn_part)
     small_second, small_third = gather_near(small_far)
-    small_second, attn_far = tie(small_second, attn_far)
     small = [small_far, small_second, small_third, gather_last(small_second)]
+    later_weights, later_bias, later_embed, small[0] = tie(
+        block_weights, rel_bias, embed_weights, small[0]
+    )
+    table = later_embed[:start].astype(low)
+    time_out = later_embed[start + FREQ : start + FREQ + D].astype(low).astype(wide)
     everyone = jnp.concatenate([part[:, FREQ + 2 * PDIM :] for part in small], 0)
     everyone = everyone.reshape(spread, -1)[:, : 2 * images * 4]
     everyone = everyone.reshape(spread * 2 * images, 4).astype(wide)
@@ -781,11 +785,14 @@
     attn_both = gather_last(attn_second)
     mod_low = mod_weights.astype(low)
     mod_partial = dense(scaled, mod_low).astype(low)
-    half_mod = scatter_parts(*jnp.split(mod_partial.reshape(spread, 2 * images, -1), 4))
+    mod_parts = jnp.split(mod_partial.reshape(spread, 2 * images, -1), 4)
     heads = HEADS // 2
-    bias_rows = spread_bias(jnp.where(core == 0, rel_bias[:heads], rel_bias[heads:]))
-    half_mod, attn_both, in_far, bias_rows = tie(half_mod, attn_both, in_far, bias_rows)
-    qkv_low = place_blocks([attn_far, attn_second, attn_third, attn_both], stacked).reshape(D, -1)
+    bias_rows = spread_bias(jnp.where(core == 0, later_bias[:heads], later_bias[heads:]))
+    block_weight_squares = block_squares(later_weights)
+    half_mod, in_far, attn_both, bias_rows, block_weight_squares = scatter_parts(
+        *mod_parts, meanwhile=(in_far, attn_both, bias_rows, block_weight_squares)
+    )
+    qkv_low = place_blocks([attn_far, attn_second, attn_third, attn_both], relative).reshape(D, -1)
     in_second, in_third = gather_near(in_far)
     out_part, in_far = tie(out_part, in_far)
     out_far = far_stack(out_part)
@@ -828,10 +835,10 @@
     in_both = gather_last(in_second)
     out_second, out_third = gather_near(out_far)
     heads_one, logs = attention(qkv, bias_rows)
-    heads_one, in_both = tie(heads_one, in_both)
+    heads_one, in_both, out_second = tie(heads_one, in_both, out_second)
+    out_both = gather_last(out_second)
     in_low = place_blocks([in_far, in_second, in_third, in_both], stacked).reshape(D, -1)
     proj_half = in_low[:, wide_half:]
-    in_low = in_low[:, :wide_half]
     proj_low = both_cores(proj_half, swap_cores(proj_half), core, 1)
     attn_out = both_cores(heads_one, heads_two, core, 1)
     branch_one = dense(attn_out, proj_low).reshape(images, length, D)
@@ -839,10 +846,10 @@
     normed2, inverse2 = layer_norm(hidden1)
     mlp_in = flat(moved(normed2, 3))
     mlp_in_two = swap_cores(mlp_in)
-    act, slope = feed_in(mlp_in, in_low)
-    act, out_second, out_third, mlp_in_two = tie(act, out_second, out_third, mlp_in_two)
-    out_both = gather_last(out_second)
-    act_two, slope_two = feed_in(mlp_in_two, in_low)
+    mlp_in, out_third = tie(mlp_in, out_third)
+    act, slope = feed_in(mlp_in, in_low, wide_half)
+    act, mlp_in_two = tie(act, mlp_in_two)
+    act_two, slope_two = feed_in(mlp_in_two, in_low, wide_half)
     act_two, out_both = tie(act_two, out_both)
     out_low = place_blocks([out_far, out_second, out_third, out_both], stacked).reshape(D, -1)
     branch_theirs = out_of(act_two, out_low, low)
@@ -919,20 +926,26 @@
     proj_third = send(proj_third, plane_peers((2, 1)))
     rel_half = gather_bias(d_spread)
     packed = jnp.concatenate([rel_half.reshape(-1), (loss_here * jnp.ones(1, wide))])
-    packed = dp_sum(packed)
-    d_attn_theirs = swap_cores(out_of(d_qkv_two, qkv_low, low))
-    d_attn_mine = out_of(d_qkv, qkv_low, wide)
-    d_qkv_two, d_attn_mine, proj_second, proj_third = tie(
-        d_qkv_two, d_attn_mine, proj_second, proj_third
-    )
-    g_proj = far_share(add_low(add_low(proj_own, proj_third), proj_second))
+    bits = [1 << pos for pos in range(2, spread.bit_length() - 1)] + [1, 2]
+    for bit in bits[:-3]:
+        packed = packed + send(packed, dp_peers(bit))
     attn_own, attn_second, attn_third, attn_both = weight_grad(
         (attn_in, attn_in_two), (d_qkv, d_qkv_two), stacked
     )
-    attn_both, attn_third, packed, d_attn_mine, d_attn_theirs, g_in = tie(
-        attn_both, attn_third, packed, d_attn_mine, d_attn_theirs, g_in
-    )
+    attn_both, proj_second, proj_third, packed = tie(attn_both, proj_second, proj_third, packed)
+    packed = packed + send(packed, dp_peers(bits[-3]))
+    g_proj = far_share(add_low(add_low(proj_own, proj_third), proj_second))
     attn_back = send(attn_both, plane_peers((2, 1)))
+    d_qkv_two, attn_both, attn_third = tie(d_qkv_two, attn_both, attn_third)
+    d_attn_theirs = out_of(d_qkv_two, qkv_low, low)
+    d_qkv, d_attn_theirs, attn_back, packed = tie(d_qkv, d_attn_theirs, attn_back, packed)
+    packed = packed + send(packed, dp_peers(bits[-2]))
+    d_attn_theirs = swap_cores(d_attn_theirs)
+    attn_second = send(add_low(attn_second, attn_back), plane_peers((1, 2)))
+    attn_third = send(attn_third, plane_peers((2, 1)))
+    d_attn_mine = out_of(d_qkv, qkv_low, wide)
+    d_attn_mine, g_in, packed = tie(d_attn_mine, g_in, packed)
+    packed = packed + send(packed, dp_peers(bits[-1]))
     d_attn_in = (d_attn_mine + d_attn_theirs.astype(wide)).reshape(images, length, D)
     d_scale1 = jnp.sum(d_attn_in * normed1, 1)
     d_shift1 = jnp.sum(d_attn_in, 1)
@@ -947,12 +960,12 @@
     d_keep = jnp.where(core == 0, d_modulation[:, :mod_half], d_modulation[:, mod_half:])
     d_give = jnp.where(core == 0, d_modulation[:, mod_half:], d_modulation[:, :mod_half])
     d_pair = both_cores(d_keep, swap_cores(d_give), core, 0)
-    d_pair, attn_back = tie(d_pair, attn_back)
-    attn_second = send(add_low(attn_second, attn_back), plane_peers((1, 2)))
-    attn_third = send(attn_third, plane_peers((2, 1)))
-    d_parts = gather_parts(d_pair)
-    d_parts[0], attn_second, attn_third = tie(d_parts[0], attn_second, attn_third)
+    d_pair, attn_second, attn_third, packed = tie(d_pair, attn_second, attn_third, packed)
+    d_far = gather_far(d_pair)
+    attn_own, d_far, g_patch = tie(attn_own, d_far, g_patch)
     g_qkv = far_share(add_low(add_low(attn_own, attn_third), attn_second))
+    d_second, d_third = gather_near(d_far)
+    d_parts = [d_far, d_second, d_third, gather_last(d_second)]
     d_all = jnp.concatenate(d_parts, 0).reshape(spread * 2 * images, mod_half)
     mod_grad = outer_sum(scaled, d_all)
     d_scaled = dense_trans(d_all, mod_low)
@@ -990,7 +1003,7 @@
     for low_end, width in spans:
         pieces.append(zero_part[:, low_end : low_end + width])
         pieces.append(one_part[:, low_end : low_end + width])
-    block_grad = jnp.concatenate(pieces, 1).astype(wide)
+    block_grad = jnp.concatenate(pieces, 1)
 
     packed_other = swap_cores(packed)
     rel_grad = both_cores(
@@ -1001,20 +1014,17 @@
     first_core = (core == 0).astype(wide)
 
     def replica_squares(block, mod, embed):
-        copied = block_squares(block) + embed_squares(embed)
-        return first_core * copied + mod_squares(mod, core)
-
-    grad_parts, weight_parts = jnp.split(
-        all_sum(
-            jnp.concatenate(
-                [
-                    g_squares + mod_squares(mod_grad, core) + first_core * embed_squares(embed_grad),
-                    replica_squares(block_weights, mod_weights, embed_weights),
-                ]
-            )
-        ),
-        2,
-    )
+        return first_core * (block + embed_squares(embed)) + mod_squares(mod, core)
+
+    squares = jnp.concatenate(
+        [
+            g_squares + mod_squares(mod_grad, core) + first_core * embed_squares(embed_grad),
+            replica_squares(block_weight_squares, mod_weights, embed_weights),
+        ]
+    )
+    squares, block_grad, rel_grad = all_sum(squares, (block_grad, rel_grad))
+    block_grad = block_grad.astype(wide)
+    grad_parts, weight_parts = jnp.split(squares, 2)
     grad_sq = jnp.concatenate([grad_parts, jnp.sum(rel_grad * rel_grad)[None]])
     weight_sq = jnp.concatenate([weight_parts, jnp.sum(rel_bias * rel_bias)[None]])
     grad_norm = jnp.sqrt(jnp.sum(grad_sq))
@@ -1027,32 +1037,24 @@
         embed_grad, embed_first, embed_second, embed_weights, clip
     )
     rel_m, rel_s, rel_step = adam_update(rel_grad, rel_first, rel_second, rel_bias, clip)
-    update_parts = all_sum(replica_squares(block_step, mod_step, embed_step))
+    update_parts = all_sum(replica_squares(block_squares(block_step), mod_step, embed_step))
     update_sq = jnp.concatenate([update_parts, jnp.sum(rel_step * rel_step)[None]])
     weight_norm = jnp.sqrt(weight_sq)
     update_norm = jnp.sqrt(update_sq)
     ratio = weight_norm / update_norm
-    block_ratio = jnp.concatenate(
-        [
-            jnp.broadcast_to(ratio[0], (3 * D,)),
-            jnp.broadcast_to(ratio[1], (D,)),
-            jnp.broadcast_to(ratio[2], (MLPW,)),
-            jnp.broadcast_to(ratio[3], (MLPW,)),
-        ]
-    )
-    global_cols = core * mod_weights.shape[1] + jnp.arange(
-        mod_weights.shape[1], dtype=jnp.int32
-    )
-    mod_ratio = jnp.where(global_cols < 6 * D, ratio[4], ratio[5])
-    embed_ratio = jnp.concatenate(
-        [
-            jnp.broadcast_to(ratio[6], (NCLASS + 1,)),
-            jnp.broadcast_to(ratio[7], (FREQ,)),
-            jnp.broadcast_to(ratio[8], (D,)),
-            jnp.broadcast_to(ratio[9], (PDIM,)),
-            jnp.broadcast_to(ratio[10], (PDIM,)),
-        ]
-    )
+    def spread_ratio(length, bounds, first, shift=0):
+        place = shift + jnp.arange(length, dtype=jnp.int32)
+        chosen = ratio[first]
+        for step, bound in enumerate(bounds):
+            chosen = jnp.where(place >= bound, ratio[first + step + 1], chosen)
+        return chosen
+
+    block_ratio = spread_ratio(block_weights.shape[1], [3 * D, 4 * D, 4 * D + MLPW], 0)
+    mod_columns = mod_weights.shape[1]
+    mod_ratio = spread_ratio(mod_columns, [6 * D], 4, core * mod_columns)
+    ends = start + FREQ + D
+    embed_bounds = [start, start + FREQ, ends, ends + PDIM]
+    embed_ratio = spread_ratio(embed_weights.shape[0], embed_bounds, 6)
     block_new = block_weights - LEARN_RATE * block_ratio[None, :] * block_step
     mod_new = mod_weights - LEARN_RATE * mod_ratio[None, :] * mod_step
     embed_new = embed_weights - LEARN_RATE * embed_ratio[:, None] * embed_step

time: 806 us -> 767 us (0.952)
  blocking collectives: 21.5 us -> 0 us
  Pallas kernels: 289 us -> 275 us
  local copies, waits for them, and re-layouts: 76.8 us -> 64.7 us
    all_gather x1 -> x0, blocking collectives: 21.5 us -> none  [far_stack(): return lax.all_gather(block, 'far', axis=0)]
    ppermute x57 -> x60, waiting for transfers between devices: 110 us -> 131 us  [send(): return lax.ppermute(values, DP + ('mod',), peers)]
    all_gather x2, waiting for transfers between devices: 14.9 us -> 0.01 us  [far_stack(): return lax.all_gather(block, 'far', axis=0)]
    ppermute x57 -> x60, starting transfers between devices: 64.9 us -> 66.3 us  [send(): return lax.ppermute(values, DP + ('mod',), peers)]
  transfers between devices with their start and end apart: 82 -> 85, of which waited for: 37 -> 35; matrix products, arithmetic and copies ran while one was open for 20% -> 22% of each run, Pallas kernels for 31% -> 31%
where the time goes in v4:
time: 767 us; the launch traced here: 761 us
  Pallas kernels  275 us (36%)
  other arithmetic  137 us (18%)
  waiting for transfers between devices  136 us (18%)
  starting transfers between devices  74.3 us (10%)
  local copies, waits for them, and re-layouts  64.7 us (8%)
  matrix products  52 us (7%)
  between operations  21.8 us (3%)
    ppermute x60, waiting for transfers between devices, send(): return lax.ppermute(values, DP + ('mod',), peers)  131 us
    ppermute x60, starting transfers between devices, send(): return lax.ppermute(values, DP + ('mod',), peers)  66.3 us
    pallas_call x6, Pallas kernels, out_of(): pl.pallas_call(out_of_kernel, grid=(rows // tile,), in_specs=[pl.BlockSpe...  61.5 us
    pallas_call x3, Pallas kernels, weight_grad(): pl.pallas_call(weight_grad_kernel, grid_spec=pltpu.PrefetchScalarGridSpec...  50.8 us
    pallas_call x2, Pallas kernels, attention_back(): pl.pallas_call(functools.partial(attention_back_kernel, heads), grid=(row...  41.3 us
    pallas_call x2, Pallas kernels, attention(): pl.pallas_call(functools.partial(attention_kernel, heads), grid=(rows //...  30 us
    pallas_call x6, Pallas kernels, move_call(): pl.pallas_call(functools.partial(kernel, counts, slots), grid_spec=pltpu....  26.1 us
    pallas_call x2, Pallas kernels, feed_in(): pl.pallas_call(feed_in_kernel, grid=(columns // tile,), in_specs=[whole_b...  24.6 us
  transfers between devices with their start and end apart: 85, of which 35 were waited for; matrix products, arithmetic and copies ran while one was open for 22% of the time, Pallas kernels for 31%

profile of v4, /device:TPU:0, one launch (start us, length us, event | category | flops | bytes accessed | tf_op | source)
XLA Modules:
  0.0 760.6 jit_solution(4330667795372199922)
XLA Ops:
  45.7 11.9 %collective-permute-done.8 = bf16[1,72,1792]{2,1,0:T(8,128)(2,1)} collective-permute-done((bf16[1,72,1792]{2,1,0:T(8,128)(2,1)S(1)}, bf16[1,72,1792]{2,1,0:T(8,128)(2,1)}, u32[]{:S(2)}, u32[]{:S(2)}) %collective-permute-start.8) | collective-permute-done | bytes 258080 | tf_op jit(solution)/shard_map/ppermute | solution.py:106
  71.1 11.4 %collective-permute-done.10.refs_1_ = bf16[4,72,1792]{2,1,0:T(8,128)(2,1)} collective-permute-done((bf16[4,72,1792]{2,1,0:T(8,128)(2,1)S(1)}, bf16[4,72,1792]{2,1,0:T(8,128)(2,1)}, u32[]{:S(2)}, u32[]{:S(2)}) %collective-permute-start.10) | collective-permute-done | bytes 1032224 | tf_op jit(solution)/shard_map/ppermute | solution.py:106
  95.4 12.5 %collective-permute-done.14.refs_3_ = bf16[4,72,1792]{2,1,0:T(8,128)(2,1)} collective-permute-done((bf16[4,72,1792]{2,1,0:T(8,128)(2,1)}, bf16[4,72,1792]{2,1,0:T(8,128)(2,1)}, u32[]{:S(2)}, u32[]{:S(2)}) %collective-permute-start.14) | collective-permute-done | bytes 1032224 | tf_op jit(solution)/shard_map/ppermute | solution.py:106
  133.1 9.4 %into_heads.2.qkv_ref = bf16[1024,1792]{1,0:T(8,128)(2,1)} custom-call(bf16[1024,1152]{1,0:T(8,128)(2,1)} %bitcast.226, bf16[1152,1792]{1,0:T(8,128)(2,1)} %bitcast.220), custom_call_target="tpu_custom_call" | custom-call | flops 4227858432 | bytes 3670016 | tf_op jit(solution)/shard_map/into_heads/pallas_call | solution.py:530
  142.5 9.2 %into_heads.3.qkv_ref = bf16[1024,1792]{1,0:T(8,128)(2,1)} custom-call(bf16[1024,1152]{1,0:T(8,128)(2,1)} %collective-permute-done.20.values_ref.left_two, bf16[1152,1792]{1,0:T(8,128)(2,1)} %bitcast.221), custom_call_target="tpu_custom_call" | custom-call | flops 4227858432 | bytes 3670016 | tf_op jit(solution)/shard_map/into_heads/pallas_call | solution.py:530
  151.7 15.0 %attention.2 = (bf16[1024,576]{1,0:T(8,128)(2,1)}, f32[1024,8]{1,0:T(8,128)}) custom-call(bf16[1024,1792]{1,0:T(8,128)(2,1)} %into_heads.3.qkv_ref, f32[8,16,512]{2,1,0:T(8,128)} %pad.13.spread_ref), custom_call_target="tpu_custom_call" | custom-call | flops 2147483648 | bytes 7340032 | tf_op jit(solution)/shard_map/attention/pallas_call | solution.py:343
  170.4 15.0 %attention.3 = (bf16[1024,576]{1,0:T(8,128)(2,1)}, f32[1024,8]{1,0:T(8,128)}) custom-call(bf16[1024,1792]{1,0:T(8,128)(2,1)} %into_heads.2.qkv_ref, f32[8,16,512]{2,1,0:T(8,128)} %pad.13.spread_ref), custom_call_target="tpu_custom_call" | custom-call | flops 2147483648 | bytes 7340032 | tf_op jit(solution)/shard_map/attention/pallas_call | solution.py:343
  185.4 15.2 %collective-permute-done.24.refs_1_ = bf16[4,72,2304]{2,1,0:T(8,128)(2,1)} collective-permute-done((bf16[4,72,2304]{2,1,0:T(8,128)(2,1)}, bf16[4,72,2304]{2,1,0:T(8,128)(2,1)}, u32[]{:S(2)}, u32[]{:S(2)}) %collective-permute-start.24) | collective-permute-done | bytes 1327136 | tf_op jit(solution)/shard_map/ppermute | solution.py:106
  239.6 15.9 %collective-permute-done.27.refs_2_ = bf16[4,72,2304]{2,1,0:T(8,128)(2,1)} collective-permute-done((bf16[4,72,2304]{2,1,0:T(8,128)(2,1)S(1)}, bf16[4,72,2304]{2,1,0:T(8,128)(2,1)}, u32[]{:S(2)}, u32[]{:S(2)}) %collective-permute-start.27) | collective-permute-done | bytes 1327136 | tf_op jit(solution)/shard_map/ppermute | solution.py:106
  255.5 12.2 %feed_in.2 = (bf16[1024,2304]{1,0:T(8,128)(2,1)}, bf16[1024,2304]{1,0:T(8,128)(2,1)}) custom-call(bf16[1024,1152]{1,0:T(8,128)(2,1)} %bitcast.37.values_ref.left_one, bf16[1152,2880]{1,0:T(8,128)(2,1)} %bitcast.210), custom_call_target="tpu_custom_call" | custom-call | flops 5435817984 | bytes 9437184 | tf_op jit(solution)/shard_map/feed_in/pallas_call | solution.py:470
  267.7 12.3 %feed_in.3 = (bf16[1024,2304]{1,0:T(8,128)(2,1)}, bf16[1024,2304]{1,0:T(8,128)(2,1)}) custom-call(bf16[1024,1152]{1,0:T(8,128)(2,1)} %collective-permute-done.28.values_ref.left_two, bf16[1152,2880]{1,0:T(8,128)(2,1)} %bitcast.211), custom_call_target="tpu_custom_call" | custom-call | flops 5435817984 | bytes 9437184 | tf_op jit(solution)/shard_map/feed_in/pallas_call | solution.py:470
  285.7 10.7 %out_of.7 = bf16[1024,1152]{1,0:T(8,128)(2,1)} custom-call(bf16[1024,2304]{1,0:T(8,128)(2,1)} %get-tuple-element.171.values_ref.right_two, bf16[1152,2304]{1,0:T(8,128)(2,1)} %bitcast.215), custom_call_target="tpu_custom_call" | custom-call | flops 5435817984 | bytes 4718592 | tf_op jit(solution)/shard_map/out_of/pallas_call | solution.py:552
  296.5 10.9 %out_of.6 = f32[1024,1152]{1,0:T(8,128)} custom-call(bf16[1024,2304]{1,0:T(8,128)(2,1)} %get-tuple-element.165.values_ref.right_one, bf16[1152,2304]{1,0:T(8,128)(2,1)} %bitcast.216), custom_call_target="tpu_custom_call" | custom-call | flops 5435817984 | bytes 4718592 | tf_op jit(solution)/shard_map/out_of/pallas_call | solution.py:552
  324.9 11.1 %feed_back.2.values_ref.right_one = bf16[1024,2304]{1,0:T(8,128)(2,1)} custom-call(bf16[1024,1152]{1,0:T(8,128)(2,1)} %bitcast.42.values_ref.left_one, bf16[1152,2304]{1,0:T(8,128)(2,1)} %bitcast.217, bf16[1024,2304]{1,0:T(8,128)(2,1)} %get-tuple-element.172.slope_ref), custom_call_target="tpu_custom_call" | custom-call | flops 5435817984 | bytes 9437184 | tf_op jit(solution)/shard_map/feed_back/pallas_call | solution.py:498
  336.0 17.9 %weight_grad.3 = (bf16[4,72,2304]{2,1,0:T(8,128)(2,1)}, bf16[4,72,2304]{2,1,0:T(8,128)(2,1)}, bf16[4,72,2304]{2,1,0:T(8,128)(2,1)}, bf16[4,72,2304]{2,1,0:T(8,128)(2,1)}) custom-call(s32[16]{0:T(128)} %xor.69.places, bf16[1024,1152]{1,0:T(8,128)(2,1)} %bitcast.42.values_ref.left_one, bf16[1024,1152]{1,0:T(8,128)(2,1)} %collective-permute-done.31.left_two.values_ref, ...), custom_call_target="tpu_custom_call" | custom-call | flops 10871635968 | bytes 10616832 | tf_op jit(solution)/shard_map/weight_grad/pallas_call | solution.py:591
  355.3 10.9 %feed_back.3.right_two.values_ref = bf16[1024,2304]{1,0:T(8,128)(2,1)} custom-call(bf16[1024,1152]{1,0:T(8,128)(2,1)} %collective-permute-done.31.left_two.values_ref, bf16[1152,2304]{1,0:T(8,128)(2,1)} %bitcast.218, bf16[1024,2304]{1,0:T(8,128)(2,1)} %get-tuple-element.179.slope_ref), custom_call_target="tpu_custom_call" | custom-call | flops 5435817984 | bytes 9437184 | tf_op jit(solution)/shard_map/feed_back/pallas_call | solution.py:498
  366.2 10.7 %out_of.9 = bf16[1024,1152]{1,0:T(8,128)(2,1)} custom-call(bf16[1024,2304]{1,0:T(8,128)(2,1)} %feed_back.3.right_two.values_ref, bf16[1152,2880]{1,0:T(8,128)(2,1)} %bitcast.212), custom_call_target="tpu_custom_call" | custom-call | flops 5435817984 | bytes 4718592 | tf_op jit(solution)/shard_map/out_of/pallas_call | solution.py:552
  377.5 10.9 %out_of.8 = f32[1024,1152]{1,0:T(8,128)} custom-call(bf16[1024,2304]{1,0:T(8,128)(2,1)} %feed_back.2.values_ref.right_one, bf16[1152,2880]{1,0:T(8,128)(2,1)} %bitcast.213), custom_call_target="tpu_custom_call" | custom-call | flops 5435817984 | bytes 4718592 | tf_op jit(solution)/shard_map/out_of/pallas_call | solution.py:552
  392.5 18.0 %weight_grad.4 = (bf16[4,72,2304]{2,1,0:T(8,128)(2,1)}, bf16[4,72,2304]{2,1,0:T(8,128)(2,1)}, bf16[4,72,2304]{2,1,0:T(8,128)(2,1)}, bf16[4,72,2304]{2,1,0:T(8,128)(2,1)}) custom-call(s32[16]{0:T(128)} %xor.69.places, bf16[1024,1152]{1,0:T(8,128)(2,1)} %bitcast.37.values_ref.left_one, bf16[1024,1152]{1,0:T(8,128)(2,1)} %collective-permute-done.28.values_ref.left_two, ...), custom_call_target="tpu_custom_call" | custom-call | flops 10871635968 | bytes 10616832 | tf_op jit(solution)/shard_map/weight_grad/pallas_call | solution.py:591
  465.3 20.5 %attention_back.2 = (bf16[1024,1792]{1,0:T(8,128)(2,1)}, f32[8,16,512]{2,1,0:T(8,128)}) custom-call(bf16[1024,1792]{1,0:T(8,128)(2,1)} %into_heads.2.qkv_ref, bf16[1024,576]{1,0:T(8,128)(2,1)} %get-tuple-element.191.upstream_ref, f32[1024,8]{1,0:T(8,128)} %get-tuple-element.192.log_ref, f32[8,16,512]{2,1,0:T(8,128)} %pad.13.spread_ref), custom_call_target="tpu_custom_call" | custom-call | flops 5368709120 | bytes 11010048 | tf_op jit(solution)/shard_map/attention_back/pallas_call | solution.py:417
  491.3 20.8 %attention_back.3 = (bf16[1024,1792]{1,0:T(8,128)(2,1)}, f32[8,16,512]{2,1,0:T(8,128)}) custom-call(bf16[1024,1792]{1,0:T(8,128)(2,1)} %into_heads.3.qkv_ref, bf16[1024,576]{1,0:T(8,128)(2,1)} %copy.121.upstream_ref, f32[1024,8]{1,0:T(8,128)} %get-tuple-element.204.log_ref, f32[8,16,512]{2,1,0:T(8,128)} %pad.13.spread_ref), custom_call_target="tpu_custom_call" | custom-call | flops 5368709120 | bytes 11010048 | tf_op jit(solution)/shard_map/attention_back/pallas_call | solution.py:417
  523.1 14.9 %weight_grad.5 = (bf16[4,72,1792]{2,1,0:T(8,128)(2,1)}, bf16[4,72,1792]{2,1,0:T(8,128)(2,1)}, bf16[4,72,1792]{2,1,0:T(8,128)(2,1)}, bf16[4,72,1792]{2,1,0:T(8,128)(2,1)}) custom-call(s32[16]{0:T(128)} %xor.69.places, bf16[1024,1152]{1,0:T(8,128)(2,1)} %bitcast.227, bf16[1024,1152]{1,0:T(8,128)(2,1)} %collective-permute-done.20.values_ref.left_two, ...), custom_call_target="tpu_custom_call" | custom-call | flops 8455716864 | bytes 8257536 | tf_op jit(solution)/shard_map/weight_grad/pallas_call | solution.py:591
  545.3 9.1 %out_of.10 = bf16[1024,1152]{1,0:T(8,128)(2,1)} custom-call(bf16[1024,1792]{1,0:T(8,128)(2,1)} %get-tuple-element.217.right_two.values_ref, bf16[1152,1792]{1,0:T(8,128)(2,1)} %bitcast.222), custom_call_target="tpu_custom_call" | custom-call | flops 4227858432 | bytes 4718592 | tf_op jit(solution)/shard_map/out_of/pallas_call | solution.py:552
  566.9 9.4 %out_of.11 = f32[1024,1152]{1,0:T(8,128)} custom-call(bf16[1024,1792]{1,0:T(8,128)(2,1)} %get-tuple-element.219.right_one.values_ref, bf16[1152,1792]{1,0:T(8,128)(2,1)} %bitcast.223), custom_call_target="tpu_custom_call" | custom-call | flops 4227858432 | bytes 4718592 | tf_op jit(solution)/shard_map/out_of/pallas_call | solution.py:552
  (647 shorter events, 423.2 us)
Async XLA Ops:
  7.2 100.7 %all-gather.5.cloned.1.call-start = ((), (), s32[]{:S(2)}) async-start(), calls=%async_computation.7 | async-start | bytes 2119680 | tf_op jit(solution)/shard_map/all_gather | solution.py:253
  60.0 106.9 %all-gather.7.cloned.1.call-start = ((), (), s32[]{:S(2)}) async-start(), calls=%async_computation.8 | async-start | bytes 1658880 | tf_op jit(solution)/shard_map/all_gather | solution.py:253
  126.9 358.9 %reduce-scatter.7.cloned.1.call-start = ((), (), s32[]{:S(2)}) async-start(), calls=%async_computation.4 | async-start | bytes 1658880 | tf_op jit(solution)/shard_map/reduce_scatter | solution.py:257
  127.0 39.9 %collective-permute-start.21 = (bf16[4,72,2880]{2,1,0:T(8,128)(2,1)}, bf16[4,72,2880]{2,1,0:T(8,128)(2,1)}, u32[]{:S(2)}, u32[]{:S(2)}) collective-permute-start(bf16[4,72,2880]{2,1,0:T(8,128)(2,1)} %bitcast.230), channel_id=1, source_target_pairs={{0,2},{1,5},{2,0},{3,7},{4,6},{5,1},{6,4},{7,3},{8,10},{9,13},{10,... | collective-permute-start | bytes 4976648 | tf_op jit(solution)/shard_map/ppermute | solution.py:106
  127.5 39.4 %collective-permute-start.22 = (bf16[4,72,2880]{2,1,0:T(8,128)(2,1)}, bf16[4,72,2880]{2,1,0:T(8,128)(2,1)}, u32[]{:S(2)}, u32[]{:S(2)}) collective-permute-start(bf16[4,72,2880]{2,1,0:T(8,128)(2,1)} %bitcast.231), channel_id=1, source_target_pairs={{0,4},{1,3},{2,6},{3,1},{4,0},{5,7},{6,2},{7,5},{8,12},{9,11},{10,... | collective-permute-start | bytes 4976648 | tf_op jit(solution)/shard_map/ppermute | solution.py:106
  166.9 36.2 %collective-permute-start.23 = (bf16[4,72,2880]{2,1,0:T(8,128)(2,1)}, bf16[4,72,2880]{2,1,0:T(8,128)(2,1)S(1)}, u32[]{:S(2)}, u32[]{:S(2)}) collective-permute-start(bf16[4,72,2880]{2,1,0:T(8,128)(2,1)} %collective-permute-done.21.refs_1_), channel_id=1, source_target_pairs={{0,4},{1,3},{2,6},{3,1},{4,0},{5,7},{6,2},{7,5},{8,12},{9,11},{10,... | collective-permute-start | bytes 4976648 | tf_op jit(solution)/shard_map/ppermute | solution.py:106
  168.3 32.4 %collective-permute-start.24 = (bf16[4,72,2304]{2,1,0:T(8,128)(2,1)}, bf16[4,72,2304]{2,1,0:T(8,128)(2,1)}, u32[]{:S(2)}, u32[]{:S(2)}) collective-permute-start(bf16[4,72,2304]{2,1,0:T(8,128)(2,1)} %bitcast.233), channel_id=1, source_target_pairs={{0,2},{1,5},{2,0},{3,7},{4,6},{5,1},{6,4},{7,3},{8,10},{9,13},{10,... | collective-permute-start | bytes 3981320 | tf_op jit(solution)/shard_map/ppermute | solution.py:106
  237.2 30.5 %collective-permute-start.28 = (bf16[1024,1152]{1,0:T(8,128)(2,1)}, bf16[1024,1152]{1,0:T(8,128)(2,1)}, u32[]{:S(2)}, u32[]{:S(2)}) collective-permute-start(bf16[1024,1152]{1,0:T(8,128)(2,1)} %bitcast.37.values_ref.left_one), channel_id=1, source_target_pairs={{0,1},{1,0},{2,3},{3,2},{4,5},{5,4},{6,7},{7,6},{8,9},{9,8},{10,11... | collective-permute-start | bytes 7077896 | tf_op jit(solution)/shard_map/ppermute | solution.py:110
  238.9 41.1 %collective-permute-start.29 = (bf16[4,72,2304]{2,1,0:T(8,128)(2,1)}, bf16[4,72,2304]{2,1,0:T(8,128)(2,1)}, u32[]{:S(2)}, u32[]{:S(2)}) collective-permute-start(bf16[4,72,2304]{2,1,0:T(8,128)(2,1)} %collective-permute-done.24.refs_1_), channel_id=1, source_target_pairs={{0,4},{1,3},{2,6},{3,1},{4,0},{5,7},{6,2},{7,5},{8,12},{9,11},{10,... | collective-permute-start | bytes 3981320 | tf_op jit(solution)/shard_map/ppermute | solution.py:106
  353.9 34.5 %collective-permute-start.32 = (bf16[4,72,2304]{2,1,0:T(8,128)(2,1)}, bf16[4,72,2304]{2,1,0:T(8,128)(2,1)}, u32[]{:S(2)}, u32[]{:S(2)}) collective-permute-start(bf16[4,72,2304]{2,1,0:T(8,128)(2,1)} %get-tuple-element.177), channel_id=1, source_target_pairs={{0,4},{1,3},{2,6},{3,1},{4,0},{5,7},{6,2},{7,5},{8,12},{9,11},{10,... | collective-permute-start | bytes 3981320 | tf_op jit(solution)/shard_map/ppermute | solution.py:106
  376.8 33.7 %collective-permute-start.33 = (bf16[1024,1152]{1,0:T(8,128)(2,1)}, bf16[1024,1152]{1,0:T(8,128)(2,1)}, u32[]{:S(2)}, u32[]{:S(2)}) collective-permute-start(bf16[1024,1152]{1,0:T(8,128)(2,1)} %out_of.9), channel_id=1, source_target_pairs={{0,1},{1,0},{2,3},{3,2},{4,5},{5,4},{6,7},{7,6},{8,9},{9,8},{10,11... | collective-permute-start | bytes 7077896 | tf_op jit(solution)/shard_map/ppermute | solution.py:110
  376.8 51.2 %collective-permute-start.35 = (bf16[4,72,2304]{2,1,0:T(8,128)(2,1)}, bf16[4,72,2304]{2,1,0:T(8,128)(2,1)}, u32[]{:S(2)}, u32[]{:S(2)}) collective-permute-start(bf16[4,72,2304]{2,1,0:T(8,128)(2,1)} %get-tuple-element.186), channel_id=1, source_target_pairs={{0,4},{1,3},{2,6},{3,1},{4,0},{5,7},{6,2},{7,5},{8,12},{9,11},{10,... | collective-permute-start | bytes 3981320 | tf_op jit(solution)/shard_map/ppermute | solution.py:106
  391.5 36.6 %collective-permute-start.34 = (bf16[4,72,2304]{2,1,0:T(8,128)(2,1)}, bf16[4,72,2304]{2,1,0:T(8,128)(2,1)}, u32[]{:S(2)}, u32[]{:S(2)}) collective-permute-start(bf16[4,72,2304]{2,1,0:T(8,128)(2,1)} %add_convert_fusion.10), channel_id=1, source_target_pairs={{0,2},{1,5},{2,0},{3,7},{4,6},{5,1},{6,4},{7,3},{8,10},{9,13},{10,... | collective-permute-start | bytes 3981320 | tf_op jit(solution)/shard_map/ppermute | solution.py:106
  428.1 26.0 %collective-permute-start.36 = (bf16[4,72,2304]{2,1,0:T(8,128)(2,1)}, bf16[4,72,2304]{2,1,0:T(8,128)(2,1)}, u32[]{:S(2)}, u32[]{:S(2)}) collective-permute-start(bf16[4,72,2304]{2,1,0:T(8,128)(2,1)} %get-tuple-element.189), channel_id=1, source_target_pairs={{0,4},{1,3},{2,6},{3,1},{4,0},{5,7},{6,2},{7,5},{8,12},{9,11},{10,... | collective-permute-start | bytes 3981320 | tf_op jit(solution)/shard_map/ppermute | solution.py:106
  447.1 129.3 %reduce-scatter.9.cloned.1.call-start = ((), (), s32[]{:S(2)}) async-start(), calls=%async_computation.5 | async-start | bytes 1658880 | tf_op jit(solution)/shard_map/reduce_scatter | solution.py:257
  456.8 32.1 %collective-permute-start.39 = (bf16[4,72,2304]{2,1,0:T(8,128)(2,1)}, bf16[4,72,2304]{2,1,0:T(8,128)(2,1)}, u32[]{:S(2)}, u32[]{:S(2)}) collective-permute-start(bf16[4,72,2304]{2,1,0:T(8,128)(2,1)} %add_convert_fusion.6), channel_id=1, source_target_pairs={{0,2},{1,5},{2,0},{3,7},{4,6},{5,1},{6,4},{7,3},{8,10},{9,13},{10,... | collective-permute-start | bytes 3981320 | tf_op jit(solution)/shard_map/ppermute | solution.py:106
  457.9 31.0 %collective-permute-start.40 = (bf16[4,72,2304]{2,1,0:T(8,128)(2,1)}, bf16[4,72,2304]{2,1,0:T(8,128)(2,1)}, u32[]{:S(2)}, u32[]{:S(2)}) collective-permute-start(bf16[4,72,2304]{2,1,0:T(8,128)(2,1)} %get-tuple-element.201), channel_id=1, source_target_pairs={{0,4},{1,3},{2,6},{3,1},{4,0},{5,7},{6,2},{7,5},{8,12},{9,11},{10,... | collective-permute-start | bytes 3981320 | tf_op jit(solution)/shard_map/ppermute | solution.py:106
  460.6 25.1 %collective-permute-start.38 = (bf16[1024,576]{0,1:T(8,128)(2,1)}, bf16[1024,576]{0,1:T(8,128)(2,1)S(1)}, u32[]{:S(2)}, u32[]{:S(2)}) collective-permute-start(bf16[1024,576]{0,1:T(8,128)(2,1)} %copy.120), channel_id=1, source_target_pairs={{0,1},{1,0},{2,3},{3,2},{4,5},{5,4},{6,7},{7,6},{8,9},{9,8},{10,11... | collective-permute-start | bytes 3538952 | tf_op jit(solution)/shard_map/ppermute | solution.py:110
  490.3 30.2 %collective-permute-start.41 = (bf16[4,72,576]{2,1,0:T(8,128)(2,1)}, bf16[4,72,576]{2,1,0:T(8,128)(2,1)S(1)}, u32[]{:S(2)}, u32[]{:S(2)}) collective-permute-start(bf16[4,72,576]{2,1,0:T(8,128)(2,1)} %get-tuple-element.206), channel_id=1, source_target_pairs={{0,4},{1,3},{2,6},{3,1},{4,0},{5,7},{6,2},{7,5},{8,12},{9,11},{10,... | collective-permute-start | bytes 995336 | tf_op jit(solution)/shard_map/ppermute | solution.py:106
  542.4 119.7 %reduce-scatter.13.cloned.1.call-start = ((), (), s32[]{:S(2)}) async-start(), calls=%async_computation.9 | async-start | bytes 460800
  554.5 27.9 %collective-permute-start.48 = (bf16[1024,1152]{1,0:T(8,128)(2,1)}, bf16[1024,1152]{1,0:T(8,128)(2,1)S(1)}, u32[]{:S(2)}, u32[]{:S(2)}) collective-permute-start(bf16[1024,1152]{1,0:T(8,128)(2,1)} %out_of.10), channel_id=1, source_target_pairs={{0,1},{1,0},{2,3},{3,2},{4,5},{5,4},{6,7},{7,6},{8,9},{9,8},{10,11... | collective-permute-start | bytes 7077896 | tf_op jit(solution)/shard_map/ppermute | solution.py:110
  565.3 28.0 %collective-permute-start.51 = (bf16[4,72,1792]{2,1,0:T(8,128)(2,1)}, bf16[4,72,1792]{2,1,0:T(8,128)(2,1)}, u32[]{:S(2)}, u32[]{:S(2)}) collective-permute-start(bf16[4,72,1792]{2,1,0:T(8,128)(2,1)} %get-tuple-element.228), channel_id=1, source_target_pairs={{0,4},{1,3},{2,6},{3,1},{4,0},{5,7},{6,2},{7,5},{8,12},{9,11},{10,... | collective-permute-start | bytes 3096584 | tf_op jit(solution)/shard_map/ppermute | solution.py:106
  608.2 53.8 %reduce-scatter.11.cloned.1.call-start = ((), (), s32[]{:S(2)}) async-start(), calls=%async_computation.6 | async-start | bytes 1290240 | tf_op jit(solution)/shard_map/reduce_scatter | solution.py:257
  609.7 66.4 %collective-permute-start.53 = (f32[7689]{0:T(1024)}, f32[7689]{0:T(1024)}, u32[]{:S(2)}, u32[]{:S(2)}) collective-permute-start(f32[7689]{0:T(1024)} %add.581), channel_id=1, source_target_pairs={{0,1},{1,0},{2,3},{3,2},{4,5},{5,4},{6,7},{7,6},{8,9},{9,8},{10,11... | collective-permute-start | bytes 92276 | tf_op jit(solution)/shard_map/ppermute | solution.py:110
  (171 other events, 1710.0 us)
Sparse Core Ops, SparseCore 0:
  60.1 37.9 all-gather.4
  127.1 30.7 all-gather.6
  447.2 30.3 reduce-scatter.6
  542.5 29.7 reduce-scatter.8
  608.3 19.3 reduce-scatter.12
  630.6 26.2 reduce-scatter.10

commit v5 on v4

--- a/solution.py
+++ b/solution.py
@@ -607,6 +607,160 @@
     )(places, *left, *right)
 
 
+def norm_rows(values):
+    center = values - jnp.mean(values, -1, keepdims=True)
+    inverse = lax.rsqrt(jnp.mean(center * center, -1, keepdims=True) + 1e-06)
+    return center * inverse, inverse
+
+
+def row_sum(values):
+    return jnp.sum(values, 0, keepdims=True)
+
+
+def image_call(kernel, name, operands, outs, images, sums=(), core=None):
+    tokens = GRID * GRID
+    lead = () if core is None else (core,)
+
+    def spec(shape, whole):
+        if whole:
+            return pl.BlockSpec(
+                shape, lambda step, *_: (0,) * len(shape), pipeline_mode=pl.Buffered(1)
+            )
+        if len(shape) == 3:
+            return pl.BlockSpec((1,) + shape[1:], lambda step, *_: (step, 0, 0))
+        return pl.BlockSpec((tokens, shape[1]), lambda step, *_: (step, 0))
+
+    rows = images * tokens
+
+    def is_whole(shape):
+        return len(shape) == 2 and shape[0] != rows
+
+    summed = [pl.BlockSpec(item.shape, lambda step, *_: (0, 0)) for item in sums]
+    return pl.pallas_call(
+        kernel,
+        grid_spec=pltpu.PrefetchScalarGridSpec(
+            num_scalar_prefetch=len(lead),
+            grid=(images,),
+            in_specs=[spec(item.shape, is_whole(item.shape)) for item in operands],
+            out_specs=[spec(item.shape, False) for item in outs] + summed,
+        ),
+        out_shape=list(outs) + list(sums),
+        compiler_params=pltpu.CompilerParams(vmem_limit_bytes=VMEM),
+        cost_estimate=pl.CostEstimate(
+            flops=4 * rows * D * D if lead else 64 * rows * D,
+            bytes_accessed=16 * rows * D,
+            transcendentals=0,
+        ),
+        name=name,
+    )(*lead, *operands)
+
+
+def core_rows(ref, core, mine):
+    half = D // 2
+    first = core * half if mine else (1 - core) * half
+    return ref[pl.ds(pl.multiple_of(first, 16), half), :]
+
+
+def merge_kernel(
+    core_ref, one_ref, two_ref, mine_ref, other_ref, hidden_ref, mod_ref, branch_ref, out_ref, in_ref
+):
+    core = core_ref[0]
+    one, two, mod = (one_ref[...], two_ref[...], mod_ref[0])
+
+    def columns(ref):
+        return product(one, core_rows(ref, core, True), ((1,), (0,))) + product(
+            two, core_rows(ref, core, False), ((1,), (0,))
+        )
+
+    mine, other = (columns(mine_ref), columns(other_ref))
+    first = jnp.where(core == 0, mine, other)
+    branch = jnp.concatenate([first, jnp.where(core == 0, other, mine)], 1)
+    hidden = hidden_ref[...] + mod[2:3] * branch
+    normed, _ = norm_rows(hidden)
+    branch_ref[...] = branch.astype(jnp.bfloat16)
+    out_ref[...] = hidden
+    in_ref[...] = (normed * (1.0 + mod[4:5]) + mod[3:4]).astype(jnp.bfloat16)
+
+
+def ends_kernel(
+    count, mine_ref, theirs_ref, hidden_ref, noise_ref, head_ref, mod_ref, *refs
+):
+    d_hidden_ref, d_branch_ref, d_mod_ref, g_head_ref, loss_ref = refs
+    wide, low = (jnp.float32, jnp.bfloat16)
+
+    @pl.when(pl.program_id(0) == 0)
+    def _():
+        g_head_ref[...] = jnp.zeros_like(g_head_ref)
+        loss_ref[...] = jnp.zeros_like(loss_ref)
+
+    mod, head = (mod_ref[0], head_ref[...])
+    branch = mine_ref[...] + theirs_ref[...].astype(wide)
+    normed, inverse = norm_rows(hidden_ref[...] + mod[5:6] * branch)
+    final_in = (normed * (1.0 + mod[7:8]) + mod[6:7]).astype(low)
+    error = product(final_in, head, ((1,), (1,))) - noise_ref[...]
+    loss_ref[...] += jnp.sum(error * error)
+    d_predicted = (error * (2.0 / count)).astype(low)
+    d_final = product(d_predicted, head, ((1,), (0,)))
+    g_head_ref[...] += product(d_predicted, final_in, ((0,), (0,)))
+    d_hidden = norm_back(d_final * (1.0 + mod[7:8]), normed, inverse)
+    d_hidden_ref[...] = d_hidden
+    d_branch_ref[...] = (mod[5:6] * d_hidden).astype(low)
+    blank = jnp.zeros((5, D), wide)
+    gate, shift, scale = (row_sum(d_hidden * branch), row_sum(d_final), row_sum(d_final * normed))
+    d_mod_ref[0] = jnp.concatenate([blank, gate, shift, scale], 0)
+
+
+def merge_back_kernel(
+    core_ref, mine_ref, theirs_ref, hidden_ref, branch_ref, d_hidden_ref, p_mine, p_other, mod_ref,
+    d_mod_ref, *refs
+):
+    d_out_ref, d_branch_ref, d_one_ref, d_two_ref, d_mod_out_ref = refs
+    core = core_ref[0]
+    wide, low = (jnp.float32, jnp.bfloat16)
+    mod, half = (mod_ref[0], D // 2)
+    d_in = mine_ref[...] + theirs_ref[...].astype(wide)
+    normed, inverse = norm_rows(hidden_ref[...])
+    d_hidden = d_hidden_ref[...] + norm_back(d_in * (1.0 + mod[4:5]), normed, inverse)
+    d_out_ref[...] = d_hidden
+    gate = row_sum(d_hidden * branch_ref[...].astype(wide))
+    d_branch = mod[2:3] * d_hidden
+    d_branch_ref[...] = d_branch.astype(low)
+    low_half, high_half = (d_branch[:, :half], d_branch[:, half:])
+    d_mine = jnp.where(core == 0, low_half, high_half).astype(low)
+    d_other = jnp.where(core == 0, high_half, low_half).astype(low)
+
+    def heads(mine):
+        return product(d_mine, core_rows(p_mine, core, mine), ((1,), (1,))) + product(
+            d_other, core_rows(p_other, core, mine), ((1,), (1,))
+        )
+
+    d_one_ref[...] = heads(True).astype(low)
+    d_two_ref[...] = heads(False).astype(low)
+    blank = jnp.zeros((2, D), wide)
+    sums = [blank, gate, row_sum(d_in), row_sum(d_in * normed), d_mod_ref[0][5:8]]
+    d_mod_out_ref[0] = jnp.concatenate(sums, 0)
+
+
+def start_back_kernel(
+    mine_ref, theirs_ref, hidden_ref, d_hidden_ref, mixed_ref, mod_ref, d_mod_ref, *refs
+):
+    d_mod_out_ref, g_patch_ref = refs
+    wide = jnp.float32
+
+    @pl.when(pl.program_id(0) == 0)
+    def _():
+        g_patch_ref[...] = jnp.zeros_like(g_patch_ref)
+
+    mod = mod_ref[0]
+    d_in = mine_ref[...] + theirs_ref[...].astype(wide)
+    normed, inverse = norm_rows(hidden_ref[...])
+    d_hidden = d_hidden_ref[...] + norm_back(d_in * (1.0 + mod[1:2]), normed, inverse)
+    g_patch_ref[...] += product(mixed_ref[...], d_hidden.astype(jnp.bfloat16), ((0,), (0,)))
+    d_mod_out_ref[0] = jnp.concatenate(
+        [row_sum(d_in), row_sum(d_in * normed), d_mod_ref[0][2:8]], 0
+    )
+
+
 def shifts():
     offset = jnp.arange(SIDE, dtype=jnp.int32)[:, None, None]
     column = jnp.arange(GRID, dtype=jnp.int32)
@@ -833,44 +987,54 @@
     qkv, logs_two, in_second, in_third, out_far = tie(qkv, logs_two, in_second, in_third, out_far)
     heads_two = swap_cores(heads_two)
     in_both = gather_last(in_second)
+    heads_one, logs = attention(qkv, bias_rows)
+    heads_one, in_both, out_far = tie(heads_one, in_both, out_far)
     out_second, out_third = gather_near(out_far)
-    heads_one, logs = attention(qkv, bias_rows)
-    heads_one, in_both, out_second = tie(heads_one, in_both, out_second)
+    in_low = place_blocks([in_far, in_second, in_third, in_both], stacked).reshape(D, -1)
+    in_low, out_second = tie(in_low, out_second)
+    proj_half = in_low[:, wide_half:]
+    proj_other = swap_cores(proj_half)
+    core_place = core.astype(jnp.int32).reshape(1)
+    rows_wide = jax.ShapeDtypeStruct((rows, D), wide)
+    rows_low = jax.ShapeDtypeStruct((rows, D), low)
+    rows_heads = jax.ShapeDtypeStruct((rows, half), low)
+    mod_shape = jax.ShapeDtypeStruct((images, 8, D), wide)
+    patch_shape = jax.ShapeDtypeStruct((PDIM, D), wide)
+    branch_one, hidden1, mlp_in = image_call(
+        merge_kernel,
+        "merge_heads",
+        [heads_one, heads_two, proj_half, proj_other, flat(hidden0), modulation],
+        [rows_low, rows_wide, rows_low],
+        images,
+        core=core_place,
+    )
+    mlp_in, out_third = tie(mlp_in, out_third)
+    mlp_in_two = swap_cores(mlp_in)
     out_both = gather_last(out_second)
-    in_low = place_blocks([in_far, in_second, in_third, in_both], stacked).reshape(D, -1)
-    proj_half = in_low[:, wide_half:]
-    proj_low = both_cores(proj_half, swap_cores(proj_half), core, 1)
-    attn_out = both_cores(heads_one, heads_two, core, 1)
-    branch_one = dense(attn_out, proj_low).reshape(images, length, D)
-    hidden1 = hidden0 + modulation[:, 2:3] * branch_one
-    normed2, inverse2 = layer_norm(hidden1)
-    mlp_in = flat(moved(normed2, 3))
-    mlp_in_two = swap_cores(mlp_in)
-    mlp_in, out_third = tie(mlp_in, out_third)
     act, slope = feed_in(mlp_in, in_low, wide_half)
-    act, mlp_in_two = tie(act, mlp_in_two)
+    act, mlp_in_two, out_both = tie(act, mlp_in_two, out_both)
     act_two, slope_two = feed_in(mlp_in_two, in_low, wide_half)
-    act_two, out_both = tie(act_two, out_both)
     out_low = place_blocks([out_far, out_second, out_third, out_both], stacked).reshape(D, -1)
     branch_theirs = out_of(act_two, out_low, low)
-    branch_two = sum_cores(out_of(act, out_low, wide), branch_theirs)
-    hidden2 = hidden1 + modulation[:, 5:6] * branch_two
-
-    normed3, inverse3 = layer_norm(hidden2)
-    final_in = moved(normed3, 6)
-    predicted = dense_trans(final_in, head)
-    error = predicted - noise
-    loss_here = jnp.sum(error * error)
-    d_predicted = (error * (2.0 / count)).astype(low)
-    d_final = dense(d_predicted, head)
-    g_head = outer_sum(d_predicted, final_in)
-    d_scale3 = jnp.sum(d_final * normed3, 1)
-    d_shift3 = jnp.sum(d_final, 1)
-    d_hidden2 = norm_back(d_final * (1.0 + modulation[:, 7:8]), normed3, inverse3)
-
-    d_branch_two = flat((modulation[:, 5:6] * d_hidden2).astype(low))
+    branch_theirs = swap_cores(branch_theirs)
+    branch_mine = out_of(act, out_low, wide)
+    d_hidden2, d_branch_two, d_mod, g_head, loss_tile = image_call(
+        functools.partial(ends_kernel, count),
+        "ends",
+        [
+            branch_mine,
+            branch_theirs,
+            hidden1,
+            noise.reshape(rows, -1),
+            head,
+            modulation,
+        ],
+        [rows_wide, rows_low, mod_shape],
+        images,
+        sums=[patch_shape, jax.ShapeDtypeStruct((8, 128), wide)],
+    )
+    loss_here = loss_tile[0, 0]
     d_branch_two_two = swap_cores(d_branch_two)
-    d_gate2 = jnp.sum(d_hidden2 * branch_two, 1)
     d_pre = feed_back(d_branch_two, out_low, slope)
     d_pre, d_branch_two_two = tie(d_pre, d_branch_two_two)
     d_pre_two = feed_back(d_branch_two_two, out_low, slope_two)
@@ -888,40 +1052,53 @@
         (mlp_in, mlp_in_two), (d_pre, d_pre_two), stacked
     )
     in_both, d_mlp_theirs, d_mlp_mine = tie(in_both, d_mlp_theirs, d_mlp_mine)
-    d_mlp_in = (d_mlp_mine + d_mlp_theirs.astype(wide)).reshape(images, length, D)
-    d_scale2 = jnp.sum(d_mlp_in * normed2, 1)
-    d_shift2 = jnp.sum(d_mlp_in, 1)
-    d_hidden1 = d_hidden2 + norm_back(d_mlp_in * (1.0 + modulation[:, 4:5]), normed2, inverse2)
-    d_branch_one = (modulation[:, 2:3] * d_hidden1).astype(low).reshape(rows, D)
-    d_branch_one, out_second, out_third, in_both = tie(
-        d_branch_one, out_second, out_third, in_both
+    d_hidden1, d_branch_one, d_mine, d_theirs, d_mod = image_call(
+        merge_back_kernel,
+        "merge_heads_back",
+        [
+            d_mlp_mine,
+            d_mlp_theirs,
+            hidden1,
+            branch_one,
+            d_hidden2,
+            proj_half,
+            proj_other,
+            modulation,
+            d_mod,
+        ],
+        [rows_wide, rows_low, rows_heads, rows_heads, mod_shape],
+        images,
+        core=core_place,
+    )
+    d_branch_one, d_mine, out_second, out_third, in_both = tie(
+        d_branch_one, d_mine, out_second, out_third, in_both
     )
     in_back = send(in_both, plane_peers((2, 1)))
     g_out = far_share(add_low(add_low(out_own, out_third), out_second))
-    d_gate1 = jnp.sum(d_hidden1 * branch_one, 1)
-    d_attn_out = dense_trans(d_branch_one, proj_low).astype(low)
-    d_mine = jnp.where(core == 0, d_attn_out[:, :half], d_attn_out[:, half:])
-    d_theirs = jnp.where(core == 0, d_attn_out[:, half:], d_attn_out[:, :half])
     d_theirs = swap_cores(d_theirs)
-    g_proj = outer_sum(attn_out, d_branch_one)
+    d_qkv, d_spread = attention_back(qkv, d_mine, logs, bias_rows)
+    d_qkv, d_branch_one, d_theirs, in_back, in_third = tie(
+        d_qkv, d_branch_one, d_theirs, in_back, in_third
+    )
+    in_second = send(add_low(in_second, in_back), plane_peers((1, 2)))
+    in_third = send(in_third, plane_peers((2, 1)))
+    g_proj = both_cores(
+        outer_sum(heads_one, d_branch_one), outer_sum(heads_two, d_branch_one), core, 0
+    )
     g_proj_mine = jnp.where(core == 0, g_proj[:, :half], g_proj[:, half:])
     g_proj_theirs = jnp.where(core == 0, g_proj[:, half:], g_proj[:, :half]).astype(low)
     g_proj = (g_proj_mine + swap_cores(g_proj_theirs).astype(wide)).astype(low)
-    d_mine, in_back, in_third, g_proj = tie(d_mine, in_back, in_third, g_proj)
-    in_second = send(add_low(in_second, in_back), plane_peers((1, 2)))
-    in_third = send(in_third, plane_peers((2, 1)))
-    d_qkv, d_spread = attention_back(qkv, d_mine, logs, bias_rows)
     proj_own, proj_second, proj_third, proj_both = pick_blocks(
         g_proj.reshape(spread, -1, half), stacked
     )
-    d_qkv, proj_both, d_theirs, g_out, in_second, in_third = tie(
-        d_qkv, proj_both, d_theirs, g_out, in_second, in_third
-    )
-    g_in = far_share(add_low(add_low(in_own, in_third), in_second))
+    proj_both, d_theirs = tie(proj_both, d_theirs)
     proj_back = send(proj_both, plane_peers((2, 1)))
     d_qkv_two, d_spread_two = attention_back(qkv_two, d_theirs, logs_two, bias_rows)
+    d_qkv_two, in_second, in_third, proj_back, proj_third, g_out = tie(
+        d_qkv_two, in_second, in_third, proj_back, proj_third, g_out
+    )
+    g_in = far_share(add_low(add_low(in_own, in_third), in_second))
     d_spread = d_spread + d_spread_two
-    d_qkv_two, proj_back, proj_third = tie(d_qkv_two, proj_back, proj_third)
     proj_second = send(add_low(proj_second, proj_back), plane_peers((1, 2)))
     proj_third = send(proj_third, plane_peers((2, 1)))
     rel_half = gather_bias(d_spread)
@@ -946,23 +1123,31 @@
     d_attn_mine = out_of(d_qkv, qkv_low, wide)
     d_attn_mine, g_in, packed = tie(d_attn_mine, g_in, packed)
     packed = packed + send(packed, dp_peers(bits[-1]))
-    d_attn_in = (d_attn_mine + d_attn_theirs.astype(wide)).reshape(images, length, D)
-    d_scale1 = jnp.sum(d_attn_in * normed1, 1)
-    d_shift1 = jnp.sum(d_attn_in, 1)
-    d_hidden0 = d_hidden1 + norm_back(d_attn_in * (1.0 + modulation[:, 1:2]), normed1, inverse1)
-    g_patch = outer_sum(mixed, d_hidden0.astype(low))
-
-    d_modulation = jnp.stack(
-        [d_shift1, d_scale1, d_gate1, d_shift2, d_scale2, d_gate2, d_shift3, d_scale3], 1
-    )
-    d_modulation = d_modulation.reshape(images, 8 * D).astype(low)
+    d_mod, g_patch = image_call(
+        start_back_kernel,
+        "start_back",
+        [
+            d_attn_mine,
+            d_attn_theirs,
+            flat(hidden0),
+            d_hidden1,
+            flat(mixed),
+            modulation,
+            d_mod,
+        ],
+        [mod_shape],
+        images,
+        sums=[patch_shape],
+    )
+
+    d_modulation = d_mod.reshape(images, 8 * D).astype(low)
     mod_half = 4 * D
     d_keep = jnp.where(core == 0, d_modulation[:, :mod_half], d_modulation[:, mod_half:])
     d_give = jnp.where(core == 0, d_modulation[:, mod_half:], d_modulation[:, :mod_half])
     d_pair = both_cores(d_keep, swap_cores(d_give), core, 0)
     d_pair, attn_second, attn_third, packed = tie(d_pair, attn_second, attn_third, packed)
     d_far = gather_far(d_pair)
-    attn_own, d_far, g_patch = tie(attn_own, d_far, g_patch)
+    attn_own, d_far = tie(attn_own, d_far)
     g_qkv = far_share(add_low(add_low(attn_own, attn_third), attn_second))
     d_second, d_third = gather_near(d_far)
     d_parts = [d_far, d_second, d_third, gather_last(d_second)]

time: 767 us -> 741 us (0.966)
  Pallas kernels: 275 us -> 319 us
  other arithmetic: 137 us -> 94.7 us
  matrix products: 52 us -> 29.5 us
  waiting for transfers between devices: 136 us -> 122 us
  local copies, waits for them, and re-layouts: 64.7 us -> 74.5 us
    pallas_call x0 -> x4, Pallas kernels: none -> 45.1 us  [image_call(): pl.pallas_call(kernel, grid_spec=pltpu.PrefetchScalarGridSpec(num_scalar_...]
    reduce_sum x8 -> x0, other arithmetic: 25 us -> none  [the longest x1 8.39 us: on_device(): d_gate1 = jnp.sum(d_hidden1 * branch_one, 1)]
    ppermute x60, waiting for transfers between devices: 131 us -> 118 us  [send(): return lax.ppermute(values, DP + ('mod',), peers)]
    dot_general x5 -> x3, matrix products: 12.4 us -> 3.06 us  [dense(): return jnp.dot(left, right, preferred_element_type=jnp.float32)]
    dot_general x3 -> x1, matrix products: 9.91 us -> 1.41 us  [dense_trans(): lax.dot_general(left, right, (((left.ndim - 1,), (1,)), ((), ())), prefer...]
    dot_general x4 -> x3, matrix products: 15.5 us -> 10.8 us  [outer_sum(): lax.dot_general(flat_left, flat_right, (((0,), (0,)), ((), ())), preferre...]
  transfers between devices with their start and end apart: 85 -> 85, of which waited for: 35 -> 33; matrix products, arithmetic and copies ran while one was open for 22% -> 17% of each run, Pallas kernels for 31% -> 36%
where the time goes in v5:
time: 741 us; the launch traced here: 735 us
  Pallas kernels  319 us (43%)
  waiting for transfers between devices  122 us (16%)
  other arithmetic  94.7 us (13%)
  local copies, waits for them, and re-layouts  74.5 us (10%)
  starting transfers between devices  73.3 us (10%)
  matrix products  29.5 us (4%)
  between operations  21.9 us (3%)
    ppermute x60, waiting for transfers between devices, send(): return lax.ppermute(values, DP + ('mod',), peers)  118 us
    ppermute x60, starting transfers between devices, send(): return lax.ppermute(values, DP + ('mod',), peers)  68 us
    pallas_call x6, Pallas kernels, out_of(): pl.pallas_call(out_of_kernel, grid=(rows // tile,), in_specs=[pl.BlockSpe...  61.5 us
    pallas_call x3, Pallas kernels, weight_grad(): pl.pallas_call(weight_grad_kernel, grid_spec=pltpu.PrefetchScalarGridSpec...  50.8 us
    pallas_call x4, Pallas kernels, image_call(): pl.pallas_call(kernel, grid_spec=pltpu.PrefetchScalarGridSpec(num_scalar_...  45.1 us
    pallas_call x2, Pallas kernels, attention_back(): pl.pallas_call(functools.partial(attention_back_kernel, heads), grid=(row...  40.9 us
    pallas_call x2, Pallas kernels, attention(): pl.pallas_call(functools.partial(attention_kernel, heads), grid=(rows //...  30 us
    pallas_call x6, Pallas kernels, move_call(): pl.pallas_call(functools.partial(kernel, counts, slots), grid_spec=pltpu....  25.9 us
  transfers between devices with their start and end apart: 85, of which 33 were waited for; matrix products, arithmetic and copies ran while one was open for 17% of the time, Pallas kernels for 36%

profile of v5, /device:TPU:0, one launch (start us, length us, event | category | flops | bytes accessed | tf_op | source)
XLA Modules:
  0.0 734.8 jit_solution(1456947684362412756)
XLA Ops:
  45.1 11.9 %collective-permute-done.8 = bf16[1,72,1792]{2,1,0:T(8,128)(2,1)} collective-permute-done((bf16[1,72,1792]{2,1,0:T(8,128)(2,1)S(1)}, bf16[1,72,1792]{2,1,0:T(8,128)(2,1)}, u32[]{:S(2)}, u32[]{:S(2)}) %collective-permute-start.8) | collective-permute-done | bytes 258080 | tf_op jit(solution)/shard_map/ppermute | solution.py:106
  70.6 11.4 %collective-permute-done.10.refs_1_ = bf16[4,72,1792]{2,1,0:T(8,128)(2,1)} collective-permute-done((bf16[4,72,1792]{2,1,0:T(8,128)(2,1)S(1)}, bf16[4,72,1792]{2,1,0:T(8,128)(2,1)}, u32[]{:S(2)}, u32[]{:S(2)}) %collective-permute-start.10) | collective-permute-done | bytes 1032224 | tf_op jit(solution)/shard_map/ppermute | solution.py:106
  94.2 12.5 %collective-permute-done.14.refs_3_ = bf16[4,72,1792]{2,1,0:T(8,128)(2,1)} collective-permute-done((bf16[4,72,1792]{2,1,0:T(8,128)(2,1)}, bf16[4,72,1792]{2,1,0:T(8,128)(2,1)}, u32[]{:S(2)}, u32[]{:S(2)}) %collective-permute-start.14) | collective-permute-done | bytes 1032224 | tf_op jit(solution)/shard_map/ppermute | solution.py:106
  135.6 9.2 %into_heads.2.qkv_ref = bf16[1024,1792]{1,0:T(8,128)(2,1)} custom-call(bf16[1024,1152]{1,0:T(8,128)(2,1)} %bitcast.24.values_ref.left_one, bf16[1152,1792]{1,0:T(8,128)(2,1)} %bitcast.153), custom_call_target="tpu_custom_call" | custom-call | flops 4227858432 | bytes 3670016 | tf_op jit(solution)/shard_map/into_heads/pallas_call | solution.py:530
  154.0 15.0 %attention.2 = (bf16[1024,576]{1,0:T(8,128)(2,1)}, f32[1024,8]{1,0:T(8,128)}) custom-call(bf16[1024,1792]{1,0:T(8,128)(2,1)} %into_heads.3.qkv_ref, f32[8,16,512]{2,1,0:T(8,128)} %pad.13.spread_ref), custom_call_target="tpu_custom_call" | custom-call | flops 2147483648 | bytes 7340032 | tf_op jit(solution)/shard_map/attention/pallas_call | solution.py:343
  170.5 15.0 %attention.3 = (bf16[1024,576]{1,0:T(8,128)(2,1)}, f32[1024,8]{1,0:T(8,128)}) custom-call(bf16[1024,1792]{1,0:T(8,128)(2,1)} %into_heads.2.qkv_ref, f32[8,16,512]{2,1,0:T(8,128)} %pad.13.spread_ref), custom_call_target="tpu_custom_call" | custom-call | flops 2147483648 | bytes 7340032 | tf_op jit(solution)/shard_map/attention/pallas_call | solution.py:343
  199.3 9.5 %collective-permute-done.25.refs_1_ = bf16[4,72,2304]{2,1,0:T(8,128)(2,1)S(1)} collective-permute-done((bf16[4,72,2304]{2,1,0:T(8,128)(2,1)}, bf16[4,72,2304]{2,1,0:T(8,128)(2,1)S(1)}, u32[]{:S(2)}, u32[]{:S(2)}) %collective-permute-start.25) | collective-permute-done | bytes 1327136 | tf_op jit(solution)/shard_map/ppermute | solution.py:106
  222.5 11.1 %merge_heads.1 = (bf16[1024,1152]{1,0:T(8,128)(2,1)}, f32[1024,1152]{1,0:T(8,128)}, bf16[1024,1152]{1,0:T(8,128)(2,1)}) custom-call(s32[1]{0:T(128)} %bitcast.27.core_ref, bf16[1024,576]{1,0:T(8,128)(2,1)} %get-tuple-element.174.one_ref, bf16[1024,576]{1,0:T(8,128)(2,1)} %copy.145.two_ref, bf16[1152,576]{1,0:T(8,128)(2,1)} %copy-done.7, ...), custom_call_target="tpu_custom_call" | custom-call | flops 5435817984 | bytes 18874368 | tf_op jit(solution)/shard_map/merge_heads/pallas_call | solution.py:639
  235.5 12.2 %feed_in.2 = (bf16[1024,2304]{1,0:T(8,128)(2,1)}, bf16[1024,2304]{1,0:T(8,128)(2,1)}) custom-call(bf16[1024,1152]{1,0:T(8,128)(2,1)} %get-tuple-element.182.values_ref.left_one, bf16[1152,2880]{1,0:T(8,128)(2,1)} %bitcast.143), custom_call_target="tpu_custom_call" | custom-call | flops 5435817984 | bytes 9437184 | tf_op jit(solution)/shard_map/feed_in/pallas_call | solution.py:470
  251.9 12.6 %feed_in.3 = (bf16[1024,2304]{1,0:T(8,128)(2,1)}, bf16[1024,2304]{1,0:T(8,128)(2,1)}) custom-call(bf16[1024,1152]{1,0:T(8,128)(2,1)} %collective-permute-done.28.values_ref.left_two, bf16[1152,2880]{1,0:T(8,128)(2,1)} %bitcast.144), custom_call_target="tpu_custom_call" | custom-call | flops 5435817984 | bytes 9437184 | tf_op jit(solution)/shard_map/feed_in/pallas_call | solution.py:470
  270.2 10.8 %out_of.7 = bf16[1024,1152]{1,0:T(8,128)(2,1)} custom-call(bf16[1024,2304]{1,0:T(8,128)(2,1)} %get-tuple-element.189.values_ref.right_two, bf16[1152,2304]{1,0:T(8,128)(2,1)} %bitcast.148), custom_call_target="tpu_custom_call" | custom-call | flops 5435817984 | bytes 4718592 | tf_op jit(solution)/shard_map/out_of/pallas_call | solution.py:552
  282.7 10.8 %out_of.6.mine_ref = f32[1024,1152]{1,0:T(8,128)} custom-call(bf16[1024,2304]{1,0:T(8,128)(2,1)} %get-tuple-element.186.values_ref.right_one, bf16[1152,2304]{1,0:T(8,128)(2,1)} %bitcast.149), custom_call_target="tpu_custom_call" | custom-call | flops 5435817984 | bytes 4718592 | tf_op jit(solution)/shard_map/out_of/pallas_call | solution.py:552
  295.0 10.5 %ends.1 = (f32[1024,1152]{1,0:T(8,128)}, bf16[1024,1152]{1,0:T(8,128)(2,1)}, f32[4,8,1152]{2,1,0:T(8,128)}, f32[16,1152]{1,0:T(8,128)}, f32[8,128]{1,0:T(8,128)}) custom-call(f32[1024,1152]{1,0:T(8,128)} %out_of.6.mine_ref, bf16[1024,1152]{1,0:T(8,128)(2,1)} %copy-done.20, f32[1024,1152]{1,0:T(8,128)} %get-tuple-element.190.hidden_ref, ...), custom_call_target="tpu_custom_call" | custom-call | flops 75497472 | bytes 18874368 | tf_op jit(solution)/shard_map/ends/pallas_call | solution.py:639
  306.1 11.0 %feed_back.2.values_ref.right_one = bf16[1024,2304]{1,0:T(8,128)(2,1)} custom-call(bf16[1024,1152]{1,0:T(8,128)(2,1)} %get-tuple-element.191.values_ref.left_one, bf16[1152,2304]{1,0:T(8,128)(2,1)} %bitcast.150, bf16[1024,2304]{1,0:T(8,128)(2,1)} %get-tuple-element.192.slope_ref), custom_call_target="tpu_custom_call" | custom-call | flops 5435817984 | bytes 9437184 | tf_op jit(solution)/shard_map/feed_back/pallas_call | solution.py:498
  318.5 17.9 %weight_grad.3 = (bf16[4,72,2304]{2,1,0:T(8,128)(2,1)}, bf16[4,72,2304]{2,1,0:T(8,128)(2,1)}, bf16[4,72,2304]{2,1,0:T(8,128)(2,1)}, bf16[4,72,2304]{2,1,0:T(8,128)(2,1)}) custom-call(s32[16]{0:T(128)} %xor.69.places, bf16[1024,1152]{1,0:T(8,128)(2,1)} %get-tuple-element.191.values_ref.left_one, bf16[1024,1152]{1,0:T(8,128)(2,1)} %copy-done.91, ...), custom_call_target="tpu_custom_call" | custom-call | flops 10871635968 | bytes 10616832 | tf_op jit(solution)/shard_map/weight_grad/pallas_call | solution.py:591
  337.8 10.8 %feed_back.3.right_two.values_ref = bf16[1024,2304]{1,0:T(8,128)(2,1)} custom-call(bf16[1024,1152]{1,0:T(8,128)(2,1)} %copy-done.91, bf16[1152,2304]{1,0:T(8,128)(2,1)} %bitcast.151, bf16[1024,2304]{1,0:T(8,128)(2,1)} %get-tuple-element.199.slope_ref), custom_call_target="tpu_custom_call" | custom-call | flops 5435817984 | bytes 9437184 | tf_op jit(solution)/shard_map/feed_back/pallas_call | solution.py:498
  348.7 10.7 %out_of.9 = bf16[1024,1152]{1,0:T(8,128)(2,1)} custom-call(bf16[1024,2304]{1,0:T(8,128)(2,1)} %feed_back.3.right_two.values_ref, bf16[1152,2880]{1,0:T(8,128)(2,1)} %bitcast.145), custom_call_target="tpu_custom_call" | custom-call | flops 5435817984 | bytes 4718592 | tf_op jit(solution)/shard_map/out_of/pallas_call | solution.py:552
  360.7 10.8 %out_of.8.mine_ref = f32[1024,1152]{1,0:T(8,128)} custom-call(bf16[1024,2304]{1,0:T(8,128)(2,1)} %feed_back.2.values_ref.right_one, bf16[1152,2880]{1,0:T(8,128)(2,1)} %bitcast.146), custom_call_target="tpu_custom_call" | custom-call | flops 5435817984 | bytes 4718592 | tf_op jit(solution)/shard_map/out_of/pallas_call | solution.py:552
  375.3 18.0 %weight_grad.4 = (bf16[4,72,2304]{2,1,0:T(8,128)(2,1)}, bf16[4,72,2304]{2,1,0:T(8,128)(2,1)}, bf16[4,72,2304]{2,1,0:T(8,128)(2,1)}, bf16[4,72,2304]{2,1,0:T(8,128)(2,1)}) custom-call(s32[16]{0:T(128)} %xor.69.places, bf16[1024,1152]{1,0:T(8,128)(2,1)} %get-tuple-element.182.values_ref.left_one, ...), custom_call_target="tpu_custom_call" | custom-call | flops 10871635968 | bytes 10616832 | tf_op jit(solution)/shard_map/weight_grad/pallas_call | solution.py:591
  394.8 14.8 %merge_heads_back.1 = (f32[1024,1152]{1,0:T(8,128)}, bf16[1024,1152]{1,0:T(8,128)(2,1)}, bf16[1024,576]{1,0:T(8,128)(2,1)}, bf16[1024,576]{1,0:T(8,128)(2,1)}, f32[4,8,1152]{2,1,0:T(8,128)}) custom-call(s32[1]{0:T(128)} %bitcast.27.core_ref, f32[1024,1152]{1,0:T(8,128)} %out_of.8.mine_ref, bf16[1024,1152]{1,0:T(8,128)(2,1)} %copy-done.19, ...), custom_call_target="tpu_custom_call" | custom-call | flops 5435817984 | bytes 18874368 | tf_op jit(solution)/shard_map/merge_heads_back/pallas_call | solution.py:639
  415.2 20.4 %attention_back.2 = (bf16[1024,1792]{1,0:T(8,128)(2,1)}, f32[8,16,512]{2,1,0:T(8,128)}) custom-call(bf16[1024,1792]{1,0:T(8,128)(2,1)} %into_heads.2.qkv_ref, bf16[1024,576]{1,0:T(8,128)(2,1)} %get-tuple-element.213.upstream_ref, f32[1024,8]{1,0:T(8,128)} %get-tuple-element.214.log_ref, f32[8,16,512]{2,1,0:T(8,128)} %pad.13.spread_ref), custom_call_target="tpu_custom_call" | custom-call | flops 5368709120 | bytes 11010048 | tf_op jit(solution)/shard_map/attention_back/pallas_call | solution.py:417
  470.1 20.4 %attention_back.3 = (bf16[1024,1792]{1,0:T(8,128)(2,1)}, f32[8,16,512]{2,1,0:T(8,128)}) custom-call(bf16[1024,1792]{1,0:T(8,128)(2,1)} %into_heads.3.qkv_ref, bf16[1024,576]{1,0:T(8,128)(2,1)} %copy.156.upstream_ref, f32[1024,8]{1,0:T(8,128)} %get-tuple-element.225.log_ref, f32[8,16,512]{2,1,0:T(8,128)} %pad.13.spread_ref), custom_call_target="tpu_custom_call" | custom-call | flops 5368709120 | bytes 11010048 | tf_op jit(solution)/shard_map/attention_back/pallas_call | solution.py:417
  501.4 14.9 %weight_grad.5 = (bf16[4,72,1792]{2,1,0:T(8,128)(2,1)}, bf16[4,72,1792]{2,1,0:T(8,128)(2,1)}, bf16[4,72,1792]{2,1,0:T(8,128)(2,1)}, bf16[4,72,1792]{2,1,0:T(8,128)(2,1)}) custom-call(s32[16]{0:T(128)} %xor.69.places, bf16[1024,1152]{1,0:T(8,128)(2,1)} %bitcast.24.values_ref.left_one, bf16[1024,1152]{1,0:T(8,128)(2,1)} %collective-permute-done.20.values_ref.left_two, ...), custom_call_target="tpu_custom_call" | custom-call | flops 8455716864 | bytes 8257536 | tf_op jit(solution)/shard_map/weight_grad/pallas_call | solution.py:591
  539.7 9.4 %out_of.11.mine_ref = f32[1024,1152]{1,0:T(8,128)} custom-call(bf16[1024,1792]{1,0:T(8,128)(2,1)} %get-tuple-element.247.right_one.values_ref, bf16[1152,1792]{1,0:T(8,128)(2,1)} %bitcast.156), custom_call_target="tpu_custom_call" | custom-call | flops 4227858432 | bytes 4718592 | tf_op jit(solution)/shard_map/out_of/pallas_call | solution.py:552
  (592 shorter events, 401.1 us)
Async XLA Ops:
  7.2 99.5 %all-gather.5.cloned.1.call-start = ((), (), s32[]{:S(2)}) async-start(), calls=%async_computation.7 | async-start | bytes 2119680 | tf_op jit(solution)/shard_map/all_gather | solution.py:253
  35.0 21.9 %collective-permute-start.8 = (bf16[1,72,1792]{2,1,0:T(8,128)(2,1)S(1)}, bf16[1,72,1792]{2,1,0:T(8,128)(2,1)}, u32[]{:S(2)}, u32[]{:S(2)}) collective-permute-start(bf16[1,72,1792]{2,1,0:T(8,128)(2,1)S(1)} %bitcast.167), channel_id=1, source_target_pairs={{0,16},{1,17},{2,18},{3,19},{4,20},{5,21},{6,22},{7,23},{8,24},{9,... | collective-permute-start | bytes 774152 | tf_op jit(solution)/shard_map/ppermute | solution.py:106
  35.0 21.9 %collective-permute-start.7 = (bf16[1,72,1792]{2,1,0:T(8,128)(2,1)S(1)}, bf16[1,72,1792]{2,1,0:T(8,128)(2,1)}, u32[]{:S(2)}, u32[]{:S(2)}) collective-permute-start(bf16[1,72,1792]{2,1,0:T(8,128)(2,1)S(1)} %bitcast.168), channel_id=1, source_target_pairs={{0,8},{1,9},{2,10},{3,11},{4,12},{5,13},{6,14},{7,15},{8,0},{9,1},... | collective-permute-start | bytes 774152 | tf_op jit(solution)/shard_map/ppermute | solution.py:106
  58.3 23.7 %collective-permute-start.10 = (bf16[4,72,1792]{2,1,0:T(8,128)(2,1)S(1)}, bf16[4,72,1792]{2,1,0:T(8,128)(2,1)}, u32[]{:S(2)}, u32[]{:S(2)}) collective-permute-start(bf16[4,72,1792]{2,1,0:T(8,128)(2,1)S(1)} %pad_maximum_fusion.refs_0_), channel_id=1, source_target_pairs={{0,2},{1,5},{2,0},{3,7},{4,6},{5,1},{6,4},{7,3},{8,10},{9,13},{10,... | collective-permute-start | bytes 3096584 | tf_op jit(solution)/shard_map/ppermute | solution.py:106
  58.9 23.1 %collective-permute-start.11 = (bf16[4,72,1792]{2,1,0:T(8,128)(2,1)S(1)}, bf16[4,72,1792]{2,1,0:T(8,128)(2,1)}, u32[]{:S(2)}, u32[]{:S(2)}) collective-permute-start(bf16[4,72,1792]{2,1,0:T(8,128)(2,1)S(1)} %pad_maximum_fusion.refs_0_), channel_id=1, source_target_pairs={{0,4},{1,3},{2,6},{3,1},{4,0},{5,7},{6,2},{7,5},{8,12},{9,11},{10,... | collective-permute-start | bytes 3096584 | tf_op jit(solution)/shard_map/ppermute | solution.py:106
  59.4 109.6 %all-gather.7.cloned.1.call-start = ((), (), s32[]{:S(2)}) async-start(), calls=%async_computation.8 | async-start | bytes 1658880 | tf_op jit(solution)/shard_map/all_gather | solution.py:253
  129.0 370.2 %reduce-scatter.7.cloned.1.call-start = ((), (), s32[]{:S(2)}) async-start(), calls=%async_computation.4 | async-start | bytes 1658880 | tf_op jit(solution)/shard_map/reduce_scatter | solution.py:257
  129.4 39.6 %collective-permute-start.21 = (bf16[4,72,2880]{2,1,0:T(8,128)(2,1)S(1)}, bf16[4,72,2880]{2,1,0:T(8,128)(2,1)S(1)}, u32[]{:S(2)}, u32[]{:S(2)}) collective-permute-start(bf16[4,72,2880]{2,1,0:T(8,128)(2,1)S(1)} %bitcast.160), channel_id=1, source_target_pairs={{0,2},{1,5},{2,0},{3,7},{4,6},{5,1},{6,4},{7,3},{8,10},{9,13},{10,... | collective-permute-start | bytes 4976648 | tf_op jit(solution)/shard_map/ppermute | solution.py:106
  130.0 39.1 %collective-permute-start.22 = (bf16[4,72,2880]{2,1,0:T(8,128)(2,1)S(1)}, bf16[4,72,2880]{2,1,0:T(8,128)(2,1)}, u32[]{:S(2)}, u32[]{:S(2)}) collective-permute-start(bf16[4,72,2880]{2,1,0:T(8,128)(2,1)S(1)} %bitcast.161), channel_id=1, source_target_pairs={{0,4},{1,3},{2,6},{3,1},{4,0},{5,7},{6,2},{7,5},{8,12},{9,11},{10,... | collective-permute-start | bytes 4976648 | tf_op jit(solution)/shard_map/ppermute | solution.py:106
  169.1 21.8 %collective-permute-start.23 = (bf16[4,72,2880]{2,1,0:T(8,128)(2,1)S(1)}, bf16[4,72,2880]{2,1,0:T(8,128)(2,1)S(1)}, u32[]{:S(2)}, u32[]{:S(2)}) collective-permute-start(bf16[4,72,2880]{2,1,0:T(8,128)(2,1)S(1)} %collective-permute-done.21.refs_1_), channel_id=1, source_target_pairs={{0,4},{1,3},{2,6},{3,1},{4,0},{5,7},{6,2},{7,5},{8,12},{9,11},{10,... | collective-permute-start | bytes 4976648 | tf_op jit(solution)/shard_map/ppermute | solution.py:106
  336.4 35.1 %collective-permute-start.32 = (bf16[4,72,2304]{2,1,0:T(8,128)(2,1)}, bf16[4,72,2304]{2,1,0:T(8,128)(2,1)}, u32[]{:S(2)}, u32[]{:S(2)}) collective-permute-start(bf16[4,72,2304]{2,1,0:T(8,128)(2,1)} %get-tuple-element.197), channel_id=1, source_target_pairs={{0,4},{1,3},{2,6},{3,1},{4,0},{5,7},{6,2},{7,5},{8,12},{9,11},{10,... | collective-permute-start | bytes 3981320 | tf_op jit(solution)/shard_map/ppermute | solution.py:106
  359.3 34.0 %collective-permute-start.33 = (bf16[1024,1152]{1,0:T(8,128)(2,1)}, bf16[1024,1152]{1,0:T(8,128)(2,1)S(1)}, u32[]{:S(2)}, u32[]{:S(2)}) collective-permute-start(bf16[1024,1152]{1,0:T(8,128)(2,1)} %out_of.9), channel_id=1, source_target_pairs={{0,1},{1,0},{2,3},{3,2},{4,5},{5,4},{6,7},{7,6},{8,9},{9,8},{10,11... | collective-permute-start | bytes 7077896 | tf_op jit(solution)/shard_map/ppermute | solution.py:110
  359.3 50.2 %collective-permute-start.35 = (bf16[4,72,2304]{2,1,0:T(8,128)(2,1)}, bf16[4,72,2304]{2,1,0:T(8,128)(2,1)S(1)}, u32[]{:S(2)}, u32[]{:S(2)}) collective-permute-start(bf16[4,72,2304]{2,1,0:T(8,128)(2,1)} %get-tuple-element.211), channel_id=1, source_target_pairs={{0,4},{1,3},{2,6},{3,1},{4,0},{5,7},{6,2},{7,5},{8,12},{9,11},{10,... | collective-permute-start | bytes 3981320 | tf_op jit(solution)/shard_map/ppermute | solution.py:106
  374.6 34.9 %collective-permute-start.34 = (bf16[4,72,2304]{2,1,0:T(8,128)(2,1)}, bf16[4,72,2304]{2,1,0:T(8,128)(2,1)}, u32[]{:S(2)}, u32[]{:S(2)}) collective-permute-start(bf16[4,72,2304]{2,1,0:T(8,128)(2,1)} %add_convert_fusion.7), channel_id=1, source_target_pairs={{0,2},{1,5},{2,0},{3,7},{4,6},{5,1},{6,4},{7,3},{8,10},{9,13},{10,... | collective-permute-start | bytes 3981320 | tf_op jit(solution)/shard_map/ppermute | solution.py:106
  409.6 26.1 %collective-permute-start.37 = (bf16[4,72,2304]{2,1,0:T(8,128)(2,1)}, bf16[4,72,2304]{2,1,0:T(8,128)(2,1)S(1)}, u32[]{:S(2)}, u32[]{:S(2)}) collective-permute-start(bf16[4,72,2304]{2,1,0:T(8,128)(2,1)} %get-tuple-element.218), channel_id=1, source_target_pairs={{0,4},{1,3},{2,6},{3,1},{4,0},{5,7},{6,2},{7,5},{8,12},{9,11},{10,... | collective-permute-start | bytes 3981320 | tf_op jit(solution)/shard_map/ppermute | solution.py:106
  414.0 21.7 %collective-permute-start.36 = (bf16[1024,576]{0,1:T(8,128)(2,1)}, bf16[1024,576]{0,1:T(8,128)(2,1)}, u32[]{:S(2)}, u32[]{:S(2)}) collective-permute-start(bf16[1024,576]{0,1:T(8,128)(2,1)} %copy.150), channel_id=1, source_target_pairs={{0,1},{1,0},{2,3},{3,2},{4,5},{5,4},{6,7},{7,6},{8,9},{9,8},{10,11... | collective-permute-start | bytes 3538952 | tf_op jit(solution)/shard_map/ppermute | solution.py:110
  453.7 98.0 %reduce-scatter.9.cloned.1.call-start = ((), (), s32[]{:S(2)}) async-start(), calls=%async_computation.5 | async-start | bytes 1658880 | tf_op jit(solution)/shard_map/reduce_scatter | solution.py:257
  457.7 41.4 %collective-permute-start.39 = (bf16[4,72,2304]{2,1,0:T(8,128)(2,1)}, bf16[4,72,2304]{2,1,0:T(8,128)(2,1)}, u32[]{:S(2)}, u32[]{:S(2)}) collective-permute-start(bf16[4,72,2304]{2,1,0:T(8,128)(2,1)} %add_convert_fusion.5), channel_id=1, source_target_pairs={{0,2},{1,5},{2,0},{3,7},{4,6},{5,1},{6,4},{7,3},{8,10},{9,13},{10,... | collective-permute-start | bytes 3981320 | tf_op jit(solution)/shard_map/ppermute | solution.py:106
  458.1 41.0 %collective-permute-start.40 = (bf16[4,72,2304]{2,1,0:T(8,128)(2,1)}, bf16[4,72,2304]{2,1,0:T(8,128)(2,1)}, u32[]{:S(2)}, u32[]{:S(2)}) collective-permute-start(bf16[4,72,2304]{2,1,0:T(8,128)(2,1)} %get-tuple-element.229), channel_id=1, source_target_pairs={{0,4},{1,3},{2,6},{3,1},{4,0},{5,7},{6,2},{7,5},{8,12},{9,11},{10,... | collective-permute-start | bytes 3981320 | tf_op jit(solution)/shard_map/ppermute | solution.py:106
  469.4 29.8 %collective-permute-start.41 = (bf16[4,72,576]{2,1,0:T(8,128)(2,1)}, bf16[4,72,576]{2,1,0:T(8,128)(2,1)S(1)}, u32[]{:S(2)}, u32[]{:S(2)}) collective-permute-start(bf16[4,72,576]{2,1,0:T(8,128)(2,1)} %get-tuple-element.230), channel_id=1, source_target_pairs={{0,4},{1,3},{2,6},{3,1},{4,0},{5,7},{6,2},{7,5},{8,12},{9,11},{10,... | collective-permute-start | bytes 995336 | tf_op jit(solution)/shard_map/ppermute | solution.py:106
  521.2 111.0 %reduce-scatter.13.cloned.1.call-start = ((), (), s32[]{:S(2)}) async-start(), calls=%async_computation.9 | async-start | bytes 460800
  535.5 30.8 %collective-permute-start.51 = (bf16[4,72,1792]{2,1,0:T(8,128)(2,1)}, bf16[4,72,1792]{2,1,0:T(8,128)(2,1)}, u32[]{:S(2)}, u32[]{:S(2)}) collective-permute-start(bf16[4,72,1792]{2,1,0:T(8,128)(2,1)} %get-tuple-element.259), channel_id=1, source_target_pairs={{0,4},{1,3},{2,6},{3,1},{4,0},{5,7},{6,2},{7,5},{8,12},{9,11},{10,... | collective-permute-start | bytes 3096584 | tf_op jit(solution)/shard_map/ppermute | solution.py:106
  579.1 53.1 %reduce-scatter.11.cloned.1.call-start = ((), (), s32[]{:S(2)}) async-start(), calls=%async_computation.6 | async-start | bytes 1290240 | tf_op jit(solution)/shard_map/reduce_scatter | solution.py:257
  587.2 61.2 %collective-permute-start.53 = (f32[7689]{0:T(1024)}, f32[7689]{0:T(1024)}, u32[]{:S(2)}, u32[]{:S(2)}) collective-permute-start(f32[7689]{0:T(1024)} %add.507), channel_id=1, source_target_pairs={{0,1},{1,0},{2,3},{3,2},{4,5},{5,4},{6,7},{7,6},{8,9},{9,8},{10,11... | collective-permute-start | bytes 92276 | tf_op jit(solution)/shard_map/ppermute | solution.py:110
  (158 other events, 1876.9 us)
Sparse Core Ops, SparseCore 0:
  59.5 37.9 all-gather.4
  129.1 30.7 all-gather.6
  453.8 30.2 reduce-scatter.6
  521.3 30.2 reduce-scatter.8
  579.2 17.9 reduce-scatter.12
  600.1 25.8 reduce-scatter.10

commit v6 on v5

--- a/solution.py
+++ b/solution.py
@@ -24,8 +24,8 @@
 SPREAD = 2 * GRID * GRID
 DP = ("far", "near")
 VMEM = 60 << 20
-PACE = 1
 LOG2E = math.log2(math.e)
+HALF_PAD = -(-D // 256) * 128
 
 
 FIRST_DECAY = 0.9
@@ -332,6 +332,9 @@
         summed = product(powers.astype(jnp.bfloat16), value, ((1,), (0,)))
         outs.append((summed * (1.0 / total)).astype(jnp.bfloat16))
         logs.append(top + jnp.log2(total))
+    spare = out_ref.shape[1] - heads * HD
+    if spare:
+        outs.append(jnp.zeros((values.shape[0], spare), jnp.bfloat16))
     out_ref[...] = jnp.concatenate(outs, 1)
     log_ref[...] = jnp.concatenate(logs, 1)
 
@@ -348,11 +351,11 @@
             pl.BlockSpec(spread.shape, lambda step: (0, 0, 0)),
         ],
         out_specs=[
-            pl.BlockSpec((tokens, heads * HD), lambda step: (step, 0)),
+            pl.BlockSpec((tokens, HALF_PAD), lambda step: (step, 0)),
             pl.BlockSpec((tokens, heads), lambda step: (step, 0)),
         ],
         out_shape=[
-            jax.ShapeDtypeStruct((rows, heads * HD), jnp.bfloat16),
+            jax.ShapeDtypeStruct((rows, HALF_PAD), jnp.bfloat16),
             jax.ShapeDtypeStruct((rows, heads), jnp.float32),
         ],
         scratch_shapes=[pltpu.VMEM((heads, tokens, tokens), jnp.float32)],
@@ -419,7 +422,7 @@
         grid=(rows // tokens,),
         in_specs=[
             pl.BlockSpec((tokens, columns), lambda step: (step, 0)),
-            pl.BlockSpec((tokens, heads * HD), lambda step: (step, 0)),
+            pl.BlockSpec((tokens, upstream.shape[1]), lambda step: (step, 0)),
             pl.BlockSpec((tokens, heads), lambda step: (step, 0)),
             pl.BlockSpec(spread.shape, lambda step: (0, 0, 0)),
         ],
@@ -665,12 +668,14 @@
     core_ref, one_ref, two_ref, mine_ref, other_ref, hidden_ref, mod_ref, branch_ref, out_ref, in_ref
 ):
     core = core_ref[0]
-    one, two, mod = (one_ref[...], two_ref[...], mod_ref[0])
+    half = D // 2
+    one, two, mod = (one_ref[...][:, :half], two_ref[...][:, :half], mod_ref[0])
 
     def columns(ref):
-        return product(one, core_rows(ref, core, True), ((1,), (0,))) + product(
+        total = product(one, core_rows(ref, core, True), ((1,), (0,))) + product(
             two, core_rows(ref, core, False), ((1,), (0,))
         )
+        return total[:, :half]
 
     mine, other = (columns(mine_ref), columns(other_ref))
     first = jnp.where(core == 0, mine, other)
@@ -730,12 +735,14 @@
     d_other = jnp.where(core == 0, high_half, low_half).astype(low)
 
     def heads(mine):
-        return product(d_mine, core_rows(p_mine, core, mine), ((1,), (1,))) + product(
-            d_other, core_rows(p_other, core, mine), ((1,), (1,))
+        total = product(d_mine, core_rows(p_mine, core, mine)[:, :half], ((1,), (1,))) + product(
+            d_other, core_rows(p_other, core, mine)[:, :half], ((1,), (1,))
         )
-
-    d_one_ref[...] = heads(True).astype(low)
-    d_two_ref[...] = heads(False).astype(low)
+        spare = jnp.zeros((total.shape[0], HALF_PAD - half), low)
+        return jnp.concatenate([total.astype(low), spare], 1)
+
+    d_one_ref[...] = heads(True)
+    d_two_ref[...] = heads(False)
     blank = jnp.zeros((2, D), wide)
     sums = [blank, gate, row_sum(d_in), row_sum(d_in * normed), d_mod_ref[0][5:8]]
     d_mod_out_ref[0] = jnp.concatenate(sums, 0)
@@ -778,6 +785,39 @@
     parts = d_spread[:, :, : SIDE * GRID].reshape(-1, GRID, SIDE, GRID)
     total = jnp.einsum("hxey,dxy->hed", parts, shifts(), precision=HIGH)
     return total[:, ::-1, ::-1].reshape(-1, SIDE * SIDE)
+
+
+def both_columns_kernel(core_ref, here_ref, there_ref, out_ref):
+    half, wide_half = (D // 2, MLPW // 2)
+    after = QKV_PAD + wide_half
+    spans = [(part * half, half) for part in range(3)] + [(after, half)]
+    spans = spans + [(QKV_PAD, wide_half), (after + HALF_PAD, wide_half)]
+    place = 0
+    for start, width in spans:
+        here = here_ref[:, start : start + width]
+        there = there_ref[:, start : start + width]
+        first = jnp.where(core_ref[0] == 0, here, there)
+        second = jnp.where(core_ref[0] == 0, there, here)
+        out_ref[:, place : place + 2 * width] = jnp.concatenate([first, second], 1)
+        place += 2 * width
+
+
+def both_columns(here, there, core):
+    rows = here.shape[0]
+    columns = 4 * D + 2 * MLPW
+    whole = pl.BlockSpec(here.shape, lambda step, _: (0, 0))
+    return pl.pallas_call(
+        both_columns_kernel,
+        grid_spec=pltpu.PrefetchScalarGridSpec(
+            num_scalar_prefetch=1,
+            grid=(1,),
+            in_specs=[whole, whole],
+            out_specs=pl.BlockSpec((rows, columns), lambda step, _: (0, 0)),
+        ),
+        out_shape=jax.ShapeDtypeStruct((rows, columns), here.dtype),
+        compiler_params=pltpu.CompilerParams(vmem_limit_bytes=VMEM),
+        name="both_columns",
+    )(core, here, there)
 
 
 def core_half(values, core, starts, width):
@@ -889,7 +929,8 @@
     in_part, out_part = core_half(block_low, core, [4 * D, 4 * D + MLPW], wide_half)
     pad_part = jnp.zeros((block_low.shape[0], QKV_PAD - QKV_HALF), low)
     attn_part = jnp.concatenate([q_part, k_part, v_part, pad_part], 1)
-    in_part = jnp.concatenate([in_part, p_part], 1)
+    proj_spare = jnp.zeros((block_low.shape[0], HALF_PAD - half), low)
+    in_part = jnp.concatenate([in_part, p_part, proj_spare], 1)
     attn_far = gather_far(attn_part)
     small_second, small_third = gather_near(small_far)
     small = [small_far, small_second, small_third, gather_last(small_second)]
@@ -988,16 +1029,15 @@
     heads_two = swap_cores(heads_two)
     in_both = gather_last(in_second)
     heads_one, logs = attention(qkv, bias_rows)
-    heads_one, in_both, out_far = tie(heads_one, in_both, out_far)
+    heads_one, heads_two, in_both, out_far = tie(heads_one, heads_two, in_both, out_far)
     out_second, out_third = gather_near(out_far)
     in_low = place_blocks([in_far, in_second, in_third, in_both], stacked).reshape(D, -1)
-    in_low, out_second = tie(in_low, out_second)
-    proj_half = in_low[:, wide_half:]
+    proj_half = in_low[:, wide_half : wide_half + HALF_PAD]
     proj_other = swap_cores(proj_half)
     core_place = core.astype(jnp.int32).reshape(1)
     rows_wide = jax.ShapeDtypeStruct((rows, D), wide)
     rows_low = jax.ShapeDtypeStruct((rows, D), low)
-    rows_heads = jax.ShapeDtypeStruct((rows, half), low)
+    rows_heads = jax.ShapeDtypeStruct((rows, HALF_PAD), low)
     mod_shape = jax.ShapeDtypeStruct((images, 8, D), wide)
     patch_shape = jax.ShapeDtypeStruct((PDIM, D), wide)
     branch_one, hidden1, mlp_in = image_call(
@@ -1008,12 +1048,13 @@
         images,
         core=core_place,
     )
-    mlp_in, out_third = tie(mlp_in, out_third)
+    mlp_in, out_second = tie(mlp_in, out_second)
     mlp_in_two = swap_cores(mlp_in)
+    act, slope = feed_in(mlp_in, in_low, wide_half)
+    act, mlp_in_two, out_third = tie(act, mlp_in_two, out_third)
     out_both = gather_last(out_second)
-    act, slope = feed_in(mlp_in, in_low, wide_half)
-    act, mlp_in_two, out_both = tie(act, mlp_in_two, out_both)
     act_two, slope_two = feed_in(mlp_in_two, in_low, wide_half)
+    act_two, out_both = tie(act_two, out_both)
     out_low = place_blocks([out_far, out_second, out_third, out_both], stacked).reshape(D, -1)
     branch_theirs = out_of(act_two, out_low, low)
     branch_theirs = swap_cores(branch_theirs)
@@ -1083,13 +1124,18 @@
     in_second = send(add_low(in_second, in_back), plane_peers((1, 2)))
     in_third = send(in_third, plane_peers((2, 1)))
     g_proj = both_cores(
-        outer_sum(heads_one, d_branch_one), outer_sum(heads_two, d_branch_one), core, 0
-    )
-    g_proj_mine = jnp.where(core == 0, g_proj[:, :half], g_proj[:, half:])
-    g_proj_theirs = jnp.where(core == 0, g_proj[:, half:], g_proj[:, :half]).astype(low)
+        outer_sum(heads_one, d_branch_one)[:half],
+        outer_sum(heads_two, d_branch_one)[:half],
+        core,
+        0,
+    )
+    spare = ((0, 0), (0, HALF_PAD - half))
+    g_low_half, g_high_half = (jnp.pad(g_proj[:, :half], spare), jnp.pad(g_proj[:, half:], spare))
+    g_proj_mine = jnp.where(core == 0, g_low_half, g_high_half)
+    g_proj_theirs = jnp.where(core == 0, g_high_half, g_low_half).astype(low)
     g_proj = (g_proj_mine + swap_cores(g_proj_theirs).astype(wide)).astype(low)
     proj_own, proj_second, proj_third, proj_both = pick_blocks(
-        g_proj.reshape(spread, -1, half), stacked
+        g_proj.reshape(spread, -1, HALF_PAD), stacked
     )
     proj_both, d_theirs = tie(proj_both, d_theirs)
     proj_back = send(proj_both, plane_peers((2, 1)))
@@ -1176,19 +1222,10 @@
     g_there = swap_cores(g_here)
     g_mine = g_here.astype(wide)
     g_squares = segment_sums(
-        jnp.sum(g_mine * g_mine, 0), [QKV_PAD, QKV_PAD + wide_half, QKV_PAD + wide_half + half], 0
+        jnp.sum(g_mine * g_mine, 0), [QKV_PAD, QKV_PAD + wide_half, QKV_PAD + wide_half + HALF_PAD], 0
     )
     g_squares = g_squares[jnp.array([0, 2, 1, 3] + list(range(4, 11)))]
-    zero_part = jnp.where(core == 0, g_here, g_there)
-    one_part = jnp.where(core == 0, g_there, g_here)
-    after = QKV_PAD + wide_half
-    spans = [(part * half, half) for part in range(3)] + [(after, half)]
-    spans = spans + [(QKV_PAD, wide_half), (after + half, wide_half)]
-    pieces = []
-    for low_end, width in spans:
-        pieces.append(zero_part[:, low_end : low_end + width])
-        pieces.append(one_part[:, low_end : low_end + width])
-    block_grad = jnp.concatenate(pieces, 1)
+    block_grad = both_columns(g_here, g_there, core_place)
 
     packed_other = swap_cores(packed)
     rel_grad = both_cores(

time: 741 us -> 708 us (0.955)
  local copies, waits for them, and re-layouts: 74.5 us -> 55.9 us
    unnamed x202 -> x179, local copies, waits for them, and re-layouts: 13.1 us -> 19.3 us
  transfers between devices with their start and end apart: 85 -> 85, of which waited for: 33 -> 35; matrix products, arithmetic and copies ran while one was open for 17% -> 16% of each run, Pallas kernels for 36% -> 38%
where the time goes in v6:
time: 708 us; the launch traced here: 702 us
  Pallas kernels  323 us (46%)
  waiting for transfers between devices  115 us (16%)
  other arithmetic  94.5 us (13%)
  starting transfers between devices  69.5 us (10%)
  local copies, waits for them, and re-layouts  55.9 us (8%)
  matrix products  22.4 us (3%)
  between operations  21.5 us (3%)
    ppermute x60, waiting for transfers between devices, send(): return lax.ppermute(values, DP + ('mod',), peers)  111 us
    ppermute x60, starting transfers between devices, send(): return lax.ppermute(values, DP + ('mod',), peers)  65.5 us
    pallas_call x6, Pallas kernels, out_of(): pl.pallas_call(out_of_kernel, grid=(rows // tile,), in_specs=[pl.BlockSpe...  61.4 us
    pallas_call x3, Pallas kernels, weight_grad(): pl.pallas_call(weight_grad_kernel, grid_spec=pltpu.PrefetchScalarGridSpec...  50.9 us
    pallas_call x4, Pallas kernels, image_call(): pl.pallas_call(kernel, grid_spec=pltpu.PrefetchScalarGridSpec(num_scalar_...  45.8 us
    pallas_call x2, Pallas kernels, attention_back(): pl.pallas_call(functools.partial(attention_back_kernel, heads), grid=(row...  41.2 us
    pallas_call x2, Pallas kernels, attention(): pl.pallas_call(functools.partial(attention_kernel, heads), grid=(rows //...  30 us
    pallas_call x6, Pallas kernels, move_call(): pl.pallas_call(functools.partial(kernel, counts, slots), grid_spec=pltpu....  25.9 us
  transfers between devices with their start and end apart: 85, of which 35 were waited for; matrix products, arithmetic and copies ran while one was open for 16% of the time, Pallas kernels for 38%

profile of v6, /device:TPU:0, one launch (start us, length us, event | category | flops | bytes accessed | tf_op | source)
XLA Modules:
  0.0 701.8 jit_solution(7670788354571249913)
XLA Ops:
  45.1 11.8 %collective-permute-done.8 = bf16[1,72,1792]{2,1,0:T(8,128)(2,1)} collective-permute-done((bf16[1,72,1792]{2,1,0:T(8,128)(2,1)S(1)}, bf16[1,72,1792]{2,1,0:T(8,128)(2,1)}, u32[]{:S(2)}, u32[]{:S(2)}) %collective-permute-start.8) | collective-permute-done | bytes 258080 | tf_op jit(solution)/shard_map/ppermute | solution.py:106
  70.5 11.4 %collective-permute-done.10.refs_1_ = bf16[4,72,1792]{2,1,0:T(8,128)(2,1)} collective-permute-done((bf16[4,72,1792]{2,1,0:T(8,128)(2,1)S(1)}, bf16[4,72,1792]{2,1,0:T(8,128)(2,1)}, u32[]{:S(2)}, u32[]{:S(2)}) %collective-permute-start.10) | collective-permute-done | bytes 1032224 | tf_op jit(solution)/shard_map/ppermute | solution.py:106
  94.2 12.5 %collective-permute-done.14.refs_3_ = bf16[4,72,1792]{2,1,0:T(8,128)(2,1)} collective-permute-done((bf16[4,72,1792]{2,1,0:T(8,128)(2,1)}, bf16[4,72,1792]{2,1,0:T(8,128)(2,1)}, u32[]{:S(2)}, u32[]{:S(2)}) %collective-permute-start.14) | collective-permute-done | bytes 1032224 | tf_op jit(solution)/shard_map/ppermute | solution.py:106
  134.0 9.2 %into_heads.2.qkv_ref = bf16[1024,1792]{1,0:T(8,128)(2,1)} custom-call(bf16[1024,1152]{1,0:T(8,128)(2,1)} %bitcast.157, bf16[1152,1792]{1,0:T(8,128)(2,1)} %bitcast.151), custom_call_target="tpu_custom_call" | custom-call | flops 4227858432 | bytes 3670016 | tf_op jit(solution)/shard_map/into_heads/pallas_call | solution.py:533
  143.2 9.2 %into_heads.3.qkv_ref = bf16[1024,1792]{1,0:T(8,128)(2,1)} custom-call(bf16[1024,1152]{1,0:T(8,128)(2,1)} %collective-permute-done.20.values_ref.left_two, bf16[1152,1792]{1,0:T(8,128)(2,1)} %bitcast.152), custom_call_target="tpu_custom_call" | custom-call | flops 4227858432 | bytes 3670016 | tf_op jit(solution)/shard_map/into_heads/pallas_call | solution.py:533
  152.4 15.0 %attention.2 = (bf16[1024,640]{1,0:T(8,128)(2,1)}, f32[1024,8]{1,0:T(8,128)}) custom-call(bf16[1024,1792]{1,0:T(8,128)(2,1)} %into_heads.3.qkv_ref, f32[8,16,512]{2,1,0:T(8,128)} %pad.20.spread_ref), custom_call_target="tpu_custom_call" | custom-call | flops 2147483648 | bytes 7340032 | tf_op jit(solution)/shard_map/attention/pallas_call | solution.py:346
  169.6 15.0 %attention.3 = (bf16[1024,640]{1,0:T(8,128)(2,1)}, f32[1024,8]{1,0:T(8,128)}) custom-call(bf16[1024,1792]{1,0:T(8,128)(2,1)} %into_heads.2.qkv_ref, f32[8,16,512]{2,1,0:T(8,128)} %pad.20.spread_ref), custom_call_target="tpu_custom_call" | custom-call | flops 2147483648 | bytes 7340032 | tf_op jit(solution)/shard_map/attention/pallas_call | solution.py:346
  203.3 11.4 %merge_heads.1 = (bf16[1024,1152]{1,0:T(8,128)(2,1)}, f32[1024,1152]{1,0:T(8,128)}, bf16[1024,1152]{1,0:T(8,128)(2,1)}) custom-call(s32[1]{0:T(128)} %bitcast.27.core_ref, bf16[1024,640]{1,0:T(8,128)(2,1)} %get-tuple-element.176.one_ref, bf16[1024,640]{1,0:T(8,128)(2,1)} %copy-done.30, bf16[1152,640]{1,0:T(8,128)(2,1)} %copy-done.11, ...), custom_call_target="tpu_custom_call" | custom-call | flops 5435817984 | bytes 18874368 | tf_op jit(solution)/shard_map/merge_heads/pallas_call | solution.py:642
  219.1 12.2 %feed_in.2 = (bf16[1024,2304]{1,0:T(8,128)(2,1)}, bf16[1024,2304]{1,0:T(8,128)(2,1)}) custom-call(bf16[1024,1152]{1,0:T(8,128)(2,1)} %get-tuple-element.183.values_ref.left_one, bf16[1152,2944]{1,0:T(8,128)(2,1)} %bitcast.141), custom_call_target="tpu_custom_call" | custom-call | flops 5435817984 | bytes 9437184 | tf_op jit(solution)/shard_map/feed_in/pallas_call | solution.py:473
  235.1 12.7 %feed_in.3 = (bf16[1024,2304]{1,0:T(8,128)(2,1)}, bf16[1024,2304]{1,0:T(8,128)(2,1)}) custom-call(bf16[1024,1152]{1,0:T(8,128)(2,1)} %collective-permute-done.27.values_ref.left_two, bf16[1152,2944]{1,0:T(8,128)(2,1)} %bitcast.142), custom_call_target="tpu_custom_call" | custom-call | flops 5435817984 | bytes 9437184 | tf_op jit(solution)/shard_map/feed_in/pallas_call | solution.py:473
  256.0 10.7 %out_of.7 = bf16[1024,1152]{1,0:T(8,128)(2,1)} custom-call(bf16[1024,2304]{1,0:T(8,128)(2,1)} %get-tuple-element.191.values_ref.right_two, bf16[1152,2304]{1,0:T(8,128)(2,1)} %bitcast.146), custom_call_target="tpu_custom_call" | custom-call | flops 5435817984 | bytes 4718592 | tf_op jit(solution)/shard_map/out_of/pallas_call | solution.py:555
  268.5 10.8 %out_of.6.mine_ref = f32[1024,1152]{1,0:T(8,128)} custom-call(bf16[1024,2304]{1,0:T(8,128)(2,1)} %get-tuple-element.186.values_ref.right_one, bf16[1152,2304]{1,0:T(8,128)(2,1)} %bitcast.147), custom_call_target="tpu_custom_call" | custom-call | flops 5435817984 | bytes 4718592 | tf_op jit(solution)/shard_map/out_of/pallas_call | solution.py:555
  280.7 10.6 %ends.1 = (f32[1024,1152]{1,0:T(8,128)}, bf16[1024,1152]{1,0:T(8,128)(2,1)}, f32[4,8,1152]{2,1,0:T(8,128)}, f32[16,1152]{1,0:T(8,128)}, f32[8,128]{1,0:T(8,128)}) custom-call(f32[1024,1152]{1,0:T(8,128)} %out_of.6.mine_ref, bf16[1024,1152]{1,0:T(8,128)(2,1)} %copy-done.21, f32[1024,1152]{1,0:T(8,128)} %get-tuple-element.192.hidden_ref, ...), custom_call_target="tpu_custom_call" | custom-call | flops 75497472 | bytes 18874368 | tf_op jit(solution)/shard_map/ends/pallas_call | solution.py:642
  291.9 11.0 %feed_back.2.values_ref.right_one = bf16[1024,2304]{1,0:T(8,128)(2,1)} custom-call(bf16[1024,1152]{1,0:T(8,128)(2,1)} %get-tuple-element.193.values_ref.left_one, bf16[1152,2304]{1,0:T(8,128)(2,1)} %bitcast.148, bf16[1024,2304]{1,0:T(8,128)(2,1)} %get-tuple-element.194.slope_ref), custom_call_target="tpu_custom_call" | custom-call | flops 5435817984 | bytes 9437184 | tf_op jit(solution)/shard_map/feed_back/pallas_call | solution.py:501
  304.3 17.9 %weight_grad.3 = (bf16[4,72,2304]{2,1,0:T(8,128)(2,1)}, bf16[4,72,2304]{2,1,0:T(8,128)(2,1)}, bf16[4,72,2304]{2,1,0:T(8,128)(2,1)}, bf16[4,72,2304]{2,1,0:T(8,128)(2,1)}) custom-call(s32[16]{0:T(128)} %xor.69.places, bf16[1024,1152]{1,0:T(8,128)(2,1)} %get-tuple-element.193.values_ref.left_one, bf16[1024,1152]{1,0:T(8,128)(2,1)} %copy-done.79, ...), custom_call_target="tpu_custom_call" | custom-call | flops 10871635968 | bytes 10616832 | tf_op jit(solution)/shard_map/weight_grad/pallas_call | solution.py:594
  323.3 10.8 %feed_back.3.right_two.values_ref = bf16[1024,2304]{1,0:T(8,128)(2,1)} custom-call(bf16[1024,1152]{1,0:T(8,128)(2,1)} %copy-done.79, bf16[1152,2304]{1,0:T(8,128)(2,1)} %bitcast.149, bf16[1024,2304]{1,0:T(8,128)(2,1)} %get-tuple-element.201.slope_ref), custom_call_target="tpu_custom_call" | custom-call | flops 5435817984 | bytes 9437184 | tf_op jit(solution)/shard_map/feed_back/pallas_call | solution.py:501
  334.1 10.6 %out_of.9 = bf16[1024,1152]{1,0:T(8,128)(2,1)} custom-call(bf16[1024,2304]{1,0:T(8,128)(2,1)} %feed_back.3.right_two.values_ref, bf16[1152,2944]{1,0:T(8,128)(2,1)} %bitcast.143), custom_call_target="tpu_custom_call" | custom-call | flops 5435817984 | bytes 4718592 | tf_op jit(solution)/shard_map/out_of/pallas_call | solution.py:555
  346.1 10.9 %out_of.8.mine_ref = f32[1024,1152]{1,0:T(8,128)} custom-call(bf16[1024,2304]{1,0:T(8,128)(2,1)} %feed_back.2.values_ref.right_one, bf16[1152,2944]{1,0:T(8,128)(2,1)} %bitcast.144), custom_call_target="tpu_custom_call" | custom-call | flops 5435817984 | bytes 4718592 | tf_op jit(solution)/shard_map/out_of/pallas_call | solution.py:555
  360.9 18.0 %weight_grad.4 = (bf16[4,72,2304]{2,1,0:T(8,128)(2,1)}, bf16[4,72,2304]{2,1,0:T(8,128)(2,1)}, bf16[4,72,2304]{2,1,0:T(8,128)(2,1)}, bf16[4,72,2304]{2,1,0:T(8,128)(2,1)}) custom-call(s32[16]{0:T(128)} %xor.69.places, bf16[1024,1152]{1,0:T(8,128)(2,1)} %get-tuple-element.183.values_ref.left_one, ...), custom_call_target="tpu_custom_call" | custom-call | flops 10871635968 | bytes 10616832 | tf_op jit(solution)/shard_map/weight_grad/pallas_call | solution.py:594
  380.3 15.1 %merge_heads_back.1 = (f32[1024,1152]{1,0:T(8,128)}, bf16[1024,1152]{1,0:T(8,128)(2,1)}, bf16[1024,640]{1,0:T(8,128)(2,1)}, bf16[1024,640]{1,0:T(8,128)(2,1)}, f32[4,8,1152]{2,1,0:T(8,128)}) custom-call(s32[1]{0:T(128)} %bitcast.27.core_ref, f32[1024,1152]{1,0:T(8,128)} %out_of.8.mine_ref, bf16[1024,1152]{1,0:T(8,128)(2,1)} %copy-done.19, ...), custom_call_target="tpu_custom_call" | custom-call | flops 5435817984 | bytes 18874368 | tf_op jit(solution)/shard_map/merge_heads_back/pallas_call | solution.py:642
  398.2 20.6 %attention_back.2 = (bf16[1024,1792]{1,0:T(8,128)(2,1)}, f32[8,16,512]{2,1,0:T(8,128)}) custom-call(bf16[1024,1792]{1,0:T(8,128)(2,1)} %into_heads.2.qkv_ref, bf16[1024,640]{1,0:T(8,128)(2,1)} %get-tuple-element.215.upstream_ref, f32[1024,8]{1,0:T(8,128)} %get-tuple-element.216.log_ref, f32[8,16,512]{2,1,0:T(8,128)} %pad.20.spread_ref), custom_call_target="tpu_custom_call" | custom-call | flops 5368709120 | bytes 11010048 | tf_op jit(solution)/shard_map/attention_back/pallas_call | solution.py:420
  443.0 20.6 %attention_back.3 = (bf16[1024,1792]{1,0:T(8,128)(2,1)}, f32[8,16,512]{2,1,0:T(8,128)}) custom-call(bf16[1024,1792]{1,0:T(8,128)(2,1)} %into_heads.3.qkv_ref, bf16[1024,640]{1,0:T(8,128)(2,1)} %collective-permute-done.36.upstream_ref, f32[1024,8]{1,0:T(8,128)} %get-tuple-element.227.log_ref, f32[8,16,512]{2,1,0:T(8,128)} %pad.20.spread_ref), custom_call_target="tpu_custom_call" | custom-call | flops 5368709120 | bytes 11010048 | tf_op jit(solution)/shard_map/attention_back/pallas_call | solution.py:420
  474.5 14.9 %weight_grad.5 = (bf16[4,72,1792]{2,1,0:T(8,128)(2,1)}, bf16[4,72,1792]{2,1,0:T(8,128)(2,1)}, bf16[4,72,1792]{2,1,0:T(8,128)(2,1)}, bf16[4,72,1792]{2,1,0:T(8,128)(2,1)}) custom-call(s32[16]{0:T(128)} %xor.69.places, bf16[1024,1152]{1,0:T(8,128)(2,1)} %bitcast.158, bf16[1024,1152]{1,0:T(8,128)(2,1)} %collective-permute-done.20.values_ref.left_two, ...), custom_call_target="tpu_custom_call" | custom-call | flops 8455716864 | bytes 8257536 | tf_op jit(solution)/shard_map/weight_grad/pallas_call | solution.py:594
  513.5 9.4 %out_of.11.mine_ref = f32[1024,1152]{1,0:T(8,128)} custom-call(bf16[1024,1792]{1,0:T(8,128)(2,1)} %get-tuple-element.249.right_one.values_ref, bf16[1152,1792]{1,0:T(8,128)(2,1)} %bitcast.154), custom_call_target="tpu_custom_call" | custom-call | flops 4227858432 | bytes 4718592 | tf_op jit(solution)/shard_map/out_of/pallas_call | solution.py:555
  (558 shorter events, 367.8 us)
Async XLA Ops:
  7.2 99.5 %all-gather.5.cloned.1.call-start = ((), (), s32[]{:S(2)}) async-start(), calls=%async_computation.7 | async-start | bytes 2119680 | tf_op jit(solution)/shard_map/all_gather | solution.py:253
  35.0 21.9 %collective-permute-start.8 = (bf16[1,72,1792]{2,1,0:T(8,128)(2,1)S(1)}, bf16[1,72,1792]{2,1,0:T(8,128)(2,1)}, u32[]{:S(2)}, u32[]{:S(2)}) collective-permute-start(bf16[1,72,1792]{2,1,0:T(8,128)(2,1)S(1)} %bitcast.165), channel_id=1, source_target_pairs={{0,16},{1,17},{2,18},{3,19},{4,20},{5,21},{6,22},{7,23},{8,24},{9,... | collective-permute-start | bytes 774152 | tf_op jit(solution)/shard_map/ppermute | solution.py:106
  35.0 21.9 %collective-permute-start.7 = (bf16[1,72,1792]{2,1,0:T(8,128)(2,1)S(1)}, bf16[1,72,1792]{2,1,0:T(8,128)(2,1)}, u32[]{:S(2)}, u32[]{:S(2)}) collective-permute-start(bf16[1,72,1792]{2,1,0:T(8,128)(2,1)S(1)} %bitcast.166), channel_id=1, source_target_pairs={{0,8},{1,9},{2,10},{3,11},{4,12},{5,13},{6,14},{7,15},{8,0},{9,1},... | collective-permute-start | bytes 774152 | tf_op jit(solution)/shard_map/ppermute | solution.py:106
  58.3 23.7 %collective-permute-start.10 = (bf16[4,72,1792]{2,1,0:T(8,128)(2,1)S(1)}, bf16[4,72,1792]{2,1,0:T(8,128)(2,1)}, u32[]{:S(2)}, u32[]{:S(2)}) collective-permute-start(bf16[4,72,1792]{2,1,0:T(8,128)(2,1)S(1)} %pad_maximum_fusion.refs_0_), channel_id=1, source_target_pairs={{0,2},{1,5},{2,0},{3,7},{4,6},{5,1},{6,4},{7,3},{8,10},{9,13},{10,... | collective-permute-start | bytes 3096584 | tf_op jit(solution)/shard_map/ppermute | solution.py:106
  58.9 23.1 %collective-permute-start.11 = (bf16[4,72,1792]{2,1,0:T(8,128)(2,1)S(1)}, bf16[4,72,1792]{2,1,0:T(8,128)(2,1)}, u32[]{:S(2)}, u32[]{:S(2)}) collective-permute-start(bf16[4,72,1792]{2,1,0:T(8,128)(2,1)S(1)} %pad_maximum_fusion.refs_0_), channel_id=1, source_target_pairs={{0,4},{1,3},{2,6},{3,1},{4,0},{5,7},{6,2},{7,5},{8,12},{9,11},{10,... | collective-permute-start | bytes 3096584 | tf_op jit(solution)/shard_map/ppermute | solution.py:106
  59.4 108.4 %all-gather.7.cloned.1.call-start = ((), (), s32[]{:S(2)}) async-start(), calls=%async_computation.8 | async-start | bytes 1658880 | tf_op jit(solution)/shard_map/all_gather | solution.py:253
  127.6 344.6 %reduce-scatter.7.cloned.1.call-start = ((), (), s32[]{:S(2)}) async-start(), calls=%async_computation.4 | async-start | bytes 1658880 | tf_op jit(solution)/shard_map/reduce_scatter | solution.py:257
  127.9 39.9 %collective-permute-start.21 = (bf16[4,72,2944]{2,1,0:T(8,128)(2,1)}, bf16[4,72,2944]{2,1,0:T(8,128)(2,1)}, u32[]{:S(2)}, u32[]{:S(2)}) collective-permute-start(bf16[4,72,2944]{2,1,0:T(8,128)(2,1)} %bitcast.160), channel_id=1, source_target_pairs={{0,2},{1,5},{2,0},{3,7},{4,6},{5,1},{6,4},{7,3},{8,10},{9,13},{10,... | collective-permute-start | bytes 5087240 | tf_op jit(solution)/shard_map/ppermute | solution.py:106
  128.4 39.4 %collective-permute-start.22 = (bf16[4,72,2944]{2,1,0:T(8,128)(2,1)}, bf16[4,72,2944]{2,1,0:T(8,128)(2,1)}, u32[]{:S(2)}, u32[]{:S(2)}) collective-permute-start(bf16[4,72,2944]{2,1,0:T(8,128)(2,1)} %bitcast.161), channel_id=1, source_target_pairs={{0,4},{1,3},{2,6},{3,1},{4,0},{5,7},{6,2},{7,5},{8,12},{9,11},{10,... | collective-permute-start | bytes 5087240 | tf_op jit(solution)/shard_map/ppermute | solution.py:106
  167.8 21.9 %collective-permute-start.24 = (bf16[4,72,2944]{2,1,0:T(8,128)(2,1)}, bf16[4,72,2944]{2,1,0:T(8,128)(2,1)S(1)}, u32[]{:S(2)}, u32[]{:S(2)}) collective-permute-start(bf16[4,72,2944]{2,1,0:T(8,128)(2,1)} %collective-permute-done.21.refs_1_), channel_id=1, source_target_pairs={{0,4},{1,3},{2,6},{3,1},{4,0},{5,7},{6,2},{7,5},{8,12},{9,11},{10,... | collective-permute-start | bytes 5087240 | tf_op jit(solution)/shard_map/ppermute | solution.py:106
  218.1 31.2 %collective-permute-start.29 = (bf16[4,72,2304]{2,1,0:T(8,128)(2,1)}, bf16[4,72,2304]{2,1,0:T(8,128)(2,1)S(1)}, u32[]{:S(2)}, u32[]{:S(2)}) collective-permute-start(bf16[4,72,2304]{2,1,0:T(8,128)(2,1)} %collective-permute-done.26.refs_1_), channel_id=1, source_target_pairs={{0,4},{1,3},{2,6},{3,1},{4,0},{5,7},{6,2},{7,5},{8,12},{9,11},{10,... | collective-permute-start | bytes 3981320 | tf_op jit(solution)/shard_map/ppermute | solution.py:106
  322.2 34.8 %collective-permute-start.32 = (bf16[4,72,2304]{2,1,0:T(8,128)(2,1)}, bf16[4,72,2304]{2,1,0:T(8,128)(2,1)}, u32[]{:S(2)}, u32[]{:S(2)}) collective-permute-start(bf16[4,72,2304]{2,1,0:T(8,128)(2,1)} %get-tuple-element.199), channel_id=1, source_target_pairs={{0,4},{1,3},{2,6},{3,1},{4,0},{5,7},{6,2},{7,5},{8,12},{9,11},{10,... | collective-permute-start | bytes 3981320 | tf_op jit(solution)/shard_map/ppermute | solution.py:106
  344.7 34.1 %collective-permute-start.33 = (bf16[1024,1152]{1,0:T(8,128)(2,1)}, bf16[1024,1152]{1,0:T(8,128)(2,1)S(1)}, u32[]{:S(2)}, u32[]{:S(2)}) collective-permute-start(bf16[1024,1152]{1,0:T(8,128)(2,1)} %out_of.9), channel_id=1, source_target_pairs={{0,1},{1,0},{2,3},{3,2},{4,5},{5,4},{6,7},{7,6},{8,9},{9,8},{10,11... | collective-permute-start | bytes 7077896 | tf_op jit(solution)/shard_map/ppermute | solution.py:110
  344.7 50.7 %collective-permute-start.35 = (bf16[4,72,2304]{2,1,0:T(8,128)(2,1)}, bf16[4,72,2304]{2,1,0:T(8,128)(2,1)S(1)}, u32[]{:S(2)}, u32[]{:S(2)}) collective-permute-start(bf16[4,72,2304]{2,1,0:T(8,128)(2,1)} %get-tuple-element.213), channel_id=1, source_target_pairs={{0,4},{1,3},{2,6},{3,1},{4,0},{5,7},{6,2},{7,5},{8,12},{9,11},{10,... | collective-permute-start | bytes 3981320 | tf_op jit(solution)/shard_map/ppermute | solution.py:106
  360.1 35.3 %collective-permute-start.34 = (bf16[4,72,2304]{2,1,0:T(8,128)(2,1)}, bf16[4,72,2304]{2,1,0:T(8,128)(2,1)}, u32[]{:S(2)}, u32[]{:S(2)}) collective-permute-start(bf16[4,72,2304]{2,1,0:T(8,128)(2,1)} %add_convert_fusion.7), channel_id=1, source_target_pairs={{0,2},{1,5},{2,0},{3,7},{4,6},{5,1},{6,4},{7,3},{8,10},{9,13},{10,... | collective-permute-start | bytes 3981320 | tf_op jit(solution)/shard_map/ppermute | solution.py:106
  395.4 23.4 %collective-permute-start.37 = (bf16[4,72,2304]{2,1,0:T(8,128)(2,1)}, bf16[4,72,2304]{2,1,0:T(8,128)(2,1)}, u32[]{:S(2)}, u32[]{:S(2)}) collective-permute-start(bf16[4,72,2304]{2,1,0:T(8,128)(2,1)} %get-tuple-element.220), channel_id=1, source_target_pairs={{0,4},{1,3},{2,6},{3,1},{4,0},{5,7},{6,2},{7,5},{8,12},{9,11},{10,... | collective-permute-start | bytes 3981320 | tf_op jit(solution)/shard_map/ppermute | solution.py:106
  430.2 94.5 %reduce-scatter.9.cloned.1.call-start = ((), (), s32[]{:S(2)}) async-start(), calls=%async_computation.5 | async-start | bytes 1658880 | tf_op jit(solution)/shard_map/reduce_scatter | solution.py:257
  433.4 38.8 %collective-permute-start.39 = (bf16[4,72,2304]{2,1,0:T(8,128)(2,1)}, bf16[4,72,2304]{2,1,0:T(8,128)(2,1)}, u32[]{:S(2)}, u32[]{:S(2)}) collective-permute-start(bf16[4,72,2304]{2,1,0:T(8,128)(2,1)} %add_convert_fusion.6), channel_id=1, source_target_pairs={{0,2},{1,5},{2,0},{3,7},{4,6},{5,1},{6,4},{7,3},{8,10},{9,13},{10,... | collective-permute-start | bytes 3981320 | tf_op jit(solution)/shard_map/ppermute | solution.py:106
  433.8 38.4 %collective-permute-start.40 = (bf16[4,72,2304]{2,1,0:T(8,128)(2,1)}, bf16[4,72,2304]{2,1,0:T(8,128)(2,1)}, u32[]{:S(2)}, u32[]{:S(2)}) collective-permute-start(bf16[4,72,2304]{2,1,0:T(8,128)(2,1)} %get-tuple-element.231), channel_id=1, source_target_pairs={{0,4},{1,3},{2,6},{3,1},{4,0},{5,7},{6,2},{7,5},{8,12},{9,11},{10,... | collective-permute-start | bytes 3981320 | tf_op jit(solution)/shard_map/ppermute | solution.py:106
  442.1 30.1 %collective-permute-start.41 = (bf16[4,72,640]{2,1,0:T(8,128)(2,1)}, bf16[4,72,640]{2,1,0:T(8,128)(2,1)S(1)}, u32[]{:S(2)}, u32[]{:S(2)}) collective-permute-start(bf16[4,72,640]{2,1,0:T(8,128)(2,1)} %get-tuple-element.232), channel_id=1, source_target_pairs={{0,4},{1,3},{2,6},{3,1},{4,0},{5,7},{6,2},{7,5},{8,12},{9,11},{10,... | collective-permute-start | bytes 1105928 | tf_op jit(solution)/shard_map/ppermute | solution.py:106
  494.3 110.4 %reduce-scatter.13.cloned.1.call-start = ((), (), s32[]{:S(2)}) async-start(), calls=%async_computation.9 | async-start | bytes 460800
  509.0 30.3 %collective-permute-start.51 = (bf16[4,72,1792]{2,1,0:T(8,128)(2,1)}, bf16[4,72,1792]{2,1,0:T(8,128)(2,1)}, u32[]{:S(2)}, u32[]{:S(2)}) collective-permute-start(bf16[4,72,1792]{2,1,0:T(8,128)(2,1)} %get-tuple-element.261), channel_id=1, source_target_pairs={{0,4},{1,3},{2,6},{3,1},{4,0},{5,7},{6,2},{7,5},{8,12},{9,11},{10,... | collective-permute-start | bytes 3096584 | tf_op jit(solution)/shard_map/ppermute | solution.py:106
  552.2 52.6 %reduce-scatter.11.cloned.1.call-start = ((), (), s32[]{:S(2)}) async-start(), calls=%async_computation.6 | async-start | bytes 1290240 | tf_op jit(solution)/shard_map/reduce_scatter | solution.py:257
  561.3 60.0 %collective-permute-start.53 = (f32[7689]{0:T(1024)}, f32[7689]{0:T(1024)}, u32[]{:S(2)}, u32[]{:S(2)}) collective-permute-start(f32[7689]{0:T(1024)} %add.509), channel_id=1, source_target_pairs={{0,1},{1,0},{2,3},{3,2},{4,5},{5,4},{6,7},{7,6},{8,9},{9,8},{10,11... | collective-permute-start | bytes 92276 | tf_op jit(solution)/shard_map/ppermute | solution.py:110
  (145 other events, 1535.0 us)
Sparse Core Ops, SparseCore 0:
  59.5 37.9 all-gather.4
  127.7 30.7 all-gather.6
  430.4 30.3 reduce-scatter.6
  494.5 30.2 reduce-scatter.8
  552.3 18.2 reduce-scatter.12
  573.4 25.5 reduce-scatter.10

commit v7 on v6

--- a/solution.py
+++ b/solution.py
@@ -787,15 +787,15 @@
     return total[:, ::-1, ::-1].reshape(-1, SIDE * SIDE)
 
 
-def both_columns_kernel(core_ref, here_ref, there_ref, out_ref):
+def both_columns_kernel(core_ref, *refs):
+    here_refs, there_refs, out_ref = (refs[:4], refs[4:8], refs[8])
     half, wide_half = (D // 2, MLPW // 2)
-    after = QKV_PAD + wide_half
-    spans = [(part * half, half) for part in range(3)] + [(after, half)]
-    spans = spans + [(QKV_PAD, wide_half), (after + HALF_PAD, wide_half)]
+    spans = [(0, part * half, half) for part in range(3)] + [(2, 0, half)]
+    spans = spans + [(1, 0, wide_half), (3, 0, wide_half)]
     place = 0
-    for start, width in spans:
-        here = here_ref[:, start : start + width]
-        there = there_ref[:, start : start + width]
+    for piece, start, width in spans:
+        here = here_refs[piece][:, start : start + width]
+        there = there_refs[piece][:, start : start + width]
         first = jnp.where(core_ref[0] == 0, here, there)
         second = jnp.where(core_ref[0] == 0, there, here)
         out_ref[:, place : place + 2 * width] = jnp.concatenate([first, second], 1)
@@ -803,21 +803,20 @@
 
 
 def both_columns(here, there, core):
-    rows = here.shape[0]
+    rows = here[0].shape[0]
     columns = 4 * D + 2 * MLPW
-    whole = pl.BlockSpec(here.shape, lambda step, _: (0, 0))
     return pl.pallas_call(
         both_columns_kernel,
         grid_spec=pltpu.PrefetchScalarGridSpec(
             num_scalar_prefetch=1,
             grid=(1,),
-            in_specs=[whole, whole],
+            in_specs=[pl.BlockSpec(item.shape, lambda step, _: (0, 0)) for item in here + there],
             out_specs=pl.BlockSpec((rows, columns), lambda step, _: (0, 0)),
         ),
-        out_shape=jax.ShapeDtypeStruct((rows, columns), here.dtype),
+        out_shape=jax.ShapeDtypeStruct((rows, columns), here[0].dtype),
         compiler_params=pltpu.CompilerParams(vmem_limit_bytes=VMEM),
         name="both_columns",
-    )(core, here, there)
+    )(core, *here, *there)
 
 
 def core_half(values, core, starts, width):
@@ -934,8 +933,8 @@
     attn_far = gather_far(attn_part)
     small_second, small_third = gather_near(small_far)
     small = [small_far, small_second, small_third, gather_last(small_second)]
-    later_weights, later_bias, later_embed, small[0] = tie(
-        block_weights, rel_bias, embed_weights, small[0]
+    later_weights, later_bias, later_embed, later_mod, small[0] = tie(
+        block_weights, rel_bias, embed_weights, mod_weights, small[0]
     )
     table = later_embed[:start].astype(low)
     time_out = later_embed[start + FREQ : start + FREQ + D].astype(low).astype(wide)
@@ -966,7 +965,7 @@
     sorted_sinus = sort_images(sinus)
     sorted_act = sort_images(time_act)
     classes = jnp.arange(start, dtype=jnp.int32)[None, :]
-    sorted_onehot = sort_images(all_chosen[:, None].astype(wide)).astype(jnp.int32) == classes
+    sorted_class = sort_images(all_chosen[:, None].astype(wide)).astype(jnp.int32)
     first_column = lax.axis_index(DP) * share
     sorted_slope = sort_images(
         silu_slope(lax.dynamic_slice_in_dim(pre_time, first_column, share, 1))
@@ -983,9 +982,31 @@
     mod_parts = jnp.split(mod_partial.reshape(spread, 2 * images, -1), 4)
     heads = HEADS // 2
     bias_rows = spread_bias(jnp.where(core == 0, later_bias[:heads], later_bias[heads:]))
-    block_weight_squares = block_squares(later_weights)
-    half_mod, in_far, attn_both, bias_rows, block_weight_squares = scatter_parts(
-        *mod_parts, meanwhile=(in_far, attn_both, bias_rows, block_weight_squares)
+    first_core = (core == 0).astype(wide)
+    weight_squares = first_core * (block_squares(later_weights) + embed_squares(later_embed))
+    weight_squares = weight_squares + mod_squares(later_mod, core)
+    (
+        half_mod,
+        in_far,
+        attn_both,
+        bias_rows,
+        weight_squares,
+        sorted_act,
+        sorted_sinus,
+        sorted_slope,
+        sorted_class,
+    ) = scatter_parts(
+        *mod_parts,
+        meanwhile=(
+            in_far,
+            attn_both,
+            bias_rows,
+            weight_squares,
+            sorted_act,
+            sorted_sinus,
+            sorted_slope,
+            sorted_class,
+        ),
     )
     qkv_low = place_blocks([attn_far, attn_second, attn_third, attn_both], relative).reshape(D, -1)
     in_second, in_third = gather_near(in_far)
@@ -1203,7 +1224,7 @@
     theirs = jnp.split(swap_cores(d_scaled), 4)
     d_scaled = d_scaled + jnp.concatenate([theirs[0], theirs[2], theirs[1], theirs[3]], 0)
     d_cond = sort_images(d_scaled * silu_slope(cond))
-    g_table = first_contract(sorted_onehot.astype(wide), d_cond)
+    g_table = first_contract((sorted_class == classes).astype(wide), d_cond)
     g_time_out = first_contract(sorted_act, d_cond)
     d_time = lax.dot_general(
         d_cond, time_out, (((1,), (1,)), ((), ())), precision=HIGH, preferred_element_type=wide
@@ -1218,13 +1239,12 @@
     g_time_in = first_contract(sorted_sinus, d_time_here * sorted_slope)
     embed_grad = jnp.concatenate([g_table, g_time_in, g_time_out, g_ends], 0)
 
-    g_here = jnp.concatenate([g_qkv, g_in, g_proj, g_out], 1)
-    g_there = swap_cores(g_here)
-    g_mine = g_here.astype(wide)
-    g_squares = segment_sums(
-        jnp.sum(g_mine * g_mine, 0), [QKV_PAD, QKV_PAD + wide_half, QKV_PAD + wide_half + HALF_PAD], 0
-    )
-    g_squares = g_squares[jnp.array([0, 2, 1, 3] + list(range(4, 11)))]
+    g_here = [g_qkv, g_in, g_proj, g_out]
+    g_there = [swap_cores(piece) for piece in g_here]
+    g_squares = sum(
+        jnp.where(jnp.arange(11) == matrix, jnp.sum(piece.astype(wide) ** 2), 0.0)
+        for matrix, piece in zip((0, 2, 1, 3), g_here)
+    )
     block_grad = both_columns(g_here, g_there, core_place)
 
     packed_other = swap_cores(packed)
@@ -1241,7 +1261,7 @@
     squares = jnp.concatenate(
         [
             g_squares + mod_squares(mod_grad, core) + first_core * embed_squares(embed_grad),
-            replica_squares(block_weight_squares, mod_weights, embed_weights),
+            weight_squares,
         ]
     )
     squares, block_grad, rel_grad = all_sum(squares, (block_grad, rel_grad))

time: 708 us -> 704 us (level)
  waiting for transfers between devices: 115 us -> 104 us
  starting transfers between devices: 69.5 us -> 76.7 us
    ppermute x60, waiting for transfers between devices: 111 us -> 95.1 us  [send(): return lax.ppermute(values, DP + ('mod',), peers)]
    unnamed x179 -> x204, local copies, waits for them, and re-layouts: 19.3 us -> 14.7 us
  transfers between devices with their start and end apart: 85 -> 88, of which waited for: 35 -> 38; matrix products, arithmetic and copies ran while one was open for 16% -> 16% of each run, Pallas kernels for 38% -> 39%
where the time goes in v7:
time: 704 us; the launch traced here: 697 us
  Pallas kernels  323 us (46%)
  waiting for transfers between devices  104 us (15%)
  other arithmetic  98.2 us (14%)
  starting transfers between devices  76.7 us (11%)
  local copies, waits for them, and re-layouts  51.1 us (7%)
  between operations  21.9 us (3%)
  matrix products  21.1 us (3%)
    ppermute x60, waiting for transfers between devices, send(): return lax.ppermute(values, DP + ('mod',), peers)  95.1 us
    ppermute x60, starting transfers between devices, send(): return lax.ppermute(values, DP + ('mod',), peers)  72.4 us
    pallas_call x6, Pallas kernels, out_of(): pl.pallas_call(out_of_kernel, grid=(rows // tile,), in_specs=[pl.BlockSpe...  61.5 us
    pallas_call x3, Pallas kernels, weight_grad(): pl.pallas_call(weight_grad_kernel, grid_spec=pltpu.PrefetchScalarGridSpec...  50.9 us
    pallas_call x4, Pallas kernels, image_call(): pl.pallas_call(kernel, grid_spec=pltpu.PrefetchScalarGridSpec(num_scalar_...  45.5 us
    pallas_call x2, Pallas kernels, attention_back(): pl.pallas_call(functools.partial(attention_back_kernel, heads), grid=(row...  41.2 us
    pallas_call x2, Pallas kernels, attention(): pl.pallas_call(functools.partial(attention_kernel, heads), grid=(rows //...  30 us
    pallas_call x6, Pallas kernels, move_call(): pl.pallas_call(functools.partial(kernel, counts, slots), grid_spec=pltpu....  25.9 us
  transfers between devices with their start and end apart: 88, of which 38 were waited for; matrix products, arithmetic and copies ran while one was open for 16% of the time, Pallas kernels for 39%

profile of v7, /device:TPU:0, one launch (start us, length us, event | category | flops | bytes accessed | tf_op | source)
XLA Modules:
  0.0 696.7 jit_solution(4145181188536176007)
XLA Ops:
  96.8 11.7 %collective-permute-done.14.refs_3_ = bf16[4,72,1792]{2,1,0:T(8,128)(2,1)} collective-permute-done((bf16[4,72,1792]{2,1,0:T(8,128)(2,1)}, bf16[4,72,1792]{2,1,0:T(8,128)(2,1)}, u32[]{:S(2)}, u32[]{:S(2)}) %collective-permute-start.14) | collective-permute-done | bytes 1032224 | tf_op jit(solution)/shard_map/ppermute | solution.py:106
  138.0 9.2 %into_heads.2.qkv_ref = bf16[1024,1792]{1,0:T(8,128)(2,1)} custom-call(bf16[1024,1152]{1,0:T(8,128)(2,1)} %bitcast.161, bf16[1152,1792]{1,0:T(8,128)(2,1)} %bitcast.155), custom_call_target="tpu_custom_call" | custom-call | flops 4227858432 | bytes 3670016 | tf_op jit(solution)/shard_map/into_heads/pallas_call | solution.py:533
  147.2 9.2 %into_heads.3.qkv_ref = bf16[1024,1792]{1,0:T(8,128)(2,1)} custom-call(bf16[1024,1152]{1,0:T(8,128)(2,1)} %collective-permute-done.20.values_ref.left_two, bf16[1152,1792]{1,0:T(8,128)(2,1)} %bitcast.156), custom_call_target="tpu_custom_call" | custom-call | flops 4227858432 | bytes 3670016 | tf_op jit(solution)/shard_map/into_heads/pallas_call | solution.py:533
  156.4 15.0 %attention.2 = (bf16[1024,640]{1,0:T(8,128)(2,1)}, f32[1024,8]{1,0:T(8,128)}) custom-call(bf16[1024,1792]{1,0:T(8,128)(2,1)} %into_heads.3.qkv_ref, f32[8,16,512]{2,1,0:T(8,128)} %pad.20.spread_ref), custom_call_target="tpu_custom_call" | custom-call | flops 2147483648 | bytes 7340032 | tf_op jit(solution)/shard_map/attention/pallas_call | solution.py:346
  173.6 15.0 %attention.3 = (bf16[1024,640]{1,0:T(8,128)(2,1)}, f32[1024,8]{1,0:T(8,128)}) custom-call(bf16[1024,1792]{1,0:T(8,128)(2,1)} %into_heads.2.qkv_ref, f32[8,16,512]{2,1,0:T(8,128)} %pad.20.spread_ref), custom_call_target="tpu_custom_call" | custom-call | flops 2147483648 | bytes 7340032 | tf_op jit(solution)/shard_map/attention/pallas_call | solution.py:346
  207.0 11.2 %merge_heads.1 = (bf16[1024,1152]{1,0:T(8,128)(2,1)}, f32[1024,1152]{1,0:T(8,128)}, bf16[1024,1152]{1,0:T(8,128)(2,1)}) custom-call(s32[1]{0:T(128)} %bitcast.29.core_ref, bf16[1024,640]{1,0:T(8,128)(2,1)} %get-tuple-element.182.one_ref, bf16[1024,640]{1,0:T(8,128)(2,1)} %copy-done.30, bf16[1152,640]{1,0:T(8,128)(2,1)} %copy-done.11, ...), custom_call_target="tpu_custom_call" | custom-call | flops 5435817984 | bytes 18874368 | tf_op jit(solution)/shard_map/merge_heads/pallas_call | solution.py:642
  222.8 12.2 %feed_in.2 = (bf16[1024,2304]{1,0:T(8,128)(2,1)}, bf16[1024,2304]{1,0:T(8,128)(2,1)}) custom-call(bf16[1024,1152]{1,0:T(8,128)(2,1)} %get-tuple-element.189.values_ref.left_one, bf16[1152,2944]{1,0:T(8,128)(2,1)} %bitcast.145), custom_call_target="tpu_custom_call" | custom-call | flops 5435817984 | bytes 9437184 | tf_op jit(solution)/shard_map/feed_in/pallas_call | solution.py:473
  238.8 12.7 %feed_in.3 = (bf16[1024,2304]{1,0:T(8,128)(2,1)}, bf16[1024,2304]{1,0:T(8,128)(2,1)}) custom-call(bf16[1024,1152]{1,0:T(8,128)(2,1)} %collective-permute-done.27.values_ref.left_two, bf16[1152,2944]{1,0:T(8,128)(2,1)} %bitcast.146), custom_call_target="tpu_custom_call" | custom-call | flops 5435817984 | bytes 9437184 | tf_op jit(solution)/shard_map/feed_in/pallas_call | solution.py:473
  259.7 10.7 %out_of.7 = bf16[1024,1152]{1,0:T(8,128)(2,1)} custom-call(bf16[1024,2304]{1,0:T(8,128)(2,1)} %get-tuple-element.197.values_ref.right_two, bf16[1152,2304]{1,0:T(8,128)(2,1)} %bitcast.150), custom_call_target="tpu_custom_call" | custom-call | flops 5435817984 | bytes 4718592 | tf_op jit(solution)/shard_map/out_of/pallas_call | solution.py:555
  272.3 10.9 %out_of.6.mine_ref = f32[1024,1152]{1,0:T(8,128)} custom-call(bf16[1024,2304]{1,0:T(8,128)(2,1)} %get-tuple-element.192.values_ref.right_one, bf16[1152,2304]{1,0:T(8,128)(2,1)} %bitcast.151), custom_call_target="tpu_custom_call" | custom-call | flops 5435817984 | bytes 4718592 | tf_op jit(solution)/shard_map/out_of/pallas_call | solution.py:555
  284.6 10.6 %ends.1 = (f32[1024,1152]{1,0:T(8,128)}, bf16[1024,1152]{1,0:T(8,128)(2,1)}, f32[4,8,1152]{2,1,0:T(8,128)}, f32[16,1152]{1,0:T(8,128)}, f32[8,128]{1,0:T(8,128)}) custom-call(f32[1024,1152]{1,0:T(8,128)} %out_of.6.mine_ref, bf16[1024,1152]{1,0:T(8,128)(2,1)} %copy-done.20, f32[1024,1152]{1,0:T(8,128)} %get-tuple-element.198.hidden_ref, ...), custom_call_target="tpu_custom_call" | custom-call | flops 75497472 | bytes 18874368 | tf_op jit(solution)/shard_map/ends/pallas_call | solution.py:642
  295.7 11.1 %feed_back.2.values_ref.right_one = bf16[1024,2304]{1,0:T(8,128)(2,1)} custom-call(bf16[1024,1152]{1,0:T(8,128)(2,1)} %get-tuple-element.199.values_ref.left_one, bf16[1152,2304]{1,0:T(8,128)(2,1)} %bitcast.152, bf16[1024,2304]{1,0:T(8,128)(2,1)} %get-tuple-element.200.slope_ref), custom_call_target="tpu_custom_call" | custom-call | flops 5435817984 | bytes 9437184 | tf_op jit(solution)/shard_map/feed_back/pallas_call | solution.py:501
  308.1 18.0 %weight_grad.3 = (bf16[4,72,2304]{2,1,0:T(8,128)(2,1)}, bf16[4,72,2304]{2,1,0:T(8,128)(2,1)}, bf16[4,72,2304]{2,1,0:T(8,128)(2,1)}, bf16[4,72,2304]{2,1,0:T(8,128)(2,1)}) custom-call(s32[16]{0:T(128)} %xor.69.places, bf16[1024,1152]{1,0:T(8,128)(2,1)} %get-tuple-element.199.values_ref.left_one, bf16[1024,1152]{1,0:T(8,128)(2,1)} %copy-done.89, ...), custom_call_target="tpu_custom_call" | custom-call | flops 10871635968 | bytes 10616832 | tf_op jit(solution)/shard_map/weight_grad/pallas_call | solution.py:594
  327.6 10.8 %feed_back.3.right_two.values_ref = bf16[1024,2304]{1,0:T(8,128)(2,1)} custom-call(bf16[1024,1152]{1,0:T(8,128)(2,1)} %copy-done.89, bf16[1152,2304]{1,0:T(8,128)(2,1)} %bitcast.153, bf16[1024,2304]{1,0:T(8,128)(2,1)} %get-tuple-element.207.slope_ref), custom_call_target="tpu_custom_call" | custom-call | flops 5435817984 | bytes 9437184 | tf_op jit(solution)/shard_map/feed_back/pallas_call | solution.py:501
  338.4 10.6 %out_of.9 = bf16[1024,1152]{1,0:T(8,128)(2,1)} custom-call(bf16[1024,2304]{1,0:T(8,128)(2,1)} %feed_back.3.right_two.values_ref, bf16[1152,2944]{1,0:T(8,128)(2,1)} %bitcast.147), custom_call_target="tpu_custom_call" | custom-call | flops 5435817984 | bytes 4718592 | tf_op jit(solution)/shard_map/out_of/pallas_call | solution.py:555
  349.6 10.8 %out_of.8.mine_ref = f32[1024,1152]{1,0:T(8,128)} custom-call(bf16[1024,2304]{1,0:T(8,128)(2,1)} %feed_back.2.values_ref.right_one, bf16[1152,2944]{1,0:T(8,128)(2,1)} %bitcast.148), custom_call_target="tpu_custom_call" | custom-call | flops 5435817984 | bytes 4718592 | tf_op jit(solution)/shard_map/out_of/pallas_call | solution.py:555
  364.8 18.0 %weight_grad.4 = (bf16[4,72,2304]{2,1,0:T(8,128)(2,1)}, bf16[4,72,2304]{2,1,0:T(8,128)(2,1)}, bf16[4,72,2304]{2,1,0:T(8,128)(2,1)}, bf16[4,72,2304]{2,1,0:T(8,128)(2,1)}) custom-call(s32[16]{0:T(128)} %xor.69.places, bf16[1024,1152]{1,0:T(8,128)(2,1)} %get-tuple-element.189.values_ref.left_one, ...), custom_call_target="tpu_custom_call" | custom-call | flops 10871635968 | bytes 10616832 | tf_op jit(solution)/shard_map/weight_grad/pallas_call | solution.py:594
  384.3 15.1 %merge_heads_back.1 = (f32[1024,1152]{1,0:T(8,128)}, bf16[1024,1152]{1,0:T(8,128)(2,1)}, bf16[1024,640]{1,0:T(8,128)(2,1)}, bf16[1024,640]{1,0:T(8,128)(2,1)}, f32[4,8,1152]{2,1,0:T(8,128)}) custom-call(s32[1]{0:T(128)} %bitcast.29.core_ref, f32[1024,1152]{1,0:T(8,128)} %out_of.8.mine_ref, bf16[1024,1152]{1,0:T(8,128)(2,1)} %copy-done.17, ...), custom_call_target="tpu_custom_call" | custom-call | flops 5435817984 | bytes 18874368 | tf_op jit(solution)/shard_map/merge_heads_back/pallas_call | solution.py:642
  401.6 20.6 %attention_back.2 = (bf16[1024,1792]{1,0:T(8,128)(2,1)}, f32[8,16,512]{2,1,0:T(8,128)}) custom-call(bf16[1024,1792]{1,0:T(8,128)(2,1)} %into_heads.2.qkv_ref, bf16[1024,640]{1,0:T(8,128)(2,1)} %get-tuple-element.221.upstream_ref, f32[1024,8]{1,0:T(8,128)} %get-tuple-element.222.log_ref, f32[8,16,512]{2,1,0:T(8,128)} %pad.20.spread_ref), custom_call_target="tpu_custom_call" | custom-call | flops 5368709120 | bytes 11010048 | tf_op jit(solution)/shard_map/attention_back/pallas_call | solution.py:420
  447.1 20.6 %attention_back.3 = (bf16[1024,1792]{1,0:T(8,128)(2,1)}, f32[8,16,512]{2,1,0:T(8,128)}) custom-call(bf16[1024,1792]{1,0:T(8,128)(2,1)} %into_heads.3.qkv_ref, bf16[1024,640]{1,0:T(8,128)(2,1)} %collective-permute-done.36.upstream_ref, f32[1024,8]{1,0:T(8,128)} %get-tuple-element.233.log_ref, f32[8,16,512]{2,1,0:T(8,128)} %pad.20.spread_ref), custom_call_target="tpu_custom_call" | custom-call | flops 5368709120 | bytes 11010048 | tf_op jit(solution)/shard_map/attention_back/pallas_call | solution.py:420
  478.4 14.9 %weight_grad.5 = (bf16[4,72,1792]{2,1,0:T(8,128)(2,1)}, bf16[4,72,1792]{2,1,0:T(8,128)(2,1)}, bf16[4,72,1792]{2,1,0:T(8,128)(2,1)}, bf16[4,72,1792]{2,1,0:T(8,128)(2,1)}) custom-call(s32[16]{0:T(128)} %xor.69.places, bf16[1024,1152]{1,0:T(8,128)(2,1)} %bitcast.162, bf16[1024,1152]{1,0:T(8,128)(2,1)} %collective-permute-done.20.values_ref.left_two, ...), custom_call_target="tpu_custom_call" | custom-call | flops 8455716864 | bytes 8257536 | tf_op jit(solution)/shard_map/weight_grad/pallas_call | solution.py:594
  498.7 9.1 %out_of.10 = bf16[1024,1152]{1,0:T(8,128)(2,1)} custom-call(bf16[1024,1792]{1,0:T(8,128)(2,1)} %get-tuple-element.253.right_two.values_ref, bf16[1152,1792]{1,0:T(8,128)(2,1)} %bitcast.157), custom_call_target="tpu_custom_call" | custom-call | flops 4227858432 | bytes 4718592 | tf_op jit(solution)/shard_map/out_of/pallas_call | solution.py:555
  513.2 9.4 %out_of.11.mine_ref = f32[1024,1152]{1,0:T(8,128)} custom-call(bf16[1024,1792]{1,0:T(8,128)(2,1)} %get-tuple-element.255.right_one.values_ref, bf16[1152,1792]{1,0:T(8,128)(2,1)} %bitcast.158), custom_call_target="tpu_custom_call" | custom-call | flops 4227858432 | bytes 4718592 | tf_op jit(solution)/shard_map/out_of/pallas_call | solution.py:555
  529.9 8.6 %start_back.1 = (f32[4,8,1152]{2,1,0:T(8,128)}, f32[16,1152]{1,0:T(8,128)}) custom-call(f32[1024,1152]{1,0:T(8,128)} %out_of.11.mine_ref, bf16[1024,1152]{1,0:T(8,128)(2,1)} %copy-done.19, f32[1024,1152]{1,0:T(8,128)} %bitcast.143, f32[1024,1152]{1,0:T(8,128)} %get-tuple-element.262.d_hidden_ref, bf16[1024,16]{1,0:T(8,128)(2,1)} %bitcast.167, ...), custom_call_target="tpu_custom_call" | custom-call | flops 75497472 | bytes 18874368 | tf_op jit(solution)/shard_map/start_back/pallas_call | solution.py:642
  (589 shorter events, 368.8 us)
Async XLA Ops:
  7.2 101.2 %all-gather.5.cloned.1.call-start = ((), (), s32[]{:S(2)}) async-start(), calls=%async_computation.7 | async-start | bytes 2119680 | tf_op jit(solution)/shard_map/all_gather | solution.py:253
  29.4 30.7 %collective-permute-start.4 = (bf16[4,289,72]{2,1,0:T(8,128)(2,1)}, bf16[4,289,72]{2,1,0:T(8,128)(2,1)}, u32[]{:S(2)}, u32[]{:S(2)}) collective-permute-start(bf16[4,289,72]{2,1,0:T(8,128)(2,1)} %pad_maximum_fusion.2.refs_0_), channel_id=1, source_target_pairs={{0,2},{1,5},{2,0},{3,7},{4,6},{5,1},{6,4},{7,3},{8,10},{9,13},{10,... | collective-permute-start | bytes 499400 | tf_op jit(solution)/shard_map/ppermute | solution.py:106
  30.9 31.0 %collective-permute-start.5 = (bf16[4,289,72]{2,1,0:T(8,128)(2,1)}, bf16[4,289,72]{2,1,0:T(8,128)(2,1)}, u32[]{:S(2)}, u32[]{:S(2)}) collective-permute-start(bf16[4,289,72]{2,1,0:T(8,128)(2,1)} %pad_maximum_fusion.2.refs_0_), channel_id=1, source_target_pairs={{0,4},{1,3},{2,6},{3,1},{4,0},{5,7},{6,2},{7,5},{8,12},{9,11},{10,... | collective-permute-start | bytes 499400 | tf_op jit(solution)/shard_map/ppermute | solution.py:106
  38.2 25.1 %collective-permute-start.9 = (bf16[1,72,1792]{2,1,0:T(8,128)(2,1)}, bf16[1,72,1792]{2,1,0:T(8,128)(2,1)}, u32[]{:S(2)}, u32[]{:S(2)}) collective-permute-start(bf16[1,72,1792]{2,1,0:T(8,128)(2,1)} %bitcast.171), channel_id=1, source_target_pairs={{0,24},{1,25},{2,26},{3,27},{4,28},{5,29},{6,30},{7,31},{8,16},{9,... | collective-permute-start | bytes 774152 | tf_op jit(solution)/shard_map/ppermute | solution.py:106
  65.7 23.4 %collective-permute-start.10 = (bf16[4,72,1792]{2,1,0:T(8,128)(2,1)}, bf16[4,72,1792]{2,1,0:T(8,128)(2,1)}, u32[]{:S(2)}, u32[]{:S(2)}) collective-permute-start(bf16[4,72,1792]{2,1,0:T(8,128)(2,1)} %pad_maximum_fusion.refs_0_), channel_id=1, source_target_pairs={{0,2},{1,5},{2,0},{3,7},{4,6},{5,1},{6,4},{7,3},{8,10},{9,13},{10,... | collective-permute-start | bytes 3096584 | tf_op jit(solution)/shard_map/ppermute | solution.py:106
  66.2 23.2 %collective-permute-start.11 = (bf16[4,72,1792]{2,1,0:T(8,128)(2,1)}, bf16[4,72,1792]{2,1,0:T(8,128)(2,1)}, u32[]{:S(2)}, u32[]{:S(2)}) collective-permute-start(bf16[4,72,1792]{2,1,0:T(8,128)(2,1)} %pad_maximum_fusion.refs_0_), channel_id=1, source_target_pairs={{0,4},{1,3},{2,6},{3,1},{4,0},{5,7},{6,2},{7,5},{8,12},{9,11},{10,... | collective-permute-start | bytes 3096584 | tf_op jit(solution)/shard_map/ppermute | solution.py:106
  67.7 103.7 %all-gather.7.cloned.1.call-start = ((), (), s32[]{:S(2)}) async-start(), calls=%async_computation.8 | async-start | bytes 1658880 | tf_op jit(solution)/shard_map/all_gather | solution.py:253
  130.4 345.9 %reduce-scatter.7.cloned.1.call-start = ((), (), s32[]{:S(2)}) async-start(), calls=%async_computation.4 | async-start | bytes 1658880 | tf_op jit(solution)/shard_map/reduce_scatter | solution.py:257
  130.9 40.6 %collective-permute-start.21 = (bf16[4,72,2944]{2,1,0:T(8,128)(2,1)}, bf16[4,72,2944]{2,1,0:T(8,128)(2,1)}, u32[]{:S(2)}, u32[]{:S(2)}) collective-permute-start(bf16[4,72,2944]{2,1,0:T(8,128)(2,1)} %bitcast.164), channel_id=1, source_target_pairs={{0,2},{1,5},{2,0},{3,7},{4,6},{5,1},{6,4},{7,3},{8,10},{9,13},{10,... | collective-permute-start | bytes 5087240 | tf_op jit(solution)/shard_map/ppermute | solution.py:106
  132.4 39.0 %collective-permute-start.22 = (bf16[4,72,2944]{2,1,0:T(8,128)(2,1)}, bf16[4,72,2944]{2,1,0:T(8,128)(2,1)}, u32[]{:S(2)}, u32[]{:S(2)}) collective-permute-start(bf16[4,72,2944]{2,1,0:T(8,128)(2,1)} %bitcast.165), channel_id=1, source_target_pairs={{0,4},{1,3},{2,6},{3,1},{4,0},{5,7},{6,2},{7,5},{8,12},{9,11},{10,... | collective-permute-start | bytes 5087240 | tf_op jit(solution)/shard_map/ppermute | solution.py:106
  222.2 30.8 %collective-permute-start.29 = (bf16[4,72,2304]{2,1,0:T(8,128)(2,1)}, bf16[4,72,2304]{2,1,0:T(8,128)(2,1)S(1)}, u32[]{:S(2)}, u32[]{:S(2)}) collective-permute-start(bf16[4,72,2304]{2,1,0:T(8,128)(2,1)} %collective-permute-done.26.refs_1_), channel_id=1, source_target_pairs={{0,4},{1,3},{2,6},{3,1},{4,0},{5,7},{6,2},{7,5},{8,12},{9,11},{10,... | collective-permute-start | bytes 3981320 | tf_op jit(solution)/shard_map/ppermute | solution.py:106
  326.1 34.3 %collective-permute-start.32 = (bf16[4,72,2304]{2,1,0:T(8,128)(2,1)}, bf16[4,72,2304]{2,1,0:T(8,128)(2,1)}, u32[]{:S(2)}, u32[]{:S(2)}) collective-permute-start(bf16[4,72,2304]{2,1,0:T(8,128)(2,1)} %get-tuple-element.205), channel_id=1, source_target_pairs={{0,4},{1,3},{2,6},{3,1},{4,0},{5,7},{6,2},{7,5},{8,12},{9,11},{10,... | collective-permute-start | bytes 3981320 | tf_op jit(solution)/shard_map/ppermute | solution.py:106
  349.1 33.8 %collective-permute-start.33 = (bf16[1024,1152]{1,0:T(8,128)(2,1)}, bf16[1024,1152]{1,0:T(8,128)(2,1)S(1)}, u32[]{:S(2)}, u32[]{:S(2)}) collective-permute-start(bf16[1024,1152]{1,0:T(8,128)(2,1)} %out_of.9), channel_id=1, source_target_pairs={{0,1},{1,0},{2,3},{3,2},{4,5},{5,4},{6,7},{7,6},{8,9},{9,8},{10,11... | collective-permute-start | bytes 7077896 | tf_op jit(solution)/shard_map/ppermute | solution.py:110
  349.1 50.3 %collective-permute-start.35 = (bf16[4,72,2304]{2,1,0:T(8,128)(2,1)}, bf16[4,72,2304]{2,1,0:T(8,128)(2,1)S(1)}, u32[]{:S(2)}, u32[]{:S(2)}) collective-permute-start(bf16[4,72,2304]{2,1,0:T(8,128)(2,1)} %get-tuple-element.219), channel_id=1, source_target_pairs={{0,4},{1,3},{2,6},{3,1},{4,0},{5,7},{6,2},{7,5},{8,12},{9,11},{10,... | collective-permute-start | bytes 3981320 | tf_op jit(solution)/shard_map/ppermute | solution.py:106
  363.5 35.9 %collective-permute-start.34 = (bf16[4,72,2304]{2,1,0:T(8,128)(2,1)}, bf16[4,72,2304]{2,1,0:T(8,128)(2,1)}, u32[]{:S(2)}, u32[]{:S(2)}) collective-permute-start(bf16[4,72,2304]{2,1,0:T(8,128)(2,1)} %add_convert_fusion.7), channel_id=1, source_target_pairs={{0,2},{1,5},{2,0},{3,7},{4,6},{5,1},{6,4},{7,3},{8,10},{9,13},{10,... | collective-permute-start | bytes 3981320 | tf_op jit(solution)/shard_map/ppermute | solution.py:106
  433.5 95.0 %reduce-scatter.9.cloned.1.call-start = ((), (), s32[]{:S(2)}) async-start(), calls=%async_computation.5 | async-start | bytes 1658880 | tf_op jit(solution)/shard_map/reduce_scatter | solution.py:257
  436.7 39.7 %collective-permute-start.39 = (bf16[4,72,2304]{2,1,0:T(8,128)(2,1)}, bf16[4,72,2304]{2,1,0:T(8,128)(2,1)}, u32[]{:S(2)}, u32[]{:S(2)}) collective-permute-start(bf16[4,72,2304]{2,1,0:T(8,128)(2,1)} %add_convert_fusion.6), channel_id=1, source_target_pairs={{0,2},{1,5},{2,0},{3,7},{4,6},{5,1},{6,4},{7,3},{8,10},{9,13},{10,... | collective-permute-start | bytes 3981320 | tf_op jit(solution)/shard_map/ppermute | solution.py:106
  438.0 38.3 %collective-permute-start.40 = (bf16[4,72,2304]{2,1,0:T(8,128)(2,1)}, bf16[4,72,2304]{2,1,0:T(8,128)(2,1)}, u32[]{:S(2)}, u32[]{:S(2)}) collective-permute-start(bf16[4,72,2304]{2,1,0:T(8,128)(2,1)} %get-tuple-element.237), channel_id=1, source_target_pairs={{0,4},{1,3},{2,6},{3,1},{4,0},{5,7},{6,2},{7,5},{8,12},{9,11},{10,... | collective-permute-start | bytes 3981320 | tf_op jit(solution)/shard_map/ppermute | solution.py:106
  445.5 30.8 %collective-permute-start.41 = (bf16[4,72,640]{2,1,0:T(8,128)(2,1)}, bf16[4,72,640]{2,1,0:T(8,128)(2,1)S(1)}, u32[]{:S(2)}, u32[]{:S(2)}) collective-permute-start(bf16[4,72,640]{2,1,0:T(8,128)(2,1)} %get-tuple-element.238), channel_id=1, source_target_pairs={{0,4},{1,3},{2,6},{3,1},{4,0},{5,7},{6,2},{7,5},{8,12},{9,11},{10,... | collective-permute-start | bytes 1105928 | tf_op jit(solution)/shard_map/ppermute | solution.py:106
  497.6 111.7 %reduce-scatter.13.cloned.1.call-start = ((), (), s32[]{:S(2)}) async-start(), calls=%async_computation.9 | async-start | bytes 460800
  509.2 34.6 %collective-permute-start.51 = (bf16[4,72,1792]{2,1,0:T(8,128)(2,1)}, bf16[4,72,1792]{2,1,0:T(8,128)(2,1)}, u32[]{:S(2)}, u32[]{:S(2)}) collective-permute-start(bf16[4,72,1792]{2,1,0:T(8,128)(2,1)} %get-tuple-element.267), channel_id=1, source_target_pairs={{0,4},{1,3},{2,6},{3,1},{4,0},{5,7},{6,2},{7,5},{8,12},{9,11},{10,... | collective-permute-start | bytes 3096584 | tf_op jit(solution)/shard_map/ppermute | solution.py:106
  542.0 81.8 %collective-permute-start.74 = (bf16[72,2304]{1,0:T(8,128)(2,1)}, bf16[72,2304]{1,0:T(8,128)(2,1)}, u32[]{:S(2)}, u32[]{:S(2)}) collective-permute-start(bf16[72,2304]{1,0:T(8,128)(2,1)} %bitcast.35.refs_3_), channel_id=1, source_target_pairs={{0,1},{1,0},{2,3},{3,2},{4,5},{5,4},{6,7},{7,6},{8,9},{9,8},{10,11... | collective-permute-start | bytes 995336 | tf_op jit(solution)/shard_map/ppermute | solution.py:110
  556.0 53.4 %reduce-scatter.11.cloned.1.call-start = ((), (), s32[]{:S(2)}) async-start(), calls=%async_computation.6 | async-start | bytes 1290240 | tf_op jit(solution)/shard_map/reduce_scatter | solution.py:257
  556.0 67.7 %collective-permute-start.72 = (bf16[72,2304]{1,0:T(8,128)(2,1)}, bf16[72,2304]{1,0:T(8,128)(2,1)}, u32[]{:S(2)}, u32[]{:S(2)}) collective-permute-start(bf16[72,2304]{1,0:T(8,128)(2,1)} %bitcast.39.refs_1_), channel_id=1, source_target_pairs={{0,1},{1,0},{2,3},{3,2},{4,5},{5,4},{6,7},{7,6},{8,9},{9,8},{10,11... | collective-permute-start | bytes 995336 | tf_op jit(solution)/shard_map/ppermute | solution.py:110
  (162 other events, 1719.8 us)
Sparse Core Ops, SparseCore 0:
  67.8 38.2 all-gather.4
  130.5 32.1 all-gather.6
  433.7 30.8 reduce-scatter.6
  497.8 30.6 reduce-scatter.8
  556.1 19.0 reduce-scatter.12
  578.0 29.5 reduce-scatter.10

commit v8 on v7

--- a/solution.py
+++ b/solution.py
@@ -1188,7 +1188,7 @@
     attn_second = send(add_low(attn_second, attn_back), plane_peers((1, 2)))
     attn_third = send(attn_third, plane_peers((2, 1)))
     d_attn_mine = out_of(d_qkv, qkv_low, wide)
-    d_attn_mine, g_in, packed = tie(d_attn_mine, g_in, packed)
+    d_attn_mine, packed = tie(d_attn_mine, packed)
     packed = packed + send(packed, dp_peers(bits[-1]))
     d_mod, g_patch = image_call(
         start_back_kernel,
@@ -1212,7 +1212,9 @@
     d_keep = jnp.where(core == 0, d_modulation[:, :mod_half], d_modulation[:, mod_half:])
     d_give = jnp.where(core == 0, d_modulation[:, mod_half:], d_modulation[:, :mod_half])
     d_pair = both_cores(d_keep, swap_cores(d_give), core, 0)
-    d_pair, attn_second, attn_third, packed = tie(d_pair, attn_second, attn_third, packed)
+    d_pair, attn_second, attn_third, packed, g_in = tie(
+        d_pair, attn_second, attn_third, packed, g_in
+    )
     d_far = gather_far(d_pair)
     attn_own, d_far = tie(attn_own, d_far)
     g_qkv = far_share(add_low(add_low(attn_own, attn_third), attn_second))

time: 704 us -> 705 us (level)
    unnamed x204 -> x202, local copies, waits for them, and re-layouts: 14.7 us -> 14.9 us
where the time goes in v8:
time: 705 us; the launch traced here: 698 us
  Pallas kernels  324 us (46%)
  waiting for transfers between devices  103 us (15%)
  other arithmetic  98.7 us (14%)
  starting transfers between devices  77.8 us (11%)
  local copies, waits for them, and re-layouts  51.3 us (7%)
  between operations  21.8 us (3%)
  matrix products  21 us (3%)
    ppermute x60, waiting for transfers between devices, send(): return lax.ppermute(values, DP + ('mod',), peers)  98.3 us
    ppermute x60, starting transfers between devices, send(): return lax.ppermute(values, DP + ('mod',), peers)  72.4 us
    pallas_call x6, Pallas kernels, out_of(): pl.pallas_call(out_of_kernel, grid=(rows // tile,), in_specs=[pl.BlockSpe...  61.8 us
    pallas_call x3, Pallas kernels, weight_grad(): pl.pallas_call(weight_grad_kernel, grid_spec=pltpu.PrefetchScalarGridSpec...  50.9 us
    pallas_call x4, Pallas kernels, image_call(): pl.pallas_call(kernel, grid_spec=pltpu.PrefetchScalarGridSpec(num_scalar_...  45.6 us
    pallas_call x2, Pallas kernels, attention_back(): pl.pallas_call(functools.partial(attention_back_kernel, heads), grid=(row...  41.2 us
    pallas_call x2, Pallas kernels, attention(): pl.pallas_call(functools.partial(attention_kernel, heads), grid=(rows //...  30 us
    pallas_call x6, Pallas kernels, move_call(): pl.pallas_call(functools.partial(kernel, counts, slots), grid_spec=pltpu....  25.9 us
  transfers between devices with their start and end apart: 88, of which 38 were waited for; matrix products, arithmetic and copies ran while one was open for 16% of the time, Pallas kernels for 39%

profile of v8, /device:TPU:0, one launch (start us, length us, event | category | flops | bytes accessed | tf_op | source)
XLA Modules:
  0.0 697.7 jit_solution(4909990458366758564)
XLA Ops:
  96.8 11.6 %collective-permute-done.14.refs_3_ = bf16[4,72,1792]{2,1,0:T(8,128)(2,1)} collective-permute-done((bf16[4,72,1792]{2,1,0:T(8,128)(2,1)}, bf16[4,72,1792]{2,1,0:T(8,128)(2,1)}, u32[]{:S(2)}, u32[]{:S(2)}) %collective-permute-start.14) | collective-permute-done | bytes 1032224 | tf_op jit(solution)/shard_map/ppermute | solution.py:106
  138.1 9.2 %into_heads.2.qkv_ref = bf16[1024,1792]{1,0:T(8,128)(2,1)} custom-call(bf16[1024,1152]{1,0:T(8,128)(2,1)} %bitcast.161, bf16[1152,1792]{1,0:T(8,128)(2,1)} %bitcast.155), custom_call_target="tpu_custom_call" | custom-call | flops 4227858432 | bytes 3670016 | tf_op jit(solution)/shard_map/into_heads/pallas_call | solution.py:533
  147.3 9.2 %into_heads.3.qkv_ref = bf16[1024,1792]{1,0:T(8,128)(2,1)} custom-call(bf16[1024,1152]{1,0:T(8,128)(2,1)} %collective-permute-done.20.values_ref.left_two, bf16[1152,1792]{1,0:T(8,128)(2,1)} %bitcast.156), custom_call_target="tpu_custom_call" | custom-call | flops 4227858432 | bytes 3670016 | tf_op jit(solution)/shard_map/into_heads/pallas_call | solution.py:533
  156.5 15.0 %attention.2 = (bf16[1024,640]{1,0:T(8,128)(2,1)}, f32[1024,8]{1,0:T(8,128)}) custom-call(bf16[1024,1792]{1,0:T(8,128)(2,1)} %into_heads.3.qkv_ref, f32[8,16,512]{2,1,0:T(8,128)} %pad.20.spread_ref), custom_call_target="tpu_custom_call" | custom-call | flops 2147483648 | bytes 7340032 | tf_op jit(solution)/shard_map/attention/pallas_call | solution.py:346
  173.6 15.0 %attention.3 = (bf16[1024,640]{1,0:T(8,128)(2,1)}, f32[1024,8]{1,0:T(8,128)}) custom-call(bf16[1024,1792]{1,0:T(8,128)(2,1)} %into_heads.2.qkv_ref, f32[8,16,512]{2,1,0:T(8,128)} %pad.20.spread_ref), custom_call_target="tpu_custom_call" | custom-call | flops 2147483648 | bytes 7340032 | tf_op jit(solution)/shard_map/attention/pallas_call | solution.py:346
  207.0 11.2 %merge_heads.1 = (bf16[1024,1152]{1,0:T(8,128)(2,1)}, f32[1024,1152]{1,0:T(8,128)}, bf16[1024,1152]{1,0:T(8,128)(2,1)}) custom-call(s32[1]{0:T(128)} %bitcast.29.core_ref, bf16[1024,640]{1,0:T(8,128)(2,1)} %get-tuple-element.182.one_ref, bf16[1024,640]{1,0:T(8,128)(2,1)} %copy-done.29, bf16[1152,640]{1,0:T(8,128)(2,1)} %copy-done.11, ...), custom_call_target="tpu_custom_call" | custom-call | flops 5435817984 | bytes 18874368 | tf_op jit(solution)/shard_map/merge_heads/pallas_call | solution.py:642
  222.9 12.3 %feed_in.2 = (bf16[1024,2304]{1,0:T(8,128)(2,1)}, bf16[1024,2304]{1,0:T(8,128)(2,1)}) custom-call(bf16[1024,1152]{1,0:T(8,128)(2,1)} %get-tuple-element.189.values_ref.left_one, bf16[1152,2944]{1,0:T(8,128)(2,1)} %bitcast.145), custom_call_target="tpu_custom_call" | custom-call | flops 5435817984 | bytes 9437184 | tf_op jit(solution)/shard_map/feed_in/pallas_call | solution.py:473
  238.8 12.7 %feed_in.3 = (bf16[1024,2304]{1,0:T(8,128)(2,1)}, bf16[1024,2304]{1,0:T(8,128)(2,1)}) custom-call(bf16[1024,1152]{1,0:T(8,128)(2,1)} %collective-permute-done.27.values_ref.left_two, bf16[1152,2944]{1,0:T(8,128)(2,1)} %bitcast.146), custom_call_target="tpu_custom_call" | custom-call | flops 5435817984 | bytes 9437184 | tf_op jit(solution)/shard_map/feed_in/pallas_call | solution.py:473
  259.8 10.7 %out_of.7 = bf16[1024,1152]{1,0:T(8,128)(2,1)} custom-call(bf16[1024,2304]{1,0:T(8,128)(2,1)} %get-tuple-element.197.values_ref.right_two, bf16[1152,2304]{1,0:T(8,128)(2,1)} %bitcast.150), custom_call_target="tpu_custom_call" | custom-call | flops 5435817984 | bytes 4718592 | tf_op jit(solution)/shard_map/out_of/pallas_call | solution.py:555
  272.3 10.9 %out_of.6.mine_ref = f32[1024,1152]{1,0:T(8,128)} custom-call(bf16[1024,2304]{1,0:T(8,128)(2,1)} %get-tuple-element.192.values_ref.right_one, bf16[1152,2304]{1,0:T(8,128)(2,1)} %bitcast.151), custom_call_target="tpu_custom_call" | custom-call | flops 5435817984 | bytes 4718592 | tf_op jit(solution)/shard_map/out_of/pallas_call | solution.py:555
  284.6 10.6 %ends.1 = (f32[1024,1152]{1,0:T(8,128)}, bf16[1024,1152]{1,0:T(8,128)(2,1)}, f32[4,8,1152]{2,1,0:T(8,128)}, f32[16,1152]{1,0:T(8,128)}, f32[8,128]{1,0:T(8,128)}) custom-call(f32[1024,1152]{1,0:T(8,128)} %out_of.6.mine_ref, bf16[1024,1152]{1,0:T(8,128)(2,1)} %copy-done.20, f32[1024,1152]{1,0:T(8,128)} %get-tuple-element.198.hidden_ref, ...), custom_call_target="tpu_custom_call" | custom-call | flops 75497472 | bytes 18874368 | tf_op jit(solution)/shard_map/ends/pallas_call | solution.py:642
  295.7 11.1 %feed_back.2.values_ref.right_one = bf16[1024,2304]{1,0:T(8,128)(2,1)} custom-call(bf16[1024,1152]{1,0:T(8,128)(2,1)} %get-tuple-element.199.values_ref.left_one, bf16[1152,2304]{1,0:T(8,128)(2,1)} %bitcast.152, bf16[1024,2304]{1,0:T(8,128)(2,1)} %get-tuple-element.200.slope_ref), custom_call_target="tpu_custom_call" | custom-call | flops 5435817984 | bytes 9437184 | tf_op jit(solution)/shard_map/feed_back/pallas_call | solution.py:501
  308.2 18.0 %weight_grad.3 = (bf16[4,72,2304]{2,1,0:T(8,128)(2,1)}, bf16[4,72,2304]{2,1,0:T(8,128)(2,1)}, bf16[4,72,2304]{2,1,0:T(8,128)(2,1)}, bf16[4,72,2304]{2,1,0:T(8,128)(2,1)}) custom-call(s32[16]{0:T(128)} %xor.69.places, bf16[1024,1152]{1,0:T(8,128)(2,1)} %get-tuple-element.199.values_ref.left_one, bf16[1024,1152]{1,0:T(8,128)(2,1)} %copy-done.88, ...), custom_call_target="tpu_custom_call" | custom-call | flops 10871635968 | bytes 10616832 | tf_op jit(solution)/shard_map/weight_grad/pallas_call | solution.py:594
  327.5 10.9 %feed_back.3.right_two.values_ref = bf16[1024,2304]{1,0:T(8,128)(2,1)} custom-call(bf16[1024,1152]{1,0:T(8,128)(2,1)} %copy-done.88, bf16[1152,2304]{1,0:T(8,128)(2,1)} %bitcast.153, bf16[1024,2304]{1,0:T(8,128)(2,1)} %get-tuple-element.207.slope_ref), custom_call_target="tpu_custom_call" | custom-call | flops 5435817984 | bytes 9437184 | tf_op jit(solution)/shard_map/feed_back/pallas_call | solution.py:501
  338.4 10.6 %out_of.9 = bf16[1024,1152]{1,0:T(8,128)(2,1)} custom-call(bf16[1024,2304]{1,0:T(8,128)(2,1)} %feed_back.3.right_two.values_ref, bf16[1152,2944]{1,0:T(8,128)(2,1)} %bitcast.147), custom_call_target="tpu_custom_call" | custom-call | flops 5435817984 | bytes 4718592 | tf_op jit(solution)/shard_map/out_of/pallas_call | solution.py:555
  349.7 10.8 %out_of.8.mine_ref = f32[1024,1152]{1,0:T(8,128)} custom-call(bf16[1024,2304]{1,0:T(8,128)(2,1)} %feed_back.2.values_ref.right_one, bf16[1152,2944]{1,0:T(8,128)(2,1)} %bitcast.148), custom_call_target="tpu_custom_call" | custom-call | flops 5435817984 | bytes 4718592 | tf_op jit(solution)/shard_map/out_of/pallas_call | solution.py:555
  364.7 18.0 %weight_grad.4 = (bf16[4,72,2304]{2,1,0:T(8,128)(2,1)}, bf16[4,72,2304]{2,1,0:T(8,128)(2,1)}, bf16[4,72,2304]{2,1,0:T(8,128)(2,1)}, bf16[4,72,2304]{2,1,0:T(8,128)(2,1)}) custom-call(s32[16]{0:T(128)} %xor.69.places, bf16[1024,1152]{1,0:T(8,128)(2,1)} %get-tuple-element.189.values_ref.left_one, ...), custom_call_target="tpu_custom_call" | custom-call | flops 10871635968 | bytes 10616832 | tf_op jit(solution)/shard_map/weight_grad/pallas_call | solution.py:594
  384.2 15.1 %merge_heads_back.1 = (f32[1024,1152]{1,0:T(8,128)}, bf16[1024,1152]{1,0:T(8,128)(2,1)}, bf16[1024,640]{1,0:T(8,128)(2,1)}, bf16[1024,640]{1,0:T(8,128)(2,1)}, f32[4,8,1152]{2,1,0:T(8,128)}) custom-call(s32[1]{0:T(128)} %bitcast.29.core_ref, f32[1024,1152]{1,0:T(8,128)} %out_of.8.mine_ref, bf16[1024,1152]{1,0:T(8,128)(2,1)} %copy-done.17, ...), custom_call_target="tpu_custom_call" | custom-call | flops 5435817984 | bytes 18874368 | tf_op jit(solution)/shard_map/merge_heads_back/pallas_call | solution.py:642
  401.6 20.6 %attention_back.2 = (bf16[1024,1792]{1,0:T(8,128)(2,1)}, f32[8,16,512]{2,1,0:T(8,128)}) custom-call(bf16[1024,1792]{1,0:T(8,128)(2,1)} %into_heads.2.qkv_ref, bf16[1024,640]{1,0:T(8,128)(2,1)} %get-tuple-element.221.upstream_ref, f32[1024,8]{1,0:T(8,128)} %get-tuple-element.222.log_ref, f32[8,16,512]{2,1,0:T(8,128)} %pad.20.spread_ref), custom_call_target="tpu_custom_call" | custom-call | flops 5368709120 | bytes 11010048 | tf_op jit(solution)/shard_map/attention_back/pallas_call | solution.py:420
  447.2 20.6 %attention_back.3 = (bf16[1024,1792]{1,0:T(8,128)(2,1)}, f32[8,16,512]{2,1,0:T(8,128)}) custom-call(bf16[1024,1792]{1,0:T(8,128)(2,1)} %into_heads.3.qkv_ref, bf16[1024,640]{1,0:T(8,128)(2,1)} %collective-permute-done.36.upstream_ref, f32[1024,8]{1,0:T(8,128)} %get-tuple-element.233.log_ref, f32[8,16,512]{2,1,0:T(8,128)} %pad.20.spread_ref), custom_call_target="tpu_custom_call" | custom-call | flops 5368709120 | bytes 11010048 | tf_op jit(solution)/shard_map/attention_back/pallas_call | solution.py:420
  478.4 14.9 %weight_grad.5 = (bf16[4,72,1792]{2,1,0:T(8,128)(2,1)}, bf16[4,72,1792]{2,1,0:T(8,128)(2,1)}, bf16[4,72,1792]{2,1,0:T(8,128)(2,1)}, bf16[4,72,1792]{2,1,0:T(8,128)(2,1)}) custom-call(s32[16]{0:T(128)} %xor.69.places, bf16[1024,1152]{1,0:T(8,128)(2,1)} %bitcast.162, bf16[1024,1152]{1,0:T(8,128)(2,1)} %collective-permute-done.20.values_ref.left_two, ...), custom_call_target="tpu_custom_call" | custom-call | flops 8455716864 | bytes 8257536 | tf_op jit(solution)/shard_map/weight_grad/pallas_call | solution.py:594
  495.3 8.9 %out_of.10 = bf16[1024,1152]{1,0:T(8,128)(2,1)} custom-call(bf16[1024,1792]{1,0:T(8,128)(2,1)} %get-tuple-element.253.right_two.values_ref, bf16[1152,1792]{1,0:T(8,128)(2,1)} %bitcast.157), custom_call_target="tpu_custom_call" | custom-call | flops 4227858432 | bytes 4718592 | tf_op jit(solution)/shard_map/out_of/pallas_call | solution.py:555
  517.0 9.8 %out_of.11.mine_ref = f32[1024,1152]{1,0:T(8,128)} custom-call(bf16[1024,1792]{1,0:T(8,128)(2,1)} %get-tuple-element.255.right_one.values_ref, bf16[1152,1792]{1,0:T(8,128)(2,1)} %bitcast.158), custom_call_target="tpu_custom_call" | custom-call | flops 4227858432 | bytes 4718592 | tf_op jit(solution)/shard_map/out_of/pallas_call | solution.py:555
  528.8 8.7 %start_back.1 = (f32[4,8,1152]{2,1,0:T(8,128)}, f32[16,1152]{1,0:T(8,128)}) custom-call(f32[1024,1152]{1,0:T(8,128)} %out_of.11.mine_ref, bf16[1024,1152]{1,0:T(8,128)(2,1)} %copy-done.19, f32[1024,1152]{1,0:T(8,128)} %bitcast.143, f32[1024,1152]{1,0:T(8,128)} %get-tuple-element.259.d_hidden_ref, bf16[1024,16]{1,0:T(8,128)(2,1)} %bitcast.167, ...), custom_call_target="tpu_custom_call" | custom-call | flops 75497472 | bytes 18874368 | tf_op jit(solution)/shard_map/start_back/pallas_call | solution.py:642
  (587 shorter events, 369.5 us)
Async XLA Ops:
  7.2 101.2 %all-gather.5.cloned.1.call-start = ((), (), s32[]{:S(2)}) async-start(), calls=%async_computation.7 | async-start | bytes 2119680 | tf_op jit(solution)/shard_map/all_gather | solution.py:253
  29.4 30.7 %collective-permute-start.4 = (bf16[4,289,72]{2,1,0:T(8,128)(2,1)}, bf16[4,289,72]{2,1,0:T(8,128)(2,1)}, u32[]{:S(2)}, u32[]{:S(2)}) collective-permute-start(bf16[4,289,72]{2,1,0:T(8,128)(2,1)} %pad_maximum_fusion.2.refs_0_), channel_id=1, source_target_pairs={{0,2},{1,5},{2,0},{3,7},{4,6},{5,1},{6,4},{7,3},{8,10},{9,13},{10,... | collective-permute-start | bytes 499400 | tf_op jit(solution)/shard_map/ppermute | solution.py:106
  30.9 31.0 %collective-permute-start.5 = (bf16[4,289,72]{2,1,0:T(8,128)(2,1)}, bf16[4,289,72]{2,1,0:T(8,128)(2,1)}, u32[]{:S(2)}, u32[]{:S(2)}) collective-permute-start(bf16[4,289,72]{2,1,0:T(8,128)(2,1)} %pad_maximum_fusion.2.refs_0_), channel_id=1, source_target_pairs={{0,4},{1,3},{2,6},{3,1},{4,0},{5,7},{6,2},{7,5},{8,12},{9,11},{10,... | collective-permute-start | bytes 499400 | tf_op jit(solution)/shard_map/ppermute | solution.py:106
  38.2 25.1 %collective-permute-start.9 = (bf16[1,72,1792]{2,1,0:T(8,128)(2,1)}, bf16[1,72,1792]{2,1,0:T(8,128)(2,1)}, u32[]{:S(2)}, u32[]{:S(2)}) collective-permute-start(bf16[1,72,1792]{2,1,0:T(8,128)(2,1)} %bitcast.171), channel_id=1, source_target_pairs={{0,24},{1,25},{2,26},{3,27},{4,28},{5,29},{6,30},{7,31},{8,16},{9,... | collective-permute-start | bytes 774152 | tf_op jit(solution)/shard_map/ppermute | solution.py:106
  65.7 23.4 %collective-permute-start.10 = (bf16[4,72,1792]{2,1,0:T(8,128)(2,1)}, bf16[4,72,1792]{2,1,0:T(8,128)(2,1)}, u32[]{:S(2)}, u32[]{:S(2)}) collective-permute-start(bf16[4,72,1792]{2,1,0:T(8,128)(2,1)} %pad_maximum_fusion.refs_0_), channel_id=1, source_target_pairs={{0,2},{1,5},{2,0},{3,7},{4,6},{5,1},{6,4},{7,3},{8,10},{9,13},{10,... | collective-permute-start | bytes 3096584 | tf_op jit(solution)/shard_map/ppermute | solution.py:106
  66.2 23.2 %collective-permute-start.11 = (bf16[4,72,1792]{2,1,0:T(8,128)(2,1)}, bf16[4,72,1792]{2,1,0:T(8,128)(2,1)}, u32[]{:S(2)}, u32[]{:S(2)}) collective-permute-start(bf16[4,72,1792]{2,1,0:T(8,128)(2,1)} %pad_maximum_fusion.refs_0_), channel_id=1, source_target_pairs={{0,4},{1,3},{2,6},{3,1},{4,0},{5,7},{6,2},{7,5},{8,12},{9,11},{10,... | collective-permute-start | bytes 3096584 | tf_op jit(solution)/shard_map/ppermute | solution.py:106
  67.7 103.8 %all-gather.7.cloned.1.call-start = ((), (), s32[]{:S(2)}) async-start(), calls=%async_computation.8 | async-start | bytes 1658880 | tf_op jit(solution)/shard_map/all_gather | solution.py:253
  130.4 346.0 %reduce-scatter.7.cloned.1.call-start = ((), (), s32[]{:S(2)}) async-start(), calls=%async_computation.4 | async-start | bytes 1658880 | tf_op jit(solution)/shard_map/reduce_scatter | solution.py:257
  130.8 40.6 %collective-permute-start.21 = (bf16[4,72,2944]{2,1,0:T(8,128)(2,1)}, bf16[4,72,2944]{2,1,0:T(8,128)(2,1)}, u32[]{:S(2)}, u32[]{:S(2)}) collective-permute-start(bf16[4,72,2944]{2,1,0:T(8,128)(2,1)} %bitcast.164), channel_id=1, source_target_pairs={{0,2},{1,5},{2,0},{3,7},{4,6},{5,1},{6,4},{7,3},{8,10},{9,13},{10,... | collective-permute-start | bytes 5087240 | tf_op jit(solution)/shard_map/ppermute | solution.py:106
  132.4 39.1 %collective-permute-start.22 = (bf16[4,72,2944]{2,1,0:T(8,128)(2,1)}, bf16[4,72,2944]{2,1,0:T(8,128)(2,1)}, u32[]{:S(2)}, u32[]{:S(2)}) collective-permute-start(bf16[4,72,2944]{2,1,0:T(8,128)(2,1)} %bitcast.165), channel_id=1, source_target_pairs={{0,4},{1,3},{2,6},{3,1},{4,0},{5,7},{6,2},{7,5},{8,12},{9,11},{10,... | collective-permute-start | bytes 5087240 | tf_op jit(solution)/shard_map/ppermute | solution.py:106
  222.2 30.9 %collective-permute-start.29 = (bf16[4,72,2304]{2,1,0:T(8,128)(2,1)}, bf16[4,72,2304]{2,1,0:T(8,128)(2,1)S(1)}, u32[]{:S(2)}, u32[]{:S(2)}) collective-permute-start(bf16[4,72,2304]{2,1,0:T(8,128)(2,1)} %collective-permute-done.26.refs_1_), channel_id=1, source_target_pairs={{0,4},{1,3},{2,6},{3,1},{4,0},{5,7},{6,2},{7,5},{8,12},{9,11},{10,... | collective-permute-start | bytes 3981320 | tf_op jit(solution)/shard_map/ppermute | solution.py:106
  326.1 34.4 %collective-permute-start.32 = (bf16[4,72,2304]{2,1,0:T(8,128)(2,1)}, bf16[4,72,2304]{2,1,0:T(8,128)(2,1)}, u32[]{:S(2)}, u32[]{:S(2)}) collective-permute-start(bf16[4,72,2304]{2,1,0:T(8,128)(2,1)} %get-tuple-element.205), channel_id=1, source_target_pairs={{0,4},{1,3},{2,6},{3,1},{4,0},{5,7},{6,2},{7,5},{8,12},{9,11},{10,... | collective-permute-start | bytes 3981320 | tf_op jit(solution)/shard_map/ppermute | solution.py:106
  349.0 33.8 %collective-permute-start.33 = (bf16[1024,1152]{1,0:T(8,128)(2,1)}, bf16[1024,1152]{1,0:T(8,128)(2,1)S(1)}, u32[]{:S(2)}, u32[]{:S(2)}) collective-permute-start(bf16[1024,1152]{1,0:T(8,128)(2,1)} %out_of.9), channel_id=1, source_target_pairs={{0,1},{1,0},{2,3},{3,2},{4,5},{5,4},{6,7},{7,6},{8,9},{9,8},{10,11... | collective-permute-start | bytes 7077896 | tf_op jit(solution)/shard_map/ppermute | solution.py:110
  349.0 50.3 %collective-permute-start.35 = (bf16[4,72,2304]{2,1,0:T(8,128)(2,1)}, bf16[4,72,2304]{2,1,0:T(8,128)(2,1)S(1)}, u32[]{:S(2)}, u32[]{:S(2)}) collective-permute-start(bf16[4,72,2304]{2,1,0:T(8,128)(2,1)} %get-tuple-element.219), channel_id=1, source_target_pairs={{0,4},{1,3},{2,6},{3,1},{4,0},{5,7},{6,2},{7,5},{8,12},{9,11},{10,... | collective-permute-start | bytes 3981320 | tf_op jit(solution)/shard_map/ppermute | solution.py:106
  363.6 35.8 %collective-permute-start.34 = (bf16[4,72,2304]{2,1,0:T(8,128)(2,1)}, bf16[4,72,2304]{2,1,0:T(8,128)(2,1)}, u32[]{:S(2)}, u32[]{:S(2)}) collective-permute-start(bf16[4,72,2304]{2,1,0:T(8,128)(2,1)} %add_convert_fusion.7), channel_id=1, source_target_pairs={{0,2},{1,5},{2,0},{3,7},{4,6},{5,1},{6,4},{7,3},{8,10},{9,13},{10,... | collective-permute-start | bytes 3981320 | tf_op jit(solution)/shard_map/ppermute | solution.py:106
  433.6 110.6 %reduce-scatter.9.cloned.1.call-start = ((), (), s32[]{:S(2)}) async-start(), calls=%async_computation.5 | async-start | bytes 1658880 | tf_op jit(solution)/shard_map/reduce_scatter | solution.py:257
  436.7 39.6 %collective-permute-start.39 = (bf16[4,72,2304]{2,1,0:T(8,128)(2,1)}, bf16[4,72,2304]{2,1,0:T(8,128)(2,1)}, u32[]{:S(2)}, u32[]{:S(2)}) collective-permute-start(bf16[4,72,2304]{2,1,0:T(8,128)(2,1)} %add_convert_fusion.6), channel_id=1, source_target_pairs={{0,2},{1,5},{2,0},{3,7},{4,6},{5,1},{6,4},{7,3},{8,10},{9,13},{10,... | collective-permute-start | bytes 3981320 | tf_op jit(solution)/shard_map/ppermute | solution.py:106
  438.0 38.3 %collective-permute-start.40 = (bf16[4,72,2304]{2,1,0:T(8,128)(2,1)}, bf16[4,72,2304]{2,1,0:T(8,128)(2,1)}, u32[]{:S(2)}, u32[]{:S(2)}) collective-permute-start(bf16[4,72,2304]{2,1,0:T(8,128)(2,1)} %get-tuple-element.237), channel_id=1, source_target_pairs={{0,4},{1,3},{2,6},{3,1},{4,0},{5,7},{6,2},{7,5},{8,12},{9,11},{10,... | collective-permute-start | bytes 3981320 | tf_op jit(solution)/shard_map/ppermute | solution.py:106
  445.6 30.8 %collective-permute-start.41 = (bf16[4,72,640]{2,1,0:T(8,128)(2,1)}, bf16[4,72,640]{2,1,0:T(8,128)(2,1)S(1)}, u32[]{:S(2)}, u32[]{:S(2)}) collective-permute-start(bf16[4,72,640]{2,1,0:T(8,128)(2,1)} %get-tuple-element.238), channel_id=1, source_target_pairs={{0,4},{1,3},{2,6},{3,1},{4,0},{5,7},{6,2},{7,5},{8,12},{9,11},{10,... | collective-permute-start | bytes 1105928 | tf_op jit(solution)/shard_map/ppermute | solution.py:106
  512.9 97.4 %reduce-scatter.13.cloned.1.call-start = ((), (), s32[]{:S(2)}) async-start(), calls=%async_computation.9 | async-start | bytes 460800
  513.0 30.6 %collective-permute-start.51 = (bf16[4,72,1792]{2,1,0:T(8,128)(2,1)}, bf16[4,72,1792]{2,1,0:T(8,128)(2,1)}, u32[]{:S(2)}, u32[]{:S(2)}) collective-permute-start(bf16[4,72,1792]{2,1,0:T(8,128)(2,1)} %get-tuple-element.264), channel_id=1, source_target_pairs={{0,4},{1,3},{2,6},{3,1},{4,0},{5,7},{6,2},{7,5},{8,12},{9,11},{10,... | collective-permute-start | bytes 3096584 | tf_op jit(solution)/shard_map/ppermute | solution.py:106
  541.3 83.4 %collective-permute-start.74 = (bf16[72,2304]{1,0:T(8,128)(2,1)}, bf16[72,2304]{1,0:T(8,128)(2,1)}, u32[]{:S(2)}, u32[]{:S(2)}) collective-permute-start(bf16[72,2304]{1,0:T(8,128)(2,1)} %bitcast.35.refs_3_), channel_id=1, source_target_pairs={{0,1},{1,0},{2,3},{3,2},{4,5},{5,4},{6,7},{7,6},{8,9},{9,8},{10,11... | collective-permute-start | bytes 995336 | tf_op jit(solution)/shard_map/ppermute | solution.py:110
  556.7 53.6 %reduce-scatter.11.cloned.1.call-start = ((), (), s32[]{:S(2)}) async-start(), calls=%async_computation.6 | async-start | bytes 1290240 | tf_op jit(solution)/shard_map/reduce_scatter | solution.py:257
  566.7 58.0 %collective-permute-start.72 = (bf16[72,2304]{1,0:T(8,128)(2,1)}, bf16[72,2304]{1,0:T(8,128)(2,1)}, u32[]{:S(2)}, u32[]{:S(2)}) collective-permute-start(bf16[72,2304]{1,0:T(8,128)(2,1)} %bitcast.40.refs_1_), channel_id=1, source_target_pairs={{0,1},{1,0},{2,3},{3,2},{4,5},{5,4},{6,7},{7,6},{8,9},{9,8},{10,11... | collective-permute-start | bytes 995336 | tf_op jit(solution)/shard_map/ppermute | solution.py:110
  (161 other events, 1712.3 us)
Sparse Core Ops, SparseCore 0:
  67.9 38.2 all-gather.4
  130.5 32.1 all-gather.6
  433.7 30.8 reduce-scatter.6
  513.0 31.1 reduce-scatter.8
  556.9 19.1 reduce-scatter.12
  578.9 29.9 reduce-scatter.10
